TPU v7x, 32 devices: a whole 2x2x4 slice. The times are simulated.
32 devices in a mesh: tile: 8 (over z, y), opt: 4 (over x, core).
Axes of the slice: x: 2, y: 2, z: 4, core: 2. Of those that a mesh axis runs over, the one named last changes fastest.
Arguments:
- inputs: bfloat16 [4, 16, 24, 24, 800], P('opt', 'tile'), may hold values from -6 to 6
- cotangent: bfloat16 [4, 16, 24, 24, 800], P('opt', 'tile'), may hold values from -6 to 6
- master: float32 [16, 800, 400], P('opt', 'tile'), may hold values from -0.21875 to 0.21875
- moment_one: float32 [16, 800, 400], P('opt', 'tile'), may hold values from -512 to 512
- moment_two: float32 [16, 800, 400], P('opt', 'tile'), may hold values from 9216 to 36864
- left_basis: float32 [16, 800, 800], P('opt', None, 'tile'), as said below
- column_basis: float32 [16, 400, 400], P('opt'), as said below
- small_params: float32 [57, 800], replicated
- small_first: float32 [57, 800], replicated, may hold values from -512 to 512
- small_second: float32 [57, 800], replicated, may hold values from 9216 to 36864
- land_mask: int32 [16, 24, 24], P('tile'), may hold values 0 or 1
- tile_count: int32 [8], replicated, may hold values from 1 to 2, as said below
- neighbours: int32 [16, 8], P('tile'), may hold values from -1 to 15, as said below
- block_order: int32 [16], replicated, may hold values from 0 to 15, each once
- cell_weight: int32 [4], replicated, may hold values from 1024 to 8192
- step_count: int32 [1], replicated, may hold values from 1 to 4
Outputs:
- block_output: bfloat16 [4, 16, 24, 24, 800], P('opt', 'tile')
- input_grad: float32 [4, 16, 24, 24, 800], P('opt', 'tile')
- new_master: float32 [16, 800, 400], P('opt', 'tile')
- new_master_low: bfloat16 [16, 800, 400], P('opt', 'tile')
- new_moment_one: float32 [16, 800, 400], P('opt', 'tile')
- new_moment_two: float32 [16, 800, 400], P('opt', 'tile')
- new_small: float32 [57, 800], replicated
- new_small_first: float32 [57, 800], replicated
- new_small_second: float32 [57, 800], replicated
Inputs may be any that keep to these rules, and one draw needn't show every extreme that they name: `tile_count`: every entry is at least 1 and at most 2; some index has exactly 2. `neighbours`: entries are -1 or a live slot; empty slots have only -1; if slot a names slot b in one direction, b names a in the opposite direction. Each left_basis[s] is orthogonal. Each column_basis[s] is orthogonal.
All inputs are finite; a program needn't handle non-finite values. No bound on the sum of `land_mask` on one device may be relied on, other than what follows from the above.
Results may differ from a plain program's by a relative error of at most 0.007.
The roundings to bfloat16 on the way count: a program that leaves them out, or rounds other values in their place, can miss the bound.
Values may be sent and summed in bfloat16 or wider, within the bound.
A program may use at most 192 MiB of HBM per device.

v0:
```python
import math

import jax
import jax.numpy as jnp
from jax import lax
from jax.sharding import PartitionSpec as P

G = 16


highest_precision = lax.Precision.HIGHEST
epsilon = 1e-05
adam_eps = 1e-08
decay_rate = 0.5
small_rate = 0.05


def edge_rims(field_in):
    return (field_in[:, :3], field_in[:, -3:], field_in[:, :, :3], field_in[:, :, -3:])


def assemble(own_tiles, upper_rim, lower_rim, left_rim, right_rim, neighbours):
    total_rows = upper_rim.shape[0]
    side_len = own_tiles.shape[1]

    def take_rim(source, column):
        extended = jnp.concatenate([source, jnp.zeros((1,) + source.shape[1:], source.dtype)], 0)
        chosen = jnp.where(neighbours[:, column] < 0, total_rows, neighbours[:, column])
        return jnp.take(extended, chosen, axis=0)

    top_band = jnp.concatenate(
        [
            take_rim(lower_rim, 0)[:, :, side_len - 3 :],
            take_rim(lower_rim, 1),
            take_rim(lower_rim, 2)[:, :, :3],
        ],
        2,
    )
    mid_band = jnp.concatenate([take_rim(right_rim, 3), own_tiles, take_rim(left_rim, 4)], 2)
    bottom_band = jnp.concatenate(
        [
            take_rim(upper_rim, 5)[:, :, side_len - 3 :],
            take_rim(upper_rim, 6),
            take_rim(upper_rim, 7)[:, :, :3],
        ],
        2,
    )
    return jnp.concatenate([top_band, mid_band, bottom_band], 1)


def depthwise(padded, kernel):
    side_len = padded.shape[1] - 6
    summed = jnp.zeros(padded.shape[:1] + (side_len, side_len, padded.shape[3]), jnp.float32)
    for tap_index in range(49):
        tap_row = tap_index // 7
        tap_col = tap_index % 7
        summed = summed + kernel[tap_index] * padded[
            :, tap_row : tap_row + side_len, tap_col : tap_col + side_len
        ].astype(jnp.float32)
    return summed


def spread_back(d_padded, kernel):
    side_len = d_padded.shape[1] - 6
    summed = jnp.zeros(d_padded.shape[:1] + (side_len, side_len, d_padded.shape[3]), jnp.float32)
    for tap_index in range(49):
        tap_row = 6 - tap_index // 7
        tap_col = 6 - tap_index % 7
        summed = (
            summed
            + kernel[tap_index]
            * d_padded[:, tap_row : tap_row + side_len, tap_col : tap_col + side_len]
        )
    return summed


def per_device(
    inputs,
    cotangent,
    master,
    moment_one,
    moment_two,
    left_basis,
    column_basis,
    small_params,
    small_first,
    small_second,
    land_mask,
    tile_count,
    neighbours,
    block_order,
    cell_weight,
    step_count,
):
    position = lax.axis_index("tile")
    sample = lax.axis_index("opt")
    slot_count = inputs.shape[1]
    side_len = inputs.shape[2]
    channels = inputs.shape[4]
    cell_count = slot_count * side_len * side_len
    per_group = channels // G
    occupied_slot = (jnp.arange(slot_count) < tile_count[position]).astype(jnp.float32)
    ocean_mask = land_mask.astype(jnp.float32) * occupied_slot[:, None, None]
    flat_ocean = ocean_mask.reshape(cell_count, 1)
    weight_cells = flat_ocean[:, :, None]
    low_master = master.astype(jnp.bfloat16)
    row_gathered = lax.all_gather(low_master, "tile", axis=1, tiled=True)
    all_slots = lax.all_gather(row_gathered, "opt", axis=0, tiled=True)
    block_total = all_slots.shape[0]
    half_count = block_total // 2
    block_cols = all_slots.shape[2]
    inverse = (
        jnp.zeros((block_total,), jnp.int32)
        .at[block_order]
        .set(jnp.arange(block_total, dtype=jnp.int32))
    )
    by_block = jnp.take(all_slots, inverse, axis=0)
    w_first = by_block[:half_count].transpose(1, 0, 2).reshape(channels, half_count * block_cols)
    w_second = by_block[half_count:].transpose(0, 2, 1).reshape(half_count * block_cols, channels)
    field_in = inputs[0].astype(jnp.float32)
    masked = (ocean_mask[..., None] * field_in).astype(jnp.bfloat16)
    upper_rim, lower_rim, left_rim, right_rim = edge_rims(masked)
    upper_all, lower_all, left_all, right_all = (
        lax.all_gather(upper_rim, "tile", axis=0, tiled=True),
        lax.all_gather(lower_rim, "tile", axis=0, tiled=True),
        lax.all_gather(left_rim, "tile", axis=0, tiled=True),
        lax.all_gather(right_rim, "tile", axis=0, tiled=True),
    )
    padded = assemble(masked, upper_all, lower_all, left_all, right_all, neighbours)
    conv_out = depthwise(padded, small_params[:49]) + small_params[49]
    grouped = conv_out.reshape(cell_count, G, per_group)
    sum_first = jnp.sum(weight_cells * grouped, axis=(0, 2))
    sum_square = jnp.sum(weight_cells * grouped * grouped, axis=(0, 2))
    occupied = jnp.sum(ocean_mask)
    sum_first, sum_square, occupied = lax.psum((sum_first, sum_square, occupied), "tile")
    counted = occupied * per_group
    group_mean = sum_first / counted
    variance = sum_square / counted - group_mean * group_mean
    inv_std = lax.rsqrt(variance + epsilon)
    normed_group = (grouped - group_mean[:, None]) * inv_std[:, None]
    normed = normed_group.reshape(cell_count, channels)
    gain = small_params[50]
    shaped = (normed * gain + small_params[51]).astype(jnp.bfloat16)
    pre_act = jnp.dot(shaped, w_first, preferred_element_type=jnp.float32) + small_params[
        53:57
    ].reshape(-1)
    activation = jax.nn.gelu(pre_act).astype(jnp.bfloat16)
    branch = jnp.dot(activation, w_second, preferred_element_type=jnp.float32) + small_params[52]
    residual_in = field_in.reshape(cell_count, channels)
    block_output = (flat_ocean * (residual_in + branch)).reshape(inputs.shape).astype(jnp.bfloat16)
    weights_float = cell_weight.astype(jnp.float32)
    sample_weight = weights_float[sample] * weights_float.shape[0] / jnp.sum(weights_float)
    scaled = sample_weight * cotangent[0].astype(jnp.float32).reshape(cell_count, channels)
    d_branch = (flat_ocean * scaled).astype(jnp.bfloat16)
    d_bias_out = jnp.sum(d_branch, axis=0, dtype=jnp.float32)
    d_second = lax.dot_general(
        activation, d_branch, (((0,), (0,)), ((), ())), preferred_element_type=jnp.float32
    )
    d_act = lax.dot_general(
        d_branch, w_second, (((1,), (1,)), ((), ())), preferred_element_type=jnp.float32
    )
    gelu_value, gelu_back = jax.vjp(jax.nn.gelu, pre_act)
    d_pre = gelu_back(d_act)[0].astype(jnp.bfloat16)
    d_hidden_bias = jnp.sum(d_pre, axis=0, dtype=jnp.float32)
    d_first = lax.dot_general(
        shaped, d_pre, (((0,), (0,)), ((), ())), preferred_element_type=jnp.float32
    )
    d_shaped = lax.dot_general(
        d_pre, w_first, (((1,), (1,)), ((), ())), preferred_element_type=jnp.float32
    )
    d_gain = jnp.sum(d_shaped * normed, axis=0)
    d_shift = jnp.sum(d_shaped, axis=0)
    d_hat = (d_shaped * gain).reshape(cell_count, G, per_group)
    part_one = jnp.sum(d_hat, axis=(0, 2))
    part_two = jnp.sum(d_hat * normed_group, axis=(0, 2))
    part_one, part_two = lax.psum((part_one, part_two), "tile")
    part_one = part_one / counted
    part_two = part_two / counted
    d_conv = inv_std[:, None] * (
        d_hat - weight_cells * (part_one[:, None] + normed_group * part_two[:, None])
    )
    d_conv_tiles = d_conv.reshape(slot_count, side_len, side_len, channels)
    d_conv_bias = jnp.sum(d_conv_tiles, axis=(0, 1, 2))
    kernel_rows = []
    for tap_index in range(49):
        tap_row = tap_index // 7
        tap_col = tap_index % 7
        window = padded[:, tap_row : tap_row + side_len, tap_col : tap_col + side_len].astype(
            jnp.float32
        )
        kernel_rows.append(jnp.sum(window * d_conv_tiles, axis=(0, 1, 2)))
    d_kernel = jnp.stack(kernel_rows, 0)
    grad_upper, grad_lower, grad_left, grad_right = edge_rims(d_conv_tiles)
    upper_back, lower_back, left_back, right_back = (
        lax.all_gather(grad_upper.astype(jnp.bfloat16), "tile", axis=0, tiled=True).astype(
            grad_upper.dtype
        ),
        lax.all_gather(grad_lower.astype(jnp.bfloat16), "tile", axis=0, tiled=True).astype(
            grad_lower.dtype
        ),
        lax.all_gather(grad_left.astype(jnp.bfloat16), "tile", axis=0, tiled=True).astype(
            grad_left.dtype
        ),
        lax.all_gather(grad_right.astype(jnp.bfloat16), "tile", axis=0, tiled=True).astype(
            grad_right.dtype
        ),
    )
    d_padded = assemble(d_conv_tiles, upper_back, lower_back, left_back, right_back, neighbours)
    d_masked = spread_back(d_padded, small_params[:49])
    input_grad = (ocean_mask[..., None] * (scaled.reshape(d_masked.shape) + d_masked))[None]
    d_small = jnp.concatenate(
        [
            d_kernel,
            d_conv_bias[None],
            d_gain[None],
            d_shift[None],
            d_bias_out[None],
            d_hidden_bias.reshape(4, channels),
        ],
        0,
    )

    def pick_block(block_id, first_grad, second_grad):
        from_first = lax.dynamic_slice_in_dim(
            first_grad, jnp.minimum(block_id, half_count - 1) * block_cols, block_cols, 1
        )
        from_second = lax.dynamic_slice_in_dim(
            second_grad,
            jnp.clip(block_id - half_count, 0, half_count - 1) * block_cols,
            block_cols,
            0,
        )
        return jnp.where(block_id < half_count, from_first, from_second.T)

    per_owner = master.shape[0]
    own_ids = lax.dynamic_slice_in_dim(block_order, sample * per_owner, per_owner)
    d_first, d_second, d_small = lax.psum((d_first, d_second, d_small), ("tile", "opt"))
    owned = jax.vmap(pick_block, in_axes=(0, None, None))(own_ids, d_first, d_second)
    rotated_gradient = jnp.einsum("bdk,bdw->bkw", left_basis, owned, precision=highest_precision)
    rotated_gradient = jnp.einsum(
        "bkw,bwv->bkv", rotated_gradient, column_basis, precision=highest_precision
    )
    correction = 1.0 - jnp.power(jnp.float32(decay_rate), step_count[0].astype(jnp.float32))
    first_new = decay_rate * moment_one + (1.0 - decay_rate) * rotated_gradient
    second_new = decay_rate * moment_two + (1.0 - decay_rate) * rotated_gradient * rotated_gradient
    step_direction = first_new / correction / (jnp.sqrt(second_new / correction) + adam_eps)
    turned_update = jnp.einsum(
        "bkv,bwv->bkw", step_direction, column_basis, precision=highest_precision
    )
    change = lax.psum_scatter(
        jnp.einsum("bdk,bkw->dbw", left_basis, turned_update, precision=highest_precision).astype(
            jnp.bfloat16
        ),
        "tile",
        scatter_dimension=0,
        tiled=True,
    ).astype(jnp.float32)
    change = change.transpose(1, 0, 2)
    new_master = master - 0.5 / math.sqrt(channels) * change
    small_one = decay_rate * small_first + (1.0 - decay_rate) * d_small
    small_two = decay_rate * small_second + (1.0 - decay_rate) * d_small * d_small
    new_small = small_params - small_rate * (small_one / correction) / (
        jnp.sqrt(small_two / correction) + adam_eps
    )
    return (
        block_output,
        input_grad,
        new_master,
        new_master.astype(jnp.bfloat16),
        first_new,
        second_new,
        new_small,
        small_one,
        small_two,
    )


def solution(mesh):
    return jax.shard_map(
        per_device,
        mesh=mesh,
        in_specs=(
            P("opt", "tile", None, None, None),
            P("opt", "tile", None, None, None),
            P("opt", "tile", None),
            P("opt", "tile", None),
            P("opt", "tile", None),
            P("opt", None, "tile"),
            P("opt", None, None),
            P(),
            P(),
            P(),
            P("tile", None, None),
            P(),
            P("tile", None),
            P(),
            P(),
            P(),
        ),
        out_specs=(
            P("opt", "tile", None, None, None),
            P("opt", "tile", None, None, None),
            P("opt", "tile", None),
            P("opt", "tile", None),
            P("opt", "tile", None),
            P("opt", "tile", None),
            P(),
            P(),
            P(),
        ),
        check_vma=False,
    )
```

profile of v0, /device:TPU:8, one launch (start us, length us, event | category | flops | bytes accessed | tf_op | source)
XLA Modules:
  0.0 1281.8 jit_solution(12149835381600504237)
XLA Ops:
  22.4 51.4 %all-gather.19.cloned.1.call-done = bf16[4,800,400]{2,0,1:T(4,128)(2,1)} async-done(((bf16[4,100,400]{2,0,1:T(4,128)(2,1)}), bf16[4,800,400]{2,0,1:T(4,128)(2,1)}) %all-gather.19.cloned.1.call-update) | async-done | bytes 2560016 | tf_op jit(solution)/shard_map/all_gather | solution.py:107
  73.8 6.9 copy.114
  104.1 20.4 %all-gather.15.cloned.1.call-done = bf16[16,24,3,800]{3,1,2,0:T(8,128)(2,1)} async-done(((bf16[2,24,3,800]{3,1,2,0:T(8,128)(2,1)}), bf16[16,24,3,800]{3,1,2,0:T(8,128)(2,1)}) %all-gather.15.cloned.1.call-update) | async-done | bytes 1843216 | tf_op jit(solution)/shard_map/all_gather | solution.py:126
  131.5 43.4 %all-gather.13.cloned.1.call-done = bf16[16,24,3,800]{3,1,2,0:T(8,128)(2,1)} async-done(((bf16[2,24,3,800]{3,1,2,0:T(8,128)(2,1)}), bf16[16,24,3,800]{3,1,2,0:T(8,128)(2,1)}) %all-gather.13.cloned.1.call-update) | async-done | bytes 1843216 | tf_op jit(solution)/shard_map/all_gather | solution.py:127
  182.0 42.6 %all-gather.11.cloned.1.call-done = bf16[16,3,24,800]{3,2,1,0:T(8,128)(2,1)} async-done(((bf16[2,3,24,800]{3,2,1,0:T(8,128)(2,1)}), bf16[16,3,24,800]{3,2,1,0:T(8,128)(2,1)}) %all-gather.11.cloned.1.call-update) | async-done | bytes 1843216 | tf_op jit(solution)/shard_map/all_gather | solution.py:125
  236.1 38.2 %all-gather.17.cloned.1.call-done = bf16[16,3,24,800]{3,2,1,0:T(8,128)(2,1)} async-done(((bf16[2,3,24,800]{3,2,1,0:T(8,128)(2,1)}), bf16[16,3,24,800]{3,2,1,0:T(8,128)(2,1)}) %all-gather.17.cloned.1.call-update) | async-done | bytes 1843216 | tf_op jit(solution)/shard_map/all_gather | solution.py:124
  292.4 10.0 maximum_maximum_fusion.2
  302.8 34.8 %fusion.140 = (f32[800]{0:T(1024)S(1)}, f32[800]{0:T(1024)S(1)}, f32[2,24,24,800]{3,2,1,0:T(8,128)}) fusion(f32[2,24,24]{2,1,0:T(8,128)S(1)} %copy-done.26, f32[800]{0:T(1024)} %get-tuple-element.154, bf16[2,27,30,800]{3,2,1,0:T(8,128)(2,1)S(1)} %get-tuple-element.273, f32[800]{0:T(1024)S(1)} %copy-done.50, f32[800]{0:T(1024)S(1)} %copy-done.51, ...), kind=kLoop, calls=%fused_computation.280 | loop fusion | flops 155748800 | bytes 83575808 | tf_op jit(solution)/shard_map/reduce_sum | solution.py:133
  338.0 17.0 %all-reduce.13 = (f32[16]{0:T(128)S(1)}, f32[]{:T(128)}, f32[16]{0:T(128)S(1)}) all-reduce(f32[16]{0:T(128)S(1)} %reduce_sum.570, f32[]{:T(128)} %get-tuple-element.248, f32[16]{0:T(128)S(1)} %reduce_sum.574), channel_id=1, replica_groups=mesh['tile'=8,'opt'=4] {'tile'}, use_global_device_ids=true, to_apply=%region_2.5 | all-reduce | flops 33 | bytes 264 | tf_op jit(solution)/shard_map/psum | solution.py:135
  365.7 10.6 gather_fusion
  376.3 10.1 broadcast_select_fusion
  386.4 9.5 fusion.205
  395.9 14.4 %convolution_add_fusion = f32[1152,3200]{1,0:T(8,128)} fusion(bf16[1152,800]{1,0:T(8,128)(2,1)} %bitcast.75, bf16[800,3200]{0,1:T(8,128)(2,1)} %bitcast.72, f32[3200]{0:T(1024)S(1)} %copy-done.79), kind=kOutput, calls=%fused_computation.25 | convolution fusion | flops 5901926400 | bytes 21721600 | tf_op jit(solution)/shard_map/dot_general | solution.py:144
  410.3 19.5 %convert_reduce_fusion = (f32[3200]{0:T(1024)S(1)}, bf16[1152,3200]{1,0:T(8,128)(2,1)}) fusion(f32[1152,3200]{1,0:T(8,128)} %convolution_add_fusion, bf16[1152,800]{1,0:T(8,128)(2,1)S(1)} %bitcast.74, bf16[3200,800]{1,0:T(8,128)(2,1)S(1)} %bitcast.71), kind=kOutput, calls=%fused_computation.33 | convolution fusion | flops 5979337728 | bytes 29094400 | tf_op jit(solution)/shard_map/dot_general | solution.py:159
  429.7 16.1 %multiply_reduce_fusion.1 = (f32[800]{0:T(1024)}, f32[800]{0:T(1024)S(1)}, f32[800]{0:T(1024)S(1)}, f32[800]{0:T(1024)}, f32[1152,800]{0,1:T(8,128)}) fusion(f32[1152,800]{0,1:T(8,128)} %copy.118, f32[800]{0:T(1024)S(1)} %mul.1348, f32[800]{0:T(1024)S(1)} %sub.46, f32[800]{0:T(1024)S(1)} %copy-done.76, bf16[1152,3200]{1,0:T(8,128)(2,1)} %get-tuple-element.288, ...), kind=kOutput, calls=%fused_computation.363 | convolution fusion | flops 5906530304 | bytes 19888000 | tf_op jit(solution)/shard_map/dot_general | solution.py:168
  451.7 17.7 %all-reduce.12 = (f32[16]{0:T(128)S(1)}, f32[16]{0:T(128)S(1)}) all-reduce(f32[16]{0:T(128)S(1)} %reduce_sum.581, f32[16]{0:T(128)S(1)} %reduce_sum.578), channel_id=1, replica_groups=mesh['tile'=8,'opt'=4] {'tile'}, use_global_device_ids=true, to_apply=%region_15.18 | all-reduce | flops 32 | bytes 256 | tf_op jit(solution)/shard_map/psum | solution.py:176
  469.9 36.1 %fusion.104 = (f32[800]{0:T(1024)S(1)}, f32[800]{0:T(1024)S(1)}, f32[800]{0:T(1024)S(1)}, f32[800]{0:T(1024)S(1)}, f32[800]{0:T(1024)S(1)}, /*index=5*/f32[800]{...) fusion(bf16[2,27,30,800]{3,2,1,0:T(8,128)(2,1)} %copy-done.1, ...), kind=kLoop, calls=%fused_computation.244 | loop fusion | flops 56203200 | bytes 44311808 | tf_op jit(solution)/shard_map/reduce_sum | solution.py:191
  506.0 7.7 fusion.86
  532.8 32.3 %fusion.53 = (f32[800]{0:T(1024)S(1)}, f32[800]{0:T(1024)S(1)}, f32[800]{0:T(1024)S(1)}, f32[800]{0:T(1024)S(1)}, f32[800]{0:T(1024)S(1)}, /*index=5*/f32[800]{0...) fusion(f32[2,24,24,800]{3,2,1,0:T(8,128)} %copy-done.4, ...), kind=kLoop, calls=%fused_computation.193 | loop fusion | flops 49752000 | bytes 36921600 | tf_op jit(solution)/shard_map/reduce_sum | solution.py:191
  567.6 7.8 concatenate.209
  575.4 13.8 %fusion.177 = f32[800,3200]{1,0:T(8,128)} fusion(bf16[1152,3200]{1,0:T(8,128)(2,1)} %get-tuple-element.288, f32[1152,800]{0,1:T(8,128)} %copy.118, f32[800]{0:T(1024)S(1)} %copy-done.77, f32[800]{0:T(1024)S(1)} %mul.1348, f32[800]{0:T(1024)S(1)} %sub.46, f32[800]{0:T(1024)S(1)} %copy-done.76), kind=kOutput, calls=%fused_computation.391 | convolution fusion | flops 5902848000 | bytes 21312000 | tf_op jit(solution)/shard_map/dot_general | solution.py:165
  589.2 13.5 %fusion.178 = f32[3200,800]{0,1:T(8,128)} fusion(f32[1152,800]{0,1:T(8,128)S(1)} %copy-done.18, f32[1152]{0:T(1024)S(1)} %copy-done.80, f32[1152,3200]{1,0:T(8,128)} %convolution_add_fusion), kind=kOutput, calls=%fused_computation.392 | convolution fusion | flops 5933260800 | bytes 28676608 | tf_op jit(solution)/shard_map/dot_general | solution.py:156
  616.4 15.0 %fusion.171 = bf16[1152,800]{0,1:T(8,128)(2,1)} fusion(f32[1152,800]{0,1:T(8,128)} %copy.115, bf16[3200,800]{1,0:T(8,128)(2,1)} %bitcast.70, f32[800]{0:T(1024)S(1)} %copy-done.85, f32[1152]{0:T(1024)S(1)} %copy-done.80, f32[1152,3200]{1,0:T(8,128)} %convolution_add_fusion), kind=kOutput, calls=%fused_computation.372 | convolution fusion | flops 5935104000 | bytes 25403008 | tf_op jit(solution)/shard_map/dot_general | solution.py:148
  675.9 40.3 %all-gather.23.cloned.1.call-done = bf16[16,24,3,800]{3,1,2,0:T(8,128)(2,1)} async-done(((bf16[2,24,3,800]{3,1,2,0:T(8,128)(2,1)}), bf16[16,24,3,800]{3,1,2,0:T(8,128)(2,1)}) %all-gather.23.cloned.1.call-update) | async-done | bytes 1843216 | tf_op jit(solution)/shard_map/all_gather | solution.py:204
  732.2 8.6 maximum_maximum_fusion
  740.8 308.4 %all-reduce.19.cloned.1.call-done = (f32[800,3200]{1,0:T(8,128)}, f32[3200,800]{0,1:T(8,128)}, f32[57,800]{1,0:T(8,128)}) async-done(((f32[800,3200]{1,0:T(8,128)}, f32[3200,800]{0,1:T(8,128)}, f32[57,800]{1,0:T(8,128)}), (f32[800,3200]{1,0:T(8,128)}, f32[3200,800]{0,1:T(8,128)}, f32[57,800]{1,0:T(8,128)})) %all-reduce.19.cloned.1.call-update) | async-done | bytes 20662416 | tf_op jit(solution)/shard_map/psum | solution.py:237
  1049.2 40.0 %while.2 = (s32[]{:T(128)}, f32[800,3200]{1,0:T(8,128)}, s32[4,2]{0,1:T(2,128)S(1)}, f32[4,800,400]{1,2,0:T(8,128)}, s32[]{:T(128)}) while((s32[]{:T(128)}, f32[800,3200]{1,0:T(8,128)}, s32[4,2]{0,1:T(2,128)S(1)}, f32[4,800,400]{1,2,0:T(8,128)}, s32[]{:T(128)}) %tuple.192), condition=%wide.while_cond, body=%wide.while_body.sunk | while | flops 2 | bytes 7987305 | solution.py:224
  1089.2 12.2 copy.127
  1101.4 15.4 %while.3 = (s32[]{:T(128)}, f32[3200,800]{1,0:T(8,128)}, s32[4,2]{0,1:T(2,128)S(1)}, f32[4,400,800]{2,1,0:T(8,128)}, s32[]{:T(128)}) while((s32[]{:T(128)}, f32[3200,800]{1,0:T(8,128)}, s32[4,2]{0,1:T(2,128)S(1)}, f32[4,400,800]{2,1,0:T(8,128)}, s32[]{:T(128)}) %tuple.195), condition=%wide.while_cond.1, body=%wide.while_body.1.sunk | while | flops 2 | bytes 2867813 | solution.py:227
  1116.9 9.5 fusion.7
  1126.4 6.4 fusion.186
  1142.9 117.4 %fusion.144 = f32[1,2,24,24,800]{4,3,2,1,0:T(8,128)} fusion(f32[2,27,30,800]{3,2,1,0:T(8,128)} %get-tuple-element.270, f32[2,24,24,800]{3,2,1,0:T(8,128)} %copy-done.4, f32[2,24,3,800]{3,2,1,0:T(4,128)} %copy-done.11, f32[2,24,3,800]{3,2,1,0:T(4,128)} %copy.122, f32[2,27,30,800]{3,2,1,0:T(8,128)} %get-tuple-element.269, f32[800]{0:T(1024)} %get-tuple-element.155, ...), kind=kLoop, calls=%fused_computation.285 | loop fusion | flops 98611200 | bytes 165127808 | tf_op jit(solution)/shard_map/broadcast_in_dim | solution.py:210
  (440 shorter events, 270.7 us)
Async XLA Ops:
  7.2 1119.2 %copy-start = (f32[4,400,400]{2,1,0:T(8,128)S(1)}, f32[4,400,400]{2,1,0:T(8,128)}, u32[]{:S(2)}) copy-start(f32[4,400,400]{2,1,0:T(8,128)} %param.30) | copy-start | bytes 7680004
  7.2 66.6 %all-gather.19.cloned.1.call-start = ((), (), s32[]{:S(2)}) async-start(), calls=%async_computation.4 | async-start | bytes 3686400 | tf_op jit(solution)/shard_map/all_gather | solution.py:107
  9.5 115.0 %all-gather.15.cloned.1.call-start = ((), (), s32[]{:S(2)}) async-start(), calls=%async_computation.2 | async-start | bytes 2322432 | tf_op jit(solution)/shard_map/all_gather | solution.py:126
  12.9 85.7 %copy-start.25 = (f32[2,24,24]{2,1,0:T(8,128)}, f32[2,24,24]{2,1,0:T(8,128)S(1)}, u32[]{:S(2)}) copy-start(f32[2,24,24]{2,1,0:T(8,128)S(1)} %get-tuple-element.249) | copy-start | bytes 13828
  17.9 157.0 %all-gather.13.cloned.1.call-start = ((), (), s32[]{:S(2)}) async-start(), calls=%async_computation.1 | async-start | bytes 2322432 | tf_op jit(solution)/shard_map/all_gather | solution.py:127
  19.7 204.9 %all-gather.11.cloned.1.call-start = ((), (), s32[]{:S(2)}) async-start(), calls=%async_computation | async-start | bytes 2322432 | tf_op jit(solution)/shard_map/all_gather | solution.py:125
  21.8 252.5 %all-gather.17.cloned.1.call-start = ((), (), s32[]{:S(2)}) async-start(), calls=%async_computation.3 | async-start | bytes 2322432 | tf_op jit(solution)/shard_map/all_gather | solution.py:124
  22.4 58.4 %copy-start.27 = (f32[57,800]{1,0:T(8,128)S(1)}, f32[57,800]{1,0:T(8,128)}, u32[]{:S(2)}) copy-start(f32[57,800]{1,0:T(8,128)} %param.31) | copy-start | bytes 547204
  22.4 59.8 %copy-start.93 = (s32[16]{0:T(128)S(1)}, s32[16]{0:T(128)}, u32[]{:S(2)}) copy-start(s32[16]{0:T(128)} %param.37) | copy-start | bytes 196
  22.4 64.2 %copy-start.29 = (s32[2,8]{1,0:T(2,128)S(1)}, s32[2,8]{1,0:T(2,128)}, u32[]{:S(2)}) copy-start(s32[2,8]{1,0:T(2,128)} %param.36) | copy-start | bytes 196
  22.4 343.3 %all-gather.21.cloned.1.call-start = ((), (), s32[]{:S(2)}) async-start(), calls=%async_computation.5 | async-start | bytes 14336000 | tf_op jit(solution)/shard_map/all_gather | solution.py:108
  80.7 554.6 %all-gather.27.cloned.1.call-start = ((), (), s32[]{:S(2)}) async-start(), calls=%async_computation.8 | async-start | bytes 2322432 | tf_op jit(solution)/shard_map/all_gather | solution.py:195
  95.8 206.6 %copy-start.30 = (f32[800]{0:T(1024)}, f32[800]{0:T(1024)S(1)}, u32[]{:S(2)}) copy-start(f32[800]{0:T(1024)S(1)} %get-tuple-element.190) | copy-start | bytes 9604
  95.8 206.6 %copy-start.32 = (f32[800]{0:T(1024)}, f32[800]{0:T(1024)S(1)}, u32[]{:S(2)}) copy-start(f32[800]{0:T(1024)S(1)} %get-tuple-element.191) | copy-start | bytes 9604
  95.8 206.6 %copy-start.34 = (f32[800]{0:T(1024)}, f32[800]{0:T(1024)S(1)}, u32[]{:S(2)}) copy-start(f32[800]{0:T(1024)S(1)} %get-tuple-element.192) | copy-start | bytes 9604
  95.8 206.6 %copy-start.36 = (f32[800]{0:T(1024)}, f32[800]{0:T(1024)S(1)}, u32[]{:S(2)}) copy-start(f32[800]{0:T(1024)S(1)} %get-tuple-element.193) | copy-start | bytes 9604
  95.8 206.6 %copy-start.38 = (f32[800]{0:T(1024)}, f32[800]{0:T(1024)S(1)}, u32[]{:S(2)}) copy-start(f32[800]{0:T(1024)S(1)} %get-tuple-element.194) | copy-start | bytes 9604
  469.8 36.2 %copy-start.2 = (bf16[2,27,30,800]{3,2,1,0:T(8,128)(2,1)S(1)}, bf16[2,27,30,800]{3,2,1,0:T(8,128)(2,1)}, u32[]{:S(2)}) copy-start(bf16[2,27,30,800]{3,2,1,0:T(8,128)(2,1)} %copy-done.1) | copy-start | bytes 7776004
  469.8 36.2 %copy-start.8 = (bf16[2,24,24,800]{3,2,1,0:T(8,128)(2,1)S(1)}, bf16[2,24,24,800]{3,2,1,0:T(8,128)(2,1)}, u32[]{:S(2)}) copy-start(bf16[2,24,24,800]{3,2,1,0:T(8,128)(2,1)} %copy-done.6) | copy-start | bytes 5529604
  469.8 36.2 %copy-start.14 = (bf16[2,24,3,800]{3,2,1,0:T(4,128)(2,1)S(1)}, bf16[2,24,3,800]{3,2,1,0:T(4,128)(2,1)}, u32[]{:S(2)}) copy-start(bf16[2,24,3,800]{3,2,1,0:T(4,128)(2,1)} %copy.111) | copy-start | bytes 691204
  515.9 134.9 %all-gather.29.cloned.1.call-start = ((), (), s32[]{:S(2)}) async-start(), calls=%async_computation.9 | async-start | bytes 2322432 | tf_op jit(solution)/shard_map/all_gather | solution.py:198
  516.6 149.4 %all-gather.25.cloned.1.call-start = ((), (), s32[]{:S(2)}) async-start(), calls=%async_computation.7 | async-start | bytes 2322432 | tf_op jit(solution)/shard_map/all_gather | solution.py:201
  525.9 190.3 %all-gather.23.cloned.1.call-start = ((), (), s32[]{:S(2)}) async-start(), calls=%async_computation.6 | async-start | bytes 2322432 | tf_op jit(solution)/shard_map/all_gather | solution.py:204
  567.5 481.7 %all-reduce.19.cloned.1.call-start = ((), (), s32[]{:S(2)}) async-start(), calls=%async_computation.11 | async-start | bytes 41418752 | tf_op jit(solution)/shard_map/psum | solution.py:237
  602.7 664.6 %all-reduce.17.cloned.1.call-start = ((), (), s32[]{:S(2)}) async-start(), calls=%async_computation.10 | async-start | bytes 5734400
  675.8 48.0 %copy-start.88 = (pred[2]{0:T(512)(128)(4,1)S(1)}, pred[2]{0:T(512)(128)(4,1)}, u32[]{:S(2)}) copy-start(pred[2]{0:T(512)(128)(4,1)} %get-tuple-element.263) | copy-start | bytes 10
  675.8 49.5 %copy-start.84 = (pred[2]{0:T(512)(128)(4,1)S(1)}, pred[2]{0:T(512)(128)(4,1)}, u32[]{:S(2)}) copy-start(pred[2]{0:T(512)(128)(4,1)} %get-tuple-element.261) | copy-start | bytes 10
  675.8 50.8 %copy-start.90 = (pred[2]{0:T(512)(128)(4,1)S(1)}, pred[2]{0:T(512)(128)(4,1)}, u32[]{:S(2)}) copy-start(pred[2]{0:T(512)(128)(4,1)} %get-tuple-element.257) | copy-start | bytes 10
  675.8 51.9 %copy-start.83 = (pred[2]{0:T(512)(128)(4,1)S(1)}, pred[2]{0:T(512)(128)(4,1)}, u32[]{:S(2)}) copy-start(pred[2]{0:T(512)(128)(4,1)} %get-tuple-element.255) | copy-start | bytes 10
  675.8 53.0 %copy-start.91 = (pred[2]{0:T(512)(128)(4,1)S(1)}, pred[2]{0:T(512)(128)(4,1)}, u32[]{:S(2)}) copy-start(pred[2]{0:T(512)(128)(4,1)} %get-tuple-element.251) | copy-start | bytes 10
  675.9 54.0 %copy-start.82 = (pred[2]{0:T(512)(128)(4,1)S(1)}, pred[2]{0:T(512)(128)(4,1)}, u32[]{:S(2)}) copy-start(pred[2]{0:T(512)(128)(4,1)} %get-tuple-element.289) | copy-start | bytes 10
  1142.9 122.3 %copy-start.28 = (f32[57,800]{1,0:T(8,128)S(1)}, f32[57,800]{1,0:T(8,128)}, u32[]{:S(2)}) copy-start(f32[57,800]{1,0:T(8,128)} %param.31) | copy-start | bytes 547204
  (77 other events, 878.3 us)
Sparse Core Ops, SparseCore 0:
  10.8 63.0 all-gather.18
  76.6 47.8 all-gather.14
  127.2 47.6 all-gather.12
  176.9 47.6 all-gather.10
  226.6 47.6 all-gather.16
  275.7 74.2 all-gather.20
  516.0 50.1 all-gather.26
  568.4 47.6 all-gather.28
  618.2 47.6 all-gather.24
  668.5 47.6 all-gather.22
  723.2 325.9 all-reduce.18
  1143.0 121.0 all-reduce.16
where the time goes:
time: 1300 us; the launch traced here: 1280 us
  waiting for transfers between devices  546 us (42%)
  other arithmetic  327 us (25%)
  local copies, waits for them, and re-layouts  236 us (18%)
  matrix products  117 us (9%)
  blocking collectives  34.7 us (3%)
  between operations  19.8 us (2%)
    psum x1, waiting for transfers between devices, per_device(): lax.psum((d_first, d_second, d_small), ('tile', 'opt'))  308 us
    broadcast_in_dim x1, other arithmetic, per_device(): (ocean_mask[..., None] * (scaled.reshape(d_masked.shape) + d_masked))[None]  117 us
    reduce_sum x4, other arithmetic, per_device(): kernel_rows.append(jnp.sum(window * d_conv_tiles, axis=(0, 1, 2)))  82.2 us
    gather x32, local copies, waits for them, and re-layouts  55.4 us
    gather x16, local copies, waits for them, and re-layouts, take_rim(): return jnp.take(extended, chosen, axis=0)  53.2 us
    all_gather x1, waiting for transfers between devices, per_device(): row_gathered = lax.all_gather(low_master, 'tile', axis=1, tiled=True)  51.4 us
    all_gather x1, waiting for transfers between devices, per_device(): lax.all_gather(right_rim, 'tile', axis=0, tiled=True)  43.4 us
    all_gather x1, waiting for transfers between devices, per_device(): lax.all_gather(lower_rim, 'tile', axis=0, tiled=True)  42.6 us
  transfers between devices with their start and end apart: 12, of which 7 were waited for; matrix products, arithmetic and copies ran while one was open for 35% of the time, Pallas kernels for 0%

commit v1 on v0

v1 whole, which is shorter than its diff:
```python
import math

import jax
import jax.numpy as jnp
from jax import lax
from jax.experimental import pallas as pl
from jax.experimental.pallas import tpu as pltpu
from jax.sharding import PartitionSpec as P

GROUPS = 16
LANES = 128
RIM = 3
PITCH = 40
BF = jnp.bfloat16
F32 = jnp.float32

highest = lax.Precision.HIGHEST
epsilon = 1e-05
adam_eps = 1e-08
decay_rate = 0.5
small_rate = 0.05
ROOT = 0.7978845608028654
CUBE = 0.044715


class Grid:
    def __init__(self, n_tile, n_opt):
        b = 4 if n_tile % 16 == 0 else 2
        self.n_tile, self.n_opt = n_tile, n_opt
        self.size = {"a": n_tile // b, "b": b, "x": n_opt // 2, "c": 2}
        self.stride = {"a": b * n_opt, "b": n_opt, "x": 2, "c": 1}

    def own(self):
        t, o = lax.axis_index("tile"), lax.axis_index("opt")
        b = self.size["b"]
        return {"a": t // b, "b": t % b, "x": o // 2, "c": o % 2}

    def swap(self, value, dim, k, keep=None):
        total = self.n_tile * self.n_opt
        pairs = []
        for d in range(total):
            at = d // self.stride[dim] % self.size[dim]
            to = d + ((at ^ k) - at) * self.stride[dim]
            pairs.append((d, to))
        return lax.ppermute(value, ("tile", "opt"), pairs)

    def tile_swap(self, value, k, sends=None, takes=None):
        pairs = []
        for t in range(self.n_tile):
            u = t ^ k
            if (sends is None or t < sends) and (takes is None or u < takes):
                for o in range(self.n_opt):
                    pairs.append((t * self.n_opt + o, u * self.n_opt + o))
        return lax.ppermute(value, ("tile", "opt"), pairs)

    def total(self, value, dims):
        for dim in dims:
            k = 1
            while k < self.size[dim]:
                value = value + self.swap(value, dim, k)
                k *= 2
        return value

    def gather(self, value, dim):
        return jnp.stack([value] + [self.swap(value, dim, k) for k in range(1, self.size[dim])])


def natural(rel, own, size):
    return jnp.concatenate([lax.dynamic_slice_in_dim(rel, j ^ own, 1, 0) for j in range(size)], 0)


def store_rims(src, outs, slot, side):
    outs[slot, 0] = src[pl.ds(0, RIM * side), :].astype(BF)
    outs[slot, 1] = src[pl.ds((side - RIM) * side, RIM * side), :].astype(BF)
    for e in range(RIM):
        rows = pl.ds(e * side, side)
        outs[slot, 2, rows] = src[pl.ds(e, side, stride=side), :].astype(BF)
        outs[slot, 3, rows] = src[pl.ds(side - RIM + e, side, stride=side), :].astype(BF)


def send_out(chunk, own, rims, outs, sems, n_chunk):
    for k in range(len(outs)):

        @pl.when(chunk ^ own == k)
        def _():
            pltpu.make_async_copy(rims.at[chunk], outs[k], sems.at[chunk]).start()

    @pl.when(chunk == n_chunk - 1)
    def _():
        for c in range(n_chunk):
            pltpu.make_async_copy(rims.at[c], outs[0], sems.at[c]).wait()


def rims_of_input(inputs, mask_lanes, own_tile, n_tile):
    slots, side, _, channels = inputs.shape
    n_chunk = -(-channels // LANES)

    def kernel(own_ref, x_ref, m_ref, *rest):
        outs, (cells, rims, sems) = rest[:n_tile], rest[n_tile:]
        chunk = pl.program_id(0)
        for s in range(slots):
            for i in range(side):
                cells[pl.ds(i * side, side), :] = (
                    x_ref[s, i].astype(F32) * m_ref[s, pl.ds(i * side, side), :]
                )
            store_rims(cells, rims.at[chunk], s, side)
        send_out(chunk, own_ref[0], rims, outs, sems, n_chunk)

    piece = (slots, 4, RIM * side, LANES)
    return pl.pallas_call(
        kernel,
        grid_spec=pltpu.PrefetchScalarGridSpec(
            num_scalar_prefetch=1,
            grid=(n_chunk,),
            in_specs=[
                pl.BlockSpec((slots, side, side, LANES), lambda c, _: (0, 0, 0, c)),
                pl.BlockSpec((slots, side * side, LANES), lambda c, _: (0, 0, 0)),
            ],
            out_specs=[pl.BlockSpec(memory_space=pl.ANY)] * n_tile,
            scratch_shapes=[
                pltpu.VMEM((side * side, LANES), F32),
                pltpu.VMEM((n_chunk,) + piece, BF),
                pltpu.SemaphoreType.DMA((n_chunk,)),
            ],
        ),
        out_shape=[jax.ShapeDtypeStruct(piece, BF)] * n_tile,
        compiler_params=pltpu.CompilerParams(vmem_limit_bytes=32 << 20),
        name="rims_of_input",
    )(own_tile, inputs, mask_lanes)


def pick_halos(pieces, neighbours_rel, own_tile, side):
    n_tile = len(pieces)
    slots = pieces[0].shape[0]
    band = RIM * side

    def kernel(own_ref, nbr_ref, *rest):
        takes, outs, (held, sems) = rest[:n_tile], rest[n_tile : 2 * n_tile], rest[2 * n_tile :]
        own = own_ref[0]
        copies = [pltpu.make_async_copy(takes[k], held.at[k], sems.at[k]) for k in range(n_tile)]
        for c in copies:
            c.start()
        for c in copies:
            c.wait()
        for k in range(n_tile):
            for s in range(slots):

                def rim(direction, which):
                    slot = nbr_ref[(k * slots + s) * 8 + direction]
                    at = jnp.maximum(slot, 0)
                    value = held[(at // slots) ^ own, at % slots, which].astype(F32)
                    return jnp.where(slot >= 0, value, 0.0)

                for to, (direction, which) in enumerate(((1, 1), (6, 0), (3, 3), (4, 2))):
                    outs[k][s, to] = rim(direction, which).astype(BF)
                for corner, (direction, which, first) in enumerate(
                    ((0, 1, side - RIM), (2, 1, 0), (5, 0, side - RIM), (7, 0, 0))
                ):
                    value = rim(direction, which)
                    rows = [value[e * side + first : e * side + first + RIM] for e in range(RIM)]
                    rows.append(jnp.zeros((16 - RIM * RIM, LANES), F32))
                    outs[k][s, 4, pl.ds(16 * corner, 16)] = jnp.concatenate(rows, 0).astype(BF)
                outs[k][s, 4, pl.ds(64, band - 64)] = jnp.zeros((band - 64, LANES), BF)

    return pl.pallas_call(
        kernel,
        grid_spec=pltpu.PrefetchScalarGridSpec(
            num_scalar_prefetch=2,
            grid=(1,),
            in_specs=[pl.BlockSpec(memory_space=pl.ANY)] * n_tile,
            out_specs=[pl.BlockSpec((slots, 5, band, LANES), lambda i, *_: (0, 0, 0, 0))] * n_tile,
            scratch_shapes=[
                pltpu.VMEM((n_tile, slots, 4, band, LANES), BF),
                pltpu.SemaphoreType.DMA((n_tile,)),
            ],
        ),
        out_shape=[jax.ShapeDtypeStruct((slots, 5, band, LANES), BF)] * n_tile,
        compiler_params=pltpu.CompilerParams(vmem_limit_bytes=32 << 20),
        name="pick_halos",
    )(own_tile, neighbours_rel, *pieces)


def exchange_halos(grid, rims, neighbours_rel, own_tile, side, n_chunk):
    arrived = [rims[0]] + [
        grid.tile_swap(rims[k], k, takes=n_chunk) for k in range(1, grid.n_tile)
    ]
    halos = pick_halos(arrived, neighbours_rel, own_tile, side)
    return [halos[0]] + [grid.tile_swap(halos[k], k, sends=n_chunk) for k in range(1, grid.n_tile)]


def fill_halo(pad, halo, side):
    last = side + RIM
    up, down, left, right, corner = (halo(k) for k in range(5))
    for e in range(RIM):
        rows = slice(e * side, e * side + side)
        pad[pl.ds(e * PITCH + 8, side), :] = up[rows]
        pad[pl.ds((last + e) * PITCH + 8, side), :] = down[rows]
        pad[pl.ds(RIM * PITCH + 8 - RIM + e, side, stride=PITCH), :] = left[rows]
        pad[pl.ds(RIM * PITCH + 8 + side + e, side, stride=PITCH), :] = right[rows]
    places = ((0, 8 - RIM), (0, 8 + side), (last, 8 - RIM), (last, 8 + side))
    for k, (row, col) in enumerate(places):
        for e in range(RIM):
            at = 16 * k + RIM * e
            pad[pl.ds((row + e) * PITCH + col, RIM), :] = corner[at : at + RIM]


def conv_pass(pad, side, weight, emit):
    for block in range(side // 8):
        sums = [None] * side
        for b in range(7):
            taps = [weight(a, b) for a in range(7)]
            for r in range(side + 2 * RIM):
                cells = pad[pl.ds(r * PITCH + 8 - RIM + b + 8 * block, 8), :]
                for a in range(7):
                    i = r - a
                    if 0 <= i < side:
                        term = taps[a] * cells
                        sums[i] = term if sums[i] is None else sums[i] + term
        emit(block, sums)


def load_halos(first, halos, held, sems):
    @pl.when(first)
    def _():
        copies = [pltpu.make_async_copy(h, held.at[k], sems.at[k]) for k, h in enumerate(halos)]
        for c in copies:
            c.start()
        for c in copies:
            c.wait()


def conv_cost(n_chunk, slots, side, nbytes):
    return pl.CostEstimate(
        flops=n_chunk * slots * side * side * LANES * 98 * 100, bytes_accessed=nbytes, transcendentals=0
    )


def conv_forward(inputs, mask_lanes, halos, taps, own_tile):
    slots, side, _, channels = inputs.shape
    n_chunk = -(-channels // LANES)
    n_tile = len(halos)

    def kernel(own_ref, x_ref, m_ref, w_ref, *rest):
        given, (o_ref, s_ref), (pad, held, sems) = rest[:n_tile], rest[n_tile : n_tile + 2], rest[n_tile + 2 :]
        chunk, slot = pl.program_id(0), pl.program_id(1)
        load_halos((chunk == 0) & (slot == 0), given, held, sems)
        for i in range(side):
            pad[pl.ds((i + RIM) * PITCH + 8, side), :] = (
                x_ref[0, i].astype(F32) * m_ref[0, pl.ds(i * side, side), :]
            )
        fill_halo(pad, lambda k: held[chunk ^ own_ref[0], slot, k].astype(F32), side)
        bias = w_ref[49]
        totals = [jnp.zeros((8, LANES), F32), jnp.zeros((8, LANES), F32)]

        def emit(block, sums):
            for i in range(side):
                value = sums[i] + bias
                rows = pl.ds(i * side + 8 * block, 8)
                o_ref[0, rows, :] = value
                weighted = m_ref[0, rows, :] * value
                totals[0] = totals[0] + weighted
                totals[1] = totals[1] + weighted * value

        conv_pass(pad, side, lambda a, b: w_ref[7 * a + b], emit)
        s_ref[0, 0], s_ref[0, 1] = totals

    cells = side * side
    return pl.pallas_call(
        kernel,
        grid_spec=pltpu.PrefetchScalarGridSpec(
            num_scalar_prefetch=1,
            grid=(n_chunk, slots),
            in_specs=[
                pl.BlockSpec((1, side, side, LANES), lambda c, s, _: (s, 0, 0, c)),
                pl.BlockSpec((1, cells, LANES), lambda c, s, _: (s, 0, 0)),
                pl.BlockSpec((50, 8, LANES), lambda c, s, _: (0, 0, c)),
            ]
            + [pl.BlockSpec(memory_space=pl.ANY)] * n_tile,
            out_specs=[
                pl.BlockSpec((1, cells, LANES), lambda c, s, _: (s, 0, c)),
                pl.BlockSpec((1, 2, 8, LANES), lambda c, s, _: (s, 0, 0, c)),
            ],
            scratch_shapes=[
                pltpu.VMEM(((side + 2 * RIM) * PITCH, LANES), F32),
                pltpu.VMEM((n_tile,) + halos[0].shape, BF),
                pltpu.SemaphoreType.DMA((n_tile,)),
            ],
        ),
        out_shape=[
            jax.ShapeDtypeStruct((slots, cells, channels), F32),
            jax.ShapeDtypeStruct((slots, 2, 8, channels), F32),
        ],
        cost_estimate=conv_cost(n_chunk, slots, side, 10 << 20),
        compiler_params=pltpu.CompilerParams(vmem_limit_bytes=32 << 20),
        name="conv_forward",
    )(own_tile, inputs, mask_lanes, taps, *halos)


def conv_gradient(d_shaped, conv_out, mask_lanes, coefs, own_tile, n_tile, side):
    slots, cells, channels = d_shaped.shape
    n_chunk = -(-channels // LANES)

    def kernel(own_ref, d_ref, v_ref, m_ref, c_ref, o_ref, *rest):
        outs, (held, rims, sems) = rest[:n_tile], rest[n_tile:]
        chunk = pl.program_id(0)
        one, two, three = c_ref[0, :1], c_ref[1, :1], c_ref[2, :1]
        for s in range(slots):
            value = d_ref[s] * one - m_ref[s] * (two + three * v_ref[s])
            o_ref[s] = value
            held[...] = value
            store_rims(held, rims.at[chunk], s, side)
        send_out(chunk, own_ref[0], rims, outs, sems, n_chunk)

    piece = (slots, 4, RIM * side, LANES)
    block = pl.BlockSpec((slots, cells, LANES), lambda c, _: (0, 0, c))
    return pl.pallas_call(
        kernel,
        grid_spec=pltpu.PrefetchScalarGridSpec(
            num_scalar_prefetch=1,
            grid=(n_chunk,),
            in_specs=[
                block,
                block,
                pl.BlockSpec((slots, cells, LANES), lambda c, _: (0, 0, 0)),
                pl.BlockSpec((3, 8, LANES), lambda c, _: (0, 0, c)),
            ],
            out_specs=[block] + [pl.BlockSpec(memory_space=pl.ANY)] * n_tile,
            scratch_shapes=[
                pltpu.VMEM((cells, LANES), F32),
                pltpu.VMEM((n_chunk,) + piece, BF),
                pltpu.SemaphoreType.DMA((n_chunk,)),
            ],
        ),
        out_shape=[jax.ShapeDtypeStruct((slots, cells, channels), F32)]
        + [jax.ShapeDtypeStruct(piece, BF)] * n_tile,
        compiler_params=pltpu.CompilerParams(vmem_limit_bytes=32 << 20),
        name="conv_gradient",
    )(own_tile, d_shaped, conv_out, mask_lanes, coefs)


def tap_gradient(inputs, mask_lanes, halos, d_conv, own_tile):
    slots, side, _, channels = inputs.shape
    n_chunk = -(-channels // LANES)
    n_tile = len(halos)
    cells = side * side

    def kernel(own_ref, x_ref, m_ref, d_ref, *rest):
        given, o_ref, (pad, held, sums, sems) = rest[:n_tile], rest[n_tile], rest[n_tile + 1 :]
        chunk, slot = pl.program_id(0), pl.program_id(1)
        load_halos((chunk == 0) & (slot == 0), given, held, sems)
        for i in range(side):
            pad[pl.ds((i + RIM) * PITCH + 8, side), :] = (
                x_ref[0, i].astype(F32) * m_ref[0, pl.ds(i * side, side), :]
            )
        fill_halo(pad, lambda k: held[chunk ^ own_ref[0], slot, k].astype(F32), side)

        @pl.when(slot == 0)
        def _():
            sums[...] = jnp.zeros_like(sums)

        for block in range(side // 8):
            grads = [d_ref[0, pl.ds(i * side + 8 * block, 8), :] for i in range(side)]
            total = grads[0]
            for i in range(1, side):
                total = total + grads[i]
            sums[49] += total
            for b in range(7):
                taps = [None] * 7
                for r in range(side + 2 * RIM):
                    window = pad[pl.ds(r * PITCH + 8 - RIM + b + 8 * block, 8), :]
                    for a in range(7):
                        i = r - a
                        if 0 <= i < side:
                            term = window * grads[i]
                            taps[a] = term if taps[a] is None else taps[a] + term
                for a in range(7):
                    sums[7 * a + b] += taps[a]

        @pl.when(slot == slots - 1)
        def _():
            o_ref[...] = jnp.sum(sums[...], axis=1)

    return pl.pallas_call(
        kernel,
        grid_spec=pltpu.PrefetchScalarGridSpec(
            num_scalar_prefetch=1,
            grid=(n_chunk, slots),
            in_specs=[
                pl.BlockSpec((1, side, side, LANES), lambda c, s, _: (s, 0, 0, c)),
                pl.BlockSpec((1, cells, LANES), lambda c, s, _: (s, 0, 0)),
                pl.BlockSpec((1, cells, LANES), lambda c, s, _: (s, 0, c)),
            ]
            + [pl.BlockSpec(memory_space=pl.ANY)] * n_tile,
            out_specs=pl.BlockSpec((50, LANES), lambda c, s, _: (0, c)),
            scratch_shapes=[
                pltpu.VMEM(((side + 2 * RIM) * PITCH, LANES), F32),
                pltpu.VMEM((n_tile,) + halos[0].shape, BF),
                pltpu.VMEM((50, 8, LANES), F32),
                pltpu.SemaphoreType.DMA((n_tile,)),
            ],
        ),
        out_shape=jax.ShapeDtypeStruct((50, channels), F32),
        cost_estimate=conv_cost(n_chunk, slots, side, 10 << 20),
        compiler_params=pltpu.CompilerParams(vmem_limit_bytes=32 << 20),
        name="tap_gradient",
    )(own_tile, inputs, mask_lanes, d_conv, *halos)


def conv_backward(d_conv, halos, cotangent, mask_lanes, taps, weight_lanes, own_tile):
    slots, side, _, channels = cotangent.shape
    n_chunk = -(-channels // LANES)
    n_tile = len(halos)
    cells = side * side

    def kernel(own_ref, d_ref, g_ref, m_ref, w_ref, l_ref, *rest):
        given, o_ref, (pad, held, sems) = rest[:n_tile], rest[n_tile], rest[n_tile + 1 :]
        chunk, slot = pl.program_id(0), pl.program_id(1)
        load_halos((chunk == 0) & (slot == 0), given, held, sems)
        for i in range(side):
            pad[pl.ds((i + RIM) * PITCH + 8, side), :] = d_ref[0, pl.ds(i * side, side), :]
        fill_halo(pad, lambda k: held[chunk ^ own_ref[0], slot, k].astype(F32), side)
        weight = l_ref[...]

        def emit(block, sums):
            for i in range(side):
                rows = pl.ds(i * side + 8 * block, 8)
                scaled = weight * g_ref[0, i, pl.ds(8 * block, 8), :].astype(F32)
                o_ref[0, rows, :] = m_ref[0, rows, :] * (scaled + sums[i])

        conv_pass(pad, side, lambda a, b: w_ref[7 * (6 - a) + 6 - b], emit)

    return pl.pallas_call(
        kernel,
        grid_spec=pltpu.PrefetchScalarGridSpec(
            num_scalar_prefetch=1,
            grid=(n_chunk, slots),
            in_specs=[
                pl.BlockSpec((1, cells, LANES), lambda c, s, _: (s, 0, c)),
                pl.BlockSpec((1, side, side, LANES), lambda c, s, _: (s, 0, 0, c)),
                pl.BlockSpec((1, cells, LANES), lambda c, s, _: (s, 0, 0)),
                pl.BlockSpec((50, 8, LANES), lambda c, s, _: (0, 0, c)),
                pl.BlockSpec((8, LANES), lambda c, s, _: (0, 0)),
            ]
            + [pl.BlockSpec(memory_space=pl.ANY)] * n_tile,
            out_specs=pl.BlockSpec((1, cells, LANES), lambda c, s, _: (s, 0, c)),
            scratch_shapes=[
                pltpu.VMEM(((side + 2 * RIM) * PITCH, LANES), F32),
                pltpu.VMEM((n_tile,) + halos[0].shape, BF),
                pltpu.SemaphoreType.DMA((n_tile,)),
            ],
        ),
        out_shape=jax.ShapeDtypeStruct((slots, cells, channels), F32),
        cost_estimate=conv_cost(n_chunk, slots, side, 12 << 20),
        compiler_params=pltpu.CompilerParams(vmem_limit_bytes=32 << 20),
        name="conv_backward",
    )(own_tile, d_conv, cotangent, mask_lanes, taps, weight_lanes, *halos)


def spread_lanes(value, parts, width):
    rows, channels = value.shape
    run = channels // parts
    if run == width:
        return value
    gap = jnp.zeros((rows, width - run), value.dtype)
    pieces = []
    for t in range(parts):
        pieces += [value[:, t * run : (t + 1) * run], gap]
    return jnp.concatenate(pieces, 1)


def close_lanes(value, parts, run):
    width = value.shape[1] // parts
    if run == width:
        return value
    return jnp.concatenate([value[:, t * width : t * width + run] for t in range(parts)], 1)


def arrange(body, args, specs, rows, channels, parts, width, name):
    step = 3 * LANES if rows % (3 * LANES) == 0 else LANES

    def kernel(*refs):
        given, (gap_ref, turned_ref, sum_ref) = refs[: len(args)], refs[len(args) :]
        low = body(*given).astype(BF)
        value = low.astype(F32)
        gap_ref[...] = spread_lanes(value, parts, width).astype(BF)
        turned_ref[...] = value.T.astype(BF)

        @pl.when(pl.program_id(0) == 0)
        def _():
            sum_ref[...] = jnp.zeros_like(sum_ref)

        sum_ref[...] += jnp.sum(value, axis=0, keepdims=True)

    return pl.pallas_call(
        kernel,
        grid=(rows // step,),
        in_specs=specs(step),
        out_specs=[
            pl.BlockSpec((step, parts * width), lambda i: (i, 0)),
            pl.BlockSpec((channels, step), lambda i: (0, i)),
            pl.BlockSpec((1, channels), lambda i: (0, 0)),
        ],
        out_shape=[
            jax.ShapeDtypeStruct((rows, parts * width), BF),
            jax.ShapeDtypeStruct((channels, rows), BF),
            jax.ShapeDtypeStruct((1, channels), F32),
        ],
        compiler_params=pltpu.CompilerParams(vmem_limit_bytes=48 << 20),
        name=name,
    )(*args)


def feed_forward(inverse, place, shaped, shaped_t, d_branch, d_branch_t, hidden_bias, weights, grid, run, piece_rows):
    rows, depth = shaped.shape
    channels = shaped_t.shape[0]
    half, _, cols = hidden_bias.shape
    pairs = len(weights)
    n_tile = grid.n_tile
    width = depth // n_tile
    side_b, side_a, side_x = grid.size["b"], grid.size["a"], grid.size["x"]
    per_owner = 2 * pairs
    tile_rows = 3 * LANES if rows % (3 * LANES) == 0 else LANES
    flat = [w for pair in weights for w in pair]

    def kernel(inv_ref, place_ref, s_ref, st_ref, d_ref, dt_ref, hb_ref, *rest):
        given = rest[: 2 * pairs]
        branch_ref, ds_ref, keep_ref, send_ref, bias_ref = rest[2 * pairs : 2 * pairs + 5]
        packed, first, second, act, dpre, grads, sems, out_sems = rest[2 * pairs + 5 :]
        step = pl.program_id(0)
        own_a, own_b, own_x, own_c = (place_ref[i] for i in range(4))

        def where(slot):
            owner, inside = slot // per_owner, slot % per_owner
            return (owner // 2) ^ own_x, (owner % 2) ^ own_c, inside // 2, inside % 2

        def fetch(h, buffer):
            for which in range(2):
                rel_x, rel_c, pair, _ = where(inv_ref[h + which * half])
                for m in range(pairs):
                    for c in range(2):

                        @pl.when((pair == m) & (rel_c == c))
                        def _():
                            for t in range(n_tile):
                                rel_a, rel_b = (t // side_b) ^ own_a, (t % side_b) ^ own_b
                                if m % 2 == 0:
                                    at = (rel_b * side_x + rel_x) * side_a + rel_a
                                else:
                                    at = (rel_x * side_b + rel_b) * side_a + rel_a
                                pltpu.make_async_copy(
                                    given[2 * m + c].at[at],
                                    packed.at[buffer, which, pl.ds(t * width, width)],
                                    sems.at[buffer, which, t],
                                ).start()

        @pl.when(step == 0)
        def _():
            fetch(0, 0)
            grads[:, :, pl.ds(channels, grads.shape[2] - channels), :] = jnp.zeros(
                (2, grads.shape[1], grads.shape[2] - channels, 2 * cols), BF
            )

        @pl.when(step + 1 < half)
        def _():
            fetch(step + 1, (step + 1) % 2)

        now = step % 2
        slots = [where(inv_ref[step + which * half]) for which in range(2)]
        for which, held in enumerate((first, second)):
            for t in range(n_tile):
                pltpu.make_async_copy(
                    given[0].at[0], packed.at[now, which, pl.ds(t * width, width)], sems.at[now, which, t]
                ).wait()
            for parity in range(2):

                @pl.when(slots[which][3] == parity)
                def _():
                    held[...] = packed[now, which, :, parity * cols : (parity + 1) * cols]

        hidden = hb_ref[0]
        total = jnp.zeros((1, cols), F32)
        across = (((1,), (1,)), ((), ()))
        for i in range(rows // tile_rows):
            at = pl.ds(i * tile_rows, tile_rows)
            pre = jnp.dot(s_ref[at, :], first[...], preferred_element_type=F32) + hidden
            d_act = jnp.dot(d_ref[at, :], second[...], preferred_element_type=F32)
            square = pre * pre
            bend = jnp.tanh(ROOT * pre * (1.0 + CUBE * square))
            half_up = 0.5 * (1.0 + bend)
            low = (pre * half_up).astype(BF)
            slope = half_up + (0.5 * ROOT) * pre * (1.0 - bend * bend) * (1.0 + (3.0 * CUBE) * square)
            back = (d_act * slope).astype(BF)
            act[at, :] = low
            dpre[at, :] = back
            total = total + jnp.sum(back.astype(F32), axis=0, keepdims=True)
            out_add = lax.dot_general(low, second[...], across, preferred_element_type=F32)
            in_add = lax.dot_general(back, first[...], across, preferred_element_type=F32)

            @pl.when(step == 0)
            def _():
                branch_ref[at, :] = out_add
                ds_ref[at, :] = in_add

            @pl.when(step > 0)
            def _():
                branch_ref[at, :] += out_add
                ds_ref[at, :] += in_add

        bias_ref[0] = total
        for which, (left, right) in enumerate(((st_ref, dpre), (dt_ref, act))):
            rel_x, rel_c, pair, half_of_pair = slots[which]
            value = jnp.dot(left[...], right[...], preferred_element_type=F32).astype(BF)
            for parity in range(2):

                @pl.when(half_of_pair == parity)
                def _():
                    grads[rel_c, rel_x * pairs + pair, pl.ds(0, channels), parity * cols : (parity + 1) * cols] = value

        @pl.when(step == half - 1)
        def _():
            copies = []
            for c, out in enumerate((keep_ref, send_ref)):
                copies.append(pltpu.make_async_copy(grads.at[c], out, out_sems.at[c]))
            for c in copies:
                c.start()
            for c in copies:
                c.wait()

    whole = lambda *shape: pl.BlockSpec(shape, lambda h, *_: (0,) * len(shape))
    grad_shape = (side_x * pairs, piece_rows * n_tile, 2 * cols)
    return pl.pallas_call(
        kernel,
        grid_spec=pltpu.PrefetchScalarGridSpec(
            num_scalar_prefetch=2,
            grid=(half,),
            in_specs=[
                whole(rows, depth),
                whole(channels, rows),
                whole(rows, depth),
                whole(channels, rows),
                pl.BlockSpec((1, 1, cols), lambda h, *_: (h, 0, 0)),
            ]
            + [pl.BlockSpec(memory_space=pl.ANY)] * len(flat),
            out_specs=[
                whole(rows, depth),
                whole(rows, depth),
                pl.BlockSpec(memory_space=pl.ANY),
                pl.BlockSpec(memory_space=pl.ANY),
                pl.BlockSpec((1, 1, cols), lambda h, *_: (h, 0, 0)),
            ],
            scratch_shapes=[
                pltpu.VMEM((2, 2, depth, 2 * cols), BF),
                pltpu.VMEM((depth, cols), BF),
                pltpu.VMEM((depth, cols), BF),
                pltpu.VMEM((rows, cols), BF),
                pltpu.VMEM((rows, cols), BF),
                pltpu.VMEM((2,) + grad_shape, BF),
                pltpu.SemaphoreType.DMA((2, 2, n_tile)),
                pltpu.SemaphoreType.DMA((2,)),
            ],
        ),
        out_shape=[
            jax.ShapeDtypeStruct((rows, depth), F32),
            jax.ShapeDtypeStruct((rows, depth), F32),
            jax.ShapeDtypeStruct(grad_shape, BF),
            jax.ShapeDtypeStruct(grad_shape, BF),
            jax.ShapeDtypeStruct((half, 1, cols), F32),
        ],
        cost_estimate=pl.CostEstimate(
            flops=12 * rows * channels * half * cols, bytes_accessed=40 << 20, transcendentals=rows * half * cols
        ),
        compiler_params=pltpu.CompilerParams(vmem_limit_bytes=63 << 20),
        name="feed_forward",
    )(inverse, place, shaped, shaped_t, d_branch, d_branch_t, hidden_bias, *flat)


def close_out(branch, d_shaped, inputs, conv_out, mask_lanes, out_bias, parts, run):
    rows, channels = inputs.shape
    depth = branch.shape[1]
    step = 3 * LANES if rows % (3 * LANES) == 0 else LANES

    def kernel(b_ref, d_ref, x_ref, v_ref, m_ref, o_ref, out_ref, ds_ref, sum_ref):
        branch_here = close_lanes(b_ref[...], parts, run) + o_ref[...]
        out_ref[...] = (m_ref[:, :1] * (x_ref[...].astype(F32) + branch_here)).astype(BF)
        grads = close_lanes(d_ref[...], parts, run)
        ds_ref[...] = grads

        @pl.when(pl.program_id(0) == 0)
        def _():
            sum_ref[...] = jnp.zeros_like(sum_ref)

        sum_ref[0] += jnp.sum(grads, axis=0, keepdims=True)
        sum_ref[1] += jnp.sum(grads * v_ref[...], axis=0, keepdims=True)

    line = lambda n: pl.BlockSpec((step, n), lambda i: (i, 0))
    return pl.pallas_call(
        kernel,
        grid=(rows // step,),
        in_specs=[
            line(depth),
            line(depth),
            line(channels),
            line(channels),
            line(LANES),
            pl.BlockSpec((1, channels), lambda i: (0, 0)),
        ],
        out_specs=[line(channels), line(channels), pl.BlockSpec((2, 1, channels), lambda i: (0, 0, 0))],
        out_shape=[
            jax.ShapeDtypeStruct((rows, channels), BF),
            jax.ShapeDtypeStruct((rows, channels), F32),
            jax.ShapeDtypeStruct((2, 1, channels), F32),
        ],
        compiler_params=pltpu.CompilerParams(vmem_limit_bytes=60 << 20),
        name="close_out",
    )(branch, d_shaped, inputs, conv_out, mask_lanes, out_bias)


def up_to(value, unit):
    return -(-value // unit) * unit


def pack_pairs(value):
    slots, rows, cols = value.shape
    return value.reshape(slots // 2, 2, rows, cols).transpose(0, 2, 1, 3).reshape(slots // 2, rows, 2 * cols)


def unpack_pairs(value):
    pairs, rows, cols = value.shape
    return value.reshape(pairs, rows, 2, cols // 2).transpose(0, 2, 1, 3).reshape(2 * pairs, rows, cols // 2)


def gather_weights(grid, packed):
    gathered = []
    for m in range(packed.shape[0]):
        value = packed[m]
        for dim in ("a", "x", "b") if m % 2 == 0 else ("a", "b", "x"):
            value = grid.gather(value, dim)
        value = value.reshape((-1,) + packed.shape[1:])
        gathered.append((value, grid.swap(value, "c", 1)))
    return gathered


def add_up(parts):
    total = parts[0].astype(F32)
    for part in parts[1:]:
        total = total + part.astype(F32)
    return total.astype(BF)


def take(value, index, axis):
    return lax.dynamic_index_in_dim(value, index, axis, keepdims=False)


def reduce_gradients(grid, own, keep, send, pairs):
    size = grid.size
    whole, cols = keep.shape[1:]
    piece = whole // grid.n_tile
    both = add_up([keep, grid.swap(send, "c", 1)]).reshape(size["x"], pairs, size["b"], size["a"] * piece, cols)
    results = []
    for m in range(pairs):
        value = both[:, m]
        for dim in ("x", "b") if m % 2 == 0 else ("b", "x"):
            if dim == "x":
                value = add_up([value[0]] + [grid.swap(value[k], "x", k) for k in range(1, size["x"])])
            else:
                axis = value.ndim - 3
                others = [
                    grid.swap(take(value, own["b"] ^ k, axis), "b", k) for k in range(1, size["b"])
                ]
                value = add_up([take(value, own["b"], axis)] + others)
        value = value.reshape(size["a"], piece, cols)
        others = [grid.swap(take(value, own["a"] ^ k, 0), "a", k) for k in range(1, size["a"])]
        results.append(add_up([take(value, own["a"], 0)] + others))
    return results


def gather_gradients(grid, own, pieces):
    wholes = []
    for value in pieces:
        value = natural(grid.gather(value, "a"), own["a"], grid.size["a"])
        value = value.reshape((-1,) + value.shape[2:])
        value = natural(grid.gather(value, "b"), own["b"], grid.size["b"])
        wholes.append(value.reshape((-1,) + value.shape[2:]))
    return jnp.stack(wholes)


def per_device(
    grid,
    inputs,
    cotangent,
    master,
    moment_one,
    moment_two,
    left_basis,
    column_basis,
    small_params,
    small_first,
    small_second,
    land_mask,
    tile_count,
    neighbours,
    block_order,
    cell_weight,
    step_count,
):
    own = grid.own()
    position = lax.axis_index("tile")
    sample = lax.axis_index("opt")
    own_tile = jnp.reshape(position, (1,)).astype(jnp.int32)
    inputs, cotangent = inputs[0], cotangent[0]
    slots, side, _, channels = inputs.shape
    cells = side * side
    rows = slots * cells
    n_tile = grid.n_tile
    n_chunk = -(-channels // LANES)
    per_group = channels // GROUPS
    per_owner, run, cols = master.shape
    pairs = per_owner // 2
    block_total = block_order.shape[0]
    half = block_total // 2
    width = up_to(run, 16)

    live = (jnp.arange(slots) < tile_count[position]).astype(F32)
    mask = (land_mask.astype(F32) * live[:, None, None]).reshape(slots, cells)
    mask_lanes = jnp.broadcast_to(mask[:, :, None], (slots, cells, LANES))
    flat_mask = mask_lanes.reshape(rows, LANES)
    taps = jnp.broadcast_to(small_params[:50, None, :], (50, 8, channels))
    neighbours_rel = jnp.stack(
        [neighbours] + [grid.tile_swap(neighbours, k) for k in range(1, n_tile)]
    ).reshape(-1)

    low_master = jnp.pad(pack_pairs(master.astype(BF)), ((0, 0), (0, width - run), (0, 0)))
    rims = rims_of_input(inputs, mask_lanes, own_tile, n_tile)
    halos = exchange_halos(grid, rims, neighbours_rel, own_tile, side, n_chunk)
    weights = gather_weights(grid, low_master)

    weights_float = cell_weight.astype(F32)
    sample_weight = weights_float[sample] * weights_float.shape[0] / jnp.sum(weights_float)
    weight_lanes = jnp.broadcast_to(sample_weight, (8, LANES))
    weight_row = jnp.broadcast_to(sample_weight, (1, LANES))
    flat_cotangent = cotangent.reshape(rows, channels)

    def d_branch_body(g_ref, m_ref, w_ref):
        return m_ref[:, :1] * (w_ref[:, :1] * g_ref[...].astype(F32))

    d_branch, d_branch_t, d_out_bias = arrange(
        d_branch_body,
        (flat_cotangent, flat_mask, weight_row),
        lambda step: [
            pl.BlockSpec((step, channels), lambda i: (i, 0)),
            pl.BlockSpec((step, LANES), lambda i: (i, 0)),
            pl.BlockSpec((1, LANES), lambda i: (0, 0)),
        ],
        rows,
        channels,
        n_tile,
        width,
        "arrange_d_branch",
    )
    low_left = left_basis.astype(BF).reshape(per_owner, n_tile, run, run)
    left_rel = [take(low_left, position, 1)] + [
        grid.tile_swap(take(low_left, position ^ k, 1), k) for k in range(1, n_tile)
    ]
    left_rows = jnp.concatenate(left_rel, 2)

    conv_out, sums = conv_forward(inputs, mask_lanes, halos, taps, own_tile)
    sums = jnp.sum(sums, axis=(0, 2))
    occupied = jnp.broadcast_to(jnp.sum(mask), (1, channels))
    sums = grid.total(jnp.concatenate([sums, occupied], 0), ("b", "a"))
    counted = sums[2, 0] * per_group
    by_group = sums[:2].reshape(2, GROUPS, per_group).sum(2)
    group_mean = by_group[0] / counted
    variance = by_group[1] / counted - group_mean * group_mean
    inv_std = jnp.repeat(lax.rsqrt(variance + epsilon), per_group)
    mean = jnp.repeat(group_mean, per_group)
    gain, shift = small_params[50], small_params[51]
    norm_coefs = jnp.stack([inv_std, mean * inv_std, gain, shift])

    def shaped_body(v_ref, c_ref):
        normed = v_ref[...] * c_ref[0:1] - c_ref[1:2]
        return normed * c_ref[2:3] + c_ref[3:4]

    flat_conv = conv_out.reshape(rows, channels)
    shaped, shaped_t, _ = arrange(
        shaped_body,
        (flat_conv, norm_coefs),
        lambda step: [
            pl.BlockSpec((step, channels), lambda i: (i, 0)),
            pl.BlockSpec((4, channels), lambda i: (0, 0)),
        ],
        rows,
        channels,
        n_tile,
        width,
        "arrange_shaped",
    )

    block_ids = jnp.arange(block_total, dtype=jnp.int32)
    inverse = jnp.sum(
        jnp.where(block_order[None, :] == block_ids[:, None], block_ids[None, :], 0), axis=1
    ).astype(jnp.int32)
    place = jnp.stack([own["a"], own["b"], own["x"], own["c"]]).astype(jnp.int32)
    hidden_bias = small_params[53:57].reshape(half, 1, cols)
    piece_rows = up_to(channels // n_tile, 8)
    branch, d_shaped, grads_keep, grads_send, d_hidden = feed_forward(
        inverse, place, shaped, shaped_t, d_branch, d_branch_t, hidden_bias, weights, grid, run, piece_rows
    )
    block_output, d_shaped, d_sums = close_out(
        branch, d_shaped, inputs.reshape(rows, channels), flat_conv, flat_mask, small_params[52:53], n_tile, run
    )
    pieces = reduce_gradients(grid, own, grads_keep, grads_send, pairs)

    d_shift = d_sums[0, 0]
    d_gain = inv_std * (d_sums[1, 0] - mean * d_shift)
    parts = grid.total(jnp.stack([gain * d_shift, gain * d_gain]), ("b", "a"))
    parts = jnp.repeat(parts.reshape(2, GROUPS, per_group).sum(2) / counted, per_group, axis=1)
    grad_coefs = jnp.stack(
        [
            inv_std * gain,
            inv_std * (parts[0] - mean * inv_std * parts[1]),
            inv_std * inv_std * parts[1],
        ]
    )
    d_conv, *grad_rims = conv_gradient(
        d_shaped.reshape(slots, cells, channels),
        conv_out,
        mask_lanes,
        jnp.broadcast_to(grad_coefs[:, None, :], (3, 8, channels)),
        own_tile,
        n_tile,
        side,
    )
    grad_halos = exchange_halos(grid, grad_rims, neighbours_rel, own_tile, side, n_chunk)
    d_taps = tap_gradient(inputs, mask_lanes, halos, d_conv, own_tile)
    input_grad = conv_backward(d_conv, grad_halos, cotangent, mask_lanes, taps, weight_lanes, own_tile)

    correction = 1.0 - jnp.power(F32(decay_rate), step_count[0].astype(F32))
    d_small = jnp.concatenate(
        [d_taps, d_gain[None], d_shift[None], d_out_bias, d_hidden.reshape(4, channels)], 0
    )
    d_small = grid.total(d_small, ("c", "x", "b", "a"))
    small_one = decay_rate * small_first + (1.0 - decay_rate) * d_small
    small_two = decay_rate * small_second + (1.0 - decay_rate) * d_small * d_small
    new_small = small_params - small_rate * (small_one / correction) / (
        jnp.sqrt(small_two / correction) + adam_eps
    )

    owned = unpack_pairs(gather_gradients(grid, own, pieces)[:, :channels])
    rotated = jnp.einsum("bdk,bdw->bkw", left_basis, owned.astype(F32), precision=highest)
    rotated = jnp.einsum("bkw,bwv->bkv", rotated, column_basis, precision=highest)
    first_new = decay_rate * moment_one + (1.0 - decay_rate) * rotated
    second_new = decay_rate * moment_two + (1.0 - decay_rate) * rotated * rotated
    direction = first_new / correction / (jnp.sqrt(second_new / correction) + adam_eps)
    turned = jnp.einsum("bkv,bwv->bkw", direction, column_basis, precision=highest).astype(BF)
    turned = grid.gather(grid.gather(pack_pairs(turned), "a"), "b")
    turned = turned.transpose(2, 1, 0, 3, 4).reshape(pairs, n_tile * run, 2 * cols)
    change = jnp.einsum("bdk,bkw->bdw", left_rows, unpack_pairs(turned), preferred_element_type=F32)
    new_master = master - 0.5 / math.sqrt(channels) * change
    return (
        block_output.reshape((1,) + inputs.shape),
        input_grad.reshape((1,) + inputs.shape),
        new_master,
        new_master.astype(BF),
        first_new,
        second_new,
        new_small,
        small_one,
        small_two,
    )


def solution(mesh):
    grid = Grid(mesh.shape["tile"], mesh.shape["opt"])

    def step(*args):
        return per_device(grid, *args)

    return jax.shard_map(
        step,
        mesh=mesh,
        in_specs=(
            P("opt", "tile", None, None, None),
            P("opt", "tile", None, None, None),
            P("opt", "tile", None),
            P("opt", "tile", None),
            P("opt", "tile", None),
            P("opt", None, "tile"),
            P("opt", None, None),
            P(),
            P(),
            P(),
            P("tile", None, None),
            P(),
            P("tile", None),
            P(),
            P(),
            P(),
        ),
        out_specs=(
            P("opt", "tile", None, None, None),
            P("opt", "tile", None, None, None),
            P("opt", "tile", None),
            P("opt", "tile", None),
            P("opt", "tile", None),
            P("opt", "tile", None),
            P(),
            P(),
            P(),
        ),
        check_vma=False,
    )
```

time: 1300 us -> 750 us (0.58)
  waiting for transfers between devices: 546 us -> 190 us
  other arithmetic: 327 us -> 50.8 us
  Pallas kernels: 0 us -> 181 us
  starting transfers between devices: 0.49 us -> 165 us
  local copies, waits for them, and re-layouts: 236 us -> 134 us
  matrix products: 117 us -> 16.2 us
  blocking collectives: 34.7 us -> 0 us
  between operations: 19.8 us -> 5.29 us
    psum x1 -> x0, waiting for transfers between devices: 308 us -> none  [per_device(): lax.psum((d_first, d_second, d_small), ('tile', 'opt'))]
    all_gather x10 -> x0, waiting for transfers between devices: 236 us -> none  [the longest x1 51.4 us: per_device(): row_gathered = lax.all_gather(low_master, 'tile', axis=1, tiled=True)]
    ppermute x0 -> x88, waiting for transfers between devices: none -> 190 us  [the longest x46 117 us: swap(): return lax.ppermute(value, ('tile', 'opt'), pairs)]
    pallas_call x0 -> x11, Pallas kernels: none -> 181 us  [the longest x1 93.7 us: feed_forward(): pl.pallas_call(kernel, grid_spec=pltpu.PrefetchScalarGridSpec(num_scalar_...]
    ppermute x0 -> x88, starting transfers between devices: none -> 165 us  [the longest x42 106 us: tile_swap(): return lax.ppermute(value, ('tile', 'opt'), pairs)]
    reduce_sum x11 -> x5, other arithmetic: 124 us -> 1.65 us  [the longest x1 0.74 us: per_device(): occupied = jnp.broadcast_to(jnp.sum(mask), (1, channels))]
    gather x49 -> x0, local copies, waits for them, and re-layouts: 119 us -> none
    broadcast_in_dim x2 -> x0, other arithmetic: 117 us -> none  [the longest x1 117 us: per_device(): (ocean_mask[..., None] * (scaled.reshape(d_masked.shape) + d_masked))[None]]
  transfers between devices with their start and end apart: 12 -> 88, of which waited for: 7 -> 36; matrix products, arithmetic and copies ran while one was open for 35% -> 20% of each run, Pallas kernels for 0% -> 12%
where the time goes in v1:
time: 750 us; the launch traced here: 742 us
  waiting for transfers between devices  190 us (25%)
  Pallas kernels  181 us (24%)
  starting transfers between devices  165 us (22%)
  local copies, waits for them, and re-layouts  134 us (18%)
  other arithmetic  50.8 us (7%)
  matrix products  16.2 us (2%)
    ppermute x46, waiting for transfers between devices, swap(): return lax.ppermute(value, ('tile', 'opt'), pairs)  117 us
    ppermute x42, starting transfers between devices, tile_swap(): return lax.ppermute(value, ('tile', 'opt'), pairs)  106 us
    pallas_call x1, Pallas kernels, feed_forward(): pl.pallas_call(kernel, grid_spec=pltpu.PrefetchScalarGridSpec(num_scalar_...  93.7 us
    ppermute x42, waiting for transfers between devices, tile_swap(): return lax.ppermute(value, ('tile', 'opt'), pairs)  72.4 us
    ppermute x46, starting transfers between devices, swap(): return lax.ppermute(value, ('tile', 'opt'), pairs)  59 us
    unnamed x174, local copies, waits for them, and re-layouts  42.2 us
    ppermute x5, local copies, waits for them, and re-layouts, swap(): return lax.ppermute(value, ('tile', 'opt'), pairs)  30.5 us
    another operation x8, local copies, waits for them, and re-layouts, gather(): jnp.stack([value] + [self.swap(value, dim, k) for k in range(1, self.size...  26.4 us
  transfers between devices with their start and end apart: 88, of which 36 were waited for; matrix products, arithmetic and copies ran while one was open for 20% of the time, Pallas kernels for 12%

profile of v1, /device:TPU:8, one launch (start us, length us, event | category | flops | bytes accessed | tf_op | source)
XLA Modules:
  0.0 742.4 jit_solution(14494794379024076377)
XLA Ops:
  14.9 5.1 collective-permute-done.31
  20.0 14.1 %collective-permute-done.32 = bf16[112,800]{0,1:T(8,128)(2,1)S(1)} collective-permute-done((bf16[112,800]{0,1:T(8,128)(2,1)S(1)}, bf16[112,800]{0,1:T(8,128)(2,1)S(1)}, u32[]{:S(2)}, u32[]{:S(2)}) %collective-permute-start.32) | collective-permute-done | bytes 179232 | tf_op jit(solution)/shard_map/ppermute | solution.py:45
  58.7 7.0 collective-permute-done.27
  83.7 14.1 %collective-permute-done.34 = bf16[2,4,112,800]{3,2,1,0:T(8,128)(2,1)} collective-permute-done((bf16[2,4,112,800]{3,2,1,0:T(8,128)(2,1)}, bf16[2,4,112,800]{3,2,1,0:T(8,128)(2,1)}, u32[]{:S(2)}, u32[]{:S(2)}) %collective-permute-start.34) | collective-permute-done | bytes 1433632 | tf_op jit(solution)/shard_map/ppermute | solution.py:45
  107.7 5.7 copy.195
  121.3 5.7 copy.190
  128.7 8.0 %collective-permute-start.12 = (bf16[2,4,72,128]{3,2,1,0:T(8,128)(2,1)}, bf16[2,4,72,128]{3,2,1,0:T(8,128)(2,1)S(1)}, u32[]{:S(2)}, u32[]{:S(2)}) collective-permute-start(bf16[2,4,72,128]{3,2,1,0:T(8,128)(2,1)} %get-tuple-element.63), channel_id=1, source_target_pairs={{0,24},{1,25},{2,26},{3,27},{8,16},{9,17},{10,18},{11,19},{12,20},... | collective-permute-start | bytes 442376 | tf_op jit(solution)/shard_map/ppermute | solution.py:54
  142.4 6.9 collective-permute-done.12.rest_6_
  157.1 4.6 collective-permute-done.9.rest_3_
  182.7 9.6 %collective-permute-done.17.rest_4_ = bf16[2,5,72,128]{3,2,1,0:T(8,128)(2,1)S(1)} collective-permute-done((bf16[2,5,72,128]{3,2,1,0:T(8,128)(2,1)S(1)}, bf16[2,5,72,128]{3,2,1,0:T(8,128)(2,1)S(1)}, u32[]{:S(2)}, u32[]{:S(2)}) %collective-permute-start.17) | collective-permute-done | bytes 184352 | tf_op jit(solution)/shard_map/ppermute | solution.py:54
  198.3 6.9 collective-permute-done.19.rest_6_
  206.0 17.6 %conv_forward.1 = (f32[2,576,800]{2,1,0:T(8,128)S(1)}, f32[2,2,8,800]{3,2,1,0:T(8,128)S(1)}) custom-call(s32[1]{0:T(128)} %bitcast.4.own_ref, bf16[2,24,24,800]{3,2,1,0:T(8,128)(2,1)S(1)} %bitcast.189, f32[2,576,128]{2,1,0:T(8,128)S(1)} %broadcast_in_dim.65.m_ref, f32[50,8,800]{2,1,0:T(8,128)S(1)} %broadcast_in_dim.66.w_ref, ...), custom_call_target="tpu_custom_call" | custom-call | flops 10115481600 | bytes 10485760 | tf_op jit(solution)/shard_map/conv_forward/pallas_call | solution.py:268
  249.3 5.1 arrange_shaped.1
  256.9 93.7 %feed_forward.1 = (f32[1152,896]{1,0:T(8,128)}, f32[1152,896]{1,0:T(8,128)}, bf16[4,832,800]{2,1,0:T(8,128)(2,1)}, bf16[4,832,800]{2,1,0:T(8,128)(2,1)}, f32[8,1,400]{2,1,0:T(1,128)}) custom-call(s32[16]{0:T(128)} %select_reduce_fusion.inv_ref, s32[4]{0:T(128)} %pad_add_fusion.1.place_ref, bf16[1152,896]{1,0:T(8,128)(2,1)} %copy-done.12, ...), custom_call_target="tpu_custom_call" | custom-call | flops 35389440000 | bytes 41943040 | tf_op jit(solution)/shard_map/feed_forward/pallas_call | solution.py:631
  350.6 10.0 %copy.205 = bf16[4,832,800]{1,2,0:T(8,128)(2,1)} copy(bf16[4,832,800]{2,1,0:T(8,128)(2,1)} %get-tuple-element.102) | data formatting | bytes 10649600 | tf_op jit(solution)/shard_map/feed_forward/pallas_call | solution.py:631
  361.3 11.5 %close_out.1 = (bf16[1152,800]{1,0:T(8,128)(2,1)}, f32[1152,800]{1,0:T(8,128)}, f32[2,1,800]{2,1,0:T(1,128)}) custom-call(f32[1152,896]{1,0:T(8,128)} %get-tuple-element.79.b_ref, f32[1152,896]{1,0:T(8,128)} %get-tuple-element.80.d_ref, bf16[1152,800]{1,0:T(8,128)(2,1)} %bitcast.187, f32[1152,800]{1,0:T(8,128)} %bitcast.186, f32[1152,128]{1,0:T(8,128)} %copy-done.4, ...), custom_call_target="tpu_custom_call" | custom-call | tf_op jit(solution)/shard_map/close_out/pallas_call | solution.py:696
  379.3 19.8 %copy.206 = bf16[4,832,800]{2,1,0:T(8,128)(2,1)} copy(bf16[4,832,800]{1,2,0:T(8,128)(2,1)} %collective-permute-done.60) | data formatting | bytes 10649600 | tf_op jit(solution)/shard_map/ppermute | solution.py:45
  399.1 5.9 add_convert_fusion
  422.3 17.9 %collective-permute-done.61 = bf16[2,416,800]{2,1,0:T(8,128)(2,1)} collective-permute-done((bf16[2,416,800]{2,1,0:T(8,128)(2,1)}, bf16[2,416,800]{2,1,0:T(8,128)(2,1)}, u32[]{:S(2)}, u32[]{:S(2)}) %collective-permute-start.61) | collective-permute-done | bytes 1331232 | tf_op jit(solution)/shard_map/ppermute | solution.py:45
  449.0 17.6 %tap_gradient.1 = f32[50,800]{1,0:T(8,128)S(1)} custom-call(s32[1]{0:T(128)} %bitcast.4.own_ref, bf16[2,24,24,800]{3,2,1,0:T(8,128)(2,1)S(1)} %bitcast.190, f32[2,576,128]{2,1,0:T(8,128)S(1)} %broadcast_in_dim.65.m_ref, f32[2,576,800]{2,1,0:T(8,128)S(1)} %get-tuple-element.84.d_ref, bf16[2,5,72,128]{3,2,1,0:T(8,128)(2,1)S(1)} %copy-done.16, ...), custom_call_target="tpu_custom_call" | custom-call | flops 10115481600 | bytes 10485760 | tf_op jit(solution)/shard_map/tap_gradient/pallas_call | solution.py:383
  491.9 10.6 %collective-permute-done.65 = bf16[104,800]{1,0:T(8,128)(2,1)S(1)} collective-permute-done((bf16[104,800]{1,0:T(8,128)(2,1)S(1)}, bf16[104,800]{1,0:T(8,128)(2,1)S(1)}, u32[]{:S(2)}, u32[]{:S(2)}) %collective-permute-start.65) | collective-permute-done | bytes 166432 | tf_op jit(solution)/shard_map/ppermute | solution.py:45
  507.9 9.7 %collective-permute-done.74 = bf16[104,800]{1,0:T(8,128)(2,1)S(1)} collective-permute-done((bf16[104,800]{1,0:T(8,128)(2,1)S(1)}, bf16[104,800]{1,0:T(8,128)(2,1)S(1)}, u32[]{:S(2)}, u32[]{:S(2)}) %collective-permute-start.74) | collective-permute-done | bytes 166432 | tf_op jit(solution)/shard_map/ppermute | solution.py:45
  523.9 10.6 %collective-permute-done.68 = bf16[104,800]{1,0:T(8,128)(2,1)S(1)} collective-permute-done((bf16[104,800]{1,0:T(8,128)(2,1)S(1)}, bf16[104,800]{1,0:T(8,128)(2,1)S(1)}, u32[]{:S(2)}, u32[]{:S(2)}) %collective-permute-start.68) | collective-permute-done | bytes 166432 | tf_op jit(solution)/shard_map/ppermute | solution.py:45
  545.2 5.0 collective-permute-start.42
  563.6 4.8 collective-permute-start.44
  605.2 6.6 fusion.9
  626.1 4.7 collective-permute-start.47
  634.2 21.4 %collective-permute-done.47.rest_2_ = bf16[2,5,72,128]{3,2,1,0:T(8,128)(2,1)S(1)} collective-permute-done((bf16[2,5,72,128]{3,2,1,0:T(8,128)(2,1)S(1)}, bf16[2,5,72,128]{3,2,1,0:T(8,128)(2,1)S(1)}, u32[]{:S(2)}, u32[]{:S(2)}) %collective-permute-start.47) | collective-permute-done | bytes 184352 | tf_op jit(solution)/shard_map/ppermute | solution.py:54
  663.6 4.7 collective-permute-start.51
  668.3 4.6 collective-permute-start.52
  686.8 8.8 %collective-permute-done.51.rest_6_ = bf16[2,5,72,128]{3,2,1,0:T(8,128)(2,1)} collective-permute-done((bf16[2,5,72,128]{3,2,1,0:T(8,128)(2,1)S(1)}, bf16[2,5,72,128]{3,2,1,0:T(8,128)(2,1)}, u32[]{:S(2)}, u32[]{:S(2)}) %collective-permute-start.51) | collective-permute-done | bytes 184352 | tf_op jit(solution)/shard_map/ppermute | solution.py:54
  702.3 18.4 %conv_backward.1 = f32[2,576,800]{2,1,0:T(8,128)} custom-call(s32[1]{0:T(128)} %bitcast.4.own_ref, f32[2,576,800]{2,1,0:T(8,128)S(1)} %copy-done.10, bf16[2,24,24,800]{3,2,1,0:T(8,128)(2,1)S(1)} %bitcast.193, f32[2,576,128]{2,1,0:T(8,128)S(1)} %broadcast_in_dim.65.m_ref, f32[50,8,800]{2,1,0:T(8,128)S(1)} %copy-done.8, f32[8,128]{1,0:T(8,128)S(1)} %broadcast_in_dim.77.l_ref, ...), custom_call_target="tpu_custom_call" | custom-call | flops 10115481600 | bytes 12582912 | tf_op jit(solution)/shard_map/conv_backward/pallas_call | solution.py:432
  (454 shorter events, 340.7 us)
Async XLA Ops:
  6.1 31.0 %collective-permute-start.24 = (bf16[112,800]{0,1:T(8,128)(2,1)S(1)}, bf16[112,800]{0,1:T(8,128)(2,1)S(1)}, u32[]{:S(2)}, u32[]{:S(2)}) collective-permute-start(bf16[112,800]{0,1:T(8,128)(2,1)S(1)} %get-tuple-element.217), channel_id=1, source_target_pairs={{0,8},{1,9},{2,10},{3,11},{4,12},{5,13},{6,14},{7,15},{8,0},{9,1},... | collective-permute-start | bytes 537608 | tf_op jit(solution)/shard_map/ppermute | solution.py:45
  7.2 30.3 %collective-permute-start.25 = (bf16[112,800]{0,1:T(8,128)(2,1)S(1)}, bf16[112,800]{0,1:T(8,128)(2,1)S(1)}, u32[]{:S(2)}, u32[]{:S(2)}) collective-permute-start(bf16[112,800]{0,1:T(8,128)(2,1)S(1)} %get-tuple-element.217), channel_id=1, source_target_pairs={{0,16},{1,17},{2,18},{3,19},{4,20},{5,21},{6,22},{7,23},{8,24},{9,... | collective-permute-start | bytes 537608 | tf_op jit(solution)/shard_map/ppermute | solution.py:45
  11.7 29.7 %collective-permute-start.26 = (bf16[112,800]{0,1:T(8,128)(2,1)S(1)}, bf16[112,800]{0,1:T(8,128)(2,1)S(1)}, u32[]{:S(2)}, u32[]{:S(2)}) collective-permute-start(bf16[112,800]{0,1:T(8,128)(2,1)S(1)} %get-tuple-element.217), channel_id=1, source_target_pairs={{0,24},{1,25},{2,26},{3,27},{4,28},{5,29},{6,30},{7,31},{8,16},{9,... | collective-permute-start | bytes 537608 | tf_op jit(solution)/shard_map/ppermute | solution.py:45
  46.0 31.8 %collective-permute-start = (s32[2,8]{1,0:T(2,128)S(1)}, s32[2,8]{1,0:T(2,128)S(1)}, u32[]{:S(2)}, u32[]{:S(2)}) collective-permute-start(s32[2,8]{1,0:T(2,128)S(1)} %copy-done.72), channel_id=1, source_target_pairs={{0,4},{1,5},{2,6},{3,7},{4,0},{5,1},{6,2},{7,3},{8,12},{9,13},{10,... | collective-permute-start | bytes 200 | tf_op jit(solution)/shard_map/ppermute | solution.py:54
  47.5 30.3 %collective-permute-start.1 = (s32[2,8]{1,0:T(2,128)S(1)}, s32[2,8]{1,0:T(2,128)S(1)}, u32[]{:S(2)}, u32[]{:S(2)}) collective-permute-start(s32[2,8]{1,0:T(2,128)S(1)} %copy-done.72), channel_id=1, source_target_pairs={{0,8},{1,9},{2,10},{3,11},{4,12},{5,13},{6,14},{7,15},{8,0},{9,1},... | collective-permute-start | bytes 200 | tf_op jit(solution)/shard_map/ppermute | solution.py:54
  47.5 33.7 %collective-permute-start.2 = (s32[2,8]{1,0:T(2,128)S(1)}, s32[2,8]{1,0:T(2,128)S(1)}, u32[]{:S(2)}, u32[]{:S(2)}) collective-permute-start(s32[2,8]{1,0:T(2,128)S(1)} %copy-done.72), channel_id=1, source_target_pairs={{0,12},{1,13},{2,14},{3,15},{4,8},{5,9},{6,10},{7,11},{8,4},{9,5},... | collective-permute-start | bytes 200 | tf_op jit(solution)/shard_map/ppermute | solution.py:54
  58.1 39.7 %collective-permute-start.34 = (bf16[2,4,112,800]{3,2,1,0:T(8,128)(2,1)}, bf16[2,4,112,800]{3,2,1,0:T(8,128)(2,1)}, u32[]{:S(2)}, u32[]{:S(2)}) collective-permute-start(bf16[2,4,112,800]{3,2,1,0:T(8,128)(2,1)} %copy.193), channel_id=1, source_target_pairs={{0,2},{1,3},{2,0},{3,1},{4,6},{5,7},{6,4},{7,5},{8,10},{9,11},{10,... | collective-permute-start | bytes 4300808 | tf_op jit(solution)/shard_map/ppermute | solution.py:45
  72.8 40.6 %collective-permute-start.28 = (bf16[2,4,112,800]{3,2,1,0:T(8,128)(2,1)}, bf16[2,4,112,800]{3,2,1,0:T(8,128)(2,1)}, u32[]{:S(2)}, u32[]{:S(2)}) collective-permute-start(bf16[2,4,112,800]{3,2,1,0:T(8,128)(2,1)} %copy.188), channel_id=1, source_target_pairs={{0,4},{1,5},{2,6},{3,7},{4,0},{5,1},{6,2},{7,3},{8,12},{9,13},{10,... | collective-permute-start | bytes 4300808 | tf_op jit(solution)/shard_map/ppermute | solution.py:45
  77.9 49.0 %collective-permute-start.4 = (s32[2,8]{1,0:T(2,128)S(1)}, s32[2,8]{1,0:T(2,128)S(1)}, u32[]{:S(2)}, u32[]{:S(2)}) collective-permute-start(s32[2,8]{1,0:T(2,128)S(1)} %copy-done.72), channel_id=1, source_target_pairs={{0,20},{1,21},{2,22},{3,23},{4,16},{5,17},{6,18},{7,19},{8,28},{9,... | collective-permute-start | bytes 200 | tf_op jit(solution)/shard_map/ppermute | solution.py:54
  81.2 46.2 %collective-permute-start.5 = (s32[2,8]{1,0:T(2,128)S(1)}, s32[2,8]{1,0:T(2,128)S(1)}, u32[]{:S(2)}, u32[]{:S(2)}) collective-permute-start(s32[2,8]{1,0:T(2,128)S(1)} %copy-done.72), channel_id=1, source_target_pairs={{0,24},{1,25},{2,26},{3,27},{4,28},{5,29},{6,30},{7,31},{8,16},{9,... | collective-permute-start | bytes 200 | tf_op jit(solution)/shard_map/ppermute | solution.py:54
  82.3 46.4 %collective-permute-start.6 = (s32[2,8]{1,0:T(2,128)S(1)}, s32[2,8]{1,0:T(2,128)S(1)}, u32[]{:S(2)}, u32[]{:S(2)}) collective-permute-start(s32[2,8]{1,0:T(2,128)S(1)} %copy-done.72), channel_id=1, source_target_pairs={{0,28},{1,29},{2,30},{3,31},{4,24},{5,25},{6,26},{7,27},{8,20},{9,... | collective-permute-start | bytes 200 | tf_op jit(solution)/shard_map/ppermute | solution.py:54
  97.8 38.9 %collective-permute-start.10 = (bf16[2,4,72,128]{3,2,1,0:T(8,128)(2,1)S(1)}, bf16[2,4,72,128]{3,2,1,0:T(8,128)(2,1)S(1)}, u32[]{:S(2)}, u32[]{:S(2)}) collective-permute-start(bf16[2,4,72,128]{3,2,1,0:T(8,128)(2,1)S(1)} %get-tuple-element.61), channel_id=1, source_target_pairs={{0,16},{1,17},{2,18},{3,19},{4,20},{5,21},{6,22},{7,23},{8,24},{9,... | collective-permute-start | bytes 442376 | tf_op jit(solution)/shard_map/ppermute | solution.py:54
  113.4 143.6 %collective-permute-start.35 = (bf16[16,112,800]{2,1,0:T(8,128)(2,1)}, bf16[16,112,800]{2,1,0:T(8,128)(2,1)}, u32[]{:S(2)}, u32[]{:S(2)}) collective-permute-start(bf16[16,112,800]{2,1,0:T(8,128)(2,1)} %bitcast.207), channel_id=1, source_target_pairs={{0,1},{1,0},{2,3},{3,2},{4,5},{5,4},{6,7},{7,6},{8,9},{9,8},{10,11... | collective-permute-start | bytes 8601608 | tf_op jit(solution)/shard_map/ppermute | solution.py:45
  126.9 130.0 %collective-permute-start.29 = (bf16[16,112,800]{2,1,0:T(8,128)(2,1)}, bf16[16,112,800]{2,1,0:T(8,128)(2,1)}, u32[]{:S(2)}, u32[]{:S(2)}) collective-permute-start(bf16[16,112,800]{2,1,0:T(8,128)(2,1)} %bitcast.209), channel_id=1, source_target_pairs={{0,1},{1,0},{2,3},{3,2},{4,5},{5,4},{6,7},{7,6},{8,9},{9,8},{10,11... | collective-permute-start | bytes 8601608 | tf_op jit(solution)/shard_map/ppermute | solution.py:45
  377.2 30.6 %collective-permute-start.37 = (f32[2,800]{1,0:T(2,128)S(1)}, f32[2,800]{1,0:T(2,128)S(1)}, u32[]{:S(2)}, u32[]{:S(2)}) collective-permute-start(f32[2,800]{1,0:T(2,128)S(1)} %fusion.32), channel_id=1, source_target_pairs={{0,8},{1,9},{2,10},{3,11},{4,12},{5,13},{6,14},{7,15},{8,0},{9,1},... | collective-permute-start | bytes 19208 | tf_op jit(solution)/shard_map/ppermute | solution.py:45
  406.3 33.9 %collective-permute-start.61 = (bf16[2,416,800]{2,1,0:T(8,128)(2,1)}, bf16[2,416,800]{2,1,0:T(8,128)(2,1)}, u32[]{:S(2)}, u32[]{:S(2)}) collective-permute-start(bf16[2,416,800]{2,1,0:T(8,128)(2,1)} %slice_bitcast_fusion), channel_id=1, source_target_pairs={{0,2},{1,3},{2,0},{3,1},{4,6},{5,7},{6,4},{7,5},{8,10},{9,11},{10,... | collective-permute-start | bytes 3993608 | tf_op jit(solution)/shard_map/ppermute | solution.py:45
  411.0 35.1 %collective-permute-start.70 = (bf16[2,416,800]{2,1,0:T(8,128)(2,1)}, bf16[2,416,800]{2,1,0:T(8,128)(2,1)}, u32[]{:S(2)}, u32[]{:S(2)}) collective-permute-start(bf16[2,416,800]{2,1,0:T(8,128)(2,1)} %dynamic-slice_bitcast_fusion), channel_id=1, source_target_pairs={{0,4},{1,5},{2,6},{3,7},{4,0},{5,1},{6,2},{7,3},{8,12},{9,13},{10,... | collective-permute-start | bytes 3993608 | tf_op jit(solution)/shard_map/ppermute | solution.py:45
  466.7 83.5 %collective-permute-start.83 = (f32[57,800]{1,0:T(8,128)S(1)}, f32[57,800]{1,0:T(8,128)S(1)}, u32[]{:S(2)}, u32[]{:S(2)}) collective-permute-start(f32[57,800]{1,0:T(8,128)S(1)} %concatenate.31), channel_id=1, source_target_pairs={{0,1},{1,0},{2,3},{3,2},{4,5},{5,4},{6,7},{7,6},{8,9},{9,8},{10,11... | collective-permute-start | bytes 547208 | tf_op jit(solution)/shard_map/ppermute | solution.py:45
  466.8 76.4 %collective-permute-start.39 = (bf16[2,4,72,128]{3,2,1,0:T(8,128)(2,1)S(1)}, bf16[2,4,72,128]{3,2,1,0:T(8,128)(2,1)S(1)}, u32[]{:S(2)}, u32[]{:S(2)}) collective-permute-start(bf16[2,4,72,128]{3,2,1,0:T(8,128)(2,1)S(1)} %get-tuple-element.86), channel_id=1, source_target_pairs={{0,4},{1,5},{2,6},{3,7},{4,0},{5,1},{6,2},{7,3},{8,12},{9,13},{10,... | collective-permute-start | bytes 442376 | tf_op jit(solution)/shard_map/ppermute | solution.py:54
  538.1 53.9 %collective-permute-start.69 = (bf16[416,800]{1,0:T(8,128)(2,1)}, bf16[416,800]{1,0:T(8,128)(2,1)}, u32[]{:S(2)}, u32[]{:S(2)}) collective-permute-start(bf16[416,800]{1,0:T(8,128)(2,1)} %bitcast.74), channel_id=1, source_target_pairs={{0,4},{1,5},{2,6},{3,7},{4,0},{5,1},{6,2},{7,3},{8,12},{9,13},{10,... | collective-permute-start | bytes 1996808 | tf_op jit(solution)/shard_map/ppermute | solution.py:45
  543.0 52.5 %collective-permute-start.78 = (bf16[416,800]{1,0:T(8,128)(2,1)}, bf16[416,800]{1,0:T(8,128)(2,1)}, u32[]{:S(2)}, u32[]{:S(2)}) collective-permute-start(bf16[416,800]{1,0:T(8,128)(2,1)} %bitcast.91), channel_id=1, source_target_pairs={{0,4},{1,5},{2,6},{3,7},{4,0},{5,1},{6,2},{7,3},{8,12},{9,13},{10,... | collective-permute-start | bytes 1996808 | tf_op jit(solution)/shard_map/ppermute | solution.py:45
  552.5 38.3 %collective-permute-start.84 = (f32[57,800]{1,0:T(8,128)}, f32[57,800]{1,0:T(8,128)}, u32[]{:S(2)}, u32[]{:S(2)}) collective-permute-start(f32[57,800]{1,0:T(8,128)} %add.213), channel_id=1, source_target_pairs={{0,2},{1,3},{2,0},{3,1},{4,6},{5,7},{6,4},{7,5},{8,10},{9,11},{10,... | collective-permute-start | bytes 547208 | tf_op jit(solution)/shard_map/ppermute | solution.py:45
  581.8 30.0 %collective-permute-start.53 = (bf16[4,100,100]{2,1,0:T(8,128)(2,1)S(1)}, bf16[4,100,100]{2,1,0:T(8,128)(2,1)S(1)}, u32[]{:S(2)}, u32[]{:S(2)}) collective-permute-start(bf16[4,100,100]{2,1,0:T(8,128)(2,1)S(1)} %bitcast.240), channel_id=1, source_target_pairs={{0,4},{1,5},{2,6},{3,7},{4,0},{5,1},{6,2},{7,3},{8,12},{9,13},{10,... | collective-permute-start | bytes 240008 | tf_op jit(solution)/shard_map/ppermute | solution.py:54
  582.8 29.7 %collective-permute-start.54 = (bf16[4,100,100]{2,1,0:T(8,128)(2,1)S(1)}, bf16[4,100,100]{2,1,0:T(8,128)(2,1)S(1)}, u32[]{:S(2)}, u32[]{:S(2)}) collective-permute-start(bf16[4,100,100]{2,1,0:T(8,128)(2,1)S(1)} %bitcast.239), channel_id=1, source_target_pairs={{0,8},{1,9},{2,10},{3,11},{4,12},{5,13},{6,14},{7,15},{8,0},{9,1},... | collective-permute-start | bytes 240008 | tf_op jit(solution)/shard_map/ppermute | solution.py:54
  621.1 40.5 %collective-permute-start.79 = (bf16[2,100,800]{1,2,0:T(8,128)(2,1)S(1)}, bf16[2,100,800]{1,2,0:T(8,128)(2,1)S(1)}, u32[]{:S(2)}, u32[]{:S(2)}) collective-permute-start(bf16[2,100,800]{1,2,0:T(8,128)(2,1)S(1)} %bitcast.219), channel_id=1, source_target_pairs={{0,8},{1,9},{2,10},{3,11},{4,12},{5,13},{6,14},{7,15},{8,0},{9,1},... | collective-permute-start | bytes 960008 | tf_op jit(solution)/shard_map/ppermute | solution.py:45
  624.5 39.1 %collective-permute-start.80 = (bf16[2,100,800]{1,2,0:T(8,128)(2,1)S(1)}, bf16[2,100,800]{1,2,0:T(8,128)(2,1)S(1)}, u32[]{:S(2)}, u32[]{:S(2)}) collective-permute-start(bf16[2,100,800]{1,2,0:T(8,128)(2,1)S(1)} %bitcast.220), channel_id=1, source_target_pairs={{0,16},{1,17},{2,18},{3,19},{4,20},{5,21},{6,22},{7,23},{8,24},{9,... | collective-permute-start | bytes 960008 | tf_op jit(solution)/shard_map/ppermute | solution.py:45
  624.6 43.8 %collective-permute-start.81 = (bf16[2,100,800]{1,2,0:T(8,128)(2,1)S(1)}, bf16[2,100,800]{1,2,0:T(8,128)(2,1)S(1)}, u32[]{:S(2)}, u32[]{:S(2)}) collective-permute-start(bf16[2,100,800]{1,2,0:T(8,128)(2,1)S(1)} %bitcast.221), channel_id=1, source_target_pairs={{0,24},{1,25},{2,26},{3,27},{4,28},{5,29},{6,30},{7,31},{8,16},{9,... | collective-permute-start | bytes 960008 | tf_op jit(solution)/shard_map/ppermute | solution.py:45
  626.1 29.5 %collective-permute-start.47 = (bf16[2,5,72,128]{3,2,1,0:T(8,128)(2,1)S(1)}, bf16[2,5,72,128]{3,2,1,0:T(8,128)(2,1)S(1)}, u32[]{:S(2)}, u32[]{:S(2)}) collective-permute-start(bf16[2,5,72,128]{3,2,1,0:T(8,128)(2,1)S(1)} %get-tuple-element.95), channel_id=1, source_target_pairs={{0,8},{1,9},{2,10},{3,11},{4,12},{5,13},{6,14},{7,15},{8,0},{9,1},... | collective-permute-start | bytes 552968 | tf_op jit(solution)/shard_map/ppermute | solution.py:54
  663.6 32.0 %collective-permute-start.51 = (bf16[2,5,72,128]{3,2,1,0:T(8,128)(2,1)S(1)}, bf16[2,5,72,128]{3,2,1,0:T(8,128)(2,1)}, u32[]{:S(2)}, u32[]{:S(2)}) collective-permute-start(bf16[2,5,72,128]{3,2,1,0:T(8,128)(2,1)S(1)} %get-tuple-element.99), channel_id=1, source_target_pairs={{0,24},{1,25},{2,26},{3,27},{4,28},{5,29},{6,30},{7,31},{8,16},{9,... | collective-permute-start | bytes 552968 | tf_op jit(solution)/shard_map/ppermute | solution.py:54
  668.3 28.6 %collective-permute-start.52 = (bf16[2,5,72,128]{3,2,1,0:T(8,128)(2,1)S(1)}, bf16[2,5,72,128]{3,2,1,0:T(8,128)(2,1)}, u32[]{:S(2)}, u32[]{:S(2)}) collective-permute-start(bf16[2,5,72,128]{3,2,1,0:T(8,128)(2,1)S(1)} %get-tuple-element.100), channel_id=1, source_target_pairs={{0,28},{1,29},{2,30},{3,31},{4,24},{5,25},{6,26},{7,27},{8,20},{9,... | collective-permute-start | bytes 552968 | tf_op jit(solution)/shard_map/ppermute | solution.py:54
  677.6 47.2 %collective-permute-start.82 = (bf16[4,2,100,800]{3,0,2,1:T(4,128)(2,1)}, bf16[4,2,100,800]{3,0,2,1:T(4,128)(2,1)}, u32[]{:S(2)}, u32[]{:S(2)}) collective-permute-start(bf16[4,2,100,800]{3,0,2,1:T(4,128)(2,1)} %copy.214), channel_id=1, source_target_pairs={{0,4},{1,5},{2,6},{3,7},{4,0},{5,1},{6,2},{7,3},{8,12},{9,13},{10,... | collective-permute-start | bytes 3840008 | tf_op jit(solution)/shard_map/ppermute | solution.py:45
  684.5 36.2 %collective-permute-start.87 = (f32[57,800]{1,0:T(8,128)S(1)}, f32[57,800]{1,0:T(8,128)S(1)}, u32[]{:S(2)}, u32[]{:S(2)}) collective-permute-start(f32[57,800]{1,0:T(8,128)S(1)} %add.216), channel_id=1, source_target_pairs={{0,16},{1,17},{2,18},{3,19},{4,20},{5,21},{6,22},{7,23},{8,24},{9,... | collective-permute-start | bytes 547208 | tf_op jit(solution)/shard_map/ppermute | solution.py:45
  (133 other events, 1827.4 us)

commit v2 on v1

v2 whole, which is shorter than its diff:
```python
import math

import jax
import jax.numpy as jnp
from jax import lax
from jax.experimental import pallas as pl
from jax.experimental.pallas import tpu as pltpu
from jax.sharding import PartitionSpec as P

GROUPS = 16
LANES = 128
RIM = 3
PITCH = 40
BF = jnp.bfloat16
F32 = jnp.float32

highest = lax.Precision.HIGHEST
epsilon = 1e-05
adam_eps = 1e-08
decay_rate = 0.5
small_rate = 0.05
ROOT = 0.7978845608028654
CUBE = 0.044715


class Grid:
    def __init__(self, n_tile, n_opt):
        b = 4 if n_tile % 16 == 0 else 2
        self.n_tile, self.n_opt = n_tile, n_opt
        self.size = {"a": n_tile // b, "b": b, "x": n_opt // 2, "c": 2}

    def own(self):
        t, o = lax.axis_index("tile"), lax.axis_index("opt")
        b = self.size["b"]
        return {"a": t // b, "b": t % b, "x": o // 2, "c": o % 2}

    def at(self, place):
        return place["a"] * self.size["b"] + place["b"], place["x"] * 2 + place["c"]

    def partners(self, dims):
        own = self.own()
        found = []
        for dim in dims:
            if dim == "tile":
                t, o = self.at(own)
                found += [(t ^ k, o) for k in range(1, self.n_tile)]
            else:
                found += [self.beside(own, dim, k) for k in range(1, self.size[dim])]
        return found

    def beside(self, own, dim, k):
        return self.at({**own, dim: own[dim] ^ k})


def meet(devices):
    barrier = pltpu.get_barrier_semaphore()
    for device in devices:
        pl.semaphore_signal(barrier, inc=1, device_id=device, device_id_type=pl.DeviceIdType.MESH)
    pl.semaphore_wait(barrier, len(devices))


class Copies:
    def __init__(self, send_sems, recv_sems):
        self.sems = send_sems, recv_sems
        self.used = 0

    def make(self, src, dst, device):
        i = self.used
        self.used += 1
        return pltpu.make_async_remote_copy(
            src_ref=src,
            dst_ref=dst,
            send_sem=self.sems[0].at[i],
            recv_sem=self.sems[1].at[i],
            device_id=device,
            device_id_type=pl.DeviceIdType.MESH,
        )

    def start(self, src, dst, device):
        copy = self.make(src, dst, device)
        copy.start()
        return copy


def remote_params(number, mib):
    return pltpu.CompilerParams(collective_id=number, has_side_effects=True, vmem_limit_bytes=mib << 20)


def add_rows(target, sources, rows, step=16):
    @pl.loop(0, rows // step)
    def _(i):
        at = pl.ds(pl.multiple_of(i * step, step), step)
        total = target[at, :].astype(F32)
        for source in sources:
            total = total + source[at, :].astype(F32)
        target[at, :] = total.astype(BF)


def store_rims(src, outs, slot, side):
    outs[0, slot, 0] = src[pl.ds(0, RIM * side), :].astype(BF)
    outs[0, slot, 1] = src[pl.ds((side - RIM) * side, RIM * side), :].astype(BF)
    for e in range(RIM):
        rows = pl.ds(e * side, side)
        outs[0, slot, 2, rows] = src[pl.ds(e, side, stride=side), :].astype(BF)
        outs[0, slot, 3, rows] = src[pl.ds(side - RIM + e, side, stride=side), :].astype(BF)


def rims_of_input(inputs, mask_lanes):
    slots, side, _, channels = inputs.shape
    n_chunk = -(-channels // LANES)

    def kernel(x_ref, m_ref, o_ref, cells):
        for s in range(slots):
            for i in range(side):
                cells[pl.ds(i * side, side), :] = (
                    x_ref[s, i].astype(F32) * m_ref[s, pl.ds(i * side, side), :]
                )
            store_rims(cells, o_ref, s, side)

    return pl.pallas_call(
        kernel,
        grid=(n_chunk,),
        in_specs=[
            pl.BlockSpec((slots, side, side, LANES), lambda c: (0, 0, 0, c)),
            pl.BlockSpec((slots, side * side, LANES), lambda c: (0, 0, 0)),
        ],
        out_specs=pl.BlockSpec((1, slots, 4, RIM * side, LANES), lambda c: (c, 0, 0, 0, 0)),
        out_shape=jax.ShapeDtypeStruct((n_chunk, slots, 4, RIM * side, LANES), BF),
        scratch_shapes=[pltpu.VMEM((side * side, LANES), F32)],
        compiler_params=pltpu.CompilerParams(vmem_limit_bytes=32 << 20),
        name="rims_of_input",
    )(inputs, mask_lanes)


class HaloExchange:
    def __init__(self, grid, n_chunk, slots, side):
        self.grid, self.n_chunk, self.slots, self.side = grid, n_chunk, slots, side
        self.count = 2 * (grid.n_tile - 1)

    def scratch(self):
        n, s, band = self.grid.n_tile, self.slots, RIM * self.side
        return [
            pltpu.VMEM((n, s, 4, band, LANES), BF),
            pltpu.VMEM((n, s, 5, band, LANES), BF),
            pltpu.SemaphoreType.DMA((2,)),
        ]

    def halo_shape(self):
        return jax.ShapeDtypeStruct((self.n_chunk, self.slots, 5, RIM * self.side, LANES), BF)

    def send_rims(self, copies, rims, arrived, local):
        t, o = self.grid.at(self.grid.own())
        self.t, self.o = t, o
        self.first = []
        for k in range(1, self.grid.n_tile):
            to = t ^ k
            source = jnp.minimum(to, self.n_chunk - 1)
            copy = copies.make(rims.at[source], arrived.at[t], (to, o))
            self.first.append((to, copy))

            @pl.when(to < self.n_chunk)
            def _():
                copy.start()

        own = pltpu.make_async_copy(rims.at[jnp.minimum(t, self.n_chunk - 1)], arrived.at[t], local.at[0])
        own.start()
        self.own_copy = own

    def pick_and_send(self, copies, arrived, picked, halos, local, neighbours):
        grid, slots, side = self.grid, self.slots, self.side
        t, o = self.t, self.o
        self.own_copy.wait()
        for _, copy in self.first:

            @pl.when(t < self.n_chunk)
            def _():
                copy.wait_recv()

        @pl.when(t < self.n_chunk)
        def _():
            @pl.loop(0, grid.n_tile * slots)
            def _(d):
                def rim(direction, which):
                    slot = neighbours(d, direction)
                    at = jnp.maximum(slot, 0)
                    value = arrived[at // slots, at % slots, which].astype(F32)
                    return jnp.where(slot >= 0, value, 0.0)

                to_tile, to_slot = d // slots, d % slots
                for to, (direction, which) in enumerate(((1, 1), (6, 0), (3, 3), (4, 2))):
                    picked[to_tile, to_slot, to] = rim(direction, which).astype(BF)
                rows = []
                for direction, which, first in ((0, 1, side - RIM), (2, 1, 0), (5, 0, side - RIM), (7, 0, 0)):
                    value = rim(direction, which)
                    rows += [value[e * side + first : e * side + first + RIM] for e in range(RIM)]
                    rows.append(jnp.zeros((16 - RIM * RIM, LANES), F32))
                rows.append(jnp.zeros((RIM * side - 64, LANES), F32))
                picked[to_tile, to_slot, 4] = jnp.concatenate(rows, 0).astype(BF)

        own_chunk = jnp.minimum(t, self.n_chunk - 1)
        self.second = []
        for k in range(1, grid.n_tile):
            to = t ^ k
            copy = copies.make(picked.at[to], halos.at[own_chunk], (to, o))
            self.second.append((to, copy))

            @pl.when(t < self.n_chunk)
            def _():
                copy.start()

        self.back_copy = pltpu.make_async_copy(picked.at[t], halos.at[own_chunk], local.at[1])

        @pl.when(t < self.n_chunk)
        def _():
            self.back_copy.start()

    def finish(self):
        t = self.t

        @pl.when(t < self.n_chunk)
        def _():
            self.back_copy.wait()

        for to, copy in self.first:

            @pl.when(to < self.n_chunk)
            def _():
                copy.wait_send()

        for to, copy in self.second:

            @pl.when(to < self.n_chunk)
            def _():
                copy.wait_recv()

            @pl.when(t < self.n_chunk)
            def _():
                copy.wait_send()


class WeightGather:
    def __init__(self, grid, pairs, width):
        self.grid, self.pairs, self.width = grid, pairs, width
        self.count = pairs * (grid.n_tile * grid.n_opt - 1)

    def run(self, copies, packed, gathered, local):
        grid, width = self.grid, self.width
        own = grid.own()

        def place(m, rel):
            t, o = grid.at({d: own[d] ^ rel.get(d, 0) for d in own})
            return gathered.at[m, o, pl.ds(pl.multiple_of(t * width, width), width)]

        keeps = []
        known = []
        for m in range(self.pairs):
            keep = pltpu.make_async_copy(packed.at[m], place(m, {}), local.at[m])
            keep.start()
            keeps.append(keep)
            known.append([({}, None)])
        arrived = set()
        for stage in range(4):
            for m in range(self.pairs):
                order = ("a", "x", "b", "c") if m % 2 == 0 else ("a", "b", "x", "c")
                dim = order[stage]
                fresh = []
                for k in range(1, grid.size[dim]):
                    for rel, got in known[m]:
                        if got is not None and id(got) not in arrived:
                            got.wait_recv()
                            arrived.add(id(got))
                        source = packed.at[m] if not rel else place(m, rel)
                        copy = copies.start(source, place(m, rel), grid.beside(own, dim, k))
                        fresh.append(({**rel, dim: k}, copy))
                known[m] = known[m] + fresh
            yield stage
        for m in range(self.pairs):
            keeps[m].wait()
            for _, got in known[m]:
                if got is not None:
                    if id(got) not in arrived:
                        got.wait_recv()
                    got.wait_send()
        yield 4


def exchange_forward(grid, rims, packed, neighbours):
    n_chunk, slots, _, band, _ = rims.shape
    pairs, width, cols = packed.shape
    n_tile = grid.n_tile
    halo = HaloExchange(grid, n_chunk, slots, band // RIM)
    gather = WeightGather(grid, pairs, width)
    total = halo.count + gather.count + n_tile - 1

    def kernel(r_ref, p_ref, n_ref, halo_ref, w_ref, nbr_ref, arrived, picked, local, table, send, recv, locals_w, locals_n):
        own = grid.own()
        t, o = grid.at(own)
        meet(grid.partners(("tile", "x", "c")))
        copies = Copies(send, recv)
        tables = [copies.start(n_ref, nbr_ref.at[t], (t ^ k, o)) for k in range(1, n_tile)]
        keep = pltpu.make_async_copy(n_ref, nbr_ref.at[t], locals_n.at[0])
        keep.start()
        halo.send_rims(copies, r_ref, arrived, local)
        weights = gather.run(copies, p_ref, w_ref, locals_w)
        next(weights)
        keep.wait()
        for copy in tables:
            copy.wait()
        load = pltpu.make_async_copy(nbr_ref, table, locals_n.at[1])
        load.start()
        load.wait()
        halo.pick_and_send(
            copies, arrived, picked, halo_ref, local, lambda d, k: table[d // slots, d % slots, k]
        )
        for _ in weights:
            pass
        halo.finish()

    any_space = pl.BlockSpec(memory_space=pl.ANY)
    return pl.pallas_call(
        kernel,
        in_specs=[any_space] * 3,
        out_specs=[any_space] * 3,
        out_shape=[
            halo.halo_shape(),
            jax.ShapeDtypeStruct((pairs, grid.n_opt, n_tile * width, cols), BF),
            jax.ShapeDtypeStruct((n_tile,) + neighbours.shape, jnp.int32),
        ],
        scratch_shapes=halo.scratch()
        + [
            pltpu.SMEM((n_tile,) + neighbours.shape, jnp.int32),
            pltpu.SemaphoreType.DMA((total,)),
            pltpu.SemaphoreType.DMA((total,)),
            pltpu.SemaphoreType.DMA((pairs,)),
            pltpu.SemaphoreType.DMA((2,)),
        ],
        compiler_params=remote_params(1, 32),
        name="exchange_forward",
    )(rims, packed, neighbours)


def exchange_backward(grid, rims, grads, neighbours):
    n_chunk, slots, _, band, _ = rims.shape
    n_tile = grid.n_tile
    side_a, side_b, side_x = grid.size["a"], grid.size["b"], grid.size["x"]
    _, blocks, rows, cols = grads.shape
    pairs = blocks // side_x
    part = rows // side_b
    halo = HaloExchange(grid, n_chunk, slots, band // RIM)
    total = halo.count + blocks + pairs * ((side_x - 1) + (side_b - 1)) + pairs * side_x * (side_b - 1)

    def kernel(r_ref, g_ref, n_ref, halo_ref, o_ref, arrived, picked, local, here, core, far, across, send, recv, load_sems):
        own = grid.own()
        own_x, own_b = own["x"], own["b"]
        meet(grid.partners(("tile", "x", "c")))
        copies = Copies(send, recv)
        halo.send_rims(copies, r_ref, arrived, local)
        loads, cores = [], []
        order = []
        for m in range(pairs):
            order += [(k, m) for k in range(1, side_x)] if m % 2 == 0 else []
        order += [(k, m) for m in range(pairs) for k in range(side_x) if (k, m) not in order]
        index = lambda k, m: (own_x ^ k) * pairs + m
        for i, (k, m) in enumerate(order):
            at = index(k, m)
            cores.append(copies.start(g_ref.at[1 - own["c"], at], core.at[at], grid.beside(own, "c", 1)))
            load = pltpu.make_async_copy(g_ref.at[own["c"], at], here.at[at], load_sems.at[i])
            load.start()
            loads.append(load)
        sent_x = {m: [] for m in range(pairs)}
        sent_b = {m: [] for m in range(pairs)}
        rows_of = lambda b: pl.ds(pl.multiple_of(b * part, 16), part)

        def send_b(m, k):
            for j in range(1, side_b):
                to = grid.beside(own, "b", j)
                at = index(k, m)
                sent_b[m].append(
                    (k, copies.start(here.at[at, rows_of(own_b ^ j)], across.at[j - 1, at], to))
                )

        def send_x(m, k):
            at = index(k, m)
            to = grid.beside(own, "x", k)
            if m % 2 == 0:
                sent_x[m].append(copies.start(here.at[at], far.at[k - 1, m], to))
            else:
                sent_x[m].append(
                    copies.start(here.at[at, rows_of(own_b)], far.at[k - 1, m, pl.ds(0, part)], to)
                )

        for i, (k, m) in enumerate(order):
            loads[i].wait()
            cores[i].wait_recv()
            at = index(k, m)
            add_rows(here.at[at], [core.at[at]], rows)
            if m % 2 == 1:
                send_b(m, k)
            elif k > 0:
                send_x(m, k)
        halo.pick_and_send(
            copies, arrived, picked, halo_ref, local, lambda d, k: n_ref[d // slots, d % slots, k]
        )
        for m in range(pairs):
            if m % 2 == 1:
                for k, copy in sent_b[m]:
                    copy.wait()
                for k in [*range(1, side_x), 0]:
                    at = index(k, m)
                    add_rows(here.at[at, rows_of(own_b)], [across.at[j, at] for j in range(side_b - 1)], part)
                    if k > 0:
                        send_x(m, k)
            else:
                for copy in sent_x[m]:
                    copy.wait()
                add_rows(here.at[index(0, m)], [far.at[j, m] for j in range(side_x - 1)], rows)
                send_b(m, 0)
        for m in range(pairs):
            at = index(0, m)
            if m % 2 == 1:
                for copy in sent_x[m]:
                    copy.wait()
                sources = [far.at[j, m, pl.ds(0, part)] for j in range(side_x - 1)]
            else:
                for _, copy in sent_b[m]:
                    copy.wait()
                sources = [across.at[j, at] for j in range(side_b - 1)]
            add_rows(here.at[at, rows_of(own_b)], sources, part)
        outs = []
        for m in range(pairs):
            out = pltpu.make_async_copy(here.at[index(0, m), rows_of(own_b)], o_ref.at[m], load_sems.at[m])
            out.start()
            outs.append(out)
        halo.finish()
        for copy in cores:
            copy.wait_send()
        for out in outs:
            out.wait()

    any_space = pl.BlockSpec(memory_space=pl.ANY)
    return pl.pallas_call(
        kernel,
        in_specs=[any_space, any_space, pl.BlockSpec(memory_space=pltpu.SMEM)],
        out_specs=[any_space] * 2,
        out_shape=[halo.halo_shape(), jax.ShapeDtypeStruct((pairs, part, cols), BF)],
        scratch_shapes=halo.scratch()
        + [
            pltpu.VMEM((blocks, rows, cols), BF),
            pltpu.VMEM((blocks, rows, cols), BF),
            pltpu.VMEM((side_x - 1, pairs, rows, cols), BF),
            pltpu.VMEM((side_b - 1, blocks, part, cols), BF),
            pltpu.SemaphoreType.DMA((total,)),
            pltpu.SemaphoreType.DMA((total,)),
            pltpu.SemaphoreType.DMA((blocks,)),
        ],
        compiler_params=remote_params(2, 56),
        name="exchange_backward",
    )(rims, grads, neighbours)


def finish_gradients(grid, partial, small):
    pairs, part, cols = partial.shape
    side_a, side_b = grid.size["a"], grid.size["b"]
    piece = part // side_a
    steps = [(dim, 1 << i) for dim in ("c", "x", "b", "a") for i in range((grid.size[dim] - 1).bit_length())]
    total = pairs * 2 * (side_a - 1) + pairs * side_a * (side_b - 1) + len(steps)

    def kernel(p_ref, s_ref, o_ref, t_ref, mine, got, sums, send, recv, load_sems):
        own = grid.own()
        meet(grid.partners(("a", "b", "x", "c")))
        copies = Copies(send, recv)
        rows_of = lambda a: pl.ds(pl.multiple_of(a * piece, 16), piece)
        place = lambda a, b: pl.ds(pl.multiple_of((b * side_a + a) * piece, 16), piece)
        firsts, loads = [], []
        for m in range(pairs):
            firsts.append(
                [
                    copies.start(p_ref.at[m, rows_of(own["a"] ^ k)], got.at[m, k - 1], grid.beside(own, "a", k))
                    for k in range(1, side_a)
                ]
            )
            load = pltpu.make_async_copy(p_ref.at[m, rows_of(own["a"])], mine.at[m], load_sems.at[m])
            load.start()
            loads.append(load)
        t_ref[...] = s_ref[...]
        small_copies = []

        def small_step(i):
            dim, k = steps[i]
            copy = copies.start(t_ref, sums.at[i], grid.beside(own, dim, k))
            copy.wait()
            t_ref[...] = t_ref[...] + sums[i]

        small_step(0)
        seconds, thirds, keeps = [], [], []
        for m in range(pairs):
            loads[m].wait()
            for copy in firsts[m]:
                copy.wait()
            add_rows(mine.at[m], [got.at[m, k] for k in range(side_a - 1)], piece)
            keep = pltpu.make_async_copy(mine.at[m], o_ref.at[m, place(own["a"], own["b"])], load_sems.at[m])
            keep.start()
            keeps.append(keep)
            to = o_ref.at[m, place(own["a"], own["b"])]
            seconds.append(
                [(k, copies.start(mine.at[m], to, grid.beside(own, "a", k))) for k in range(1, side_a)]
            )
            thirds += [copies.start(mine.at[m], to, grid.beside(own, "b", j)) for j in range(1, side_b)]
        for i in range(1, len(steps)):
            small_step(i)
        for m in range(pairs):
            for k, copy in seconds[m]:
                copy.wait_recv()
                at = o_ref.at[m, place(own["a"] ^ k, own["b"])]
                thirds += [copies.start(at, at, grid.beside(own, "b", j)) for j in range(1, side_b)]
        for m in range(pairs):
            keeps[m].wait()
            for _, copy in seconds[m]:
                copy.wait_send()
        for copy in thirds:
            copy.wait()

    any_space = pl.BlockSpec(memory_space=pl.ANY)
    whole = pl.BlockSpec(memory_space=pltpu.VMEM)
    return pl.pallas_call(
        kernel,
        in_specs=[any_space, whole],
        out_specs=[any_space, whole],
        out_shape=[
            jax.ShapeDtypeStruct((pairs, side_b * part, cols), BF),
            jax.ShapeDtypeStruct(small.shape, F32),
        ],
        scratch_shapes=[
            pltpu.VMEM((pairs, piece, cols), BF),
            pltpu.VMEM((pairs, side_a - 1, piece, cols), BF),
            pltpu.VMEM((len(steps),) + small.shape, F32),
            pltpu.SemaphoreType.DMA((total,)),
            pltpu.SemaphoreType.DMA((total,)),
            pltpu.SemaphoreType.DMA((pairs,)),
        ],
        compiler_params=remote_params(3, 32),
        name="finish_gradients",
    )(partial, small)


def scatter_change(grid, change):
    pairs, rows, cols = change.shape
    side_a, side_b = grid.size["a"], grid.size["b"]
    part = rows // side_b
    piece = part // side_a
    total = pairs * ((side_b - 1) + (side_a - 1))

    def kernel(c_ref, o_ref, mine, from_b, from_a, send, recv, load_sems):
        own = grid.own()
        meet(grid.partners(("a", "b")))
        copies = Copies(send, recv)
        half = lambda b: pl.ds(pl.multiple_of(b * part, 16), part)
        rows_of = lambda a: pl.ds(pl.multiple_of(a * piece, 16), piece)
        firsts, loads = [], []
        for m in range(pairs):
            firsts.append(
                [
                    copies.start(c_ref.at[m, half(own["b"] ^ k)], from_b.at[k - 1, m], grid.beside(own, "b", k))
                    for k in range(1, side_b)
                ]
            )
            load = pltpu.make_async_copy(c_ref.at[m, half(own["b"])], mine.at[m], load_sems.at[m])
            load.start()
            loads.append(load)
        seconds = []
        for m in range(pairs):
            loads[m].wait()
            for copy in firsts[m]:
                copy.wait()
            add_rows(mine.at[m], [from_b.at[k, m] for k in range(side_b - 1)], part)
            seconds.append(
                [
                    copies.start(mine.at[m, rows_of(own["a"] ^ k)], from_a.at[k - 1, m], grid.beside(own, "a", k))
                    for k in range(1, side_a)
                ]
            )
        for m in range(pairs):
            for copy in seconds[m]:
                copy.wait()
            here = mine.at[m, rows_of(own["a"])]
            total_here = here[...].astype(F32)
            for k in range(side_a - 1):
                total_here = total_here + from_a[k, m].astype(F32)
            o_ref[m] = total_here

    any_space = pl.BlockSpec(memory_space=pl.ANY)
    return pl.pallas_call(
        kernel,
        in_specs=[any_space],
        out_specs=pl.BlockSpec(memory_space=pltpu.VMEM),
        out_shape=jax.ShapeDtypeStruct((pairs, piece, cols), F32),
        scratch_shapes=[
            pltpu.VMEM((pairs, part, cols), BF),
            pltpu.VMEM((side_b - 1, pairs, part, cols), BF),
            pltpu.VMEM((side_a - 1, pairs, piece, cols), BF),
            pltpu.SemaphoreType.DMA((total,)),
            pltpu.SemaphoreType.DMA((total,)),
            pltpu.SemaphoreType.DMA((pairs,)),
        ],
        compiler_params=remote_params(4, 40),
        name="scatter_change",
    )(change)


def tile_total(grid, value, number):
    n_tile = grid.n_tile

    def kernel(v_ref, o_ref, got, send, recv):
        t, o = grid.at(grid.own())
        meet(grid.partners(("tile",)))
        copies = Copies(send, recv)
        got[t] = v_ref[...]
        sent = [copies.start(v_ref, got.at[t], (t ^ k, o)) for k in range(1, n_tile)]
        for copy in sent:
            copy.wait()
        total = got[0]
        for i in range(1, n_tile):
            total = total + got[i]
        o_ref[...] = total

    whole = pl.BlockSpec(memory_space=pltpu.VMEM)
    return pl.pallas_call(
        kernel,
        in_specs=[whole],
        out_specs=whole,
        out_shape=jax.ShapeDtypeStruct(value.shape, F32),
        scratch_shapes=[
            pltpu.VMEM((n_tile,) + value.shape, F32),
            pltpu.SemaphoreType.DMA((n_tile - 1,)),
            pltpu.SemaphoreType.DMA((n_tile - 1,)),
        ],
        compiler_params=remote_params(number, 16),
        name="tile_total",
    )(value)


def fill_halo(pad, halo, side):
    last = side + RIM
    up, down, left, right, corner = (halo(k) for k in range(5))
    for e in range(RIM):
        rows = slice(e * side, e * side + side)
        pad[pl.ds(e * PITCH + 8, side), :] = up[rows]
        pad[pl.ds((last + e) * PITCH + 8, side), :] = down[rows]
        pad[pl.ds(RIM * PITCH + 8 - RIM + e, side, stride=PITCH), :] = left[rows]
        pad[pl.ds(RIM * PITCH + 8 + side + e, side, stride=PITCH), :] = right[rows]
    places = ((0, 8 - RIM), (0, 8 + side), (last, 8 - RIM), (last, 8 + side))
    for k, (row, col) in enumerate(places):
        for e in range(RIM):
            at = 16 * k + RIM * e
            pad[pl.ds((row + e) * PITCH + col, RIM), :] = corner[at : at + RIM]


def conv_pass(pad, side, weight, emit):
    for block in range(side // 8):
        sums = [None] * side
        for b in range(7):
            taps = [weight(a, b) for a in range(7)]
            for r in range(side + 2 * RIM):
                cells = pad[pl.ds(r * PITCH + 8 - RIM + b + 8 * block, 8), :]
                for a in range(7):
                    i = r - a
                    if 0 <= i < side:
                        term = taps[a] * cells
                        sums[i] = term if sums[i] is None else sums[i] + term
        emit(block, sums)


def halo_block(halos):
    return pl.BlockSpec((1, 1) + halos.shape[2:], lambda c, s: (c, s, 0, 0, 0))


def conv_cost(n_chunk, slots, side, nbytes):
    return pl.CostEstimate(
        flops=n_chunk * slots * side * side * LANES * 98 * 100, bytes_accessed=nbytes, transcendentals=0
    )


def conv_forward(inputs, mask_lanes, halos, taps):
    slots, side, _, channels = inputs.shape
    n_chunk = halos.shape[0]

    def kernel(x_ref, m_ref, w_ref, h_ref, o_ref, s_ref, pad):
        for i in range(side):
            pad[pl.ds((i + RIM) * PITCH + 8, side), :] = (
                x_ref[0, i].astype(F32) * m_ref[0, pl.ds(i * side, side), :]
            )
        fill_halo(pad, lambda k: h_ref[0, 0, k].astype(F32), side)
        bias = w_ref[49]
        totals = [jnp.zeros((8, LANES), F32), jnp.zeros((8, LANES), F32)]

        def emit(block, sums):
            for i in range(side):
                value = sums[i] + bias
                rows = pl.ds(i * side + 8 * block, 8)
                o_ref[0, rows, :] = value
                weighted = m_ref[0, rows, :] * value
                totals[0] = totals[0] + weighted
                totals[1] = totals[1] + weighted * value

        conv_pass(pad, side, lambda a, b: w_ref[7 * a + b], emit)
        s_ref[0, 0], s_ref[0, 1] = totals

    cells = side * side
    return pl.pallas_call(
        kernel,
        grid=(n_chunk, slots),
        in_specs=[
            pl.BlockSpec((1, side, side, LANES), lambda c, s: (s, 0, 0, c)),
            pl.BlockSpec((1, cells, LANES), lambda c, s: (s, 0, 0)),
            pl.BlockSpec((50, 8, LANES), lambda c, s: (0, 0, c)),
            halo_block(halos),
        ],
        out_specs=[
            pl.BlockSpec((1, cells, LANES), lambda c, s: (s, 0, c)),
            pl.BlockSpec((1, 2, 8, LANES), lambda c, s: (s, 0, 0, c)),
        ],
        scratch_shapes=[pltpu.VMEM(((side + 2 * RIM) * PITCH, LANES), F32)],
        out_shape=[
            jax.ShapeDtypeStruct((slots, cells, channels), F32),
            jax.ShapeDtypeStruct((slots, 2, 8, channels), F32),
        ],
        cost_estimate=conv_cost(n_chunk, slots, side, 10 << 20),
        compiler_params=pltpu.CompilerParams(vmem_limit_bytes=32 << 20),
        name="conv_forward",
    )(inputs, mask_lanes, taps, halos)


def conv_gradient(d_shaped, conv_out, mask_lanes, coefs, side):
    slots, cells, channels = d_shaped.shape
    n_chunk = -(-channels // LANES)

    def kernel(d_ref, v_ref, m_ref, c_ref, o_ref, r_ref, held):
        one, two, three = c_ref[0, :1], c_ref[1, :1], c_ref[2, :1]
        for s in range(slots):
            value = d_ref[s] * one - m_ref[s] * (two + three * v_ref[s])
            o_ref[s] = value
            held[...] = value
            store_rims(held, r_ref, s, side)

    piece = (slots, 4, RIM * side, LANES)
    block = pl.BlockSpec((slots, cells, LANES), lambda c: (0, 0, c))
    return pl.pallas_call(
        kernel,
        grid=(n_chunk,),
        in_specs=[
            block,
            block,
            pl.BlockSpec((slots, cells, LANES), lambda c: (0, 0, 0)),
            pl.BlockSpec((3, 8, LANES), lambda c: (0, 0, c)),
        ],
        out_specs=[block, pl.BlockSpec((1,) + piece, lambda c: (c, 0, 0, 0, 0))],
        scratch_shapes=[pltpu.VMEM((cells, LANES), F32)],
        out_shape=[
            jax.ShapeDtypeStruct((slots, cells, channels), F32),
            jax.ShapeDtypeStruct((n_chunk,) + piece, BF),
        ],
        compiler_params=pltpu.CompilerParams(vmem_limit_bytes=32 << 20),
        name="conv_gradient",
    )(d_shaped, conv_out, mask_lanes, coefs)


def tap_gradient(inputs, mask_lanes, halos, d_conv):
    slots, side, _, channels = inputs.shape
    n_chunk = halos.shape[0]
    cells = side * side

    def kernel(x_ref, m_ref, d_ref, h_ref, o_ref, pad, sums):
        slot = pl.program_id(1)
        for i in range(side):
            pad[pl.ds((i + RIM) * PITCH + 8, side), :] = (
                x_ref[0, i].astype(F32) * m_ref[0, pl.ds(i * side, side), :]
            )
        fill_halo(pad, lambda k: h_ref[0, 0, k].astype(F32), side)

        @pl.when(slot == 0)
        def _():
            sums[...] = jnp.zeros_like(sums)

        for block in range(side // 8):
            grads = [d_ref[0, pl.ds(i * side + 8 * block, 8), :] for i in range(side)]
            total = grads[0]
            for i in range(1, side):
                total = total + grads[i]
            sums[49] += total
            for b in range(7):
                taps = [None] * 7
                for r in range(side + 2 * RIM):
                    window = pad[pl.ds(r * PITCH + 8 - RIM + b + 8 * block, 8), :]
                    for a in range(7):
                        i = r - a
                        if 0 <= i < side:
                            term = window * grads[i]
                            taps[a] = term if taps[a] is None else taps[a] + term
                for a in range(7):
                    sums[7 * a + b] += taps[a]

        @pl.when(slot == slots - 1)
        def _():
            o_ref[...] = jnp.sum(sums[...], axis=1)

    return pl.pallas_call(
        kernel,
        grid=(n_chunk, slots),
        in_specs=[
            pl.BlockSpec((1, side, side, LANES), lambda c, s: (s, 0, 0, c)),
            pl.BlockSpec((1, cells, LANES), lambda c, s: (s, 0, 0)),
            pl.BlockSpec((1, cells, LANES), lambda c, s: (s, 0, c)),
            halo_block(halos),
        ],
        out_specs=pl.BlockSpec((50, LANES), lambda c, s: (0, c)),
        scratch_shapes=[
            pltpu.VMEM(((side + 2 * RIM) * PITCH, LANES), F32),
            pltpu.VMEM((50, 8, LANES), F32),
        ],
        out_shape=jax.ShapeDtypeStruct((50, channels), F32),
        cost_estimate=conv_cost(n_chunk, slots, side, 10 << 20),
        compiler_params=pltpu.CompilerParams(vmem_limit_bytes=32 << 20),
        name="tap_gradient",
    )(inputs, mask_lanes, d_conv, halos)


def conv_backward(d_conv, halos, cotangent, mask_lanes, taps, weight_lanes):
    slots, side, _, channels = cotangent.shape
    n_chunk = halos.shape[0]
    cells = side * side

    def kernel(d_ref, g_ref, m_ref, w_ref, l_ref, h_ref, o_ref, pad):
        for i in range(side):
            pad[pl.ds((i + RIM) * PITCH + 8, side), :] = d_ref[0, pl.ds(i * side, side), :]
        fill_halo(pad, lambda k: h_ref[0, 0, k].astype(F32), side)
        weight = l_ref[...]

        def emit(block, sums):
            for i in range(side):
                rows = pl.ds(i * side + 8 * block, 8)
                scaled = weight * g_ref[0, i, pl.ds(8 * block, 8), :].astype(F32)
                o_ref[0, rows, :] = m_ref[0, rows, :] * (scaled + sums[i])

        conv_pass(pad, side, lambda a, b: w_ref[7 * (6 - a) + 6 - b], emit)

    return pl.pallas_call(
        kernel,
        grid=(n_chunk, slots),
        in_specs=[
            pl.BlockSpec((1, cells, LANES), lambda c, s: (s, 0, c)),
            pl.BlockSpec((1, side, side, LANES), lambda c, s: (s, 0, 0, c)),
            pl.BlockSpec((1, cells, LANES), lambda c, s: (s, 0, 0)),
            pl.BlockSpec((50, 8, LANES), lambda c, s: (0, 0, c)),
            pl.BlockSpec((8, LANES), lambda c, s: (0, 0)),
            halo_block(halos),
        ],
        out_specs=pl.BlockSpec((1, cells, LANES), lambda c, s: (s, 0, c)),
        scratch_shapes=[pltpu.VMEM(((side + 2 * RIM) * PITCH, LANES), F32)],
        out_shape=jax.ShapeDtypeStruct((slots, cells, channels), F32),
        cost_estimate=conv_cost(n_chunk, slots, side, 12 << 20),
        compiler_params=pltpu.CompilerParams(vmem_limit_bytes=32 << 20),
        name="conv_backward",
    )(d_conv, cotangent, mask_lanes, taps, weight_lanes, halos)


def spread_lanes(value, parts, width):
    rows, channels = value.shape
    run = channels // parts
    if run == width:
        return value
    gap = jnp.zeros((rows, width - run), value.dtype)
    pieces = []
    for t in range(parts):
        pieces += [value[:, t * run : (t + 1) * run], gap]
    return jnp.concatenate(pieces, 1)


def close_lanes(value, parts, run):
    width = value.shape[1] // parts
    if run == width:
        return value
    return jnp.concatenate([value[:, t * width : t * width + run] for t in range(parts)], 1)


def arrange(body, args, specs, rows, channels, parts, width, name):
    step = 3 * LANES if rows % (3 * LANES) == 0 else LANES

    def kernel(*refs):
        given, (gap_ref, turned_ref, sum_ref) = refs[: len(args)], refs[len(args) :]
        low = body(*given).astype(BF)
        value = low.astype(F32)
        gap_ref[...] = spread_lanes(value, parts, width).astype(BF)
        turned_ref[...] = value.T.astype(BF)

        @pl.when(pl.program_id(0) == 0)
        def _():
            sum_ref[...] = jnp.zeros_like(sum_ref)

        sum_ref[...] += jnp.sum(value, axis=0, keepdims=True)

    return pl.pallas_call(
        kernel,
        grid=(rows // step,),
        in_specs=specs(step),
        out_specs=[
            pl.BlockSpec((step, parts * width), lambda i: (i, 0)),
            pl.BlockSpec((channels, step), lambda i: (0, i)),
            pl.BlockSpec((1, channels), lambda i: (0, 0)),
        ],
        out_shape=[
            jax.ShapeDtypeStruct((rows, parts * width), BF),
            jax.ShapeDtypeStruct((channels, rows), BF),
            jax.ShapeDtypeStruct((1, channels), F32),
        ],
        compiler_params=pltpu.CompilerParams(vmem_limit_bytes=48 << 20),
        name=name,
    )(*args)


def feed_forward(inverse, shaped, shaped_t, d_branch, d_branch_t, hidden_bias, weights, grad_rows):
    rows, depth = shaped.shape
    channels = shaped_t.shape[0]
    half, _, cols = hidden_bias.shape
    pairs, owners = weights.shape[:2]
    per_owner = 2 * pairs
    tile_rows = 3 * LANES if rows % (3 * LANES) == 0 else LANES

    def kernel(inv_ref, s_ref, st_ref, d_ref, dt_ref, hb_ref, w_ref, branch_ref, ds_ref, grad_ref, bias_ref, *scratch):
        packed, first, second, act, dpre, grads, sems, out_sem = scratch
        step = pl.program_id(0)

        def where(slot):
            owner, inside = slot // per_owner, slot % per_owner
            return owner, inside // 2, inside % 2

        def fetch(h, buffer):
            copies = []
            for which in range(2):
                owner, pair, _ = where(inv_ref[h + which * half])
                copies.append(
                    pltpu.make_async_copy(w_ref.at[pair, owner], packed.at[buffer, which], sems.at[buffer, which])
                )
            return copies

        @pl.when(step == 0)
        def _():
            for copy in fetch(0, 0):
                copy.start()
            if grad_rows > channels:
                rest = grad_rows - channels
                grads[:, :, pl.ds(channels, rest), :] = jnp.zeros(grads.shape[:2] + (rest, 2 * cols), BF)

        @pl.when(step + 1 < half)
        def _():
            for copy in fetch(step + 1, (step + 1) % 2):
                copy.start()

        now = step % 2
        slots = [where(inv_ref[step + which * half]) for which in range(2)]
        waits = fetch(step, now)
        for which, held in enumerate((first, second)):
            waits[which].wait()
            for parity in range(2):

                @pl.when(slots[which][2] == parity)
                def _():
                    held[...] = packed[now, which, :, parity * cols : (parity + 1) * cols]

        hidden = hb_ref[0]
        total = jnp.zeros((1, cols), F32)
        across = (((1,), (1,)), ((), ()))
        for i in range(rows // tile_rows):
            at = pl.ds(i * tile_rows, tile_rows)
            pre = jnp.dot(s_ref[at, :], first[...], preferred_element_type=F32) + hidden
            d_act = jnp.dot(d_ref[at, :], second[...], preferred_element_type=F32)
            square = pre * pre
            bend = jnp.tanh(ROOT * pre * (1.0 + CUBE * square))
            half_up = 0.5 * (1.0 + bend)
            low = (pre * half_up).astype(BF)
            slope = half_up + (0.5 * ROOT) * pre * (1.0 - bend * bend) * (1.0 + (3.0 * CUBE) * square)
            back = (d_act * slope).astype(BF)
            act[at, :] = low
            dpre[at, :] = back
            total = total + jnp.sum(back.astype(F32), axis=0, keepdims=True)
            out_add = lax.dot_general(low, second[...], across, preferred_element_type=F32)
            in_add = lax.dot_general(back, first[...], across, preferred_element_type=F32)

            @pl.when(step == 0)
            def _():
                branch_ref[at, :] = out_add
                ds_ref[at, :] = in_add

            @pl.when(step > 0)
            def _():
                branch_ref[at, :] += out_add
                ds_ref[at, :] += in_add

        bias_ref[0] = total
        for which, (left, right) in enumerate(((st_ref, dpre), (dt_ref, act))):
            owner, pair, half_of_pair = slots[which]
            value = jnp.dot(left[...], right[...], preferred_element_type=F32).astype(BF)
            for parity in range(2):

                @pl.when(half_of_pair == parity)
                def _():
                    at = (owner // 2) * pairs + pair
                    grads[owner % 2, at, pl.ds(0, channels), parity * cols : (parity + 1) * cols] = value

        @pl.when(step == half - 1)
        def _():
            out = pltpu.make_async_copy(grads, grad_ref, out_sem.at[0])
            out.start()
            out.wait()

    whole = lambda *shape: pl.BlockSpec(shape, lambda h, *_: (0,) * len(shape))
    line = pl.BlockSpec((1, 1, cols), lambda h, *_: (h, 0, 0))
    grad_shape = (2, owners // 2 * pairs, grad_rows, 2 * cols)
    return pl.pallas_call(
        kernel,
        grid_spec=pltpu.PrefetchScalarGridSpec(
            num_scalar_prefetch=1,
            grid=(half,),
            in_specs=[
                whole(rows, depth),
                whole(channels, rows),
                whole(rows, depth),
                whole(channels, rows),
                line,
                pl.BlockSpec(memory_space=pl.ANY),
            ],
            out_specs=[whole(rows, depth), whole(rows, depth), pl.BlockSpec(memory_space=pl.ANY), line],
            scratch_shapes=[
                pltpu.VMEM((2, 2, depth, 2 * cols), BF),
                pltpu.VMEM((depth, cols), BF),
                pltpu.VMEM((depth, cols), BF),
                pltpu.VMEM((rows, cols), BF),
                pltpu.VMEM((rows, cols), BF),
                pltpu.VMEM(grad_shape, BF),
                pltpu.SemaphoreType.DMA((2, 2)),
                pltpu.SemaphoreType.DMA((1,)),
            ],
        ),
        out_shape=[
            jax.ShapeDtypeStruct((rows, depth), F32),
            jax.ShapeDtypeStruct((rows, depth), F32),
            jax.ShapeDtypeStruct(grad_shape, BF),
            jax.ShapeDtypeStruct((half, 1, cols), F32),
        ],
        cost_estimate=pl.CostEstimate(
            flops=12 * rows * channels * half * cols, bytes_accessed=40 << 20, transcendentals=rows * half * cols
        ),
        compiler_params=pltpu.CompilerParams(vmem_limit_bytes=63 << 20),
        name="feed_forward",
    )(inverse, shaped, shaped_t, d_branch, d_branch_t, hidden_bias, weights)


def close_out(branch, d_shaped, inputs, conv_out, mask_lanes, out_bias, parts, run):
    rows, channels = inputs.shape
    depth = branch.shape[1]
    step = 3 * LANES if rows % (3 * LANES) == 0 else LANES

    def kernel(b_ref, d_ref, x_ref, v_ref, m_ref, o_ref, out_ref, ds_ref, sum_ref):
        branch_here = close_lanes(b_ref[...], parts, run) + o_ref[...]
        out_ref[...] = (m_ref[:, :1] * (x_ref[...].astype(F32) + branch_here)).astype(BF)
        grads = close_lanes(d_ref[...], parts, run)
        ds_ref[...] = grads

        @pl.when(pl.program_id(0) == 0)
        def _():
            sum_ref[...] = jnp.zeros_like(sum_ref)

        sum_ref[0] += jnp.sum(grads, axis=0, keepdims=True)
        sum_ref[1] += jnp.sum(grads * v_ref[...], axis=0, keepdims=True)

    line = lambda n: pl.BlockSpec((step, n), lambda i: (i, 0))
    return pl.pallas_call(
        kernel,
        grid=(rows // step,),
        in_specs=[
            line(depth),
            line(depth),
            line(channels),
            line(channels),
            line(LANES),
            pl.BlockSpec((1, channels), lambda i: (0, 0)),
        ],
        out_specs=[line(channels), line(channels), pl.BlockSpec((2, 1, channels), lambda i: (0, 0, 0))],
        out_shape=[
            jax.ShapeDtypeStruct((rows, channels), BF),
            jax.ShapeDtypeStruct((rows, channels), F32),
            jax.ShapeDtypeStruct((2, 1, channels), F32),
        ],
        compiler_params=pltpu.CompilerParams(vmem_limit_bytes=60 << 20),
        name="close_out",
    )(branch, d_shaped, inputs, conv_out, mask_lanes, out_bias)


def up_to(value, unit):
    return -(-value // unit) * unit


def pack_pairs(value):
    slots, rows, cols = value.shape
    return value.reshape(slots // 2, 2, rows, cols).transpose(0, 2, 1, 3).reshape(slots // 2, rows, 2 * cols)


def unpack_pairs(value):
    pairs, rows, cols = value.shape
    return value.reshape(pairs, rows, 2, cols // 2).transpose(0, 2, 1, 3).reshape(2 * pairs, rows, cols // 2)


def per_device(
    grid,
    inputs,
    cotangent,
    master,
    moment_one,
    moment_two,
    left_basis,
    column_basis,
    small_params,
    small_first,
    small_second,
    land_mask,
    tile_count,
    neighbours,
    block_order,
    cell_weight,
    step_count,
):
    position = lax.axis_index("tile")
    sample = lax.axis_index("opt")
    inputs, cotangent = inputs[0], cotangent[0]
    slots, side, _, channels = inputs.shape
    cells = side * side
    rows = slots * cells
    n_tile = grid.n_tile
    n_chunk = -(-channels // LANES)
    per_group = channels // GROUPS
    per_owner, run, cols = master.shape
    pairs = per_owner // 2
    block_total = block_order.shape[0]
    half = block_total // 2
    width = up_to(run, 16)

    live = (jnp.arange(slots) < tile_count[position]).astype(F32)
    mask = (land_mask.astype(F32) * live[:, None, None]).reshape(slots, cells)
    mask_lanes = jnp.broadcast_to(mask[:, :, None], (slots, cells, LANES))
    flat_mask = mask_lanes.reshape(rows, LANES)
    taps = jnp.broadcast_to(small_params[:50, None, :], (50, 8, channels))

    low_master = jnp.pad(pack_pairs(master.astype(BF)), ((0, 0), (0, width - run), (0, 0)))
    rims = rims_of_input(inputs, mask_lanes)
    halos, weights, all_neighbours = exchange_forward(grid, rims, low_master, neighbours)

    weights_float = cell_weight.astype(F32)
    sample_weight = weights_float[sample] * weights_float.shape[0] / jnp.sum(weights_float)
    weight_lanes = jnp.broadcast_to(sample_weight, (8, LANES))
    weight_row = jnp.broadcast_to(sample_weight, (1, LANES))
    flat_cotangent = cotangent.reshape(rows, channels)

    def d_branch_body(g_ref, m_ref, w_ref):
        return m_ref[:, :1] * (w_ref[:, :1] * g_ref[...].astype(F32))

    d_branch, d_branch_t, d_out_bias = arrange(
        d_branch_body,
        (flat_cotangent, flat_mask, weight_row),
        lambda step: [
            pl.BlockSpec((step, channels), lambda i: (i, 0)),
            pl.BlockSpec((step, LANES), lambda i: (i, 0)),
            pl.BlockSpec((1, LANES), lambda i: (0, 0)),
        ],
        rows,
        channels,
        n_tile,
        width,
        "arrange_d_branch",
    )
    conv_out, sums = conv_forward(inputs, mask_lanes, halos, taps)
    sums = jnp.sum(sums, axis=(0, 2))
    occupied = jnp.broadcast_to(jnp.sum(mask), (1, channels))
    sums = tile_total(grid, jnp.concatenate([sums, occupied], 0), 5)
    counted = sums[2, 0] * per_group
    by_group = sums[:2].reshape(2, GROUPS, per_group).sum(2)
    group_mean = by_group[0] / counted
    variance = by_group[1] / counted - group_mean * group_mean
    inv_std = jnp.repeat(lax.rsqrt(variance + epsilon), per_group)
    mean = jnp.repeat(group_mean, per_group)
    gain, shift = small_params[50], small_params[51]
    norm_coefs = jnp.stack([inv_std, mean * inv_std, gain, shift])

    def shaped_body(v_ref, c_ref):
        normed = v_ref[...] * c_ref[0:1] - c_ref[1:2]
        return normed * c_ref[2:3] + c_ref[3:4]

    flat_conv = conv_out.reshape(rows, channels)
    shaped, shaped_t, _ = arrange(
        shaped_body,
        (flat_conv, norm_coefs),
        lambda step: [
            pl.BlockSpec((step, channels), lambda i: (i, 0)),
            pl.BlockSpec((4, channels), lambda i: (0, 0)),
        ],
        rows,
        channels,
        n_tile,
        width,
        "arrange_shaped",
    )

    block_ids = jnp.arange(block_total, dtype=jnp.int32)
    inverse = jnp.sum(
        jnp.where(block_order[None, :] == block_ids[:, None], block_ids[None, :], 0), axis=1
    ).astype(jnp.int32)
    hidden_bias = small_params[53:57].reshape(half, 1, cols)
    branch, d_shaped, grads, d_hidden = feed_forward(
        inverse, shaped, shaped_t, d_branch, d_branch_t, hidden_bias, weights, n_tile * width
    )
    block_output, d_shaped, d_sums = close_out(
        branch, d_shaped, inputs.reshape(rows, channels), flat_conv, flat_mask, small_params[52:53], n_tile, run
    )

    d_shift = d_sums[0, 0]
    d_gain = inv_std * (d_sums[1, 0] - mean * d_shift)
    parts = tile_total(grid, jnp.stack([gain * d_shift, gain * d_gain]), 6)
    parts = jnp.repeat(parts.reshape(2, GROUPS, per_group).sum(2) / counted, per_group, axis=1)
    grad_coefs = jnp.stack(
        [
            inv_std * gain,
            inv_std * (parts[0] - mean * inv_std * parts[1]),
            inv_std * inv_std * parts[1],
        ]
    )
    d_conv, grad_rims = conv_gradient(
        d_shaped.reshape(slots, cells, channels),
        conv_out,
        mask_lanes,
        jnp.broadcast_to(grad_coefs[:, None, :], (3, 8, channels)),
        side,
    )
    grad_halos, partial = exchange_backward(grid, grad_rims, grads, all_neighbours)
    d_taps = tap_gradient(inputs, mask_lanes, halos, d_conv)
    input_grad = conv_backward(d_conv, grad_halos, cotangent, mask_lanes, taps, weight_lanes)

    correction = 1.0 - jnp.power(F32(decay_rate), step_count[0].astype(F32))
    d_small = jnp.concatenate(
        [d_taps, d_gain[None], d_shift[None], d_out_bias, d_hidden.reshape(4, channels)], 0
    )
    owned, d_small = finish_gradients(grid, partial, d_small)
    small_one = decay_rate * small_first + (1.0 - decay_rate) * d_small
    small_two = decay_rate * small_second + (1.0 - decay_rate) * d_small * d_small
    new_small = small_params - small_rate * (small_one / correction) / (
        jnp.sqrt(small_two / correction) + adam_eps
    )

    owned = unpack_pairs(owned[:, :channels])
    rotated = jnp.einsum("bdk,bdw->bkw", left_basis, owned.astype(F32), precision=highest)
    rotated = jnp.einsum("bkw,bwv->bkv", rotated, column_basis, precision=highest)
    first_new = decay_rate * moment_one + (1.0 - decay_rate) * rotated
    second_new = decay_rate * moment_two + (1.0 - decay_rate) * rotated * rotated
    direction = first_new / correction / (jnp.sqrt(second_new / correction) + adam_eps)
    turned = jnp.einsum("bkv,bwv->bkw", direction, column_basis, precision=highest)
    change = jnp.einsum("bdk,bkw->bdw", left_basis, turned, precision=highest)
    side_a, side_b = grid.size["a"], grid.size["b"]
    change = change.reshape(pairs, 2, side_a, side_b, run, cols).transpose(0, 3, 2, 4, 1, 5)
    change = jnp.pad(change.reshape(pairs, n_tile, run, 2 * cols).astype(BF), ((0, 0), (0, 0), (0, width - run), (0, 0)))
    change = scatter_change(grid, change.reshape(pairs, n_tile * width, 2 * cols))
    change = unpack_pairs(change[:, :run])
    new_master = master - 0.5 / math.sqrt(channels) * change
    return (
        block_output.reshape((1,) + inputs.shape),
        input_grad.reshape((1,) + inputs.shape),
        new_master,
        new_master.astype(BF),
        first_new,
        second_new,
        new_small,
        small_one,
        small_two,
    )


def solution(mesh):
    grid = Grid(mesh.shape["tile"], mesh.shape["opt"])

    def step(*args):
        return per_device(grid, *args)

    return jax.shard_map(
        step,
        mesh=mesh,
        in_specs=(
            P("opt", "tile", None, None, None),
            P("opt", "tile", None, None, None),
            P("opt", "tile", None),
            P("opt", "tile", None),
            P("opt", "tile", None),
            P("opt", None, "tile"),
            P("opt", None, None),
            P(),
            P(),
            P(),
            P("tile", None, None),
            P(),
            P("tile", None),
            P(),
            P(),
            P(),
        ),
        out_specs=(
            P("opt", "tile", None, None, None),
            P("opt", "tile", None, None, None),
            P("opt", "tile", None),
            P("opt", "tile", None),
            P("opt", "tile", None),
            P("opt", "tile", None),
            P(),
            P(),
            P(),
        ),
        check_vma=False,
    )
```

time: 750 us -> 698 us (0.931)
  Pallas kernels: 181 us -> 561 us
  waiting for transfers between devices: 190 us -> 0 us
  starting transfers between devices: 165 us -> 0 us
  other arithmetic: 50.8 us -> 7.2 us
  local copies, waits for them, and re-layouts: 134 us -> 96.2 us
    pallas_call x7 -> x11, Pallas kernels: 66.7 us -> 447 us  [the longest x1 124 us: exchange_forward(): pl.pallas_call(kernel, in_specs=[any_space] * 3, out_specs=[any_space] *...]
    ppermute x88 -> x0, waiting for transfers between devices: 190 us -> none  [the longest x46 117 us: swap(): return lax.ppermute(value, ('tile', 'opt'), pairs)]
    ppermute x88 -> x0, starting transfers between devices: 165 us -> none  [the longest x42 106 us: tile_swap(): return lax.ppermute(value, ('tile', 'opt'), pairs)]
    convert_element_type x0 -> x3, local copies, waits for them, and re-layouts: none -> 44.2 us  [per_device(): change.reshape(pairs, n_tile, run, 2 * cols).astype(BF)]
    ppermute x5 -> x0, local copies, waits for them, and re-layouts: 30.5 us -> none  [swap(): return lax.ppermute(value, ('tile', 'opt'), pairs)]
    another operation x10 -> x2, local copies, waits for them, and re-layouts: 30.4 us -> 1.08 us  [the longest x8 26.4 us: gather(): jnp.stack([value] + [self.swap(value, dim, k) for k in range(1, self.size...]
    another operation x14 -> x1, other arithmetic: 21.6 us -> 0.01 us  [per_device(): parts = tile_total(grid, jnp.stack([gain * d_shift, gain * d_gain]), 6)]
    convert_element_type x8 -> x1, other arithmetic: 15.5 us -> 0.31 us  [per_device(): new_master.astype(BF)]
  transfers between devices with their start and end apart: 88 -> 0, of which waited for: 36 -> 0; matrix products, arithmetic and copies ran while one was open for 20% -> 0% of each run, Pallas kernels for 12% -> 0%
where the time goes in v2:
time: 698 us; the launch traced here: 691 us
  Pallas kernels  561 us (80%)
  local copies, waits for them, and re-layouts  96.2 us (14%)
  matrix products  22.6 us (3%)
  other arithmetic  7.2 us (1%)
    pallas_call x1, Pallas kernels, exchange_forward(): pl.pallas_call(kernel, in_specs=[any_space] * 3, out_specs=[any_space] *...  124 us
    pallas_call x1, Pallas kernels, finish_gradients(): pl.pallas_call(kernel, in_specs=[any_space, whole], out_specs=[any_space,...  111 us
    pallas_call x1, Pallas kernels, feed_forward(): pl.pallas_call(kernel, grid_spec=pltpu.PrefetchScalarGridSpec(num_scalar_...  93.2 us
    pallas_call x1, Pallas kernels, exchange_backward(): pl.pallas_call(kernel, in_specs=[any_space, any_space, pl.BlockSpec(memor...  86.4 us
    pallas_call x1, Pallas kernels, scatter_change(): pl.pallas_call(kernel, in_specs=[any_space], out_specs=pl.BlockSpec(memor...  55.6 us
    convert_element_type x3, local copies, waits for them, and re-layouts, per_device(): change.reshape(pairs, n_tile, run, 2 * cols).astype(BF)  44.2 us
    unnamed x87, local copies, waits for them, and re-layouts  42.6 us
    pallas_call x2, Pallas kernels, tile_total(): pl.pallas_call(kernel, in_specs=[whole], out_specs=whole, out_shape=jax.S...  21 us

profile of v2, /device:TPU:8, one launch (start us, length us, event | category | flops | bytes accessed | tf_op | source)
XLA Modules:
  0.0 691.3 jit_solution(1906686657458572346)
XLA Ops:
  4.9 1.6 copy-done.2
  10.6 124.0 %exchange_forward.1 = (bf16[7,2,5,72,128]{4,3,2,1,0:T(8,128)(2,1)S(1)}, bf16[2,4,896,800]{3,2,1,0:T(8,128)(2,1)S(1)}, s32[8,2,8]{2,1,0:T(2,128)S(1)}) custom-call(bf16[7,2,4,72,128]{4,3,2,1,0:T(8,128)(2,1)S(1)} %copy-done.7, bf16[2,112,800]{2,1,0:T(8,128)(2,1)S(1)} %pad.9.p_ref, s32[2,8]{1,0:T(2,128)S(1)} %copy-done.15), custom_call_target="tpu_custom_call" | custom-call | tf_op jit(solution)/shard_map/exchange_forward/pallas_call | solution.py:320
  134.6 4.6 copy-done.16
  140.5 15.3 %conv_forward.1 = (f32[2,576,800]{2,1,0:T(8,128)S(1)}, f32[2,2,8,800]{3,2,1,0:T(8,128)S(1)}) custom-call(bf16[2,24,24,800]{3,2,1,0:T(8,128)(2,1)S(1)} %bitcast.61, f32[2,576,128]{2,1,0:T(8,128)S(1)} %broadcast_in_dim.65.m_ref, f32[50,8,800]{2,1,0:T(8,128)S(1)} %broadcast_in_dim.66.w_ref, bf16[7,2,5,72,128]{4,3,2,1,0:T(8,128)(2,1)S(1)} %get-tuple-element.32.h_ref), custom_call_target="tpu_custom_call" | custom-call | flops 10115481600 | bytes 10485760 | tf_op jit(solution)/shard_map/conv_forward/pallas_call | solution.py:709
  155.9 2.0 copy-done
  158.6 13.9 %tile_total.2 = f32[3,800]{1,0:T(4,128)S(1)} custom-call(f32[3,800]{1,0:T(4,128)S(1)} %concatenate.12.v_ref), custom_call_target="tpu_custom_call" | custom-call | tf_op jit(solution)/shard_map/tile_total/pallas_call | solution.py:627
  174.3 5.1 arrange_shaped.1
  184.8 4.1 arrange_d_branch.1
  193.6 93.2 %feed_forward.1 = (f32[1152,896]{1,0:T(8,128)}, f32[1152,896]{1,0:T(8,128)}, bf16[2,4,896,800]{3,2,1,0:T(8,128)(2,1)}, f32[8,1,400]{2,1,0:T(1,128)}) custom-call(s32[16]{0:T(128)} %select_reduce_fusion.inv_ref, bf16[1152,896]{1,0:T(8,128)(2,1)} %copy-done.19, bf16[800,1152]{1,0:T(8,128)(2,1)} %copy-done.21, bf16[1152,896]{1,0:T(8,128)(2,1)} %copy-done.20, ...), custom_call_target="tpu_custom_call" | custom-call | flops 35389440000 | bytes 41943040 | tf_op jit(solution)/shard_map/feed_forward/pallas_call | solution.py:1018
  287.3 11.3 %close_out.1 = (bf16[1152,800]{1,0:T(8,128)(2,1)}, f32[1152,800]{1,0:T(8,128)}, f32[2,1,800]{2,1,0:T(1,128)}) custom-call(f32[1152,896]{1,0:T(8,128)} %get-tuple-element.40.b_ref, f32[1152,896]{1,0:T(8,128)} %get-tuple-element.41.d_ref, bf16[1152,800]{1,0:T(8,128)(2,1)} %bitcast.59, f32[1152,800]{1,0:T(8,128)} %bitcast.57, f32[1152,128]{1,0:T(8,128)} %copy-done.5, ...), custom_call_target="tpu_custom_call" | custom-call | tf_op jit(solution)/shard_map/close_out/pallas_call | solution.py:1076
  299.4 7.1 %tile_total.3 = f32[2,800]{1,0:T(2,128)S(1)} custom-call(f32[2,800]{1,0:T(2,128)S(1)} %pad_maximum_fusion.3.v_ref), custom_call_target="tpu_custom_call" | custom-call | tf_op jit(solution)/shard_map/tile_total/pallas_call | solution.py:627
  307.1 2.2 copy-done.1
  309.2 2.2 copy-done.8
  311.4 2.5 conv_gradient.1
  313.9 15.4 %tap_gradient.1 = f32[50,800]{1,0:T(8,128)S(1)} custom-call(bf16[2,24,24,800]{3,2,1,0:T(8,128)(2,1)S(1)} %bitcast.62, f32[2,576,128]{2,1,0:T(8,128)S(1)} %broadcast_in_dim.65.m_ref, f32[2,576,800]{2,1,0:T(8,128)S(1)} %get-tuple-element.45.d_ref, bf16[7,2,5,72,128]{4,3,2,1,0:T(8,128)(2,1)S(1)} %copy-done.24), custom_call_target="tpu_custom_call" | custom-call | flops 10115481600 | bytes 10485760 | tf_op jit(solution)/shard_map/tap_gradient/pallas_call | solution.py:806
  329.7 86.4 %exchange_backward.1 = (bf16[7,2,5,72,128]{4,3,2,1,0:T(8,128)(2,1)}, bf16[2,448,800]{2,1,0:T(8,128)(2,1)}) custom-call(bf16[7,2,4,72,128]{4,3,2,1,0:T(8,128)(2,1)} %copy-done.13, bf16[2,4,896,800]{3,2,1,0:T(8,128)(2,1)} %get-tuple-element.47.g_ref, s32[8,2,8]{2,1,0:T(2,128)} %copy-done.14), custom_call_target="tpu_custom_call" | custom-call | tf_op jit(solution)/shard_map/exchange_backward/pallas_call | solution.py:441
  417.5 110.5 %finish_gradients.1 = (bf16[2,896,800]{2,1,0:T(8,128)(2,1)S(1)}, f32[57,800]{1,0:T(8,128)S(1)}) custom-call(bf16[2,448,800]{2,1,0:T(8,128)(2,1)S(1)} %copy-done.10, f32[57,800]{1,0:T(8,128)S(1)} %concatenate.13.s_ref), custom_call_target="tpu_custom_call" | custom-call | tf_op jit(solution)/shard_map/finish_gradients/pallas_call | solution.py:525
  530.3 4.1 fusion.1
  535.9 2.4 copy.53
  538.3 8.9 %fusion.3 = (f32[4,100,400]{1,2,0:T(8,128)S(1)}, f32[4,100,400]{1,2,0:T(8,128)S(1)}) fusion(f32[4,100,400]{1,2,0:T(8,128)} %copy.53, f32[4,100,400]{1,2,0:T(8,128)S(1)} %copy.49, f32[4,400,100]{2,1,0:T(8,128)} %fusion.1, f32[4,400,400]{2,1,0:T(8,128)} %param.22), kind=kOutput, calls=%fused_computation.8 | convolution fusion | flops 768960000 | bytes 5760000 | tf_op jit(solution)/shard_map/bkw,bwv->bkv/dot_general | solution.py:1258
  548.0 3.6 fusion.4
  551.6 6.0 convert_bitcast_fusion
  557.6 16.6 %convert_element_type.50 = bf16[2,2,4,2,100,400]{4,3,2,5,1,0:T(2,128)(2,1)} reshape(bf16[4,800,400]{1,2,0:T(8,128)(2,1)} %convert_bitcast_fusion) | data formatting | bytes 5120000 | tf_op jit(solution)/shard_map/convert_element_type | solution.py:1266
  574.2 19.5 %copy.55 = bf16[2,2,4,2,100,400]{5,1,2,3,4,0:T(2,128)(2,1)} copy(bf16[2,2,4,2,100,400]{4,3,2,5,1,0:T(2,128)(2,1)} %convert_element_type.50) | data formatting | bytes 5120000 | tf_op jit(solution)/shard_map/convert_element_type | solution.py:1266
  593.7 8.1 %convert_element_type.52 = bf16[2,8,100,800]{3,1,2,0:T(8,128)(2,1)} reshape(bf16[2,2,4,100,2,400]{5,4,2,1,3,0:T(2,128)(2,1)} %bitcast.66) | data formatting | bytes 5120000 | tf_op jit(solution)/shard_map/convert_element_type | solution.py:1266
  601.8 2.2 copy.65
  604.2 55.6 %scatter_change.1 = f32[2,112,800]{2,1,0:T(8,128)S(1)} custom-call(bf16[2,896,800]{2,1,0:T(8,128)(2,1)S(1)} %bitcast.58), custom_call_target="tpu_custom_call" | custom-call | tf_op jit(solution)/shard_map/scatter_change/pallas_call | solution.py:592
  663.7 2.5 copy.60
  666.1 2.5 copy.61
  668.6 1.9 divide_subtract_fusion
  671.8 2.2 copy-done.18
  675.3 15.9 %conv_backward.1 = f32[2,576,800]{2,1,0:T(8,128)} custom-call(f32[2,576,800]{2,1,0:T(8,128)S(1)} %copy-done.18, bf16[2,24,24,800]{3,2,1,0:T(8,128)(2,1)S(1)} %bitcast.65, f32[2,576,128]{2,1,0:T(8,128)S(1)} %broadcast_in_dim.65.m_ref, f32[50,8,800]{2,1,0:T(8,128)S(1)} %copy-done.12, f32[8,128]{1,0:T(8,128)S(1)} %broadcast_in_dim.77.l_ref, ...), custom_call_target="tpu_custom_call" | custom-call | flops 10115481600 | bytes 12582912 | tf_op jit(solution)/shard_map/conv_backward/pallas_call | solution.py:846
  (138 shorter events, 34.1 us)
Async XLA Ops:
  4.9 1.6 copy-start.2
  6.5 1.9 copy-start.30
  6.5 2.9 copy-start.15
  8.5 132.0 %copy-start.3 = (bf16[1,2,24,24,800]{4,3,2,1,0:T(8,128)(2,1)S(1)}, bf16[1,2,24,24,800]{4,3,2,1,0:T(8,128)(2,1)}, u32[]{:S(2)}) copy-start(bf16[1,2,24,24,800]{4,3,2,1,0:T(8,128)(2,1)} %param.16) | copy-start | bytes 5529604
  134.6 4.6 copy-start.16
  139.2 16.6 %copy-start.23 = (bf16[7,2,5,72,128]{4,3,2,1,0:T(8,128)(2,1)}, bf16[7,2,5,72,128]{4,3,2,1,0:T(8,128)(2,1)S(1)}, u32[]{:S(2)}) copy-start(bf16[7,2,5,72,128]{4,3,2,1,0:T(8,128)(2,1)S(1)} %get-tuple-element.32.h_ref) | copy-start | bytes 3870724
  140.5 15.3 %copy-start.11 = (f32[50,8,800]{2,1,0:T(8,128)}, f32[50,8,800]{2,1,0:T(8,128)S(1)}, u32[]{:S(2)}) copy-start(f32[50,8,800]{2,1,0:T(8,128)S(1)} %broadcast_in_dim.66.w_ref) | copy-start | bytes 3840004
  140.5 33.7 %copy-start.32 = (f32[57,800]{1,0:T(8,128)S(1)}, f32[57,800]{1,0:T(8,128)}, u32[]{:S(2)}) copy-start(f32[57,800]{1,0:T(8,128)} %param.23) | copy-start | bytes 547204
  155.9 2.0 copy-start
  157.9 24.0 %copy-start.35 = (f32[2,24,24]{2,1,0:T(8,128)S(1)}, f32[2,24,24]{2,1,0:T(8,128)}, u32[]{:S(2)}) copy-start(f32[2,24,24]{2,1,0:T(8,128)} %copy-done.34) | copy-start | bytes 13828
  157.9 24.3 %copy-start.38 = (s32[4]{0:T(128)S(1)}, s32[4]{0:T(128)}, u32[]{:S(2)}) copy-start(s32[4]{0:T(128)} %param.30) | copy-start | bytes 52
  174.3 18.6 %copy-start.39 = (s32[16]{0:T(128)S(1)}, s32[16]{0:T(128)}, u32[]{:S(2)}) copy-start(s32[16]{0:T(128)} %param.29) | copy-start | bytes 196
  179.4 1.3 copy-start.19
  189.7 1.3 copy-start.20
  307.0 2.2 copy-start.1
  309.2 2.2 copy-start.8
  311.4 2.5 copy-start.4
  311.4 2.5 copy-start.24
  313.9 15.4 %copy-start.13 = (bf16[7,2,4,72,128]{4,3,2,1,0:T(8,128)(2,1)}, bf16[7,2,4,72,128]{4,3,2,1,0:T(8,128)(2,1)S(1)}, u32[]{:S(2)}) copy-start(bf16[7,2,4,72,128]{4,3,2,1,0:T(8,128)(2,1)S(1)} %get-tuple-element.46.r_ref) | copy-start | bytes 3096580
  313.9 15.4 %copy-start.17 = (f32[2,576,800]{2,1,0:T(8,128)}, f32[2,576,800]{2,1,0:T(8,128)S(1)}, u32[]{:S(2)}) copy-start(f32[2,576,800]{2,1,0:T(8,128)S(1)} %get-tuple-element.45.d_ref) | copy-start | bytes 11059204
  313.9 15.4 %copy-start.37 = (f32[2,1,800]{2,1,0:T(1,128)S(1)}, f32[2,1,800]{2,1,0:T(1,128)}, u32[]{:S(2)}) copy-start(f32[2,1,800]{2,1,0:T(1,128)} %get-tuple-element.44) | copy-start | bytes 19204
  313.9 15.4 %copy-start.36 = (f32[8,1,400]{2,1,0:T(1,128)S(1)}, f32[8,1,400]{2,1,0:T(1,128)}, u32[]{:S(2)}) copy-start(f32[8,1,400]{2,1,0:T(1,128)} %get-tuple-element.52) | copy-start | bytes 38404
  416.1 1.4 copy-start.10
  528.9 1.4 copy-start.26
  538.3 9.7 %copy-start.27 = (f32[4,400,400]{2,1,0:T(8,128)S(1)}, f32[4,400,400]{2,1,0:T(8,128)}, u32[]{:S(2)}) copy-start(f32[4,400,400]{2,1,0:T(8,128)} %param.22) | copy-start | bytes 7680004
  547.2 4.3 copy-start.28
  547.2 4.3 copy-start.29
  661.3 7.3 %copy-start.33 = (f32[57,800]{1,0:T(8,128)S(1)}, f32[57,800]{1,0:T(8,128)}, u32[]{:S(2)}) copy-start(f32[57,800]{1,0:T(8,128)} %param.24) | copy-start | bytes 547204
  662.7 7.7 %copy-start.9 = (bf16[1,2,24,24,800]{4,3,2,1,0:T(8,128)(2,1)S(1)}, bf16[1,2,24,24,800]{4,3,2,1,0:T(8,128)(2,1)}, u32[]{:S(2)}) copy-start(bf16[1,2,24,24,800]{4,3,2,1,0:T(8,128)(2,1)} %param.17) | copy-start | bytes 5529604
  670.4 1.4 copy-start.12
  671.8 2.2 copy-start.18
  674.0 1.3 copy-start.25
  (8 other events, 8.4 us)

commit v3 on v2

--- a/solution.py
+++ b/solution.py
@@ -251,37 +251,47 @@
             t, o = grid.at({d: own[d] ^ rel.get(d, 0) for d in own})
             return gathered.at[m, o, pl.ds(pl.multiple_of(t * width, width), width)]
 
-        keeps = []
-        known = []
+        keeps, started = [], []
         for m in range(self.pairs):
             keep = pltpu.make_async_copy(packed.at[m], place(m, {}), local.at[m])
             keep.start()
             keeps.append(keep)
-            known.append([({}, None)])
-        arrived = set()
-        for stage in range(4):
-            for m in range(self.pairs):
-                order = ("a", "x", "b", "c") if m % 2 == 0 else ("a", "b", "x", "c")
-                dim = order[stage]
-                fresh = []
+
+        def forward(m, rel, dims):
+            source = packed.at[m] if not rel else place(m, rel)
+            fresh = []
+            for dim in dims:
                 for k in range(1, grid.size[dim]):
-                    for rel, got in known[m]:
-                        if got is not None and id(got) not in arrived:
-                            got.wait_recv()
-                            arrived.add(id(got))
-                        source = packed.at[m] if not rel else place(m, rel)
-                        copy = copies.start(source, place(m, rel), grid.beside(own, dim, k))
-                        fresh.append(({**rel, dim: k}, copy))
-                known[m] = known[m] + fresh
-            yield stage
+                    copy = copies.start(source, place(m, rel), grid.beside(own, dim, k))
+                    fresh.append(({**rel, dim: k}, copy))
+            started.extend(copy for _, copy in fresh)
+            return fresh
+
+        orders = [("a", "x", "b", "c") if m % 2 == 0 else ("a", "b", "x", "c") for m in range(self.pairs)]
+        waves = {}
+
+        def note(m, fresh, after):
+            for rel, copy in fresh:
+                level = sum(1 for d in rel if d != "c")
+                wave = max(rel.get("a", 0) + level - ("a" in rel), after)
+                waves.setdefault(wave, []).append((m, rel, copy))
+
         for m in range(self.pairs):
-            keeps[m].wait()
-            for _, got in known[m]:
-                if got is not None:
-                    if id(got) not in arrived:
-                        got.wait_recv()
-                    got.wait_send()
-        yield 4
+            note(m, forward(m, {}, orders[m]), 0)
+        yield 0
+        for wave in range(4 * sum(grid.size.values())):
+            for m, rel, copy in sorted(waves.pop(wave, []), key=lambda e: "c" in e[1]):
+                copy.wait_recv()
+                last = max(orders[m].index(d) for d in rel)
+                note(m, forward(m, rel, orders[m][last + 1 :]), wave + 1)
+            if not waves:
+                break
+            yield wave
+        for keep in keeps:
+            keep.wait()
+        for copy in started:
+            copy.wait_send()
+        yield -1
 
 
 def exchange_forward(grid, rims, packed, neighbours):
@@ -491,7 +501,8 @@
             copy.wait()
             t_ref[...] = t_ref[...] + sums[i]
 
-        small_step(0)
+        for i in range(len(steps)):
+            small_step(i)
         seconds, thirds, keeps = [], [], []
         for m in range(pairs):
             loads[m].wait()
@@ -506,8 +517,6 @@
                 [(k, copies.start(mine.at[m], to, grid.beside(own, "a", k))) for k in range(1, side_a)]
             )
             thirds += [copies.start(mine.at[m], to, grid.beside(own, "b", j)) for j in range(1, side_b)]
-        for i in range(1, len(steps)):
-            small_step(i)
         for m in range(pairs):
             for k, copy in seconds[m]:
                 copy.wait_recv()
@@ -1095,6 +1104,75 @@
     )(branch, d_shaped, inputs, conv_out, mask_lanes, out_bias)
 
 
+def halves(value):
+    high = value.astype(BF)
+    return high, (value - high.astype(F32)).astype(BF)
+
+
+def product(left, right, contract):
+    dims = (contract, ((), ()))
+    total = None
+    for i, a in enumerate(left):
+        for j, b in enumerate(right):
+            if i + j < 2:
+                term = lax.dot_general(a, b, dims, preferred_element_type=F32)
+                total = term if total is None else total + term
+    return total
+
+
+def rotate(owned, left_basis, column_basis, moment_one, moment_two, correction, grid, width):
+    slots, channels, run = left_basis.shape
+    cols = column_basis.shape[1]
+    pairs = slots // 2
+    side_a, side_b = grid.size["a"], grid.size["b"]
+    n_tile = grid.n_tile
+
+    def kernel(f_ref, g_ref, l_ref, c_ref, one_ref, two_ref, first_ref, second_ref, o_ref):
+        factor = f_ref[0]
+        changes = []
+        for p in range(2):
+            grad = g_ref[0, pl.ds(0, channels), p * cols : (p + 1) * cols]
+            left = halves(l_ref[p])
+            column = halves(c_ref[p])
+            rotated = product(left, (grad,), ((0,), (0,)))
+            rotated = product(halves(rotated), column, ((1,), (0,)))
+            first = decay_rate * one_ref[p] + (1.0 - decay_rate) * rotated
+            second = decay_rate * two_ref[p] + (1.0 - decay_rate) * rotated * rotated
+            first_ref[p] = first
+            second_ref[p] = second
+            direction = first * factor / (jnp.sqrt(second * factor) + adam_eps)
+            turned = product(halves(direction), column, ((1,), (1,)))
+            changes.append(product(left, halves(turned), ((1,), (0,))))
+        change = jnp.concatenate(changes, 1)
+        gap = jnp.zeros((width - run, 2 * cols), F32)
+        for t in range(n_tile):
+            piece = jnp.concatenate([change[t * run : (t + 1) * run], gap], 0)
+            place = (t % side_b) * side_a + t // side_b
+            o_ref[0, pl.ds(place * width, width), :] = piece.astype(BF)
+
+    pair = lambda *shape: pl.BlockSpec(shape, lambda m: (m,) + (0,) * (len(shape) - 1))
+    return pl.pallas_call(
+        kernel,
+        grid=(pairs,),
+        in_specs=[
+            pl.BlockSpec(memory_space=pltpu.SMEM),
+            pair(1, owned.shape[1], 2 * cols),
+            pair(2, channels, run),
+            pair(2, cols, cols),
+            pair(2, run, cols),
+            pair(2, run, cols),
+        ],
+        out_specs=[pair(2, run, cols), pair(2, run, cols), pair(1, n_tile * width, 2 * cols)],
+        out_shape=[
+            jax.ShapeDtypeStruct(moment_one.shape, F32),
+            jax.ShapeDtypeStruct(moment_one.shape, F32),
+            jax.ShapeDtypeStruct((pairs, n_tile * width, 2 * cols), BF),
+        ],
+        compiler_params=pltpu.CompilerParams(vmem_limit_bytes=60 << 20),
+        name="rotate",
+    )(1.0 / correction.reshape(1), owned, left_basis, column_basis, moment_one, moment_two)
+
+
 def up_to(value, unit):
     return -(-value // unit) * unit
 
@@ -1253,19 +1331,10 @@
         jnp.sqrt(small_two / correction) + adam_eps
     )
 
-    owned = unpack_pairs(owned[:, :channels])
-    rotated = jnp.einsum("bdk,bdw->bkw", left_basis, owned.astype(F32), precision=highest)
-    rotated = jnp.einsum("bkw,bwv->bkv", rotated, column_basis, precision=highest)
-    first_new = decay_rate * moment_one + (1.0 - decay_rate) * rotated
-    second_new = decay_rate * moment_two + (1.0 - decay_rate) * rotated * rotated
-    direction = first_new / correction / (jnp.sqrt(second_new / correction) + adam_eps)
-    turned = jnp.einsum("bkv,bwv->bkw", direction, column_basis, precision=highest)
-    change = jnp.einsum("bdk,bkw->bdw", left_basis, turned, precision=highest)
-    side_a, side_b = grid.size["a"], grid.size["b"]
-    change = change.reshape(pairs, 2, side_a, side_b, run, cols).transpose(0, 3, 2, 4, 1, 5)
-    change = jnp.pad(change.reshape(pairs, n_tile, run, 2 * cols).astype(BF), ((0, 0), (0, 0), (0, width - run), (0, 0)))
-    change = scatter_change(grid, change.reshape(pairs, n_tile * width, 2 * cols))
-    change = unpack_pairs(change[:, :run])
+    first_new, second_new, change = rotate(
+        owned, left_basis, column_basis, moment_one, moment_two, correction, grid, width
+    )
+    change = unpack_pairs(scatter_change(grid, change)[:, :run])
     new_master = master - 0.5 / math.sqrt(channels) * change
     return (
         block_output.reshape((1,) + inputs.shape),

time: 698 us -> 580 us (0.83)
  local copies, waits for them, and re-layouts: 96.2 us -> 42.5 us
  Pallas kernels: 561 us -> 527 us
  matrix products: 22.6 us -> 0 us
    convert_element_type x3 -> x0, local copies, waits for them, and re-layouts: 44.2 us -> none  [per_device(): change.reshape(pairs, n_tile, run, 2 * cols).astype(BF)]
    pallas_call x1, Pallas kernels: 124 us -> 98.5 us  [exchange_forward(): pl.pallas_call(kernel, in_specs=[any_space] * 3, out_specs=[any_space] *...]
    dot_general x4 -> x0, matrix products: 22.6 us -> none  [the longest x1 8.93 us: per_device(): jnp.einsum('bkw,bwv->bkv', rotated, column_basis, precision=highest)]
    pallas_call x1, Pallas kernels: 111 us -> 90.2 us  [finish_gradients(): pl.pallas_call(kernel, in_specs=[any_space, whole], out_specs=[any_space,...]
    pallas_call x0 -> x1, Pallas kernels: none -> 12.3 us  [rotate(): pl.pallas_call(kernel, grid=(pairs,), in_specs=[pl.BlockSpec(memory_space...]
    unnamed x87 -> x85, local copies, waits for them, and re-layouts: 42.6 us -> 35.4 us
where the time goes in v3:
time: 580 us; the launch traced here: 579 us
  Pallas kernels  527 us (91%)
  local copies, waits for them, and re-layouts  42.5 us (7%)
  other arithmetic  5.84 us (1%)
    pallas_call x1, Pallas kernels, exchange_forward(): pl.pallas_call(kernel, in_specs=[any_space] * 3, out_specs=[any_space] *...  98.5 us
    pallas_call x1, Pallas kernels, feed_forward(): pl.pallas_call(kernel, grid_spec=pltpu.PrefetchScalarGridSpec(num_scalar_...  92.3 us
    pallas_call x1, Pallas kernels, finish_gradients(): pl.pallas_call(kernel, in_specs=[any_space, whole], out_specs=[any_space,...  90.2 us
    pallas_call x1, Pallas kernels, exchange_backward(): pl.pallas_call(kernel, in_specs=[any_space, any_space, pl.BlockSpec(memor...  86.5 us
    pallas_call x1, Pallas kernels, scatter_change(): pl.pallas_call(kernel, in_specs=[any_space], out_specs=pl.BlockSpec(memor...  51.2 us
    unnamed x85, local copies, waits for them, and re-layouts  35.4 us
    pallas_call x2, Pallas kernels, tile_total(): pl.pallas_call(kernel, in_specs=[whole], out_specs=whole, out_shape=jax.S...  25.2 us
    pallas_call x1, Pallas kernels, conv_backward(): pl.pallas_call(kernel, grid=(n_chunk, slots), in_specs=[pl.BlockSpec((1,...  15.9 us

profile of v3, /device:TPU:8, one launch (start us, length us, event | category | flops | bytes accessed | tf_op | source)
XLA Modules:
  0.0 579.0 jit_solution(10857030332519324810)
XLA Ops:
  0.6 1.2 dynamic_slice.6
  2.5 1.4 fusion.7
  4.3 1.6 copy-done.2
  8.0 98.5 %exchange_forward.1 = (bf16[7,2,5,72,128]{4,3,2,1,0:T(8,128)(2,1)S(1)}, bf16[2,4,896,800]{3,2,1,0:T(8,128)(2,1)S(1)}, s32[8,2,8]{2,1,0:T(2,128)S(1)}) custom-call(bf16[7,2,4,72,128]{4,3,2,1,0:T(8,128)(2,1)S(1)} %rims_of_input.1.r_ref, bf16[2,112,800]{2,1,0:T(8,128)(2,1)S(1)} %pad.5.p_ref, s32[2,8]{1,0:T(2,128)S(1)} %copy-done.15), custom_call_target="tpu_custom_call" | custom-call | tf_op jit(solution)/shard_map/exchange_forward/pallas_call | solution.py:330
  106.5 4.6 copy-done.16
  111.3 15.3 %conv_forward.1 = (f32[2,576,800]{2,1,0:T(8,128)S(1)}, f32[2,2,8,800]{3,2,1,0:T(8,128)S(1)}) custom-call(bf16[2,24,24,800]{3,2,1,0:T(8,128)(2,1)S(1)} %bitcast.47, f32[2,576,128]{2,1,0:T(8,128)S(1)} %broadcast_in_dim.65.m_ref, f32[50,8,800]{2,1,0:T(8,128)S(1)} %broadcast_in_dim.66.w_ref, bf16[7,2,5,72,128]{4,3,2,1,0:T(8,128)(2,1)S(1)} %get-tuple-element.35.h_ref), custom_call_target="tpu_custom_call" | custom-call | flops 10115481600 | bytes 10485760 | tf_op jit(solution)/shard_map/conv_forward/pallas_call | solution.py:718
  126.7 2.0 copy-done
  129.3 18.1 %tile_total.2 = f32[3,800]{1,0:T(4,128)S(1)} custom-call(f32[3,800]{1,0:T(4,128)S(1)} %concatenate.9.v_ref), custom_call_target="tpu_custom_call" | custom-call | tf_op jit(solution)/shard_map/tile_total/pallas_call | solution.py:636
  149.2 5.1 arrange_shaped.1
  154.3 1.3 copy-done.19
  159.7 4.1 arrange_d_branch.1
  164.6 1.3 copy-done.20
  165.9 1.3 copy-done.22
  168.5 92.3 %feed_forward.1 = (f32[1152,896]{1,0:T(8,128)}, f32[1152,896]{1,0:T(8,128)}, bf16[2,4,896,800]{3,2,1,0:T(8,128)(2,1)}, f32[8,1,400]{2,1,0:T(1,128)}) custom-call(s32[16]{0:T(128)} %select_reduce_fusion.inv_ref, bf16[1152,896]{1,0:T(8,128)(2,1)} %copy-done.19, bf16[800,1152]{1,0:T(8,128)(2,1)} %copy-done.21, bf16[1152,896]{1,0:T(8,128)(2,1)} %copy-done.20, ...), custom_call_target="tpu_custom_call" | custom-call | flops 35389440000 | bytes 41943040 | tf_op jit(solution)/shard_map/feed_forward/pallas_call | solution.py:1027
  261.3 11.3 %close_out.1 = (bf16[1152,800]{1,0:T(8,128)(2,1)}, f32[1152,800]{1,0:T(8,128)}, f32[2,1,800]{2,1,0:T(1,128)}) custom-call(f32[1152,896]{1,0:T(8,128)} %get-tuple-element.43.b_ref, f32[1152,896]{1,0:T(8,128)} %get-tuple-element.44.d_ref, bf16[1152,800]{1,0:T(8,128)(2,1)} %bitcast.45, f32[1152,800]{1,0:T(8,128)} %bitcast.44, f32[1152,128]{1,0:T(8,128)} %copy-done.5, ...), custom_call_target="tpu_custom_call" | custom-call | tf_op jit(solution)/shard_map/close_out/pallas_call | solution.py:1085
  273.4 7.1 %tile_total.3 = f32[2,800]{1,0:T(2,128)S(1)} custom-call(f32[2,800]{1,0:T(2,128)S(1)} %pad_maximum_fusion.2.v_ref), custom_call_target="tpu_custom_call" | custom-call | tf_op jit(solution)/shard_map/tile_total/pallas_call | solution.py:636
  281.1 2.2 copy-done.1
  283.2 2.2 copy-done.6
  285.4 2.5 conv_gradient.1
  288.0 15.6 %tap_gradient.1 = f32[50,800]{1,0:T(8,128)S(1)} custom-call(bf16[2,24,24,800]{3,2,1,0:T(8,128)(2,1)S(1)} %bitcast.48, f32[2,576,128]{2,1,0:T(8,128)S(1)} %broadcast_in_dim.65.m_ref, f32[2,576,800]{2,1,0:T(8,128)S(1)} %get-tuple-element.48.d_ref, bf16[7,2,5,72,128]{4,3,2,1,0:T(8,128)(2,1)S(1)} %copy-done.24), custom_call_target="tpu_custom_call" | custom-call | flops 10115481600 | bytes 10485760 | tf_op jit(solution)/shard_map/tap_gradient/pallas_call | solution.py:815
  303.9 86.5 %exchange_backward.1 = (bf16[7,2,5,72,128]{4,3,2,1,0:T(8,128)(2,1)}, bf16[2,448,800]{2,1,0:T(8,128)(2,1)}) custom-call(bf16[7,2,4,72,128]{4,3,2,1,0:T(8,128)(2,1)} %copy-done.13, bf16[2,4,896,800]{3,2,1,0:T(8,128)(2,1)} %get-tuple-element.50.g_ref, s32[8,2,8]{2,1,0:T(2,128)} %copy-done.14), custom_call_target="tpu_custom_call" | custom-call | tf_op jit(solution)/shard_map/exchange_backward/pallas_call | solution.py:451
  390.4 1.4 copy-done.10
  391.8 90.2 %finish_gradients.1 = (bf16[2,896,800]{2,1,0:T(8,128)(2,1)S(1)}, f32[57,800]{1,0:T(8,128)S(1)}) custom-call(bf16[2,448,800]{2,1,0:T(8,128)(2,1)S(1)} %copy-done.10, f32[57,800]{1,0:T(8,128)S(1)} %concatenate.10.s_ref), custom_call_target="tpu_custom_call" | custom-call | tf_op jit(solution)/shard_map/finish_gradients/pallas_call | solution.py:534
  482.0 1.7 copy-done.7
  484.5 1.8 copy.44.l_ref
  488.6 12.3 %rotate.1 = (f32[4,100,400]{2,1,0:T(8,128)}, f32[4,100,400]{2,1,0:T(8,128)}, bf16[2,896,800]{2,1,0:T(8,128)(2,1)}) custom-call(f32[1]{0:T(128)} %bitcast.21.f_ref, bf16[2,896,800]{2,1,0:T(8,128)(2,1)} %copy-done.7, f32[4,800,100]{2,1,0:T(8,128)} %copy.44.l_ref, f32[4,400,400]{2,1,0:T(8,128)} %c_ref.1, f32[4,100,400]{2,1,0:T(8,128)} %copy.45.one_ref, ...), custom_call_target="tpu_custom_call" | custom-call | tf_op jit(solution)/shard_map/rotate/pallas_call | solution.py:1154
  500.9 1.9 copy-done.8
  502.8 51.2 %scatter_change.1 = f32[2,112,800]{2,1,0:T(8,128)S(1)} custom-call(bf16[2,896,800]{2,1,0:T(8,128)(2,1)S(1)} %copy-done.8), custom_call_target="tpu_custom_call" | custom-call | tf_op jit(solution)/shard_map/scatter_change/pallas_call | solution.py:601
  555.7 1.4 copy.48
  558.1 2.7 copy.50
  560.8 1.4 copy.51
  563.1 15.9 %conv_backward.1 = f32[2,576,800]{2,1,0:T(8,128)} custom-call(f32[2,576,800]{2,1,0:T(8,128)S(1)} %copy-done.18, bf16[2,24,24,800]{3,2,1,0:T(8,128)(2,1)S(1)} %bitcast.51, f32[2,576,128]{2,1,0:T(8,128)S(1)} %broadcast_in_dim.65.m_ref, f32[50,8,800]{2,1,0:T(8,128)S(1)} %copy-done.12, f32[8,128]{1,0:T(8,128)S(1)} %broadcast_in_dim.77.l_ref, ...), custom_call_target="tpu_custom_call" | custom-call | flops 10115481600 | bytes 12582912 | tf_op jit(solution)/shard_map/conv_backward/pallas_call | solution.py:855
  (128 shorter events, 17.9 us)
Async XLA Ops:
  4.3 1.6 copy-start.2
  7.2 104.0 %slice-start = ((f32[57,800]{1,0:T(8,128)}), f32[50,800]{1,0:T(8,128)S(1)}, s32[]{:S(2)}) async-start(f32[57,800]{1,0:T(8,128)} %param.23), calls=%async_computation | async-start | bytes 401408 | tf_op jit(solution)/shard_map/slice | solution.py:1228
  7.9 103.4 %copy-start.3 = (bf16[1,2,24,24,800]{4,3,2,1,0:T(8,128)(2,1)S(1)}, bf16[1,2,24,24,800]{4,3,2,1,0:T(8,128)(2,1)}, u32[]{:S(2)}) copy-start(bf16[1,2,24,24,800]{4,3,2,1,0:T(8,128)(2,1)} %param.16) | copy-start | bytes 5529604
  106.5 4.6 copy-start.16
  111.2 15.4 %copy-start.14 = (s32[8,2,8]{2,1,0:T(2,128)}, s32[8,2,8]{2,1,0:T(2,128)S(1)}, u32[]{:S(2)}) copy-start(s32[8,2,8]{2,1,0:T(2,128)S(1)} %get-tuple-element.51.n_ref) | copy-start | bytes 1540
  111.2 15.5 %copy-start.23 = (bf16[7,2,5,72,128]{4,3,2,1,0:T(8,128)(2,1)}, bf16[7,2,5,72,128]{4,3,2,1,0:T(8,128)(2,1)S(1)}, u32[]{:S(2)}) copy-start(bf16[7,2,5,72,128]{4,3,2,1,0:T(8,128)(2,1)S(1)} %get-tuple-element.35.h_ref) | copy-start | bytes 3870724
  111.3 15.4 %copy-start.11 = (f32[50,8,800]{2,1,0:T(8,128)}, f32[50,8,800]{2,1,0:T(8,128)S(1)}, u32[]{:S(2)}) copy-start(f32[50,8,800]{2,1,0:T(8,128)S(1)} %broadcast_in_dim.66.w_ref) | copy-start | bytes 3840004
  111.3 37.9 %copy-start.29 = (f32[57,800]{1,0:T(8,128)S(1)}, f32[57,800]{1,0:T(8,128)}, u32[]{:S(2)}) copy-start(f32[57,800]{1,0:T(8,128)} %param.23) | copy-start | bytes 547204
  126.6 2.0 copy-start
  149.2 7.9 %copy-start.37 = (s32[4]{0:T(128)S(1)}, s32[4]{0:T(128)}, u32[]{:S(2)}) copy-start(s32[4]{0:T(128)} %param.30) | copy-start | bytes 52
  154.3 1.3 copy-start.19
  156.8 11.0 %copy-start.38 = (s32[16]{0:T(128)S(1)}, s32[16]{0:T(128)}, u32[]{:S(2)}) copy-start(s32[16]{0:T(128)} %param.29) | copy-start | bytes 196
  281.1 2.2 copy-start.1
  283.2 2.2 copy-start.6
  285.4 2.5 copy-start.4
  285.4 2.5 copy-start.24
  287.9 15.7 %copy-start.13 = (bf16[7,2,4,72,128]{4,3,2,1,0:T(8,128)(2,1)}, bf16[7,2,4,72,128]{4,3,2,1,0:T(8,128)(2,1)S(1)}, u32[]{:S(2)}) copy-start(bf16[7,2,4,72,128]{4,3,2,1,0:T(8,128)(2,1)S(1)} %get-tuple-element.49.r_ref) | copy-start | bytes 3096580
  287.9 15.7 %copy-start.17 = (f32[2,576,800]{2,1,0:T(8,128)}, f32[2,576,800]{2,1,0:T(8,128)S(1)}, u32[]{:S(2)}) copy-start(f32[2,576,800]{2,1,0:T(8,128)S(1)} %get-tuple-element.48.d_ref) | copy-start | bytes 11059204
  287.9 15.6 %copy-start.36 = (f32[2,1,800]{2,1,0:T(1,128)S(1)}, f32[2,1,800]{2,1,0:T(1,128)}, u32[]{:S(2)}) copy-start(f32[2,1,800]{2,1,0:T(1,128)} %get-tuple-element.47) | copy-start | bytes 19204
  287.9 15.7 %copy-start.35 = (f32[8,1,400]{2,1,0:T(1,128)S(1)}, f32[8,1,400]{2,1,0:T(1,128)}, u32[]{:S(2)}) copy-start(f32[8,1,400]{2,1,0:T(1,128)} %get-tuple-element.55) | copy-start | bytes 38404
  390.4 1.4 copy-start.10
  391.8 92.7 %copy-start.28 = (f32[4,800,100]{1,0,2:T(4,128)S(1)}, f32[4,800,100]{1,0,2:T(4,128)}, u32[]{:S(2)}) copy-start(f32[4,800,100]{1,0,2:T(4,128)} %param.21) | copy-start | bytes 3840004
  391.8 94.4 %copy-start.31 = (f32[4,100,400]{2,0,1:T(4,128)S(1)}, f32[4,100,400]{2,0,1:T(4,128)}, u32[]{:S(2)}) copy-start(f32[4,100,400]{2,0,1:T(4,128)} %param.19) | copy-start | bytes 1920004
  482.0 1.7 copy-start.7
  500.9 1.9 copy-start.8
  555.3 7.8 %copy-start.18 = (f32[2,576,800]{2,1,0:T(8,128)S(1)}, f32[2,576,800]{2,1,0:T(8,128)}, u32[]{:S(2)}) copy-start(f32[2,576,800]{2,1,0:T(8,128)} %copy-done.17) | copy-start | bytes 11059204
  555.6 5.1 copy-start.30
  557.1 5.1 copy-start.33
  557.1 5.1 copy-start.34
  558.0 5.1 copy-start.12
  558.0 5.1 copy-start.25
  560.8 2.4 copy-start.9
  (8 other events, 9.0 us)

commit v4 on v3

--- a/solution.py
+++ b/solution.py
@@ -148,27 +148,31 @@
     def halo_shape(self):
         return jax.ShapeDtypeStruct((self.n_chunk, self.slots, 5, RIM * self.side, LANES), BF)
 
-    def send_rims(self, copies, rims, arrived, local):
+    def plan(self, copies, rims, arrived, picked, halos, local):
         t, o = self.grid.at(self.grid.own())
-        self.t, self.o = t, o
-        self.first = []
+        self.t, self.arrived, self.picked = t, arrived, picked
+        own_chunk = jnp.minimum(t, self.n_chunk - 1)
+        self.first, self.second = [], []
         for k in range(1, self.grid.n_tile):
             to = t ^ k
             source = jnp.minimum(to, self.n_chunk - 1)
-            copy = copies.make(rims.at[source], arrived.at[t], (to, o))
-            self.first.append((to, copy))
+            self.first.append((to, copies.make(rims.at[source], arrived.at[t], (to, o))))
+            self.second.append((to, copies.make(picked.at[to], halos.at[own_chunk], (to, o))))
+        self.own_copy = pltpu.make_async_copy(rims.at[own_chunk], arrived.at[t], local.at[0])
+        self.back_copy = pltpu.make_async_copy(picked.at[t], halos.at[own_chunk], local.at[1])
+
+    def send_rims(self):
+        for to, copy in self.first:
 
             @pl.when(to < self.n_chunk)
             def _():
                 copy.start()
 
-        own = pltpu.make_async_copy(rims.at[jnp.minimum(t, self.n_chunk - 1)], arrived.at[t], local.at[0])
-        own.start()
-        self.own_copy = own
-
-    def pick_and_send(self, copies, arrived, picked, halos, local, neighbours):
+        self.own_copy.start()
+
+    def pick_and_send(self, neighbours):
         grid, slots, side = self.grid, self.slots, self.side
-        t, o = self.t, self.o
+        t, arrived, picked = self.t, self.arrived, self.picked
         self.own_copy.wait()
         for _, copy in self.first:
 
@@ -197,18 +201,11 @@
                 rows.append(jnp.zeros((RIM * side - 64, LANES), F32))
                 picked[to_tile, to_slot, 4] = jnp.concatenate(rows, 0).astype(BF)
 
-        own_chunk = jnp.minimum(t, self.n_chunk - 1)
-        self.second = []
-        for k in range(1, grid.n_tile):
-            to = t ^ k
-            copy = copies.make(picked.at[to], halos.at[own_chunk], (to, o))
-            self.second.append((to, copy))
+        for _, copy in self.second:
 
             @pl.when(t < self.n_chunk)
             def _():
                 copy.start()
-
-        self.back_copy = pltpu.make_async_copy(picked.at[t], halos.at[own_chunk], local.at[1])
 
         @pl.when(t < self.n_chunk)
         def _():
@@ -310,7 +307,8 @@
         tables = [copies.start(n_ref, nbr_ref.at[t], (t ^ k, o)) for k in range(1, n_tile)]
         keep = pltpu.make_async_copy(n_ref, nbr_ref.at[t], locals_n.at[0])
         keep.start()
-        halo.send_rims(copies, r_ref, arrived, local)
+        halo.plan(copies, r_ref, arrived, picked, halo_ref, local)
+        halo.send_rims()
         weights = gather.run(copies, p_ref, w_ref, locals_w)
         next(weights)
         keep.wait()
@@ -319,9 +317,7 @@
         load = pltpu.make_async_copy(nbr_ref, table, locals_n.at[1])
         load.start()
         load.wait()
-        halo.pick_and_send(
-            copies, arrived, picked, halo_ref, local, lambda d, k: table[d // slots, d % slots, k]
-        )
+        halo.pick_and_send(lambda d, k: table[d // slots, d % slots, k])
         for _ in weights:
             pass
         halo.finish()
@@ -349,123 +345,144 @@
     )(rims, packed, neighbours)
 
 
-def exchange_backward(grid, rims, grads, neighbours):
+def exchange_backward(grid, rims, grads, neighbours, inputs, mask_lanes, d_conv, halos):
     n_chunk, slots, _, band, _ = rims.shape
-    n_tile = grid.n_tile
-    side_a, side_b, side_x = grid.size["a"], grid.size["b"], grid.size["x"]
+    side, channels = inputs.shape[1], inputs.shape[3]
+    side_b, side_x = grid.size["b"], grid.size["x"]
     _, blocks, rows, cols = grads.shape
     pairs = blocks // side_x
     part = rows // side_b
-    halo = HaloExchange(grid, n_chunk, slots, band // RIM)
-    total = halo.count + blocks + pairs * ((side_x - 1) + (side_b - 1)) + pairs * side_x * (side_b - 1)
-
-    def kernel(r_ref, g_ref, n_ref, halo_ref, o_ref, arrived, picked, local, here, core, far, across, send, recv, load_sems):
+    halo = HaloExchange(grid, n_chunk, slots, side)
+    total = halo.count + blocks + pairs * side_x * (side_x - 1 + side_b - 1)
+    last = n_chunk * slots - 1
+
+    def kernel(
+        r_ref, g_ref, n_ref, x_ref, m_ref, d_ref, h_ref, halo_ref, o_ref, tap_ref,
+        arrived, picked, local, here, core, far, across, pad, sums, send, recv, load_sems,
+    ):
         own = grid.own()
-        own_x, own_b = own["x"], own["b"]
-        meet(grid.partners(("tile", "x", "c")))
+        own_x, own_b, own_c = own["x"], own["b"], own["c"]
+        step = pl.program_id(0) * slots + pl.program_id(1)
         copies = Copies(send, recv)
-        halo.send_rims(copies, r_ref, arrived, local)
-        loads, cores = [], []
-        order = []
-        for m in range(pairs):
-            order += [(k, m) for k in range(1, side_x)] if m % 2 == 0 else []
+        halo.plan(copies, r_ref, arrived, picked, halo_ref, local)
+        order = [(k, m) for m in range(0, pairs, 2) for k in range(1, side_x)]
         order += [(k, m) for m in range(pairs) for k in range(side_x) if (k, m) not in order]
         index = lambda k, m: (own_x ^ k) * pairs + m
+        rows_of = lambda b: pl.ds(pl.multiple_of(b * part, 16), part)
+        cores, loads, to_x, to_b = [], [], {}, {}
         for i, (k, m) in enumerate(order):
             at = index(k, m)
-            cores.append(copies.start(g_ref.at[1 - own["c"], at], core.at[at], grid.beside(own, "c", 1)))
-            load = pltpu.make_async_copy(g_ref.at[own["c"], at], here.at[at], load_sems.at[i])
-            load.start()
-            loads.append(load)
-        sent_x = {m: [] for m in range(pairs)}
-        sent_b = {m: [] for m in range(pairs)}
-        rows_of = lambda b: pl.ds(pl.multiple_of(b * part, 16), part)
-
-        def send_b(m, k):
-            for j in range(1, side_b):
-                to = grid.beside(own, "b", j)
+            cores.append(copies.make(g_ref.at[1 - own_c, at], core.at[at], grid.beside(own, "c", 1)))
+            loads.append(pltpu.make_async_copy(g_ref.at[own_c, at], here.at[at], load_sems.at[i]))
+            if k > 0:
+                to = grid.beside(own, "x", k)
+                if m % 2 == 0:
+                    to_x[k, m] = copies.make(here.at[at], far.at[k - 1, m], to)
+                else:
+                    to_x[k, m] = copies.make(here.at[at, rows_of(own_b)], far.at[k - 1, m, pl.ds(0, part)], to)
+            if m % 2 == 1 or k == 0:
+                to_b[k, m] = [
+                    copies.make(here.at[at, rows_of(own_b ^ j)], across.at[j - 1, at], grid.beside(own, "b", j))
+                    for j in range(1, side_b)
+                ]
+
+        def start(found):
+            for copy in found:
+                copy.start()
+
+        def wait(found):
+            for copy in found:
+                copy.wait()
+
+        @pl.when(step == 0)
+        def _():
+            meet(grid.partners(("tile", "x", "c")))
+            halo.send_rims()
+            start(cores)
+            start(loads)
+
+        add_taps(x_ref, m_ref, d_ref, h_ref, tap_ref, pad, sums, slots, side)
+
+        for i, (k, m) in enumerate(order):
+
+            @pl.when(step == min(last, 3 + 2 * i))
+            def _():
+                loads[i].wait()
+                cores[i].wait()
                 at = index(k, m)
-                sent_b[m].append(
-                    (k, copies.start(here.at[at, rows_of(own_b ^ j)], across.at[j - 1, at], to))
-                )
-
-        def send_x(m, k):
-            at = index(k, m)
-            to = grid.beside(own, "x", k)
-            if m % 2 == 0:
-                sent_x[m].append(copies.start(here.at[at], far.at[k - 1, m], to))
-            else:
-                sent_x[m].append(
-                    copies.start(here.at[at, rows_of(own_b)], far.at[k - 1, m, pl.ds(0, part)], to)
-                )
-
-        for i, (k, m) in enumerate(order):
-            loads[i].wait()
-            cores[i].wait_recv()
-            at = index(k, m)
-            add_rows(here.at[at], [core.at[at]], rows)
-            if m % 2 == 1:
-                send_b(m, k)
-            elif k > 0:
-                send_x(m, k)
-        halo.pick_and_send(
-            copies, arrived, picked, halo_ref, local, lambda d, k: n_ref[d // slots, d % slots, k]
-        )
-        for m in range(pairs):
-            if m % 2 == 1:
-                for k, copy in sent_b[m]:
-                    copy.wait()
-                for k in [*range(1, side_x), 0]:
-                    at = index(k, m)
-                    add_rows(here.at[at, rows_of(own_b)], [across.at[j, at] for j in range(side_b - 1)], part)
-                    if k > 0:
-                        send_x(m, k)
-            else:
-                for copy in sent_x[m]:
-                    copy.wait()
-                add_rows(here.at[index(0, m)], [far.at[j, m] for j in range(side_x - 1)], rows)
-                send_b(m, 0)
-        for m in range(pairs):
-            at = index(0, m)
-            if m % 2 == 1:
-                for copy in sent_x[m]:
-                    copy.wait()
-                sources = [far.at[j, m, pl.ds(0, part)] for j in range(side_x - 1)]
-            else:
-                for _, copy in sent_b[m]:
-                    copy.wait()
-                sources = [across.at[j, at] for j in range(side_b - 1)]
-            add_rows(here.at[at, rows_of(own_b)], sources, part)
-        outs = []
-        for m in range(pairs):
-            out = pltpu.make_async_copy(here.at[index(0, m), rows_of(own_b)], o_ref.at[m], load_sems.at[m])
-            out.start()
-            outs.append(out)
-        halo.finish()
-        for copy in cores:
-            copy.wait_send()
-        for out in outs:
-            out.wait()
+                add_rows(here.at[at], [core.at[at]], rows)
+                if m % 2 == 1:
+                    start(to_b[k, m])
+                elif k > 0:
+                    to_x[k, m].start()
+
+        @pl.when(step == last)
+        def _():
+            halo.pick_and_send(lambda d, k: n_ref[d // slots, d % slots, k])
+            for m in range(pairs):
+                others = range(1, side_x)
+                if m % 2 == 1:
+                    for k in [*others, 0]:
+                        at = index(k, m)
+                        wait(to_b[k, m])
+                        add_rows(here.at[at, rows_of(own_b)], [across.at[j, at] for j in range(side_b - 1)], part)
+                        if k > 0:
+                            to_x[k, m].start()
+                else:
+                    wait(to_x[k, m] for k in others)
+                    add_rows(here.at[index(0, m)], [far.at[k - 1, m] for k in others], rows)
+                    start(to_b[0, m])
+            outs = []
+            for m in range(pairs):
+                at = index(0, m)
+                if m % 2 == 1:
+                    wait(to_x[k, m] for k in range(1, side_x))
+                    sources = [far.at[k - 1, m, pl.ds(0, part)] for k in range(1, side_x)]
+                else:
+                    wait(to_b[0, m])
+                    sources = [across.at[j, at] for j in range(side_b - 1)]
+                add_rows(here.at[at, rows_of(own_b)], sources, part)
+                outs.append(pltpu.make_async_copy(here.at[at, rows_of(own_b)], o_ref.at[m], load_sems.at[m]))
+                outs[-1].start()
+            halo.finish()
+            for out in outs:
+                out.wait()
 
     any_space = pl.BlockSpec(memory_space=pl.ANY)
+    cells = side * side
     return pl.pallas_call(
         kernel,
-        in_specs=[any_space, any_space, pl.BlockSpec(memory_space=pltpu.SMEM)],
-        out_specs=[any_space] * 2,
-        out_shape=[halo.halo_shape(), jax.ShapeDtypeStruct((pairs, part, cols), BF)],
+        grid=(n_chunk, slots),
+        in_specs=[
+            any_space,
+            any_space,
+            pl.BlockSpec(memory_space=pltpu.SMEM),
+            pl.BlockSpec((1, side, side, LANES), lambda c, s: (s, 0, 0, c)),
+            pl.BlockSpec((1, cells, LANES), lambda c, s: (s, 0, 0)),
+            pl.BlockSpec((1, cells, LANES), lambda c, s: (s, 0, c)),
+            halo_block(halos),
+        ],
+        out_specs=[any_space, any_space, pl.BlockSpec((50, LANES), lambda c, s: (0, c))],
+        out_shape=[
+            halo.halo_shape(),
+            jax.ShapeDtypeStruct((pairs, part, cols), BF),
+            jax.ShapeDtypeStruct((50, channels), F32),
+        ],
         scratch_shapes=halo.scratch()
         + [
             pltpu.VMEM((blocks, rows, cols), BF),
             pltpu.VMEM((blocks, rows, cols), BF),
             pltpu.VMEM((side_x - 1, pairs, rows, cols), BF),
             pltpu.VMEM((side_b - 1, blocks, part, cols), BF),
+            pltpu.VMEM(((side + 2 * RIM) * PITCH, LANES), F32),
+            pltpu.VMEM((50, 8, LANES), F32),
             pltpu.SemaphoreType.DMA((total,)),
             pltpu.SemaphoreType.DMA((total,)),
             pltpu.SemaphoreType.DMA((blocks,)),
         ],
-        compiler_params=remote_params(2, 56),
+        compiler_params=remote_params(2, 60),
         name="exchange_backward",
-    )(rims, grads, neighbours)
+    )(rims, grads, neighbours, inputs, mask_lanes, d_conv, halos)
 
 
 def finish_gradients(grid, partial, small):
@@ -552,70 +569,6 @@
     )(partial, small)
 
 
-def scatter_change(grid, change):
-    pairs, rows, cols = change.shape
-    side_a, side_b = grid.size["a"], grid.size["b"]
-    part = rows // side_b
-    piece = part // side_a
-    total = pairs * ((side_b - 1) + (side_a - 1))
-
-    def kernel(c_ref, o_ref, mine, from_b, from_a, send, recv, load_sems):
-        own = grid.own()
-        meet(grid.partners(("a", "b")))
-        copies = Copies(send, recv)
-        half = lambda b: pl.ds(pl.multiple_of(b * part, 16), part)
-        rows_of = lambda a: pl.ds(pl.multiple_of(a * piece, 16), piece)
-        firsts, loads = [], []
-        for m in range(pairs):
-            firsts.append(
-                [
-                    copies.start(c_ref.at[m, half(own["b"] ^ k)], from_b.at[k - 1, m], grid.beside(own, "b", k))
-                    for k in range(1, side_b)
-                ]
-            )
-            load = pltpu.make_async_copy(c_ref.at[m, half(own["b"])], mine.at[m], load_sems.at[m])
-            load.start()
-            loads.append(load)
-        seconds = []
-        for m in range(pairs):
-            loads[m].wait()
-            for copy in firsts[m]:
-                copy.wait()
-            add_rows(mine.at[m], [from_b.at[k, m] for k in range(side_b - 1)], part)
-            seconds.append(
-                [
-                    copies.start(mine.at[m, rows_of(own["a"] ^ k)], from_a.at[k - 1, m], grid.beside(own, "a", k))
-                    for k in range(1, side_a)
-                ]
-            )
-        for m in range(pairs):
-            for copy in seconds[m]:
-                copy.wait()
-            here = mine.at[m, rows_of(own["a"])]
-            total_here = here[...].astype(F32)
-            for k in range(side_a - 1):
-                total_here = total_here + from_a[k, m].astype(F32)
-            o_ref[m] = total_here
-
-    any_space = pl.BlockSpec(memory_space=pl.ANY)
-    return pl.pallas_call(
-        kernel,
-        in_specs=[any_space],
-        out_specs=pl.BlockSpec(memory_space=pltpu.VMEM),
-        out_shape=jax.ShapeDtypeStruct((pairs, piece, cols), F32),
-        scratch_shapes=[
-            pltpu.VMEM((pairs, part, cols), BF),
-            pltpu.VMEM((side_b - 1, pairs, part, cols), BF),
-            pltpu.VMEM((side_a - 1, pairs, piece, cols), BF),
-            pltpu.SemaphoreType.DMA((total,)),
-            pltpu.SemaphoreType.DMA((total,)),
-            pltpu.SemaphoreType.DMA((pairs,)),
-        ],
-        compiler_params=remote_params(4, 40),
-        name="scatter_change",
-    )(change)
-
-
 def tile_total(grid, value, number):
     n_tile = grid.n_tile
 
@@ -773,72 +726,83 @@
     )(d_shaped, conv_out, mask_lanes, coefs)
 
 
-def tap_gradient(inputs, mask_lanes, halos, d_conv):
-    slots, side, _, channels = inputs.shape
-    n_chunk = halos.shape[0]
-    cells = side * side
-
-    def kernel(x_ref, m_ref, d_ref, h_ref, o_ref, pad, sums):
-        slot = pl.program_id(1)
-        for i in range(side):
-            pad[pl.ds((i + RIM) * PITCH + 8, side), :] = (
-                x_ref[0, i].astype(F32) * m_ref[0, pl.ds(i * side, side), :]
-            )
-        fill_halo(pad, lambda k: h_ref[0, 0, k].astype(F32), side)
-
-        @pl.when(slot == 0)
-        def _():
-            sums[...] = jnp.zeros_like(sums)
-
-        for block in range(side // 8):
-            grads = [d_ref[0, pl.ds(i * side + 8 * block, 8), :] for i in range(side)]
-            total = grads[0]
-            for i in range(1, side):
-                total = total + grads[i]
-            sums[49] += total
-            for b in range(7):
-                taps = [None] * 7
-                for r in range(side + 2 * RIM):
-                    window = pad[pl.ds(r * PITCH + 8 - RIM + b + 8 * block, 8), :]
-                    for a in range(7):
-                        i = r - a
-                        if 0 <= i < side:
-                            term = window * grads[i]
-                            taps[a] = term if taps[a] is None else taps[a] + term
+def add_taps(x_ref, m_ref, d_ref, h_ref, o_ref, pad, sums, slots, side):
+    slot = pl.program_id(1)
+    for i in range(side):
+        pad[pl.ds((i + RIM) * PITCH + 8, side), :] = x_ref[0, i].astype(F32) * m_ref[0, pl.ds(i * side, side), :]
+    fill_halo(pad, lambda k: h_ref[0, 0, k].astype(F32), side)
+
+    @pl.when(slot == 0)
+    def _():
+        sums[...] = jnp.zeros_like(sums)
+
+    for block in range(side // 8):
+        grads = [d_ref[0, pl.ds(i * side + 8 * block, 8), :] for i in range(side)]
+        total = grads[0]
+        for i in range(1, side):
+            total = total + grads[i]
+        sums[49] += total
+        for b in range(7):
+            taps = [None] * 7
+            for r in range(side + 2 * RIM):
+                window = pad[pl.ds(r * PITCH + 8 - RIM + b + 8 * block, 8), :]
                 for a in range(7):
-                    sums[7 * a + b] += taps[a]
-
-        @pl.when(slot == slots - 1)
-        def _():
-            o_ref[...] = jnp.sum(sums[...], axis=1)
-
-    return pl.pallas_call(
-        kernel,
-        grid=(n_chunk, slots),
-        in_specs=[
-            pl.BlockSpec((1, side, side, LANES), lambda c, s: (s, 0, 0, c)),
-            pl.BlockSpec((1, cells, LANES), lambda c, s: (s, 0, 0)),
-            pl.BlockSpec((1, cells, LANES), lambda c, s: (s, 0, c)),
-            halo_block(halos),
-        ],
-        out_specs=pl.BlockSpec((50, LANES), lambda c, s: (0, c)),
-        scratch_shapes=[
-            pltpu.VMEM(((side + 2 * RIM) * PITCH, LANES), F32),
-            pltpu.VMEM((50, 8, LANES), F32),
-        ],
-        out_shape=jax.ShapeDtypeStruct((50, channels), F32),
-        cost_estimate=conv_cost(n_chunk, slots, side, 10 << 20),
-        compiler_params=pltpu.CompilerParams(vmem_limit_bytes=32 << 20),
-        name="tap_gradient",
-    )(inputs, mask_lanes, d_conv, halos)
-
-
-def conv_backward(d_conv, halos, cotangent, mask_lanes, taps, weight_lanes):
+                    i = r - a
+                    if 0 <= i < side:
+                        term = window * grads[i]
+                        taps[a] = term if taps[a] is None else taps[a] + term
+            for a in range(7):
+                sums[7 * a + b] += taps[a]
+
+    @pl.when(slot == slots - 1)
+    def _():
+        o_ref[...] = jnp.sum(sums[...], axis=1)
+
+
+def conv_backward(grid, d_conv, halos, cotangent, mask_lanes, taps, weight_lanes, change):
     slots, side, _, channels = cotangent.shape
     n_chunk = halos.shape[0]
     cells = side * side
-
-    def kernel(d_ref, g_ref, m_ref, w_ref, l_ref, h_ref, o_ref, pad):
+    pairs, rows, cols = change.shape
+    side_a, side_b = grid.size["a"], grid.size["b"]
+    part = rows // side_b
+    piece = part // side_a
+    total = pairs * ((side_b - 1) + (side_a - 1))
+    last = n_chunk * slots - 1
+
+    def kernel(
+        d_ref, g_ref, m_ref, w_ref, l_ref, h_ref, c_ref, o_ref, change_ref,
+        pad, mine, from_b, from_a, send, recv, load_sems,
+    ):
+        own = grid.own()
+        step = pl.program_id(0) * slots + pl.program_id(1)
+        copies = Copies(send, recv)
+        half = lambda b: pl.ds(pl.multiple_of(b * part, 16), part)
+        rows_of = lambda a: pl.ds(pl.multiple_of(a * piece, 16), piece)
+        firsts, seconds, loads = [], [], []
+        for m in range(pairs):
+            firsts.append(
+                [
+                    copies.make(c_ref.at[m, half(own["b"] ^ k)], from_b.at[k - 1, m], grid.beside(own, "b", k))
+                    for k in range(1, side_b)
+                ]
+            )
+            seconds.append(
+                [
+                    copies.make(mine.at[m, rows_of(own["a"] ^ k)], from_a.at[k - 1, m], grid.beside(own, "a", k))
+                    for k in range(1, side_a)
+                ]
+            )
+            loads.append(pltpu.make_async_copy(c_ref.at[m, half(own["b"])], mine.at[m], load_sems.at[m]))
+
+        @pl.when(step == 0)
+        def _():
+            meet(grid.partners(("a", "b")))
+            for m in range(pairs):
+                for copy in firsts[m]:
+                    copy.start()
+                loads[m].start()
+
         for i in range(side):
             pad[pl.ds((i + RIM) * PITCH + 8, side), :] = d_ref[0, pl.ds(i * side, side), :]
         fill_halo(pad, lambda k: h_ref[0, 0, k].astype(F32), side)
@@ -846,11 +810,32 @@
 
         def emit(block, sums):
             for i in range(side):
-                rows = pl.ds(i * side + 8 * block, 8)
+                at = pl.ds(i * side + 8 * block, 8)
                 scaled = weight * g_ref[0, i, pl.ds(8 * block, 8), :].astype(F32)
-                o_ref[0, rows, :] = m_ref[0, rows, :] * (scaled + sums[i])
+                o_ref[0, at, :] = m_ref[0, at, :] * (scaled + sums[i])
 
         conv_pass(pad, side, lambda a, b: w_ref[7 * (6 - a) + 6 - b], emit)
+
+        for m in range(pairs):
+
+            @pl.when(step == min(last, 9 + 4 * m))
+            def _():
+                loads[m].wait()
+                for copy in firsts[m]:
+                    copy.wait()
+                add_rows(mine.at[m], [from_b.at[k, m] for k in range(side_b - 1)], part)
+                for copy in seconds[m]:
+                    copy.start()
+
+        @pl.when(step == last)
+        def _():
+            for m in range(pairs):
+                for copy in seconds[m]:
+                    copy.wait()
+                value = mine[m, rows_of(own["a"])].astype(F32)
+                for k in range(side_a - 1):
+                    value = value + from_a[k, m].astype(F32)
+                change_ref[m] = value
 
     return pl.pallas_call(
         kernel,
@@ -862,14 +847,28 @@
             pl.BlockSpec((50, 8, LANES), lambda c, s: (0, 0, c)),
             pl.BlockSpec((8, LANES), lambda c, s: (0, 0)),
             halo_block(halos),
-        ],
-        out_specs=pl.BlockSpec((1, cells, LANES), lambda c, s: (s, 0, c)),
-        scratch_shapes=[pltpu.VMEM(((side + 2 * RIM) * PITCH, LANES), F32)],
-        out_shape=jax.ShapeDtypeStruct((slots, cells, channels), F32),
-        cost_estimate=conv_cost(n_chunk, slots, side, 12 << 20),
-        compiler_params=pltpu.CompilerParams(vmem_limit_bytes=32 << 20),
+            pl.BlockSpec(memory_space=pl.ANY),
+        ],
+        out_specs=[
+            pl.BlockSpec((1, cells, LANES), lambda c, s: (s, 0, c)),
+            pl.BlockSpec((pairs, piece, cols), lambda c, s: (0, 0, 0)),
+        ],
+        scratch_shapes=[
+            pltpu.VMEM(((side + 2 * RIM) * PITCH, LANES), F32),
+            pltpu.VMEM((pairs, part, cols), BF),
+            pltpu.VMEM((side_b - 1, pairs, part, cols), BF),
+            pltpu.VMEM((side_a - 1, pairs, piece, cols), BF),
+            pltpu.SemaphoreType.DMA((total,)),
+            pltpu.SemaphoreType.DMA((total,)),
+            pltpu.SemaphoreType.DMA((pairs,)),
+        ],
+        out_shape=[
+            jax.ShapeDtypeStruct((slots, cells, channels), F32),
+            jax.ShapeDtypeStruct((pairs, piece, cols), F32),
+        ],
+        compiler_params=remote_params(4, 48),
         name="conv_backward",
-    )(d_conv, cotangent, mask_lanes, taps, weight_lanes, halos)
+    )(d_conv, cotangent, mask_lanes, taps, weight_lanes, halos, change)
 
 
 def spread_lanes(value, parts, width):
@@ -1316,9 +1315,9 @@
         jnp.broadcast_to(grad_coefs[:, None, :], (3, 8, channels)),
         side,
     )
-    grad_halos, partial = exchange_backward(grid, grad_rims, grads, all_neighbours)
-    d_taps = tap_gradient(inputs, mask_lanes, halos, d_conv)
-    input_grad = conv_backward(d_conv, grad_halos, cotangent, mask_lanes, taps, weight_lanes)
+    grad_halos, partial, d_taps = exchange_backward(
+        grid, grad_rims, grads, all_neighbours, inputs, mask_lanes, d_conv, halos
+    )
 
     correction = 1.0 - jnp.power(F32(decay_rate), step_count[0].astype(F32))
     d_small = jnp.concatenate(
@@ -1334,7 +1333,10 @@
     first_new, second_new, change = rotate(
         owned, left_basis, column_basis, moment_one, moment_two, correction, grid, width
     )
-    change = unpack_pairs(scatter_change(grid, change)[:, :run])
+    input_grad, change = conv_backward(
+        grid, d_conv, grad_halos, cotangent, mask_lanes, taps, weight_lanes, change
+    )
+    change = unpack_pairs(change[:, :run])
     new_master = master - 0.5 / math.sqrt(channels) * change
     return (
         block_output.reshape((1,) + inputs.shape),

time: 580 us -> 559 us (0.964)
  Pallas kernels: 527 us -> 501 us
    pallas_call x3 -> x1, Pallas kernels: 153 us -> 89.6 us  [exchange_backward(): pl.pallas_call(kernel, grid=(n_chunk, slots), in_specs=[any_space, any_sp...]
    pallas_call x1, Pallas kernels: 15.9 us -> 53.8 us  [conv_backward(): pl.pallas_call(kernel, grid=(n_chunk, slots), in_specs=[pl.BlockSpec((1,...]
    unnamed x85 -> x92, local copies, waits for them, and re-layouts: 35.4 us -> 39.3 us
where the time goes in v4:
time: 559 us
  Pallas kernels  501 us (90%)
  local copies, waits for them, and re-layouts  47.4 us (8%)
  other arithmetic  5.84 us (1%)
    pallas_call x1, Pallas kernels, exchange_forward(): pl.pallas_call(kernel, in_specs=[any_space] * 3, out_specs=[any_space] *...  98.5 us
    pallas_call x1, Pallas kernels, feed_forward(): pl.pallas_call(kernel, grid_spec=pltpu.PrefetchScalarGridSpec(num_scalar_...  92.6 us
    pallas_call x1, Pallas kernels, finish_gradients(): pl.pallas_call(kernel, in_specs=[any_space, whole], out_specs=[any_space,...  90.1 us
    pallas_call x1, Pallas kernels, exchange_backward(): pl.pallas_call(kernel, grid=(n_chunk, slots), in_specs=[any_space, any_sp...  89.6 us
    pallas_call x1, Pallas kernels, conv_backward(): pl.pallas_call(kernel, grid=(n_chunk, slots), in_specs=[pl.BlockSpec((1,...  53.8 us
    unnamed x92, local copies, waits for them, and re-layouts  39.3 us
    pallas_call x2, Pallas kernels, tile_total(): pl.pallas_call(kernel, in_specs=[whole], out_specs=whole, out_shape=jax.S...  25.2 us
    pallas_call x1, Pallas kernels, conv_forward(): pl.pallas_call(kernel, grid=(n_chunk, slots), in_specs=[pl.BlockSpec((1,...  15.3 us

profile of v4, /device:TPU:8, one launch (start us, length us, event | category | flops | bytes accessed | tf_op | source)
XLA Modules:
  0.0 558.5 jit_solution(8534734599703303592)
XLA Ops:
  0.6 1.2 dynamic_slice.6
  2.5 1.4 fusion.7
  4.3 1.8 copy-done.2
  8.2 98.5 %exchange_forward.1 = (bf16[7,2,5,72,128]{4,3,2,1,0:T(8,128)(2,1)S(1)}, bf16[2,4,896,800]{3,2,1,0:T(8,128)(2,1)S(1)}, s32[8,2,8]{2,1,0:T(2,128)S(1)}) custom-call(bf16[7,2,4,72,128]{4,3,2,1,0:T(8,128)(2,1)S(1)} %rims_of_input.1.r_ref, bf16[2,112,800]{2,1,0:T(8,128)(2,1)S(1)} %pad.5.p_ref, s32[2,8]{1,0:T(2,128)S(1)} %copy-done.20), custom_call_target="tpu_custom_call" | custom-call | tf_op jit(solution)/shard_map/exchange_forward/pallas_call | solution.py:326
  106.8 4.7 copy-done.21
  111.5 15.3 %conv_forward.1 = (f32[2,576,800]{2,1,0:T(8,128)S(1)}, f32[2,2,8,800]{3,2,1,0:T(8,128)S(1)}) custom-call(bf16[2,24,24,800]{3,2,1,0:T(8,128)(2,1)S(1)} %bitcast.48, f32[2,576,128]{2,1,0:T(8,128)S(1)} %broadcast_in_dim.65.m_ref, f32[50,8,800]{2,1,0:T(8,128)S(1)} %broadcast_in_dim.66.w_ref, bf16[7,2,5,72,128]{4,3,2,1,0:T(8,128)(2,1)S(1)} %get-tuple-element.38.h_ref), custom_call_target="tpu_custom_call" | custom-call | flops 10115481600 | bytes 10485760 | tf_op jit(solution)/shard_map/conv_forward/pallas_call | solution.py:671
  126.9 2.0 copy-done
  129.6 18.1 %tile_total.2 = f32[3,800]{1,0:T(4,128)S(1)} custom-call(f32[3,800]{1,0:T(4,128)S(1)} %concatenate.9.v_ref), custom_call_target="tpu_custom_call" | custom-call | tf_op jit(solution)/shard_map/tile_total/pallas_call | solution.py:589
  149.5 5.1 arrange_shaped.1
  154.5 1.3 copy-done.22
  155.9 1.3 copy-done.24
  160.0 4.1 arrange_d_branch.1
  164.9 1.3 copy-done.23
  168.8 92.6 %feed_forward.1 = (f32[1152,896]{1,0:T(8,128)}, f32[1152,896]{1,0:T(8,128)}, bf16[2,4,896,800]{3,2,1,0:T(8,128)(2,1)}, f32[8,1,400]{2,1,0:T(1,128)}) custom-call(s32[16]{0:T(128)} %select_reduce_fusion.inv_ref, bf16[1152,896]{1,0:T(8,128)(2,1)} %copy-done.22, bf16[800,1152]{1,0:T(8,128)(2,1)} %copy-done.24, bf16[1152,896]{1,0:T(8,128)(2,1)} %copy-done.23, ...), custom_call_target="tpu_custom_call" | custom-call | flops 35389440000 | bytes 41943040 | tf_op jit(solution)/shard_map/feed_forward/pallas_call | solution.py:1026
  261.9 11.3 %close_out.1 = (bf16[1152,800]{1,0:T(8,128)(2,1)}, f32[1152,800]{1,0:T(8,128)}, f32[2,1,800]{2,1,0:T(1,128)}) custom-call(f32[1152,896]{1,0:T(8,128)} %get-tuple-element.46.b_ref, f32[1152,896]{1,0:T(8,128)} %get-tuple-element.47.d_ref, bf16[1152,800]{1,0:T(8,128)(2,1)} %bitcast.45, f32[1152,800]{1,0:T(8,128)} %bitcast.44, f32[1152,128]{1,0:T(8,128)} %copy-done.10, ...), custom_call_target="tpu_custom_call" | custom-call | tf_op jit(solution)/shard_map/close_out/pallas_call | solution.py:1084
  273.9 7.1 %tile_total.3 = f32[2,800]{1,0:T(2,128)S(1)} custom-call(f32[2,800]{1,0:T(2,128)S(1)} %pad_maximum_fusion.2.v_ref), custom_call_target="tpu_custom_call" | custom-call | tf_op jit(solution)/shard_map/tile_total/pallas_call | solution.py:589
  281.6 2.2 copy-done.1
  283.8 2.2 copy-done.11
  285.9 2.5 conv_gradient.1
  288.4 2.0 copy-done.4
  291.4 89.6 %exchange_backward.1 = (bf16[7,2,5,72,128]{4,3,2,1,0:T(8,128)(2,1)}, bf16[2,448,800]{2,1,0:T(8,128)(2,1)}, f32[50,800]{1,0:T(8,128)}) custom-call(bf16[7,2,4,72,128]{4,3,2,1,0:T(8,128)(2,1)} %copy-done.16, bf16[2,4,896,800]{3,2,1,0:T(8,128)(2,1)} %get-tuple-element.53.g_ref, s32[8,2,8]{2,1,0:T(2,128)} %copy-done.19, bf16[2,24,24,800]{3,2,1,0:T(8,128)(2,1)} %bitcast.46, ...), custom_call_target="tpu_custom_call" | custom-call | tf_op jit(solution)/shard_map/exchange_backward/pallas_call | solution.py:453
  382.3 1.4 copy-done.13
  383.7 90.1 %finish_gradients.1 = (bf16[2,896,800]{2,1,0:T(8,128)(2,1)S(1)}, f32[57,800]{1,0:T(8,128)S(1)}) custom-call(bf16[2,448,800]{2,1,0:T(8,128)(2,1)S(1)} %copy-done.13, f32[57,800]{1,0:T(8,128)S(1)} %concatenate.10.s_ref), custom_call_target="tpu_custom_call" | custom-call | tf_op jit(solution)/shard_map/finish_gradients/pallas_call | solution.py:551
  473.9 1.7 copy-done.12
  477.0 1.8 copy.44.l_ref
  481.2 12.4 %rotate.1 = (f32[4,100,400]{2,1,0:T(8,128)}, f32[4,100,400]{2,1,0:T(8,128)}, bf16[2,896,800]{2,1,0:T(8,128)(2,1)}) custom-call(f32[1]{0:T(128)} %bitcast.20.f_ref, bf16[2,896,800]{2,1,0:T(8,128)(2,1)} %copy-done.12, f32[4,800,100]{2,1,0:T(8,128)} %copy.44.l_ref, f32[4,400,400]{2,1,0:T(8,128)} %c_ref.1, f32[4,100,400]{2,1,0:T(8,128)} %copy.45.one_ref, ...), custom_call_target="tpu_custom_call" | custom-call | tf_op jit(solution)/shard_map/rotate/pallas_call | solution.py:1153
  493.5 1.3 copy-done.15
  494.8 53.8 %conv_backward.1 = (f32[2,576,800]{2,1,0:T(8,128)}, f32[2,112,800]{2,1,0:T(8,128)S(1)}) custom-call(f32[2,576,800]{2,1,0:T(8,128)} %copy-done.4, bf16[2,24,24,800]{3,2,1,0:T(8,128)(2,1)S(1)} %bitcast.50, f32[2,576,128]{2,1,0:T(8,128)S(1)} %copy-done.6, f32[50,8,800]{2,1,0:T(8,128)S(1)} %copy-done.9, f32[8,128]{1,0:T(8,128)S(1)} %broadcast_in_dim.77.l_ref, ...), custom_call_target="tpu_custom_call" | custom-call | tf_op jit(solution)/shard_map/conv_backward/pallas_call | solution.py:840
  550.3 1.4 copy.48
  552.7 1.4 copy.50
  554.2 1.4 copy.51
  556.5 2.0 copy.57
  (133 shorter events, 20.5 us)
Async XLA Ops:
  4.3 277.3 %copy-start.5 = (f32[2,576,128]{2,1,0:T(8,128)}, f32[2,576,128]{2,1,0:T(8,128)S(1)}, u32[]{:S(2)}) copy-start(f32[2,576,128]{2,1,0:T(8,128)S(1)} %broadcast_in_dim.65.m_ref) | copy-start | bytes 1769476
  4.3 1.8 copy-start.2
  7.4 104.0 %slice-start = ((f32[57,800]{1,0:T(8,128)}), f32[50,800]{1,0:T(8,128)S(1)}, s32[]{:S(2)}) async-start(f32[57,800]{1,0:T(8,128)} %param.23), calls=%async_computation | async-start | bytes 401408 | tf_op jit(solution)/shard_map/slice | solution.py:1227
  8.1 103.4 %copy-start.3 = (bf16[1,2,24,24,800]{4,3,2,1,0:T(8,128)(2,1)S(1)}, bf16[1,2,24,24,800]{4,3,2,1,0:T(8,128)(2,1)}, u32[]{:S(2)}) copy-start(bf16[1,2,24,24,800]{4,3,2,1,0:T(8,128)(2,1)} %param.16) | copy-start | bytes 5529604
  106.7 4.7 copy-start.21
  111.4 15.4 %copy-start.14 = (bf16[7,2,5,72,128]{4,3,2,1,0:T(8,128)(2,1)}, bf16[7,2,5,72,128]{4,3,2,1,0:T(8,128)(2,1)S(1)}, u32[]{:S(2)}) copy-start(bf16[7,2,5,72,128]{4,3,2,1,0:T(8,128)(2,1)S(1)} %get-tuple-element.38.h_ref) | copy-start | bytes 3870724
  111.4 15.5 %copy-start.19 = (s32[8,2,8]{2,1,0:T(2,128)}, s32[8,2,8]{2,1,0:T(2,128)S(1)}, u32[]{:S(2)}) copy-start(s32[8,2,8]{2,1,0:T(2,128)S(1)} %get-tuple-element.54.n_ref) | copy-start | bytes 1540
  111.5 15.4 %copy-start.8 = (f32[50,8,800]{2,1,0:T(8,128)}, f32[50,8,800]{2,1,0:T(8,128)S(1)}, u32[]{:S(2)}) copy-start(f32[50,8,800]{2,1,0:T(8,128)S(1)} %broadcast_in_dim.66.w_ref) | copy-start | bytes 3840004
  111.5 37.9 %copy-start.30 = (f32[57,800]{1,0:T(8,128)S(1)}, f32[57,800]{1,0:T(8,128)}, u32[]{:S(2)}) copy-start(f32[57,800]{1,0:T(8,128)} %param.23) | copy-start | bytes 547204
  126.9 2.0 copy-start
  149.5 8.0 %copy-start.40 = (s32[4]{0:T(128)S(1)}, s32[4]{0:T(128)}, u32[]{:S(2)}) copy-start(s32[4]{0:T(128)} %param.30) | copy-start | bytes 52
  157.1 11.0 %copy-start.41 = (s32[16]{0:T(128)S(1)}, s32[16]{0:T(128)}, u32[]{:S(2)}) copy-start(s32[16]{0:T(128)} %param.29) | copy-start | bytes 196
  281.6 2.2 copy-start.1
  283.7 2.2 copy-start.11
  288.4 2.0 copy-start.4
  291.4 89.7 %copy-start.39 = (f32[2,1,800]{2,1,0:T(1,128)S(1)}, f32[2,1,800]{2,1,0:T(1,128)}, u32[]{:S(2)}) copy-start(f32[2,1,800]{2,1,0:T(1,128)} %get-tuple-element.50) | copy-start | bytes 19204
  291.4 89.7 %copy-start.38 = (f32[8,1,400]{2,1,0:T(1,128)S(1)}, f32[8,1,400]{2,1,0:T(1,128)}, u32[]{:S(2)}) copy-start(f32[8,1,400]{2,1,0:T(1,128)} %get-tuple-element.59) | copy-start | bytes 38404
  291.4 185.6 %copy-start.29 = (f32[4,800,100]{1,0,2:T(4,128)S(1)}, f32[4,800,100]{1,0,2:T(4,128)}, u32[]{:S(2)}) copy-start(f32[4,800,100]{1,0,2:T(4,128)} %param.21) | copy-start | bytes 3840004
  382.3 1.4 copy-start.13
  383.7 95.1 %copy-start.34 = (f32[4,100,400]{2,0,1:T(4,128)S(1)}, f32[4,100,400]{2,0,1:T(4,128)}, u32[]{:S(2)}) copy-start(f32[4,100,400]{2,0,1:T(4,128)} %param.19) | copy-start | bytes 1920004
  473.9 1.7 copy-start.12
  477.0 3.0 copy-start.35
  481.1 12.4 %copy-start.6 = (f32[2,576,128]{2,1,0:T(8,128)S(1)}, f32[2,576,128]{2,1,0:T(8,128)}, u32[]{:S(2)}) copy-start(f32[2,576,128]{2,1,0:T(8,128)} %copy-done.5) | copy-start | bytes 1769476
  481.1 12.4 %copy-start.7 = (bf16[1,2,24,24,800]{4,3,2,1,0:T(8,128)(2,1)S(1)}, bf16[1,2,24,24,800]{4,3,2,1,0:T(8,128)(2,1)}, u32[]{:S(2)}) copy-start(bf16[1,2,24,24,800]{4,3,2,1,0:T(8,128)(2,1)} %param.17) | copy-start | bytes 5529604
  481.1 12.4 %copy-start.9 = (f32[50,8,800]{2,1,0:T(8,128)S(1)}, f32[50,8,800]{2,1,0:T(8,128)}, u32[]{:S(2)}) copy-start(f32[50,8,800]{2,1,0:T(8,128)} %copy-done.8) | copy-start | bytes 3840004
  550.0 2.7 copy-start.33
  550.3 3.8 copy-start.32
  551.8 3.8 copy-start.18
  551.8 3.8 copy-start.31
  551.8 3.8 copy-start.36
  551.8 3.8 copy-start.37
  552.7 3.8 copy-start.26
  (11 other events, 12.2 us)

commit v5 on v4

--- a/solution.py
+++ b/solution.py
@@ -240,7 +240,7 @@
         self.grid, self.pairs, self.width = grid, pairs, width
         self.count = pairs * (grid.n_tile * grid.n_opt - 1)
 
-    def run(self, copies, packed, gathered, local):
+    def plan(self, copies, packed, gathered, local):
         grid, width = self.grid, self.width
         own = grid.own()
 
@@ -248,101 +248,177 @@
             t, o = grid.at({d: own[d] ^ rel.get(d, 0) for d in own})
             return gathered.at[m, o, pl.ds(pl.multiple_of(t * width, width), width)]
 
-        keeps, started = [], []
-        for m in range(self.pairs):
-            keep = pltpu.make_async_copy(packed.at[m], place(m, {}), local.at[m])
-            keep.start()
-            keeps.append(keep)
-
-        def forward(m, rel, dims):
+        def onward(m, rel, dims):
             source = packed.at[m] if not rel else place(m, rel)
-            fresh = []
-            for dim in dims:
-                for k in range(1, grid.size[dim]):
-                    copy = copies.start(source, place(m, rel), grid.beside(own, dim, k))
-                    fresh.append(({**rel, dim: k}, copy))
-            started.extend(copy for _, copy in fresh)
-            return fresh
+            return [
+                ({**rel, dim: k}, copies.make(source, place(m, rel), grid.beside(own, dim, k)))
+                for dim in dims
+                for k in range(1, grid.size[dim])
+            ]
 
         orders = [("a", "x", "b", "c") if m % 2 == 0 else ("a", "b", "x", "c") for m in range(self.pairs)]
-        waves = {}
+        due = {}
 
         def note(m, fresh, after):
             for rel, copy in fresh:
                 level = sum(1 for d in rel if d != "c")
                 wave = max(rel.get("a", 0) + level - ("a" in rel), after)
-                waves.setdefault(wave, []).append((m, rel, copy))
-
+                due.setdefault(wave, []).append((m, rel, copy))
+            return [copy for _, copy in fresh]
+
+        self.keeps = [pltpu.make_async_copy(packed.at[m], place(m, {}), local.at[m]) for m in range(self.pairs)]
+        self.first = []
         for m in range(self.pairs):
-            note(m, forward(m, {}, orders[m]), 0)
-        yield 0
+            fresh = onward(m, {}, orders[m])
+            self.first += note(m, fresh, 0)
+        self.waves = []
         for wave in range(4 * sum(grid.size.values())):
-            for m, rel, copy in sorted(waves.pop(wave, []), key=lambda e: "c" in e[1]):
+            events = []
+            for m, rel, copy in sorted(due.pop(wave, []), key=lambda e: "c" in e[1]):
+                last = max(orders[m].index(d) for d in rel)
+                events.append((copy, note(m, onward(m, rel, orders[m][last + 1 :]), wave + 1)))
+            self.waves.append(events)
+            if not due:
+                break
+
+    def start(self):
+        for copy in self.keeps + self.first:
+            copy.start()
+
+    def run(self, waves):
+        for events in waves:
+            for copy, fresh in events:
                 copy.wait_recv()
-                last = max(orders[m].index(d) for d in rel)
-                note(m, forward(m, rel, orders[m][last + 1 :]), wave + 1)
-            if not waves:
-                break
-            yield wave
-        for keep in keeps:
+                for other in fresh:
+                    other.start()
+
+    def finish(self):
+        for copy in self.keeps:
+            copy.wait()
+        for copy in self.first + [c for events in self.waves for _, fresh in events for c in fresh]:
+            copy.wait_send()
+
+
+def exchange_forward(grid, rims, packed, neighbours, inputs, mask_lanes, taps, cotangent, flat_mask, weight_row, width):
+    n_chunk, slots, _, band, _ = rims.shape
+    side, channels = inputs.shape[1], inputs.shape[3]
+    cells = side * side
+    pairs, _, cols = packed.shape
+    n_tile = grid.n_tile
+    rows = slots * cells
+    block = row_block(rows)
+    early = rows // block
+    halo = HaloExchange(grid, n_chunk, slots, side)
+    gather = WeightGather(grid, pairs, packed.shape[1])
+    total = halo.count + gather.count + n_tile - 1
+    last = early + n_chunk * slots
+
+    def kernel(
+        r_ref, p_ref, n_ref, x_ref, m_ref, t_ref, g_ref, f_ref, l_ref,
+        halo_ref, w_ref, nbr_ref, conv_ref, sum_ref, gap_ref, turned_ref, bias_ref,
+        arrived, picked, local, landed, table, pad, send, recv, locals_w, locals_n,
+    ):
+        step = pl.program_id(0)
+        t, o = grid.at(grid.own())
+        copies = Copies(send, recv)
+        halo.plan(copies, r_ref, arrived, picked, landed, local)
+        gather.plan(copies, p_ref, w_ref, locals_w)
+        tables = [copies.make(n_ref, nbr_ref.at[t], (t ^ k, o)) for k in range(1, n_tile)]
+        keep = pltpu.make_async_copy(n_ref, nbr_ref.at[t], locals_n.at[0])
+        load = pltpu.make_async_copy(nbr_ref, table, locals_n.at[1])
+        halo_out = pltpu.make_async_copy(landed, halo_ref, locals_n.at[0])
+        head = len(gather.waves) // 2
+
+        @pl.when(step == 0)
+        def _():
+            meet(grid.partners(("tile", "x", "c")))
+            for copy in tables:
+                copy.start()
+            keep.start()
+            halo.send_rims()
+            gather.start()
+
+        @pl.when((step > 0) & (step <= early))
+        def _():
+            value = f_ref[:, :1] * (l_ref[:, :1] * g_ref[...].astype(F32))
+            arranged(value, gap_ref, turned_ref, bias_ref, step == 1, n_tile, width)
+
+        @pl.when(step == early)
+        def _():
             keep.wait()
-        for copy in started:
-            copy.wait_send()
-        yield -1
-
-
-def exchange_forward(grid, rims, packed, neighbours):
-    n_chunk, slots, _, band, _ = rims.shape
-    pairs, width, cols = packed.shape
-    n_tile = grid.n_tile
-    halo = HaloExchange(grid, n_chunk, slots, band // RIM)
-    gather = WeightGather(grid, pairs, width)
-    total = halo.count + gather.count + n_tile - 1
-
-    def kernel(r_ref, p_ref, n_ref, halo_ref, w_ref, nbr_ref, arrived, picked, local, table, send, recv, locals_w, locals_n):
-        own = grid.own()
-        t, o = grid.at(own)
-        meet(grid.partners(("tile", "x", "c")))
-        copies = Copies(send, recv)
-        tables = [copies.start(n_ref, nbr_ref.at[t], (t ^ k, o)) for k in range(1, n_tile)]
-        keep = pltpu.make_async_copy(n_ref, nbr_ref.at[t], locals_n.at[0])
-        keep.start()
-        halo.plan(copies, r_ref, arrived, picked, halo_ref, local)
-        halo.send_rims()
-        weights = gather.run(copies, p_ref, w_ref, locals_w)
-        next(weights)
-        keep.wait()
-        for copy in tables:
-            copy.wait()
-        load = pltpu.make_async_copy(nbr_ref, table, locals_n.at[1])
-        load.start()
-        load.wait()
-        halo.pick_and_send(lambda d, k: table[d // slots, d % slots, k])
-        for _ in weights:
-            pass
-        halo.finish()
-
+            for copy in tables:
+                copy.wait()
+            load.start()
+            load.wait()
+            halo.pick_and_send(lambda d, k: table[d // slots, d % slots, k])
+            gather.run(gather.waves[:head])
+            halo.finish()
+            halo_out.start()
+
+        for i, events in enumerate(gather.waves[head:]):
+
+            @pl.when(step == min(last, early + 4 + 3 * i))
+            def _():
+                gather.run([events])
+
+        @pl.when(step > early)
+        def _():
+            at = step - early - 1
+            conv_step(
+                x_ref, m_ref, t_ref, lambda k: landed[at // slots, at % slots, k].astype(F32), conv_ref, sum_ref, pad, side
+            )
+
+        @pl.when(step == last)
+        def _():
+            gather.finish()
+            halo_out.wait()
+
+    conv_at = lambda i: jnp.maximum(i - early - 1, 0)
+    row_at = lambda i: jnp.clip(i - 1, 0, early - 1)
     any_space = pl.BlockSpec(memory_space=pl.ANY)
     return pl.pallas_call(
         kernel,
-        in_specs=[any_space] * 3,
-        out_specs=[any_space] * 3,
+        grid=(last + 1,),
+        in_specs=[any_space] * 3
+        + [
+            pl.BlockSpec((1, side, side, LANES), lambda i: (conv_at(i) % slots, 0, 0, conv_at(i) // slots)),
+            pl.BlockSpec((1, cells, LANES), lambda i: (conv_at(i) % slots, 0, 0)),
+            pl.BlockSpec((50, 8, LANES), lambda i: (0, 0, conv_at(i) // slots)),
+            pl.BlockSpec((block, channels), lambda i: (row_at(i), 0)),
+            pl.BlockSpec((block, LANES), lambda i: (row_at(i), 0)),
+            pl.BlockSpec((1, LANES), lambda i: (0, 0)),
+        ],
+        out_specs=[any_space] * 3
+        + [
+            pl.BlockSpec((1, cells, LANES), lambda i: (conv_at(i) % slots, 0, conv_at(i) // slots)),
+            pl.BlockSpec((1, 2, 8, LANES), lambda i: (conv_at(i) % slots, 0, 0, conv_at(i) // slots)),
+            pl.BlockSpec((block, n_tile * width), lambda i: (row_at(i), 0)),
+            pl.BlockSpec((channels, block), lambda i: (0, row_at(i))),
+            pl.BlockSpec((1, channels), lambda i: (0, 0)),
+        ],
         out_shape=[
             halo.halo_shape(),
-            jax.ShapeDtypeStruct((pairs, grid.n_opt, n_tile * width, cols), BF),
+            jax.ShapeDtypeStruct((pairs, grid.n_opt, n_tile * packed.shape[1], cols), BF),
             jax.ShapeDtypeStruct((n_tile,) + neighbours.shape, jnp.int32),
+            jax.ShapeDtypeStruct((slots, cells, channels), F32),
+            jax.ShapeDtypeStruct((slots, 2, 8, channels), F32),
+            jax.ShapeDtypeStruct((rows, n_tile * width), BF),
+            jax.ShapeDtypeStruct((channels, rows), BF),
+            jax.ShapeDtypeStruct((1, channels), F32),
         ],
         scratch_shapes=halo.scratch()
         + [
+            pltpu.VMEM(halo.halo_shape().shape, BF),
             pltpu.SMEM((n_tile,) + neighbours.shape, jnp.int32),
+            pltpu.VMEM(((side + 2 * RIM) * PITCH, LANES), F32),
             pltpu.SemaphoreType.DMA((total,)),
             pltpu.SemaphoreType.DMA((total,)),
             pltpu.SemaphoreType.DMA((pairs,)),
             pltpu.SemaphoreType.DMA((2,)),
         ],
-        compiler_params=remote_params(1, 32),
+        compiler_params=remote_params(1, 40),
         name="exchange_forward",
-    )(rims, packed, neighbours)
+    )(rims, packed, neighbours, inputs, mask_lanes, taps, cotangent, flat_mask, weight_row)
 
 
 def exchange_backward(grid, rims, grads, neighbours, inputs, mask_lanes, d_conv, halos):
@@ -636,60 +712,24 @@
     return pl.BlockSpec((1, 1) + halos.shape[2:], lambda c, s: (c, s, 0, 0, 0))
 
 
-def conv_cost(n_chunk, slots, side, nbytes):
-    return pl.CostEstimate(
-        flops=n_chunk * slots * side * side * LANES * 98 * 100, bytes_accessed=nbytes, transcendentals=0
-    )
-
-
-def conv_forward(inputs, mask_lanes, halos, taps):
-    slots, side, _, channels = inputs.shape
-    n_chunk = halos.shape[0]
-
-    def kernel(x_ref, m_ref, w_ref, h_ref, o_ref, s_ref, pad):
+def conv_step(x_ref, m_ref, w_ref, halo, o_ref, s_ref, pad, side):
+    for i in range(side):
+        pad[pl.ds((i + RIM) * PITCH + 8, side), :] = x_ref[0, i].astype(F32) * m_ref[0, pl.ds(i * side, side), :]
+    fill_halo(pad, halo, side)
+    bias = w_ref[49]
+    totals = [jnp.zeros((8, LANES), F32), jnp.zeros((8, LANES), F32)]
+
+    def emit(block, sums):
         for i in range(side):
-            pad[pl.ds((i + RIM) * PITCH + 8, side), :] = (
-                x_ref[0, i].astype(F32) * m_ref[0, pl.ds(i * side, side), :]
-            )
-        fill_halo(pad, lambda k: h_ref[0, 0, k].astype(F32), side)
-        bias = w_ref[49]
-        totals = [jnp.zeros((8, LANES), F32), jnp.zeros((8, LANES), F32)]
-
-        def emit(block, sums):
-            for i in range(side):
-                value = sums[i] + bias
-                rows = pl.ds(i * side + 8 * block, 8)
-                o_ref[0, rows, :] = value
-                weighted = m_ref[0, rows, :] * value
-                totals[0] = totals[0] + weighted
-                totals[1] = totals[1] + weighted * value
-
-        conv_pass(pad, side, lambda a, b: w_ref[7 * a + b], emit)
-        s_ref[0, 0], s_ref[0, 1] = totals
-
-    cells = side * side
-    return pl.pallas_call(
-        kernel,
-        grid=(n_chunk, slots),
-        in_specs=[
-            pl.BlockSpec((1, side, side, LANES), lambda c, s: (s, 0, 0, c)),
-            pl.BlockSpec((1, cells, LANES), lambda c, s: (s, 0, 0)),
-            pl.BlockSpec((50, 8, LANES), lambda c, s: (0, 0, c)),
-            halo_block(halos),
-        ],
-        out_specs=[
-            pl.BlockSpec((1, cells, LANES), lambda c, s: (s, 0, c)),
-            pl.BlockSpec((1, 2, 8, LANES), lambda c, s: (s, 0, 0, c)),
-        ],
-        scratch_shapes=[pltpu.VMEM(((side + 2 * RIM) * PITCH, LANES), F32)],
-        out_shape=[
-            jax.ShapeDtypeStruct((slots, cells, channels), F32),
-            jax.ShapeDtypeStruct((slots, 2, 8, channels), F32),
-        ],
-        cost_estimate=conv_cost(n_chunk, slots, side, 10 << 20),
-        compiler_params=pltpu.CompilerParams(vmem_limit_bytes=32 << 20),
-        name="conv_forward",
-    )(inputs, mask_lanes, taps, halos)
+            value = sums[i] + bias
+            rows = pl.ds(i * side + 8 * block, 8)
+            o_ref[0, rows, :] = value
+            weighted = m_ref[0, rows, :] * value
+            totals[0] = totals[0] + weighted
+            totals[1] = totals[1] + weighted * value
+
+    conv_pass(pad, side, lambda a, b: w_ref[7 * a + b], emit)
+    s_ref[0, 0], s_ref[0, 1] = totals
 
 
 def conv_gradient(d_shaped, conv_out, mask_lanes, coefs, side):
@@ -890,21 +930,28 @@
     return jnp.concatenate([value[:, t * width : t * width + run] for t in range(parts)], 1)
 
 
+def row_block(rows):
+    return 3 * LANES if rows % (3 * LANES) == 0 else LANES
+
+
+def arranged(value, gap_ref, turned_ref, sum_ref, first, parts, width):
+    low = value.astype(BF).astype(F32)
+    gap_ref[...] = spread_lanes(low, parts, width).astype(BF)
+    turned_ref[...] = low.T.astype(BF)
+
+    @pl.when(first)
+    def _():
+        sum_ref[...] = jnp.zeros_like(sum_ref)
+
+    sum_ref[...] += jnp.sum(low, axis=0, keepdims=True)
+
+
 def arrange(body, args, specs, rows, channels, parts, width, name):
     step = 3 * LANES if rows % (3 * LANES) == 0 else LANES
 
     def kernel(*refs):
         given, (gap_ref, turned_ref, sum_ref) = refs[: len(args)], refs[len(args) :]
-        low = body(*given).astype(BF)
-        value = low.astype(F32)
-        gap_ref[...] = spread_lanes(value, parts, width).astype(BF)
-        turned_ref[...] = value.T.astype(BF)
-
-        @pl.when(pl.program_id(0) == 0)
-        def _():
-            sum_ref[...] = jnp.zeros_like(sum_ref)
-
-        sum_ref[...] += jnp.sum(value, axis=0, keepdims=True)
+        arranged(body(*given), gap_ref, turned_ref, sum_ref, pl.program_id(0) == 0, parts, width)
 
     return pl.pallas_call(
         kernel,
@@ -975,6 +1022,12 @@
                     held[...] = packed[now, which, :, parity * cols : (parity + 1) * cols]
 
         hidden = hb_ref[0]
+
+        @pl.when(step == 0)
+        def _():
+            branch_ref[...] = jnp.zeros_like(branch_ref)
+            ds_ref[...] = jnp.zeros_like(ds_ref)
+
         total = jnp.zeros((1, cols), F32)
         across = (((1,), (1,)), ((), ()))
         for i in range(rows // tile_rows):
@@ -993,15 +1046,8 @@
             out_add = lax.dot_general(low, second[...], across, preferred_element_type=F32)
             in_add = lax.dot_general(back, first[...], across, preferred_element_type=F32)
 
-            @pl.when(step == 0)
-            def _():
-                branch_ref[at, :] = out_add
-                ds_ref[at, :] = in_add
-
-            @pl.when(step > 0)
-            def _():
-                branch_ref[at, :] += out_add
-                ds_ref[at, :] += in_add
+            branch_ref[at, :] += out_add
+            ds_ref[at, :] += in_add
 
         bias_ref[0] = total
         for which, (left, right) in enumerate(((st_ref, dpre), (dt_ref, act))):
@@ -1226,34 +1272,27 @@
     flat_mask = mask_lanes.reshape(rows, LANES)
     taps = jnp.broadcast_to(small_params[:50, None, :], (50, 8, channels))
 
-    low_master = jnp.pad(pack_pairs(master.astype(BF)), ((0, 0), (0, width - run), (0, 0)))
-    rims = rims_of_input(inputs, mask_lanes)
-    halos, weights, all_neighbours = exchange_forward(grid, rims, low_master, neighbours)
-
     weights_float = cell_weight.astype(F32)
     sample_weight = weights_float[sample] * weights_float.shape[0] / jnp.sum(weights_float)
     weight_lanes = jnp.broadcast_to(sample_weight, (8, LANES))
     weight_row = jnp.broadcast_to(sample_weight, (1, LANES))
-    flat_cotangent = cotangent.reshape(rows, channels)
-
-    def d_branch_body(g_ref, m_ref, w_ref):
-        return m_ref[:, :1] * (w_ref[:, :1] * g_ref[...].astype(F32))
-
-    d_branch, d_branch_t, d_out_bias = arrange(
-        d_branch_body,
-        (flat_cotangent, flat_mask, weight_row),
-        lambda step: [
-            pl.BlockSpec((step, channels), lambda i: (i, 0)),
-            pl.BlockSpec((step, LANES), lambda i: (i, 0)),
-            pl.BlockSpec((1, LANES), lambda i: (0, 0)),
-        ],
-        rows,
-        channels,
-        n_tile,
+
+    low_master = jnp.pad(pack_pairs(master.astype(BF)), ((0, 0), (0, width - run), (0, 0)))
+    rims = rims_of_input(inputs, mask_lanes)
+    halos, weights, all_neighbours, conv_out, sums, d_branch, d_branch_t, d_out_bias = exchange_forward(
+        grid,
+        rims,
+        low_master,
+        neighbours,
+        inputs,
+        mask_lanes,
+        taps,
+        cotangent.reshape(rows, channels),
+        flat_mask,
+        weight_row,
         width,
-        "arrange_d_branch",
     )
-    conv_out, sums = conv_forward(inputs, mask_lanes, halos, taps)
+
     sums = jnp.sum(sums, axis=(0, 2))
     occupied = jnp.broadcast_to(jnp.sum(mask), (1, channels))
     sums = tile_total(grid, jnp.concatenate([sums, occupied], 0), 5)

time: 559 us -> 556 us (level)
  Pallas kernels: 501 us -> 493 us
    pallas_call x2 -> x1, Pallas kernels: 114 us -> 131 us  [exchange_forward(): pl.pallas_call(kernel, grid=(last + 1,), in_specs=[any_space] * 3 + [pl.B...]
    pallas_call x2, Pallas kernels: 25.2 us -> 13.2 us  [tile_total(): pl.pallas_call(kernel, in_specs=[whole], out_specs=whole, out_shape=jax.S...]
    pallas_call x1, Pallas kernels: 92.6 us -> 85.1 us  [feed_forward(): pl.pallas_call(kernel, grid_spec=pltpu.PrefetchScalarGridSpec(num_scalar_...]
where the time goes in v5:
time: 556 us; the launch traced here: 554 us
  Pallas kernels  493 us (89%)
  local copies, waits for them, and re-layouts  49.8 us (9%)
  other arithmetic  7.88 us (1%)
    pallas_call x1, Pallas kernels, exchange_forward(): pl.pallas_call(kernel, grid=(last + 1,), in_specs=[any_space] * 3 + [pl.B...  131 us
    pallas_call x1, Pallas kernels, finish_gradients(): pl.pallas_call(kernel, in_specs=[any_space, whole], out_specs=[any_space,...  91 us
    pallas_call x1, Pallas kernels, exchange_backward(): pl.pallas_call(kernel, grid=(n_chunk, slots), in_specs=[any_space, any_sp...  89.1 us
    pallas_call x1, Pallas kernels, feed_forward(): pl.pallas_call(kernel, grid_spec=pltpu.PrefetchScalarGridSpec(num_scalar_...  85.1 us
    pallas_call x1, Pallas kernels, conv_backward(): pl.pallas_call(kernel, grid=(n_chunk, slots), in_specs=[pl.BlockSpec((1,...  51.2 us
    unnamed x92, local copies, waits for them, and re-layouts  38.8 us
    pallas_call x2, Pallas kernels, tile_total(): pl.pallas_call(kernel, in_specs=[whole], out_specs=whole, out_shape=jax.S...  13.2 us
    pallas_call x1, Pallas kernels, rotate(): pl.pallas_call(kernel, grid=(pairs,), in_specs=[pl.BlockSpec(memory_space...  12.3 us

profile of v5, /device:TPU:8, one launch (start us, length us, event | category | flops | bytes accessed | tf_op | source)
XLA Modules:
  0.0 554.3 jit_solution(17835075630949717833)
XLA Ops:
  0.6 1.2 dynamic_slice.6
  2.5 1.4 fusion.7
  4.3 1.8 copy-done.1
  12.8 2.2 convert_element_type.27
  15.0 1.5 copy.52
  16.8 1.4 copy-done.6
  18.2 1.6 copy-done.8
  22.1 131.0 %exchange_forward.1 = (bf16[7,2,5,72,128]{4,3,2,1,0:T(8,128)(2,1)S(1)}, bf16[2,4,896,800]{3,2,1,0:T(8,128)(2,1)}, s32[8,2,8]{2,1,0:T(2,128)S(1)}, f32[2,576,800]...) custom-call(bf16[7,2,4,72,128]{4,3,2,1,0:T(8,128)(2,1)S(1)} %copy-do, ...), custom_call_target="tpu_custom_call" | custom-call | tf_op jit(solution)/shard_map/exchange_forward/pallas_call | solution.py:379
  154.1 1.3 copy-done.23
  157.3 6.2 %tile_total.2 = f32[3,800]{1,0:T(4,128)S(1)} custom-call(f32[3,800]{1,0:T(4,128)S(1)} %concatenate.9.v_ref), custom_call_target="tpu_custom_call" | custom-call | tf_op jit(solution)/shard_map/tile_total/pallas_call | solution.py:665
  165.3 5.1 arrange_shaped.1
  170.4 1.3 copy-done.24
  171.7 1.3 copy-done.26
  174.3 85.1 %feed_forward.1 = (f32[1152,896]{1,0:T(8,128)}, f32[1152,896]{1,0:T(8,128)}, bf16[2,4,896,800]{3,2,1,0:T(8,128)(2,1)}, f32[8,1,400]{2,1,0:T(1,128)}) custom-call(s32[16]{0:T(128)} %select_reduce_fusion.inv_ref, bf16[1152,896]{1,0:T(8,128)(2,1)} %copy-done.24, bf16[800,1152]{1,0:T(8,128)(2,1)} %copy-done.26, bf16[1152,896]{1,0:T(8,128)(2,1)} %copy-done.23, ...), custom_call_target="tpu_custom_call" | custom-call | flops 35389440000 | bytes 41943040 | tf_op jit(solution)/shard_map/feed_forward/pallas_call | solution.py:1072
  260.0 11.3 %close_out.1 = (bf16[1152,800]{1,0:T(8,128)(2,1)}, f32[1152,800]{1,0:T(8,128)}, f32[2,1,800]{2,1,0:T(1,128)}) custom-call(f32[1152,896]{1,0:T(8,128)} %get-tuple-element.45.b_ref, f32[1152,896]{1,0:T(8,128)} %get-tuple-element.46.d_ref, bf16[1152,800]{1,0:T(8,128)(2,1)} %bitcast.45, f32[1152,800]{1,0:T(8,128)} %bitcast.44, ...), custom_call_target="tpu_custom_call" | custom-call | tf_op jit(solution)/shard_map/close_out/pallas_call | solution.py:1130
  272.0 7.1 %tile_total.3 = f32[2,800]{1,0:T(2,128)S(1)} custom-call(f32[2,800]{1,0:T(2,128)S(1)} %pad_maximum_fusion.2.v_ref), custom_call_target="tpu_custom_call" | custom-call | tf_op jit(solution)/shard_map/tile_total/pallas_call | solution.py:665
  279.7 2.2 copy-done
  281.8 2.2 copy-done.13
  284.0 2.5 conv_gradient.1
  286.5 2.0 copy-done.5
  289.5 89.1 %exchange_backward.1 = (bf16[7,2,5,72,128]{4,3,2,1,0:T(8,128)(2,1)}, bf16[2,448,800]{2,1,0:T(8,128)(2,1)}, f32[50,800]{1,0:T(8,128)}) custom-call(bf16[7,2,4,72,128]{4,3,2,1,0:T(8,128)(2,1)} %copy-done.18, bf16[2,4,896,800]{3,2,1,0:T(8,128)(2,1)} %get-tuple-element.52.g_ref, s32[8,2,8]{2,1,0:T(2,128)} %copy-done.21, bf16[2,24,24,800]{3,2,1,0:T(8,128)(2,1)} %bitcast.46, ...), custom_call_target="tpu_custom_call" | custom-call | tf_op jit(solution)/shard_map/exchange_backward/pallas_call | solution.py:529
  379.9 1.4 copy-done.15
  381.3 91.0 %finish_gradients.1 = (bf16[2,896,800]{2,1,0:T(8,128)(2,1)S(1)}, f32[57,800]{1,0:T(8,128)S(1)}) custom-call(bf16[2,448,800]{2,1,0:T(8,128)(2,1)S(1)} %copy-done.15, f32[57,800]{1,0:T(8,128)S(1)} %concatenate.10.s_ref), custom_call_target="tpu_custom_call" | custom-call | tf_op jit(solution)/shard_map/finish_gradients/pallas_call | solution.py:627
  472.3 1.6 copy-done.14
  475.4 1.8 copy.44.l_ref
  479.6 12.3 %rotate.1 = (f32[4,100,400]{2,1,0:T(8,128)}, f32[4,100,400]{2,1,0:T(8,128)}, bf16[2,896,800]{2,1,0:T(8,128)(2,1)}) custom-call(f32[1]{0:T(128)} %bitcast.20.f_ref, bf16[2,896,800]{2,1,0:T(8,128)(2,1)} %copy-done.14, f32[4,800,100]{2,1,0:T(8,128)} %copy.44.l_ref, f32[4,400,400]{2,1,0:T(8,128)} %c_ref.1, f32[4,100,400]{2,1,0:T(8,128)} %copy.45.one_ref, ...), custom_call_target="tpu_custom_call" | custom-call | tf_op jit(solution)/shard_map/rotate/pallas_call | solution.py:1199
  492.0 1.3 copy-done.17
  493.3 51.2 %conv_backward.1 = (f32[2,576,800]{2,1,0:T(8,128)}, f32[2,112,800]{2,1,0:T(8,128)S(1)}) custom-call(f32[2,576,800]{2,1,0:T(8,128)} %copy-done.5, bf16[2,24,24,800]{3,2,1,0:T(8,128)(2,1)S(1)} %bitcast.50, f32[2,576,128]{2,1,0:T(8,128)S(1)} %copy-done.4, f32[50,8,800]{2,1,0:T(8,128)S(1)} %copy-done.7, f32[8,128]{1,0:T(8,128)S(1)} %broadcast_in_dim.77.l_ref, ...), custom_call_target="tpu_custom_call" | custom-call | tf_op jit(solution)/shard_map/conv_backward/pallas_call | solution.py:880
  546.1 1.4 copy.48
  548.5 1.4 copy.50
  550.0 1.4 copy.51
  552.3 2.0 copy.57
  (131 shorter events, 25.0 us)
Async XLA Ops:
  4.3 275.4 %copy-start.3 = (f32[2,576,128]{2,1,0:T(8,128)}, f32[2,576,128]{2,1,0:T(8,128)S(1)}, u32[]{:S(2)}) copy-start(f32[2,576,128]{2,1,0:T(8,128)S(1)} %broadcast_in_dim.65.m_ref) | copy-start | bytes 1769476
  4.3 1.8 copy-start.1
  6.1 3.0 copy-start.40
  6.1 5.6 %slice-start = ((f32[57,800]{1,0:T(8,128)}), f32[50,800]{1,0:T(8,128)S(1)}, s32[]{:S(2)}) async-start(f32[57,800]{1,0:T(8,128)} %param.23), calls=%async_computation | async-start | bytes 401408 | tf_op jit(solution)/shard_map/slice | solution.py:1273
  12.8 4.0 copy-start.2
  12.8 4.0 copy-start.22
  16.8 1.4 copy-start.6
  18.2 1.6 copy-start.8
  22.1 143.2 %copy-start.30 = (f32[57,800]{1,0:T(8,128)S(1)}, f32[57,800]{1,0:T(8,128)}, u32[]{:S(2)}) copy-start(f32[57,800]{1,0:T(8,128)} %param.23) | copy-start | bytes 547204
  156.6 13.7 %copy-start.21 = (s32[8,2,8]{2,1,0:T(2,128)}, s32[8,2,8]{2,1,0:T(2,128)S(1)}, u32[]{:S(2)}) copy-start(s32[8,2,8]{2,1,0:T(2,128)S(1)} %get-tuple-element.53.n_ref) | copy-start | bytes 1540
  165.3 8.4 %copy-start.41 = (s32[16]{0:T(128)S(1)}, s32[16]{0:T(128)}, u32[]{:S(2)}) copy-start(s32[16]{0:T(128)} %param.29) | copy-start | bytes 196
  279.7 2.2 copy-start
  281.8 2.2 copy-start.13
  286.5 2.0 copy-start.5
  289.5 89.2 %copy-start.39 = (f32[2,1,800]{2,1,0:T(1,128)S(1)}, f32[2,1,800]{2,1,0:T(1,128)}, u32[]{:S(2)}) copy-start(f32[2,1,800]{2,1,0:T(1,128)} %get-tuple-element.49) | copy-start | bytes 19204
  289.5 89.2 %copy-start.38 = (f32[8,1,400]{2,1,0:T(1,128)S(1)}, f32[8,1,400]{2,1,0:T(1,128)}, u32[]{:S(2)}) copy-start(f32[8,1,400]{2,1,0:T(1,128)} %get-tuple-element.59) | copy-start | bytes 38404
  289.5 185.9 %copy-start.29 = (f32[4,800,100]{1,0,2:T(4,128)S(1)}, f32[4,800,100]{1,0,2:T(4,128)}, u32[]{:S(2)}) copy-start(f32[4,800,100]{1,0,2:T(4,128)} %param.21) | copy-start | bytes 3840004
  379.9 1.4 copy-start.15
  381.3 95.9 %copy-start.34 = (f32[4,100,400]{2,0,1:T(4,128)S(1)}, f32[4,100,400]{2,0,1:T(4,128)}, u32[]{:S(2)}) copy-start(f32[4,100,400]{2,0,1:T(4,128)} %param.19) | copy-start | bytes 1920004
  472.3 1.7 copy-start.14
  475.4 3.0 copy-start.35
  479.6 12.3 %copy-start.4 = (f32[2,576,128]{2,1,0:T(8,128)S(1)}, f32[2,576,128]{2,1,0:T(8,128)}, u32[]{:S(2)}) copy-start(f32[2,576,128]{2,1,0:T(8,128)} %copy-done.3) | copy-start | bytes 1769476
  479.6 12.3 %copy-start.7 = (f32[50,8,800]{2,1,0:T(8,128)S(1)}, f32[50,8,800]{2,1,0:T(8,128)}, u32[]{:S(2)}) copy-start(f32[50,8,800]{2,1,0:T(8,128)} %broadcast_in_dim.66.t_ref.w_ref) | copy-start | bytes 3840004
  479.6 12.3 %copy-start.9 = (bf16[1,2,24,24,800]{4,3,2,1,0:T(8,128)(2,1)S(1)}, bf16[1,2,24,24,800]{4,3,2,1,0:T(8,128)(2,1)}, u32[]{:S(2)}) copy-start(bf16[1,2,24,24,800]{4,3,2,1,0:T(8,128)(2,1)} %param.17) | copy-start | bytes 5529604
  491.9 1.3 copy-start.17
  545.8 2.7 copy-start.33
  546.1 3.8 copy-start.32
  547.6 3.8 copy-start.20
  547.6 3.8 copy-start.31
  547.6 3.8 copy-start.36
  547.6 3.8 copy-start.37
  548.5 3.8 copy-start.27
  (11 other events, 12.2 us)

commit v6 on v5

--- a/solution.py
+++ b/solution.py
@@ -267,10 +267,12 @@
             return [copy for _, copy in fresh]
 
         self.keeps = [pltpu.make_async_copy(packed.at[m], place(m, {}), local.at[m]) for m in range(self.pairs)]
-        self.first = []
+        self.first, self.later = [], []
         for m in range(self.pairs):
             fresh = onward(m, {}, orders[m])
-            self.first += note(m, fresh, 0)
+            note(m, fresh, 0)
+            for rel, copy in fresh:
+                (self.later if rel.get("a", 0) > 1 else self.first).append(copy)
         self.waves = []
         for wave in range(4 * sum(grid.size.values())):
             events = []
@@ -285,6 +287,10 @@
         for copy in self.keeps + self.first:
             copy.start()
 
+    def start_later(self):
+        for copy in self.later:
+            copy.start()
+
     def run(self, waves):
         for events in waves:
             for copy, fresh in events:
@@ -295,7 +301,7 @@
     def finish(self):
         for copy in self.keeps:
             copy.wait()
-        for copy in self.first + [c for events in self.waves for _, fresh in events for c in fresh]:
+        for copy in self.first + self.later + [c for events in self.waves for _, fresh in events for c in fresh]:
             copy.wait_send()
 
 
@@ -327,7 +333,7 @@
         keep = pltpu.make_async_copy(n_ref, nbr_ref.at[t], locals_n.at[0])
         load = pltpu.make_async_copy(nbr_ref, table, locals_n.at[1])
         halo_out = pltpu.make_async_copy(landed, halo_ref, locals_n.at[0])
-        head = len(gather.waves) // 2
+        head = 2
 
         @pl.when(step == 0)
         def _():
@@ -351,6 +357,7 @@
             load.start()
             load.wait()
             halo.pick_and_send(lambda d, k: table[d // slots, d % slots, k])
+            gather.start_later()
             gather.run(gather.waves[:head])
             halo.finish()
             halo_out.start()
@@ -416,25 +423,31 @@
             pltpu.SemaphoreType.DMA((pairs,)),
             pltpu.SemaphoreType.DMA((2,)),
         ],
-        compiler_params=remote_params(1, 40),
+        compiler_params=remote_params(1, 63),
         name="exchange_forward",
     )(rims, packed, neighbours, inputs, mask_lanes, taps, cotangent, flat_mask, weight_row)
 
 
-def exchange_backward(grid, rims, grads, neighbours, inputs, mask_lanes, d_conv, halos):
+def exchange_backward(grid, rims, grads, neighbours, inputs, mask_lanes, d_conv, halos, small):
     n_chunk, slots, _, band, _ = rims.shape
     side, channels = inputs.shape[1], inputs.shape[3]
     side_b, side_x = grid.size["b"], grid.size["x"]
     _, blocks, rows, cols = grads.shape
     pairs = blocks // side_x
     part = rows // side_b
+    side_a = grid.size["a"]
+    piece = part // side_a
     halo = HaloExchange(grid, n_chunk, slots, side)
+    steps = [(dim, 1 << i) for dim in ("c", "x", "b", "a") for i in range((grid.size[dim] - 1).bit_length())]
     total = halo.count + blocks + pairs * side_x * (side_x - 1 + side_b - 1)
+    total += pairs * (2 * (side_a - 1) + side_a * (side_b - 1)) + len(steps)
     last = n_chunk * slots - 1
+    small_rows = small.shape[0]
+    small_shape = (up_to(50 + small_rows, 8), n_chunk * LANES)
 
     def kernel(
-        r_ref, g_ref, n_ref, x_ref, m_ref, d_ref, h_ref, halo_ref, o_ref, tap_ref,
-        arrived, picked, local, here, core, far, across, pad, sums, send, recv, load_sems,
+        r_ref, g_ref, n_ref, x_ref, m_ref, d_ref, h_ref, s_ref, halo_ref, o_ref, t_ref,
+        arrived, picked, local, here, core, far, across, pad, sums, got, mine, heard, send, recv, load_sems,
     ):
         own = grid.own()
         own_x, own_b, own_c = own["x"], own["b"], own["c"]
@@ -462,6 +475,26 @@
                     for j in range(1, side_b)
                 ]
 
+        own_a = own["a"]
+        row_of = lambda a, b: pl.ds(pl.multiple_of((b * side_a + a) * piece, 16), piece)
+        to_a, back_a, back_b, keeps = {}, {}, {}, []
+        for m in range(pairs):
+            at = index(0, m)
+            done = here.at[at, row_of(own_a, own_b)]
+            place = o_ref.at[m, row_of(own_a, own_b)]
+            keeps.append(pltpu.make_async_copy(done, place, load_sems.at[m]))
+            for k in range(1, side_a):
+                to = grid.beside(own, "a", k)
+                to_a[k, m] = copies.make(here.at[at, row_of(own_a ^ k, own_b)], got.at[m, k - 1], to)
+                back_a[k, m] = copies.make(done, place, to)
+            for k in range(side_a):
+                for j in range(1, side_b):
+                    came = o_ref.at[m, row_of(own_a ^ k, own_b)]
+                    back_b[k, j, m] = copies.make(done if k == 0 else came, came, grid.beside(own, "b", j))
+        small_copies = [
+            copies.make(mine, heard.at[i], grid.beside(own, dim, k)) for i, (dim, k) in enumerate(steps)
+        ]
+
         def start(found):
             for copy in found:
                 copy.start()
@@ -474,10 +507,11 @@
         def _():
             meet(grid.partners(("tile", "x", "c")))
             halo.send_rims()
+            mine[...] = jnp.zeros_like(mine)
             start(cores)
             start(loads)
 
-        add_taps(x_ref, m_ref, d_ref, h_ref, tap_ref, pad, sums, slots, side)
+        add_taps(x_ref, m_ref, d_ref, h_ref, mine, pad, sums, slots, side)
 
         for i, (k, m) in enumerate(order):
 
@@ -508,7 +542,6 @@
                     wait(to_x[k, m] for k in others)
                     add_rows(here.at[index(0, m)], [far.at[k - 1, m] for k in others], rows)
                     start(to_b[0, m])
-            outs = []
             for m in range(pairs):
                 at = index(0, m)
                 if m % 2 == 1:
@@ -518,11 +551,30 @@
                     wait(to_b[0, m])
                     sources = [across.at[j, at] for j in range(side_b - 1)]
                 add_rows(here.at[at, rows_of(own_b)], sources, part)
-                outs.append(pltpu.make_async_copy(here.at[at, rows_of(own_b)], o_ref.at[m], load_sems.at[m]))
-                outs[-1].start()
+                start(to_a[k, m] for k in range(1, side_a))
+            mine[pl.ds(50, small_rows), pl.ds(0, channels)] = s_ref[...]
+            for i, copy in enumerate(small_copies):
+                copy.start()
+                copy.wait()
+                mine[...] = mine[...] + heard[i]
+            for m in range(pairs):
+                wait(to_a[k, m] for k in range(1, side_a))
+                done = here.at[index(0, m), row_of(own_a, own_b)]
+                add_rows(done, [got.at[m, k] for k in range(side_a - 1)], piece)
+                keeps[m].start()
+                start(back_a[k, m] for k in range(1, side_a))
+                start(back_b[0, j, m] for j in range(1, side_b))
+            for k in range(1, side_a):
+                for m in range(pairs):
+                    back_a[k, m].wait_recv()
+                    start(back_b[k, j, m] for j in range(1, side_b))
             halo.finish()
-            for out in outs:
-                out.wait()
+            t_ref[...] = mine[...]
+            for m in range(pairs):
+                keeps[m].wait()
+                for k in range(1, side_a):
+                    back_a[k, m].wait_send()
+            wait(back_b.values())
 
     any_space = pl.BlockSpec(memory_space=pl.ANY)
     cells = side * side
@@ -537,12 +589,13 @@
             pl.BlockSpec((1, cells, LANES), lambda c, s: (s, 0, 0)),
             pl.BlockSpec((1, cells, LANES), lambda c, s: (s, 0, c)),
             halo_block(halos),
-        ],
-        out_specs=[any_space, any_space, pl.BlockSpec((50, LANES), lambda c, s: (0, c))],
+            pl.BlockSpec(small.shape, lambda c, s: (0, 0)),
+        ],
+        out_specs=[any_space, any_space, pl.BlockSpec(small_shape, lambda c, s: (0, 0))],
         out_shape=[
             halo.halo_shape(),
-            jax.ShapeDtypeStruct((pairs, part, cols), BF),
-            jax.ShapeDtypeStruct((50, channels), F32),
+            jax.ShapeDtypeStruct((pairs, rows, cols), BF),
+            jax.ShapeDtypeStruct(small_shape, F32),
         ],
         scratch_shapes=halo.scratch()
         + [
@@ -552,97 +605,16 @@
             pltpu.VMEM((side_b - 1, blocks, part, cols), BF),
             pltpu.VMEM(((side + 2 * RIM) * PITCH, LANES), F32),
             pltpu.VMEM((50, 8, LANES), F32),
+            pltpu.VMEM((pairs, side_a - 1, piece, cols), BF),
+            pltpu.VMEM(small_shape, F32),
+            pltpu.VMEM((len(steps),) + small_shape, F32),
             pltpu.SemaphoreType.DMA((total,)),
             pltpu.SemaphoreType.DMA((total,)),
             pltpu.SemaphoreType.DMA((blocks,)),
         ],
         compiler_params=remote_params(2, 60),
         name="exchange_backward",
-    )(rims, grads, neighbours, inputs, mask_lanes, d_conv, halos)
-
-
-def finish_gradients(grid, partial, small):
-    pairs, part, cols = partial.shape
-    side_a, side_b = grid.size["a"], grid.size["b"]
-    piece = part // side_a
-    steps = [(dim, 1 << i) for dim in ("c", "x", "b", "a") for i in range((grid.size[dim] - 1).bit_length())]
-    total = pairs * 2 * (side_a - 1) + pairs * side_a * (side_b - 1) + len(steps)
-
-    def kernel(p_ref, s_ref, o_ref, t_ref, mine, got, sums, send, recv, load_sems):
-        own = grid.own()
-        meet(grid.partners(("a", "b", "x", "c")))
-        copies = Copies(send, recv)
-        rows_of = lambda a: pl.ds(pl.multiple_of(a * piece, 16), piece)
-        place = lambda a, b: pl.ds(pl.multiple_of((b * side_a + a) * piece, 16), piece)
-        firsts, loads = [], []
-        for m in range(pairs):
-            firsts.append(
-                [
-                    copies.start(p_ref.at[m, rows_of(own["a"] ^ k)], got.at[m, k - 1], grid.beside(own, "a", k))
-                    for k in range(1, side_a)
-                ]
-            )
-            load = pltpu.make_async_copy(p_ref.at[m, rows_of(own["a"])], mine.at[m], load_sems.at[m])
-            load.start()
-            loads.append(load)
-        t_ref[...] = s_ref[...]
-        small_copies = []
-
-        def small_step(i):
-            dim, k = steps[i]
-            copy = copies.start(t_ref, sums.at[i], grid.beside(own, dim, k))
-            copy.wait()
-            t_ref[...] = t_ref[...] + sums[i]
-
-        for i in range(len(steps)):
-            small_step(i)
-        seconds, thirds, keeps = [], [], []
-        for m in range(pairs):
-            loads[m].wait()
-            for copy in firsts[m]:
-                copy.wait()
-            add_rows(mine.at[m], [got.at[m, k] for k in range(side_a - 1)], piece)
-            keep = pltpu.make_async_copy(mine.at[m], o_ref.at[m, place(own["a"], own["b"])], load_sems.at[m])
-            keep.start()
-            keeps.append(keep)
-            to = o_ref.at[m, place(own["a"], own["b"])]
-            seconds.append(
-                [(k, copies.start(mine.at[m], to, grid.beside(own, "a", k))) for k in range(1, side_a)]
-            )
-            thirds += [copies.start(mine.at[m], to, grid.beside(own, "b", j)) for j in range(1, side_b)]
-        for m in range(pairs):
-            for k, copy in seconds[m]:
-                copy.wait_recv()
-                at = o_ref.at[m, place(own["a"] ^ k, own["b"])]
-                thirds += [copies.start(at, at, grid.beside(own, "b", j)) for j in range(1, side_b)]
-        for m in range(pairs):
-            keeps[m].wait()
-            for _, copy in seconds[m]:
-                copy.wait_send()
-        for copy in thirds:
-            copy.wait()
-
-    any_space = pl.BlockSpec(memory_space=pl.ANY)
-    whole = pl.BlockSpec(memory_space=pltpu.VMEM)
-    return pl.pallas_call(
-        kernel,
-        in_specs=[any_space, whole],
-        out_specs=[any_space, whole],
-        out_shape=[
-            jax.ShapeDtypeStruct((pairs, side_b * part, cols), BF),
-            jax.ShapeDtypeStruct(small.shape, F32),
-        ],
-        scratch_shapes=[
-            pltpu.VMEM((pairs, piece, cols), BF),
-            pltpu.VMEM((pairs, side_a - 1, piece, cols), BF),
-            pltpu.VMEM((len(steps),) + small.shape, F32),
-            pltpu.SemaphoreType.DMA((total,)),
-            pltpu.SemaphoreType.DMA((total,)),
-            pltpu.SemaphoreType.DMA((pairs,)),
-        ],
-        compiler_params=remote_params(3, 32),
-        name="finish_gradients",
-    )(partial, small)
+    )(rims, grads, neighbours, inputs, mask_lanes, d_conv, halos, small)
 
 
 def tile_total(grid, value, number):
@@ -796,7 +768,8 @@
 
     @pl.when(slot == slots - 1)
     def _():
-        o_ref[...] = jnp.sum(sums[...], axis=1)
+        at = pl.multiple_of(pl.program_id(0) * LANES, LANES)
+        o_ref[pl.ds(0, 50), pl.ds(at, LANES)] = jnp.sum(sums[...], axis=1)
 
 
 def conv_backward(grid, d_conv, halos, cotangent, mask_lanes, taps, weight_lanes, change):
@@ -1354,15 +1327,13 @@
         jnp.broadcast_to(grad_coefs[:, None, :], (3, 8, channels)),
         side,
     )
-    grad_halos, partial, d_taps = exchange_backward(
-        grid, grad_rims, grads, all_neighbours, inputs, mask_lanes, d_conv, halos
+    small = jnp.concatenate([d_gain[None], d_shift[None], d_out_bias, d_hidden.reshape(4, channels)], 0)
+    grad_halos, owned, d_small = exchange_backward(
+        grid, grad_rims, grads, all_neighbours, inputs, mask_lanes, d_conv, halos, small
     )
 
     correction = 1.0 - jnp.power(F32(decay_rate), step_count[0].astype(F32))
-    d_small = jnp.concatenate(
-        [d_taps, d_gain[None], d_shift[None], d_out_bias, d_hidden.reshape(4, channels)], 0
-    )
-    owned, d_small = finish_gradients(grid, partial, d_small)
+    d_small = d_small[: small_params.shape[0], :channels]
     small_one = decay_rate * small_first + (1.0 - decay_rate) * d_small
     small_two = decay_rate * small_second + (1.0 - decay_rate) * d_small * d_small
     new_small = small_params - small_rate * (small_one / correction) / (

time: 556 us -> 543 us (0.977)
  local copies, waits for them, and re-layouts: 49.8 us -> 37 us
    pallas_call x1 -> x0, Pallas kernels: 91 us -> none  [finish_gradients(): pl.pallas_call(kernel, in_specs=[any_space, whole], out_specs=[any_space,...]
    pallas_call x1, Pallas kernels: 89.1 us -> 174 us  [exchange_backward(): pl.pallas_call(kernel, grid=(n_chunk, slots), in_specs=[any_space, any_sp...]
    unnamed x92 -> x70, local copies, waits for them, and re-layouts: 38.8 us -> 26.1 us
    pallas_call x1, Pallas kernels: 51.2 us -> 59.2 us  [conv_backward(): pl.pallas_call(kernel, grid=(n_chunk, slots), in_specs=[pl.BlockSpec((1,...]
    pallas_call x1, Pallas kernels: 131 us -> 124 us  [exchange_forward(): pl.pallas_call(kernel, grid=(last + 1,), in_specs=[any_space] * 3 + [pl.B...]
    pallas_call x2, Pallas kernels: 13.2 us -> 19.1 us  [tile_total(): pl.pallas_call(kernel, in_specs=[whole], out_specs=whole, out_shape=jax.S...]
where the time goes in v6:
time: 543 us; the launch traced here: 542 us
  Pallas kernels  494 us (91%)
  local copies, waits for them, and re-layouts  37 us (7%)
  other arithmetic  7.37 us (1%)
    pallas_call x1, Pallas kernels, exchange_backward(): pl.pallas_call(kernel, grid=(n_chunk, slots), in_specs=[any_space, any_sp...  174 us
    pallas_call x1, Pallas kernels, exchange_forward(): pl.pallas_call(kernel, grid=(last + 1,), in_specs=[any_space] * 3 + [pl.B...  124 us
    pallas_call x1, Pallas kernels, feed_forward(): pl.pallas_call(kernel, grid_spec=pltpu.PrefetchScalarGridSpec(num_scalar_...  85.1 us
    pallas_call x1, Pallas kernels, conv_backward(): pl.pallas_call(kernel, grid=(n_chunk, slots), in_specs=[pl.BlockSpec((1,...  59.2 us
    unnamed x70, local copies, waits for them, and re-layouts  26.1 us
    pallas_call x2, Pallas kernels, tile_total(): pl.pallas_call(kernel, in_specs=[whole], out_specs=whole, out_shape=jax.S...  19.1 us
    pallas_call x1, Pallas kernels, rotate(): pl.pallas_call(kernel, grid=(pairs,), in_specs=[pl.BlockSpec(memory_space...  12.3 us
    pallas_call x1, Pallas kernels, close_out(): pl.pallas_call(kernel, grid=(rows // step,), in_specs=[line(depth), line(...  11.3 us

profile of v6, /device:TPU:8, one launch (start us, length us, event | category | flops | bytes accessed | tf_op | source)
XLA Modules:
  0.0 542.4 jit_solution(12097536726398414957)
XLA Ops:
  0.7 1.3 dynamic_slice.6
  2.6 1.4 fusion.7
  4.4 1.8 copy-done.1
  7.1 1.0 copy-done.8
  8.1 1.0 broadcast_in_dim.68.f_ref.m_ref
  12.2 1.2 broadcast_in_dim.66.t_ref.w_ref
  15.1 124.3 %exchange_forward.1 = (bf16[7,2,5,72,128]{4,3,2,1,0:T(8,128)(2,1)}, bf16[2,4,896,800]{3,2,1,0:T(8,128)(2,1)}, s32[8,2,8]{2,1,0:T(2,128)}, f32[2,576,800]{2,1,0:T...) custom-call(bf16[7,2,4,72,128]{4,3,2,1,0:T(8,128)(2,1)} %copy-done.8, ...), custom_call_target="tpu_custom_call" | custom-call | tf_op jit(solution)/shard_map/exchange_forward/pallas_call | solution.py:386
  139.4 0.9 reduce_sum.56
  141.0 12.0 %tile_total.2 = f32[3,800]{1,0:T(4,128)S(1)} custom-call(f32[3,800]{1,0:T(4,128)S(1)} %concatenate.9.v_ref), custom_call_target="tpu_custom_call" | custom-call | tf_op jit(solution)/shard_map/tile_total/pallas_call | solution.py:637
  154.9 5.1 arrange_shaped.1
  159.9 1.3 copy-done.12
  161.2 1.2 copy-done.13
  163.8 85.1 %feed_forward.1 = (f32[1152,896]{1,0:T(8,128)}, f32[1152,896]{1,0:T(8,128)}, bf16[2,4,896,800]{3,2,1,0:T(8,128)(2,1)}, f32[8,1,400]{2,1,0:T(1,128)}) custom-call(s32[16]{0:T(128)} %select_reduce_fusion.inv_ref, bf16[1152,896]{1,0:T(8,128)(2,1)} %copy-done.12, bf16[800,1152]{1,0:T(8,128)(2,1)} %copy-done.13, bf16[1152,896]{1,0:T(8,128)(2,1)} %get-tuple-element.40.d_ref, ...), custom_call_target="tpu_custom_call" | custom-call | flops 35389440000 | bytes 41943040 | tf_op jit(solution)/shard_map/feed_forward/pallas_call | solution.py:1045
  249.5 11.3 %close_out.1 = (bf16[1152,800]{1,0:T(8,128)(2,1)}, f32[1152,800]{1,0:T(8,128)}, f32[2,1,800]{2,1,0:T(1,128)}) custom-call(f32[1152,896]{1,0:T(8,128)} %get-tuple-element.43.b_ref, f32[1152,896]{1,0:T(8,128)} %get-tuple-element.44.d_ref, bf16[1152,800]{1,0:T(8,128)(2,1)} %bitcast.46, f32[1152,800]{1,0:T(8,128)} %bitcast.44, ...), custom_call_target="tpu_custom_call" | custom-call | tf_op jit(solution)/shard_map/close_out/pallas_call | solution.py:1103
  263.0 7.1 %tile_total.3 = f32[2,800]{1,0:T(2,128)S(1)} custom-call(f32[2,800]{1,0:T(2,128)S(1)} %pad_maximum_fusion.3.v_ref), custom_call_target="tpu_custom_call" | custom-call | tf_op jit(solution)/shard_map/tile_total/pallas_call | solution.py:637
  270.7 2.2 copy-done
  272.8 2.2 copy-done.9
  275.0 2.5 conv_gradient.1
  277.5 2.0 copy-done.5
  279.5 1.0 copy-done.11
  280.5 174.3 %exchange_backward.1 = (bf16[7,2,5,72,128]{4,3,2,1,0:T(8,128)(2,1)}, bf16[2,896,800]{2,1,0:T(8,128)(2,1)}, f32[64,896]{1,0:T(8,128)}) custom-call(bf16[7,2,4,72,128]{4,3,2,1,0:T(8,128)(2,1)} %copy-done.11, bf16[2,4,896,800]{3,2,1,0:T(8,128)(2,1)} %get-tuple-element.50.g_ref, s32[8,2,8]{2,1,0:T(2,128)} %get-tuple-element.51.n_ref, ...), custom_call_target="tpu_custom_call" | custom-call | tf_op jit(solution)/shard_map/exchange_backward/pallas_call | solution.py:581
  455.7 1.8 copy.44.l_ref
  457.4 1.2 copy.45.one_ref
  458.6 1.2 copy.46.two_ref
  459.8 12.3 %rotate.1 = (f32[4,100,400]{2,1,0:T(8,128)}, f32[4,100,400]{2,1,0:T(8,128)}, bf16[2,896,800]{2,1,0:T(8,128)(2,1)}) custom-call(f32[1]{0:T(128)} %bitcast.20.f_ref, bf16[2,896,800]{2,1,0:T(8,128)(2,1)} %get-tuple-element.56.g_ref, f32[4,800,100]{2,1,0:T(8,128)} %copy.44.l_ref, f32[4,400,400]{2,1,0:T(8,128)} %c_ref.1, f32[4,100,400]{2,1,0:T(8,128)} %copy.45.one_ref, ...), custom_call_target="tpu_custom_call" | custom-call | tf_op jit(solution)/shard_map/rotate/pallas_call | solution.py:1172
  472.2 1.3 copy-done.10
  473.5 59.2 %conv_backward.1 = (f32[2,576,800]{2,1,0:T(8,128)}, f32[2,112,800]{2,1,0:T(8,128)S(1)}) custom-call(f32[2,576,800]{2,1,0:T(8,128)} %copy-done.5, bf16[2,24,24,800]{3,2,1,0:T(8,128)(2,1)S(1)} %bitcast.50, f32[2,576,128]{2,1,0:T(8,128)S(1)} %copy-done.4, f32[50,8,800]{2,1,0:T(8,128)S(1)} %copy-done.6, f32[8,128]{1,0:T(8,128)S(1)} %broadcast_in_dim.77.l_ref, ...), custom_call_target="tpu_custom_call" | custom-call | tf_op jit(solution)/shard_map/conv_backward/pallas_call | solution.py:853
  534.2 1.4 copy.48
  535.6 1.0 copy.49
  536.6 1.4 copy.50
  538.0 1.4 copy.51
  540.4 2.0 copy.57
  (108 shorter events, 14.2 us)
Async XLA Ops:
  0.6 8.5 %copy-start.29 = (s32[4]{0:T(128)S(1)}, s32[4]{0:T(128)}, u32[]{:S(2)}) copy-start(s32[4]{0:T(128)} %param.30) | copy-start | bytes 52
  0.7 11.6 %slice-start = ((f32[57,800]{1,0:T(8,128)}), f32[50,800]{1,0:T(8,128)S(1)}, s32[]{:S(2)}) async-start(f32[57,800]{1,0:T(8,128)} %param.23), calls=%async_computation | async-start | bytes 401408 | tf_op jit(solution)/shard_map/slice | solution.py:1246
  4.3 9.2 %copy-start.2 = (f32[2,576,128]{2,1,0:T(8,128)}, f32[2,576,128]{2,1,0:T(8,128)S(1)}, u32[]{:S(2)}) copy-start(f32[2,576,128]{2,1,0:T(8,128)S(1)} %broadcast_in_dim.65.m_ref) | copy-start | bytes 1769476
  4.3 1.8 copy-start.1
  6.1 7.3 %copy-start.15 = (f32[4,100,400]{2,0,1:T(4,128)S(1)}, f32[4,100,400]{2,0,1:T(4,128)}, u32[]{:S(2)}) copy-start(f32[4,100,400]{2,0,1:T(4,128)} %param.18) | copy-start | bytes 1920004
  7.1 1.0 copy-start.8
  15.1 139.7 %copy-start.18 = (f32[57,800]{1,0:T(8,128)S(1)}, f32[57,800]{1,0:T(8,128)}, u32[]{:S(2)}) copy-start(f32[57,800]{1,0:T(8,128)} %param.23) | copy-start | bytes 547204
  139.4 23.7 %copy-start.30 = (s32[16]{0:T(128)S(1)}, s32[16]{0:T(128)}, u32[]{:S(2)}) copy-start(s32[16]{0:T(128)} %param.29) | copy-start | bytes 196
  159.9 1.3 copy-start.12
  161.2 1.2 copy-start.13
  249.5 12.7 %copy-start.27 = (f32[8,1,400]{2,1,0:T(1,128)S(1)}, f32[8,1,400]{2,1,0:T(1,128)}, u32[]{:S(2)}) copy-start(f32[8,1,400]{2,1,0:T(1,128)} %get-tuple-element.54) | copy-start | bytes 38404
  249.5 12.9 %copy-start.28 = (f32[1,800]{1,0:T(1,128)S(1)}, f32[1,800]{1,0:T(1,128)}, u32[]{:S(2)}) copy-start(f32[1,800]{1,0:T(1,128)} %get-tuple-element.53) | copy-start | bytes 9604
  249.5 21.2 %copy-start.3 = (f32[2,576,128]{2,1,0:T(8,128)S(1)}, f32[2,576,128]{2,1,0:T(8,128)}, u32[]{:S(2)}) copy-start(f32[2,576,128]{2,1,0:T(8,128)} %copy-done.2) | copy-start | bytes 1769476
  270.7 2.2 copy-start
  272.8 2.2 copy-start.9
  277.5 2.0 copy-start.5
  279.5 1.0 copy-start.11
  280.5 175.1 %copy-start.17 = (f32[4,800,100]{1,0,2:T(4,128)S(1)}, f32[4,800,100]{1,0,2:T(4,128)}, u32[]{:S(2)}) copy-start(f32[4,800,100]{1,0,2:T(4,128)} %param.21) | copy-start | bytes 3840004
  454.8 2.7 copy-start.22
  454.8 3.8 copy-start.23
  459.8 12.4 %copy-start.4 = (f32[2,576,128]{2,1,0:T(8,128)S(1)}, f32[2,576,128]{2,1,0:T(8,128)}, u32[]{:S(2)}) copy-start(f32[2,576,128]{2,1,0:T(8,128)} %copy-done.2) | copy-start | bytes 1769476
  459.8 12.4 %copy-start.6 = (f32[50,8,800]{2,1,0:T(8,128)S(1)}, f32[50,8,800]{2,1,0:T(8,128)}, u32[]{:S(2)}) copy-start(f32[50,8,800]{2,1,0:T(8,128)} %broadcast_in_dim.66.t_ref.w_ref) | copy-start | bytes 3840004
  459.8 12.4 %copy-start.7 = (bf16[1,2,24,24,800]{4,3,2,1,0:T(8,128)(2,1)S(1)}, bf16[1,2,24,24,800]{4,3,2,1,0:T(8,128)(2,1)}, u32[]{:S(2)}) copy-start(bf16[1,2,24,24,800]{4,3,2,1,0:T(8,128)(2,1)} %param.17) | copy-start | bytes 5529604
  472.2 1.3 copy-start.10
  532.7 1.1 copy-start.16
  533.0 3.6 copy-start.21
  533.9 4.2 copy-start.20
  534.2 5.3 copy-start.19
  534.2 5.3 copy-start.24
  534.2 5.3 copy-start.25
  534.2 5.2 copy-start.26
  535.6 4.8 copy-start.14

commit v7 on v6

--- a/solution.py
+++ b/solution.py
@@ -439,7 +439,7 @@
     piece = part // side_a
     halo = HaloExchange(grid, n_chunk, slots, side)
     steps = [(dim, 1 << i) for dim in ("c", "x", "b", "a") for i in range((grid.size[dim] - 1).bit_length())]
-    total = halo.count + blocks + pairs * side_x * (side_x - 1 + side_b - 1)
+    total = halo.count + blocks + side_a * pairs * side_x * side_b * 2
     total += pairs * (2 * (side_a - 1) + side_a * (side_b - 1)) + len(steps)
     last = n_chunk * slots - 1
     small_rows = small.shape[0]
@@ -454,29 +454,48 @@
         step = pl.program_id(0) * slots + pl.program_id(1)
         copies = Copies(send, recv)
         halo.plan(copies, r_ref, arrived, picked, halo_ref, local)
-        order = [(k, m) for m in range(0, pairs, 2) for k in range(1, side_x)]
-        order += [(k, m) for m in range(pairs) for k in range(side_x) if (k, m) not in order]
+        order = [(k, m) for m in range(pairs) for k in range(1, side_x)]
+        order += [(0, m) for m in range(pairs - 1, -1, -1)]
         index = lambda k, m: (own_x ^ k) * pairs + m
-        rows_of = lambda b: pl.ds(pl.multiple_of(b * part, 16), part)
-        cores, loads, to_x, to_b = [], [], {}, {}
+        own_a = own["a"]
+        row_of = lambda a, b: pl.ds(pl.multiple_of((b * side_a + a) * piece, 16), piece)
+        part_row = lambda a: pl.ds(pl.multiple_of(a * piece, 16), piece)
+        turns = [*range(1, side_a), 0]
+        cores, loads = [], []
         for i, (k, m) in enumerate(order):
             at = index(k, m)
             cores.append(copies.make(g_ref.at[1 - own_c, at], core.at[at], grid.beside(own, "c", 1)))
             loads.append(pltpu.make_async_copy(g_ref.at[own_c, at], here.at[at], load_sems.at[i]))
-            if k > 0:
-                to = grid.beside(own, "x", k)
+        one, two, one_adds, two_adds = {}, {}, {}, {}
+        for m in range(pairs):
+            for k in turns:
+                a = own_a ^ k
+                mine_at = here.at[index(0, m), row_of(a, own_b)]
+                across_x = lambda q, b: (
+                    copies.make(
+                        here.at[index(q, m), row_of(a, b)], far.at[q - 1, m, row_of(a, b)], grid.beside(own, "x", q)
+                    )
+                )
+                across_b = lambda q, j: (
+                    copies.make(
+                        here.at[index(q, m), row_of(a, own_b ^ j)],
+                        across.at[j - 1, index(q, m), part_row(a)],
+                        grid.beside(own, "b", j),
+                    )
+                )
+                from_x = lambda b: [far.at[q - 1, m, row_of(a, b)] for q in range(1, side_x)]
+                from_b = lambda q: [across.at[j - 1, index(q, m), part_row(a)] for j in range(1, side_b)]
                 if m % 2 == 0:
-                    to_x[k, m] = copies.make(here.at[at], far.at[k - 1, m], to)
+                    one[k, m] = [across_x(q, b) for q in range(1, side_x) for b in range(side_b)]
+                    one_adds[k, m] = [(here.at[index(0, m), row_of(a, b)], from_x(b)) for b in range(side_b)]
+                    two[k, m] = [across_b(0, j) for j in range(1, side_b)]
+                    two_adds[k, m] = [(mine_at, from_b(0))]
                 else:
-                    to_x[k, m] = copies.make(here.at[at, rows_of(own_b)], far.at[k - 1, m, pl.ds(0, part)], to)
-            if m % 2 == 1 or k == 0:
-                to_b[k, m] = [
-                    copies.make(here.at[at, rows_of(own_b ^ j)], across.at[j - 1, at], grid.beside(own, "b", j))
-                    for j in range(1, side_b)
-                ]
-
-        own_a = own["a"]
-        row_of = lambda a, b: pl.ds(pl.multiple_of((b * side_a + a) * piece, 16), piece)
+                    one[k, m] = [across_b(q, j) for q in range(side_x) for j in range(1, side_b)]
+                    one_adds[k, m] = [(here.at[index(q, m), row_of(a, own_b)], from_b(q)) for q in range(side_x)]
+                    two[k, m] = [across_x(q, own_b) for q in range(1, side_x)]
+                    two_adds[k, m] = [(mine_at, from_x(own_b))]
+
         to_a, back_a, back_b, keeps = {}, {}, {}, []
         for m in range(pairs):
             at = index(0, m)
@@ -513,6 +532,9 @@
 
         add_taps(x_ref, m_ref, d_ref, h_ref, mine, pad, sums, slots, side)
 
+        ready = {}
+        for i, (k, m) in enumerate(order):
+            ready[m] = max(ready.get(m, 0), i) if m % 2 == 1 or k > 0 else ready.get(m, 0)
         for i, (k, m) in enumerate(order):
 
             @pl.when(step == min(last, 3 + 2 * i))
@@ -521,42 +543,33 @@
                 cores[i].wait()
                 at = index(k, m)
                 add_rows(here.at[at], [core.at[at]], rows)
-                if m % 2 == 1:
-                    start(to_b[k, m])
-                elif k > 0:
-                    to_x[k, m].start()
+                for n in range(pairs):
+                    if ready[n] == i:
+                        start(one[turns[0], n])
+                        start(one[turns[1], n])
 
         @pl.when(step == last)
         def _():
             halo.pick_and_send(lambda d, k: n_ref[d // slots, d % slots, k])
-            for m in range(pairs):
-                others = range(1, side_x)
-                if m % 2 == 1:
-                    for k in [*others, 0]:
-                        at = index(k, m)
-                        wait(to_b[k, m])
-                        add_rows(here.at[at, rows_of(own_b)], [across.at[j, at] for j in range(side_b - 1)], part)
+            for i in range(side_a + 1):
+                for m in range(pairs):
+                    if i < side_a:
+                        k = turns[i]
+                        wait(one[k, m])
+                        if i + 2 < side_a:
+                            start(one[turns[i + 2], m])
+                        for target, sources in one_adds[k, m]:
+                            add_rows(target, sources, piece)
+                        start(two[k, m])
+                for m in range(pairs):
+                    if i > 0:
+                        k = turns[i - 1]
+                        wait(two[k, m])
+                        for target, sources in two_adds[k, m]:
+                            add_rows(target, sources, piece)
                         if k > 0:
-                            to_x[k, m].start()
-                else:
-                    wait(to_x[k, m] for k in others)
-                    add_rows(here.at[index(0, m)], [far.at[k - 1, m] for k in others], rows)
-                    start(to_b[0, m])
-            for m in range(pairs):
-                at = index(0, m)
-                if m % 2 == 1:
-                    wait(to_x[k, m] for k in range(1, side_x))
-                    sources = [far.at[k - 1, m, pl.ds(0, part)] for k in range(1, side_x)]
-                else:
-                    wait(to_b[0, m])
-                    sources = [across.at[j, at] for j in range(side_b - 1)]
-                add_rows(here.at[at, rows_of(own_b)], sources, part)
-                start(to_a[k, m] for k in range(1, side_a))
+                            to_a[k, m].start()
             mine[pl.ds(50, small_rows), pl.ds(0, channels)] = s_ref[...]
-            for i, copy in enumerate(small_copies):
-                copy.start()
-                copy.wait()
-                mine[...] = mine[...] + heard[i]
             for m in range(pairs):
                 wait(to_a[k, m] for k in range(1, side_a))
                 done = here.at[index(0, m), row_of(own_a, own_b)]
@@ -565,6 +578,12 @@
                 start(back_a[k, m] for k in range(1, side_a))
                 start(back_b[0, j, m] for j in range(1, side_b))
             for k in range(1, side_a):
+                last_turn = k == side_a - 1
+                for copy, i in [(c, i) for i, c in enumerate(small_copies) if last_turn or i // 2 == k - 1]:
+                    if i // 2 >= k - 1:
+                        copy.start()
+                        copy.wait()
+                        mine[...] = mine[...] + heard[i]
                 for m in range(pairs):
                     back_a[k, m].wait_recv()
                     start(back_b[k, j, m] for j in range(1, side_b))
@@ -780,7 +799,7 @@
     side_a, side_b = grid.size["a"], grid.size["b"]
     part = rows // side_b
     piece = part // side_a
-    total = pairs * ((side_b - 1) + (side_a - 1))
+    total = pairs * (side_a * (side_b - 1) + (side_a - 1))
     last = n_chunk * slots - 1
 
     def kernel(
@@ -790,31 +809,36 @@
         own = grid.own()
         step = pl.program_id(0) * slots + pl.program_id(1)
         copies = Copies(send, recv)
+        own_a, own_b = own["a"], own["b"]
         half = lambda b: pl.ds(pl.multiple_of(b * part, 16), part)
-        rows_of = lambda a: pl.ds(pl.multiple_of(a * piece, 16), piece)
-        firsts, seconds, loads = [], [], []
+        row_of = lambda a, b: pl.ds(pl.multiple_of((b * side_a + a) * piece, 16), piece)
+        part_row = lambda a: pl.ds(pl.multiple_of(a * piece, 16), piece)
+        turns = [*range(1, side_a), 0]
+        firsts, seconds, loads = {}, {}, []
         for m in range(pairs):
-            firsts.append(
-                [
-                    copies.make(c_ref.at[m, half(own["b"] ^ k)], from_b.at[k - 1, m], grid.beside(own, "b", k))
-                    for k in range(1, side_b)
+            for k in turns:
+                a = own_a ^ k
+                firsts[k, m] = [
+                    copies.make(
+                        c_ref.at[m, row_of(a, own_b ^ j)], from_b.at[j - 1, m, part_row(a)], grid.beside(own, "b", j)
+                    )
+                    for j in range(1, side_b)
                 ]
-            )
-            seconds.append(
-                [
-                    copies.make(mine.at[m, rows_of(own["a"] ^ k)], from_a.at[k - 1, m], grid.beside(own, "a", k))
-                    for k in range(1, side_a)
-                ]
-            )
-            loads.append(pltpu.make_async_copy(c_ref.at[m, half(own["b"])], mine.at[m], load_sems.at[m]))
+                if k > 0:
+                    seconds[k, m] = copies.make(
+                        mine.at[m, part_row(a)], from_a.at[k - 1, m], grid.beside(own, "a", k)
+                    )
+            loads.append(pltpu.make_async_copy(c_ref.at[m, half(own_b)], mine.at[m], load_sems.at[m]))
 
         @pl.when(step == 0)
         def _():
             meet(grid.partners(("a", "b")))
-            for m in range(pairs):
-                for copy in firsts[m]:
-                    copy.start()
-                loads[m].start()
+            for load in loads:
+                load.start()
+            for k in turns:
+                for m in range(pairs):
+                    for copy in firsts[k, m]:
+                        copy.start()
 
         for i in range(side):
             pad[pl.ds((i + RIM) * PITCH + 8, side), :] = d_ref[0, pl.ds(i * side, side), :]
@@ -829,23 +853,27 @@
 
         conv_pass(pad, side, lambda a, b: w_ref[7 * (6 - a) + 6 - b], emit)
 
-        for m in range(pairs):
-
-            @pl.when(step == min(last, 9 + 4 * m))
+        for i, k in enumerate(turns):
+
+            @pl.when(step == min(last, 5 + 4 * i))
             def _():
-                loads[m].wait()
-                for copy in firsts[m]:
-                    copy.wait()
-                add_rows(mine.at[m], [from_b.at[k, m] for k in range(side_b - 1)], part)
-                for copy in seconds[m]:
-                    copy.start()
+                for m in range(pairs):
+                    if i == 0:
+                        loads[m].wait()
+                    for copy in firsts[k, m]:
+                        copy.wait()
+                    rows_here = part_row(own_a ^ k)
+                    sources = [from_b.at[j, m, rows_here] for j in range(side_b - 1)]
+                    add_rows(mine.at[m, rows_here], sources, piece)
+                    if k > 0:
+                        seconds[k, m].start()
 
         @pl.when(step == last)
         def _():
             for m in range(pairs):
-                for copy in seconds[m]:
-                    copy.wait()
-                value = mine[m, rows_of(own["a"])].astype(F32)
+                for k in range(1, side_a):
+                    seconds[k, m].wait()
+                value = mine[m, part_row(own_a)].astype(F32)
                 for k in range(side_a - 1):
                     value = value + from_a[k, m].astype(F32)
                 change_ref[m] = value

time: 543 us -> 539 us (level)
  no operation moved by 1% of the time
where the time goes in v7:
time: 539 us; the launch traced here: 538 us
  Pallas kernels  490 us (91%)
  local copies, waits for them, and re-layouts  37 us (7%)
  other arithmetic  7.37 us (1%)
    pallas_call x1, Pallas kernels, exchange_backward(): pl.pallas_call(kernel, grid=(n_chunk, slots), in_specs=[any_space, any_sp...  173 us
    pallas_call x1, Pallas kernels, exchange_forward(): pl.pallas_call(kernel, grid=(last + 1,), in_specs=[any_space] * 3 + [pl.B...  124 us
    pallas_call x1, Pallas kernels, feed_forward(): pl.pallas_call(kernel, grid_spec=pltpu.PrefetchScalarGridSpec(num_scalar_...  85.1 us
    pallas_call x1, Pallas kernels, conv_backward(): pl.pallas_call(kernel, grid=(n_chunk, slots), in_specs=[pl.BlockSpec((1,...  55.9 us
    unnamed x70, local copies, waits for them, and re-layouts  26.1 us
    pallas_call x2, Pallas kernels, tile_total(): pl.pallas_call(kernel, in_specs=[whole], out_specs=whole, out_shape=jax.S...  19.1 us
    pallas_call x1, Pallas kernels, rotate(): pl.pallas_call(kernel, grid=(pairs,), in_specs=[pl.BlockSpec(memory_space...  12.3 us
    pallas_call x1, Pallas kernels, close_out(): pl.pallas_call(kernel, grid=(rows // step,), in_specs=[line(depth), line(...  11.3 us

profile of v7, /device:TPU:8, one launch (start us, length us, event | category | flops | bytes accessed | tf_op | source)
XLA Modules:
  0.0 538.2 jit_solution(7182334430898624245)
XLA Ops:
  0.7 1.3 dynamic_slice.6
  2.6 1.4 fusion.7
  4.4 1.8 copy-done.1
  7.1 1.0 copy-done.8
  8.1 1.0 broadcast_in_dim.68.f_ref.m_ref
  12.2 1.2 broadcast_in_dim.66.t_ref.w_ref
  15.1 124.3 %exchange_forward.1 = (bf16[7,2,5,72,128]{4,3,2,1,0:T(8,128)(2,1)}, bf16[2,4,896,800]{3,2,1,0:T(8,128)(2,1)}, s32[8,2,8]{2,1,0:T(2,128)}, f32[2,576,800]{2,1,0:T...) custom-call(bf16[7,2,4,72,128]{4,3,2,1,0:T(8,128)(2,1)} %copy-done.8, ...), custom_call_target="tpu_custom_call" | custom-call | tf_op jit(solution)/shard_map/exchange_forward/pallas_call | solution.py:386
  139.4 0.9 reduce_sum.56
  141.0 12.0 %tile_total.2 = f32[3,800]{1,0:T(4,128)S(1)} custom-call(f32[3,800]{1,0:T(4,128)S(1)} %concatenate.9.v_ref), custom_call_target="tpu_custom_call" | custom-call | tf_op jit(solution)/shard_map/tile_total/pallas_call | solution.py:656
  154.9 5.1 arrange_shaped.1
  159.9 1.3 copy-done.12
  161.2 1.2 copy-done.13
  163.8 85.1 %feed_forward.1 = (f32[1152,896]{1,0:T(8,128)}, f32[1152,896]{1,0:T(8,128)}, bf16[2,4,896,800]{3,2,1,0:T(8,128)(2,1)}, f32[8,1,400]{2,1,0:T(1,128)}) custom-call(s32[16]{0:T(128)} %select_reduce_fusion.inv_ref, bf16[1152,896]{1,0:T(8,128)(2,1)} %copy-done.12, bf16[800,1152]{1,0:T(8,128)(2,1)} %copy-done.13, bf16[1152,896]{1,0:T(8,128)(2,1)} %get-tuple-element.40.d_ref, ...), custom_call_target="tpu_custom_call" | custom-call | flops 35389440000 | bytes 41943040 | tf_op jit(solution)/shard_map/feed_forward/pallas_call | solution.py:1073
  249.5 11.3 %close_out.1 = (bf16[1152,800]{1,0:T(8,128)(2,1)}, f32[1152,800]{1,0:T(8,128)}, f32[2,1,800]{2,1,0:T(1,128)}) custom-call(f32[1152,896]{1,0:T(8,128)} %get-tuple-element.43.b_ref, f32[1152,896]{1,0:T(8,128)} %get-tuple-element.44.d_ref, bf16[1152,800]{1,0:T(8,128)(2,1)} %bitcast.46, f32[1152,800]{1,0:T(8,128)} %bitcast.44, ...), custom_call_target="tpu_custom_call" | custom-call | tf_op jit(solution)/shard_map/close_out/pallas_call | solution.py:1131
  263.0 7.1 %tile_total.3 = f32[2,800]{1,0:T(2,128)S(1)} custom-call(f32[2,800]{1,0:T(2,128)S(1)} %pad_maximum_fusion.3.v_ref), custom_call_target="tpu_custom_call" | custom-call | tf_op jit(solution)/shard_map/tile_total/pallas_call | solution.py:656
  270.7 2.2 copy-done
  272.9 2.2 copy-done.9
  275.0 2.5 conv_gradient.1
  277.5 2.0 copy-done.5
  279.5 1.0 copy-done.11
  280.5 173.4 %exchange_backward.1 = (bf16[7,2,5,72,128]{4,3,2,1,0:T(8,128)(2,1)}, bf16[2,896,800]{2,1,0:T(8,128)(2,1)}, f32[64,896]{1,0:T(8,128)}) custom-call(bf16[7,2,4,72,128]{4,3,2,1,0:T(8,128)(2,1)} %copy-done.11, bf16[2,4,896,800]{3,2,1,0:T(8,128)(2,1)} %get-tuple-element.50.g_ref, s32[8,2,8]{2,1,0:T(2,128)} %get-tuple-element.51.n_ref, ...), custom_call_target="tpu_custom_call" | custom-call | tf_op jit(solution)/shard_map/exchange_backward/pallas_call | solution.py:600
  454.8 1.8 copy.44.l_ref
  456.6 1.2 copy.45.one_ref
  457.8 1.2 copy.46.two_ref
  459.0 12.3 %rotate.1 = (f32[4,100,400]{2,1,0:T(8,128)}, f32[4,100,400]{2,1,0:T(8,128)}, bf16[2,896,800]{2,1,0:T(8,128)(2,1)}) custom-call(f32[1]{0:T(128)} %bitcast.20.f_ref, bf16[2,896,800]{2,1,0:T(8,128)(2,1)} %get-tuple-element.56.g_ref, f32[4,800,100]{2,1,0:T(8,128)} %copy.44.l_ref, f32[4,400,400]{2,1,0:T(8,128)} %c_ref.1, f32[4,100,400]{2,1,0:T(8,128)} %copy.45.one_ref, ...), custom_call_target="tpu_custom_call" | custom-call | tf_op jit(solution)/shard_map/rotate/pallas_call | solution.py:1200
  471.4 1.3 copy-done.10
  472.7 55.9 %conv_backward.1 = (f32[2,576,800]{2,1,0:T(8,128)}, f32[2,112,800]{2,1,0:T(8,128)S(1)}) custom-call(f32[2,576,800]{2,1,0:T(8,128)} %copy-done.5, bf16[2,24,24,800]{3,2,1,0:T(8,128)(2,1)S(1)} %bitcast.50, f32[2,576,128]{2,1,0:T(8,128)S(1)} %copy-done.4, f32[50,8,800]{2,1,0:T(8,128)S(1)} %copy-done.6, f32[8,128]{1,0:T(8,128)S(1)} %broadcast_in_dim.77.l_ref, ...), custom_call_target="tpu_custom_call" | custom-call | tf_op jit(solution)/shard_map/conv_backward/pallas_call | solution.py:881
  530.1 1.4 copy.48
  531.5 1.0 copy.49
  532.4 1.4 copy.50
  533.9 1.4 copy.51
  536.2 2.0 copy.57
  (108 shorter events, 14.2 us)
Async XLA Ops:
  0.6 8.5 %copy-start.29 = (s32[4]{0:T(128)S(1)}, s32[4]{0:T(128)}, u32[]{:S(2)}) copy-start(s32[4]{0:T(128)} %param.30) | copy-start | bytes 52
  0.7 11.6 %slice-start = ((f32[57,800]{1,0:T(8,128)}), f32[50,800]{1,0:T(8,128)S(1)}, s32[]{:S(2)}) async-start(f32[57,800]{1,0:T(8,128)} %param.23), calls=%async_computation | async-start | bytes 401408 | tf_op jit(solution)/shard_map/slice | solution.py:1274
  4.3 9.2 %copy-start.2 = (f32[2,576,128]{2,1,0:T(8,128)}, f32[2,576,128]{2,1,0:T(8,128)S(1)}, u32[]{:S(2)}) copy-start(f32[2,576,128]{2,1,0:T(8,128)S(1)} %broadcast_in_dim.65.m_ref) | copy-start | bytes 1769476
  4.3 1.8 copy-start.1
  6.1 7.3 %copy-start.15 = (f32[4,100,400]{2,0,1:T(4,128)S(1)}, f32[4,100,400]{2,0,1:T(4,128)}, u32[]{:S(2)}) copy-start(f32[4,100,400]{2,0,1:T(4,128)} %param.18) | copy-start | bytes 1920004
  7.1 1.0 copy-start.8
  15.1 139.7 %copy-start.18 = (f32[57,800]{1,0:T(8,128)S(1)}, f32[57,800]{1,0:T(8,128)}, u32[]{:S(2)}) copy-start(f32[57,800]{1,0:T(8,128)} %param.23) | copy-start | bytes 547204
  139.4 23.7 %copy-start.30 = (s32[16]{0:T(128)S(1)}, s32[16]{0:T(128)}, u32[]{:S(2)}) copy-start(s32[16]{0:T(128)} %param.29) | copy-start | bytes 196
  159.9 1.3 copy-start.12
  161.2 1.2 copy-start.13
  249.5 12.7 %copy-start.27 = (f32[8,1,400]{2,1,0:T(1,128)S(1)}, f32[8,1,400]{2,1,0:T(1,128)}, u32[]{:S(2)}) copy-start(f32[8,1,400]{2,1,0:T(1,128)} %get-tuple-element.54) | copy-start | bytes 38404
  249.5 12.9 %copy-start.28 = (f32[1,800]{1,0:T(1,128)S(1)}, f32[1,800]{1,0:T(1,128)}, u32[]{:S(2)}) copy-start(f32[1,800]{1,0:T(1,128)} %get-tuple-element.53) | copy-start | bytes 9604
  249.5 21.2 %copy-start.3 = (f32[2,576,128]{2,1,0:T(8,128)S(1)}, f32[2,576,128]{2,1,0:T(8,128)}, u32[]{:S(2)}) copy-start(f32[2,576,128]{2,1,0:T(8,128)} %copy-done.2) | copy-start | bytes 1769476
  270.7 2.2 copy-start
  272.9 2.2 copy-start.9
  277.5 2.0 copy-start.5
  279.5 1.0 copy-start.11
  280.5 174.3 %copy-start.17 = (f32[4,800,100]{1,0,2:T(4,128)S(1)}, f32[4,800,100]{1,0,2:T(4,128)}, u32[]{:S(2)}) copy-start(f32[4,800,100]{1,0,2:T(4,128)} %param.21) | copy-start | bytes 3840004
  453.9 2.7 copy-start.22
  453.9 3.8 copy-start.23
  459.0 12.4 %copy-start.4 = (f32[2,576,128]{2,1,0:T(8,128)S(1)}, f32[2,576,128]{2,1,0:T(8,128)}, u32[]{:S(2)}) copy-start(f32[2,576,128]{2,1,0:T(8,128)} %copy-done.2) | copy-start | bytes 1769476
  459.0 12.4 %copy-start.6 = (f32[50,8,800]{2,1,0:T(8,128)S(1)}, f32[50,8,800]{2,1,0:T(8,128)}, u32[]{:S(2)}) copy-start(f32[50,8,800]{2,1,0:T(8,128)} %broadcast_in_dim.66.t_ref.w_ref) | copy-start | bytes 3840004
  459.0 12.4 %copy-start.7 = (bf16[1,2,24,24,800]{4,3,2,1,0:T(8,128)(2,1)S(1)}, bf16[1,2,24,24,800]{4,3,2,1,0:T(8,128)(2,1)}, u32[]{:S(2)}) copy-start(bf16[1,2,24,24,800]{4,3,2,1,0:T(8,128)(2,1)} %param.17) | copy-start | bytes 5529604
  471.3 1.3 copy-start.10
  528.5 1.1 copy-start.16
  528.9 3.6 copy-start.21
  529.7 4.2 copy-start.20
  530.0 5.3 copy-start.19
  530.0 5.3 copy-start.24
  530.0 5.3 copy-start.25
  530.0 5.2 copy-start.26
  531.5 4.8 copy-start.14

commit v8 on v7

--- a/solution.py
+++ b/solution.py
@@ -25,9 +25,9 @@
 
 class Grid:
     def __init__(self, n_tile, n_opt):
-        b = 4 if n_tile % 16 == 0 else 2
+        b = n_tile // 4
         self.n_tile, self.n_opt = n_tile, n_opt
-        self.size = {"a": n_tile // b, "b": b, "x": n_opt // 2, "c": 2}
+        self.size = {"a": 4, "b": b, "x": n_opt // 2, "c": 2}
 
     def own(self):
         t, o = lax.axis_index("tile"), lax.axis_index("opt")
@@ -438,16 +438,15 @@
     side_a = grid.size["a"]
     piece = part // side_a
     halo = HaloExchange(grid, n_chunk, slots, side)
-    steps = [(dim, 1 << i) for dim in ("c", "x", "b", "a") for i in range((grid.size[dim] - 1).bit_length())]
     total = halo.count + blocks + side_a * pairs * side_x * side_b * 2
-    total += pairs * (2 * (side_a - 1) + side_a * (side_b - 1)) + len(steps)
+    total += pairs * (side_a - 1 + 5 + side_a * (side_b - 1))
     last = n_chunk * slots - 1
     small_rows = small.shape[0]
     small_shape = (up_to(50 + small_rows, 8), n_chunk * LANES)
 
     def kernel(
         r_ref, g_ref, n_ref, x_ref, m_ref, d_ref, h_ref, s_ref, halo_ref, o_ref, t_ref,
-        arrived, picked, local, here, core, far, across, pad, sums, got, mine, heard, send, recv, load_sems,
+        arrived, picked, local, here, core, far, across, pad, sums, got, mine, send, recv, load_sems,
     ):
         own = grid.own()
         own_x, own_b, own_c = own["x"], own["b"], own["c"]
@@ -505,14 +504,18 @@
             for k in range(1, side_a):
                 to = grid.beside(own, "a", k)
                 to_a[k, m] = copies.make(here.at[at, row_of(own_a ^ k, own_b)], got.at[m, k - 1], to)
-                back_a[k, m] = copies.make(done, place, to)
+            got_at = lambda k: o_ref.at[m, row_of(own_a ^ k, own_b)]
+            beside_a = lambda k: grid.beside(own, "a", k)
+            back_a["near", m] = copies.make(done, place, beside_a(1))
+            back_a["over", m] = copies.make(done, place, beside_a(3))
+            back_a["over2", m] = copies.make(got_at(1), got_at(1), beside_a(3))
+            back_a["out", m] = copies.make(got_at(3), got_at(3), beside_a(1))
+            back_a["out2", m] = copies.make(got_at(2), got_at(2), beside_a(1))
             for k in range(side_a):
                 for j in range(1, side_b):
                     came = o_ref.at[m, row_of(own_a ^ k, own_b)]
                     back_b[k, j, m] = copies.make(done if k == 0 else came, came, grid.beside(own, "b", j))
-        small_copies = [
-            copies.make(mine, heard.at[i], grid.beside(own, dim, k)) for i, (dim, k) in enumerate(steps)
-        ]
+        middle = (own_a == 1) | (own_a == 2)
 
         def start(found):
             for copy in found:
@@ -575,24 +578,51 @@
                 done = here.at[index(0, m), row_of(own_a, own_b)]
                 add_rows(done, [got.at[m, k] for k in range(side_a - 1)], piece)
                 keeps[m].start()
-                start(back_a[k, m] for k in range(1, side_a))
+                back_a["near", m].start()
+
+                @pl.when(middle)
+                def _():
+                    back_a["over", m].start()
+
                 start(back_b[0, j, m] for j in range(1, side_b))
-            for k in range(1, side_a):
-                last_turn = k == side_a - 1
-                for copy, i in [(c, i) for i, c in enumerate(small_copies) if last_turn or i // 2 == k - 1]:
-                    if i // 2 >= k - 1:
-                        copy.start()
-                        copy.wait()
-                        mine[...] = mine[...] + heard[i]
+
+            def arrive(came, k, onward):
                 for m in range(pairs):
-                    back_a[k, m].wait_recv()
+                    back_a[came, m].wait_recv()
+                    if onward is not None:
+                        back_a[onward, m].start()
                     start(back_b[k, j, m] for j in range(1, side_b))
+
+            for m in range(pairs):
+                back_a["near", m].wait_recv()
+
+                @pl.when(middle)
+                def _():
+                    back_a["over2", m].start()
+
+                start(back_b[1, j, m] for j in range(1, side_b))
+
+            @pl.when(middle)
+            def _():
+                arrive("over", 3, "out")
+                arrive("over2", 2, "out2")
+
+            @pl.when(~middle)
+            def _():
+                arrive("out", 2, None)
+                arrive("out2", 3, None)
+
             halo.finish()
             t_ref[...] = mine[...]
             for m in range(pairs):
                 keeps[m].wait()
-                for k in range(1, side_a):
-                    back_a[k, m].wait_send()
+                back_a["near", m].wait_send()
+
+                @pl.when(middle)
+                def _():
+                    for name in ("over", "over2", "out", "out2"):
+                        back_a[name, m].wait_send()
+
             wait(back_b.values())
 
     any_space = pl.BlockSpec(memory_space=pl.ANY)
@@ -626,7 +656,6 @@
             pltpu.VMEM((50, 8, LANES), F32),
             pltpu.VMEM((pairs, side_a - 1, piece, cols), BF),
             pltpu.VMEM(small_shape, F32),
-            pltpu.VMEM((len(steps),) + small_shape, F32),
             pltpu.SemaphoreType.DMA((total,)),
             pltpu.SemaphoreType.DMA((total,)),
             pltpu.SemaphoreType.DMA((blocks,)),
@@ -791,7 +820,7 @@
         o_ref[pl.ds(0, 50), pl.ds(at, LANES)] = jnp.sum(sums[...], axis=1)
 
 
-def conv_backward(grid, d_conv, halos, cotangent, mask_lanes, taps, weight_lanes, change):
+def conv_backward(grid, d_conv, halos, cotangent, mask_lanes, taps, weight_lanes, change, small):
     slots, side, _, channels = cotangent.shape
     n_chunk = halos.shape[0]
     cells = side * side
@@ -799,12 +828,13 @@
     side_a, side_b = grid.size["a"], grid.size["b"]
     part = rows // side_b
     piece = part // side_a
-    total = pairs * (side_a * (side_b - 1) + (side_a - 1))
+    hops = [(dim, 1 << i) for dim in ("c", "x", "b", "a") for i in range((grid.size[dim] - 1).bit_length())]
+    total = pairs * (side_a * (side_b - 1) + (side_a - 1)) + len(hops)
     last = n_chunk * slots - 1
 
     def kernel(
-        d_ref, g_ref, m_ref, w_ref, l_ref, h_ref, c_ref, o_ref, change_ref,
-        pad, mine, from_b, from_a, send, recv, load_sems,
+        d_ref, g_ref, m_ref, w_ref, l_ref, h_ref, c_ref, s_ref, o_ref, change_ref, small_ref,
+        pad, mine, from_b, from_a, heard, send, recv, load_sems,
     ):
         own = grid.own()
         step = pl.program_id(0) * slots + pl.program_id(1)
@@ -830,15 +860,23 @@
                     )
             loads.append(pltpu.make_async_copy(c_ref.at[m, half(own_b)], mine.at[m], load_sems.at[m]))
 
+        hop_copies = [
+            copies.make(small_ref, heard.at[i], grid.beside(own, dim, k)) for i, (dim, k) in enumerate(hops)
+        ]
+
+        def start_turn(i):
+            for m in range(pairs):
+                for copy in firsts[turns[i], m]:
+                    copy.start()
+
         @pl.when(step == 0)
         def _():
-            meet(grid.partners(("a", "b")))
+            meet(grid.partners(("a", "b", "x", "c")))
             for load in loads:
                 load.start()
-            for k in turns:
-                for m in range(pairs):
-                    for copy in firsts[k, m]:
-                        copy.start()
+            start_turn(0)
+            small_ref[...] = s_ref[...]
+            hop_copies[0].start()
 
         for i in range(side):
             pad[pl.ds((i + RIM) * PITCH + 8, side), :] = d_ref[0, pl.ds(i * side, side), :]
@@ -855,18 +893,30 @@
 
         for i, k in enumerate(turns):
 
-            @pl.when(step == min(last, 5 + 4 * i))
+            @pl.when(step == min(last, 7 + 6 * i))
             def _():
                 for m in range(pairs):
                     if i == 0:
                         loads[m].wait()
                     for copy in firsts[k, m]:
                         copy.wait()
+                if i + 1 < side_a:
+                    start_turn(i + 1)
+                for m in range(pairs):
                     rows_here = part_row(own_a ^ k)
                     sources = [from_b.at[j, m, rows_here] for j in range(side_b - 1)]
                     add_rows(mine.at[m, rows_here], sources, piece)
                     if k > 0:
                         seconds[k, m].start()
+
+        for i, copy in enumerate(hop_copies):
+
+            @pl.when(step == min(last, 2 + 3 * i))
+            def _():
+                copy.wait()
+                small_ref[...] = small_ref[...] + heard[i]
+                if i + 1 < len(hops):
+                    hop_copies[i + 1].start()
 
         @pl.when(step == last)
         def _():
@@ -889,16 +939,19 @@
             pl.BlockSpec((8, LANES), lambda c, s: (0, 0)),
             halo_block(halos),
             pl.BlockSpec(memory_space=pl.ANY),
+            pl.BlockSpec(small.shape, lambda c, s: (0, 0)),
         ],
         out_specs=[
             pl.BlockSpec((1, cells, LANES), lambda c, s: (s, 0, c)),
             pl.BlockSpec((pairs, piece, cols), lambda c, s: (0, 0, 0)),
+            pl.BlockSpec(small.shape, lambda c, s: (0, 0)),
         ],
         scratch_shapes=[
             pltpu.VMEM(((side + 2 * RIM) * PITCH, LANES), F32),
             pltpu.VMEM((pairs, part, cols), BF),
             pltpu.VMEM((side_b - 1, pairs, part, cols), BF),
             pltpu.VMEM((side_a - 1, pairs, piece, cols), BF),
+            pltpu.VMEM((len(hops),) + small.shape, F32),
             pltpu.SemaphoreType.DMA((total,)),
             pltpu.SemaphoreType.DMA((total,)),
             pltpu.SemaphoreType.DMA((pairs,)),
@@ -906,10 +959,11 @@
         out_shape=[
             jax.ShapeDtypeStruct((slots, cells, channels), F32),
             jax.ShapeDtypeStruct((pairs, piece, cols), F32),
+            jax.ShapeDtypeStruct(small.shape, F32),
         ],
         compiler_params=remote_params(4, 48),
         name="conv_backward",
-    )(d_conv, cotangent, mask_lanes, taps, weight_lanes, halos, change)
+    )(d_conv, cotangent, mask_lanes, taps, weight_lanes, halos, change, small)
 
 
 def spread_lanes(value, parts, width):
@@ -1361,20 +1415,20 @@
     )
 
     correction = 1.0 - jnp.power(F32(decay_rate), step_count[0].astype(F32))
+
+    first_new, second_new, change = rotate(
+        owned, left_basis, column_basis, moment_one, moment_two, correction, grid, width
+    )
+    input_grad, change, d_small = conv_backward(
+        grid, d_conv, grad_halos, cotangent, mask_lanes, taps, weight_lanes, change, d_small
+    )
+    change = unpack_pairs(change[:, :run])
     d_small = d_small[: small_params.shape[0], :channels]
     small_one = decay_rate * small_first + (1.0 - decay_rate) * d_small
     small_two = decay_rate * small_second + (1.0 - decay_rate) * d_small * d_small
     new_small = small_params - small_rate * (small_one / correction) / (
         jnp.sqrt(small_two / correction) + adam_eps
     )
-
-    first_new, second_new, change = rotate(
-        owned, left_basis, column_basis, moment_one, moment_two, correction, grid, width
-    )
-    input_grad, change = conv_backward(
-        grid, d_conv, grad_halos, cotangent, mask_lanes, taps, weight_lanes, change
-    )
-    change = unpack_pairs(change[:, :run])
     new_master = master - 0.5 / math.sqrt(channels) * change
     return (
         block_output.reshape((1,) + inputs.shape),

time: 539 us -> 524 us (0.972)
  Pallas kernels: 490 us -> 473 us
    pallas_call x1, Pallas kernels: 173 us -> 139 us  [exchange_backward(): pl.pallas_call(kernel, grid=(n_chunk, slots), in_specs=[any_space, any_sp...]
    pallas_call x1, Pallas kernels: 55.9 us -> 73.4 us  [conv_backward(): pl.pallas_call(kernel, grid=(n_chunk, slots), in_specs=[pl.BlockSpec((1,...]
    unnamed x70 -> x66, local copies, waits for them, and re-layouts: 26.1 us -> 24.8 us
where the time goes in v8:
time: 524 us; the launch traced here: 520 us
  Pallas kernels  473 us (90%)
  local copies, waits for them, and re-layouts  35.7 us (7%)
  other arithmetic  7.38 us (1%)
    pallas_call x1, Pallas kernels, exchange_backward(): pl.pallas_call(kernel, grid=(n_chunk, slots), in_specs=[any_space, any_sp...  139 us
    pallas_call x1, Pallas kernels, exchange_forward(): pl.pallas_call(kernel, grid=(last + 1,), in_specs=[any_space] * 3 + [pl.B...  124 us
    pallas_call x1, Pallas kernels, feed_forward(): pl.pallas_call(kernel, grid_spec=pltpu.PrefetchScalarGridSpec(num_scalar_...  85.1 us
    pallas_call x1, Pallas kernels, conv_backward(): pl.pallas_call(kernel, grid=(n_chunk, slots), in_specs=[pl.BlockSpec((1,...  73.4 us
    unnamed x66, local copies, waits for them, and re-layouts  24.8 us
    pallas_call x2, Pallas kernels, tile_total(): pl.pallas_call(kernel, in_specs=[whole], out_specs=whole, out_shape=jax.S...  19.1 us
    pallas_call x1, Pallas kernels, rotate(): pl.pallas_call(kernel, grid=(pairs,), in_specs=[pl.BlockSpec(memory_space...  12.4 us
    pallas_call x1, Pallas kernels, close_out(): pl.pallas_call(kernel, grid=(rows // step,), in_specs=[line(depth), line(...  11.3 us

profile of v8, /device:TPU:8, one launch (start us, length us, event | category | flops | bytes accessed | tf_op | source)
XLA Modules:
  0.0 520.0 jit_solution(12186219950673846045)
XLA Ops:
  0.7 1.3 dynamic_slice.6
  2.6 1.4 fusion.7
  4.4 1.8 copy-done.1
  7.1 1.0 copy-done.7
  8.1 1.0 broadcast_in_dim.68.f_ref.m_ref
  12.2 1.2 broadcast_in_dim.66.t_ref.w_ref
  15.1 124.4 %exchange_forward.1 = (bf16[7,2,5,72,128]{4,3,2,1,0:T(8,128)(2,1)}, bf16[2,4,896,800]{3,2,1,0:T(8,128)(2,1)}, s32[8,2,8]{2,1,0:T(2,128)}, f32[2,576,800]{2,1,0:T...) custom-call(bf16[7,2,4,72,128]{4,3,2,1,0:T(8,128)(2,1)} %copy-done.7, ...), custom_call_target="tpu_custom_call" | custom-call | tf_op jit(solution)/shard_map/exchange_forward/pallas_call | solution.py:386
  139.5 0.9 reduce_sum.56
  141.1 12.0 %tile_total.2 = f32[3,800]{1,0:T(4,128)S(1)} custom-call(f32[3,800]{1,0:T(4,128)S(1)} %concatenate.9.v_ref), custom_call_target="tpu_custom_call" | custom-call | tf_op jit(solution)/shard_map/tile_total/pallas_call | solution.py:685
  154.9 5.1 arrange_shaped.1
  160.0 1.3 copy-done.12
  161.3 1.2 copy-done.13
  163.8 85.1 %feed_forward.1 = (f32[1152,896]{1,0:T(8,128)}, f32[1152,896]{1,0:T(8,128)}, bf16[2,4,896,800]{3,2,1,0:T(8,128)(2,1)}, f32[8,1,400]{2,1,0:T(1,128)}) custom-call(s32[16]{0:T(128)} %select_reduce_fusion.inv_ref, bf16[1152,896]{1,0:T(8,128)(2,1)} %copy-done.12, bf16[800,1152]{1,0:T(8,128)(2,1)} %copy-done.13, bf16[1152,896]{1,0:T(8,128)(2,1)} %get-tuple-element.41.d_ref, ...), custom_call_target="tpu_custom_call" | custom-call | flops 35389440000 | bytes 41943040 | tf_op jit(solution)/shard_map/feed_forward/pallas_call | solution.py:1127
  249.6 11.3 %close_out.1 = (bf16[1152,800]{1,0:T(8,128)(2,1)}, f32[1152,800]{1,0:T(8,128)}, f32[2,1,800]{2,1,0:T(1,128)}) custom-call(f32[1152,896]{1,0:T(8,128)} %get-tuple-element.44.b_ref, f32[1152,896]{1,0:T(8,128)} %get-tuple-element.45.d_ref, bf16[1152,800]{1,0:T(8,128)(2,1)} %bitcast.46, f32[1152,800]{1,0:T(8,128)} %bitcast.44, ...), custom_call_target="tpu_custom_call" | custom-call | tf_op jit(solution)/shard_map/close_out/pallas_call | solution.py:1185
  263.1 7.1 %tile_total.3 = f32[2,800]{1,0:T(2,128)S(1)} custom-call(f32[2,800]{1,0:T(2,128)S(1)} %pad_maximum_fusion.3.v_ref), custom_call_target="tpu_custom_call" | custom-call | tf_op jit(solution)/shard_map/tile_total/pallas_call | solution.py:685
  270.8 2.2 copy-done
  272.9 2.2 copy-done.8
  275.1 2.5 conv_gradient.1
  277.6 2.0 copy-done.5
  279.6 1.0 copy-done.10
  280.6 139.0 %exchange_backward.1 = (bf16[7,2,5,72,128]{4,3,2,1,0:T(8,128)(2,1)}, bf16[2,896,800]{2,1,0:T(8,128)(2,1)}, f32[64,896]{1,0:T(8,128)}) custom-call(bf16[7,2,4,72,128]{4,3,2,1,0:T(8,128)(2,1)} %copy-done.10, bf16[2,4,896,800]{3,2,1,0:T(8,128)(2,1)} %get-tuple-element.51.g_ref, s32[8,2,8]{2,1,0:T(2,128)} %get-tuple-element.52.n_ref, ...), custom_call_target="tpu_custom_call" | custom-call | tf_op jit(solution)/shard_map/exchange_backward/pallas_call | solution.py:630
  420.4 1.8 copy.44.l_ref
  422.2 1.2 copy.45.one_ref
  423.4 1.2 copy.46.two_ref
  424.6 12.4 %rotate.1 = (f32[4,100,400]{2,1,0:T(8,128)}, f32[4,100,400]{2,1,0:T(8,128)}, bf16[2,896,800]{2,1,0:T(8,128)(2,1)}) custom-call(f32[1]{0:T(128)} %bitcast.20.f_ref, bf16[2,896,800]{2,1,0:T(8,128)(2,1)} %get-tuple-element.57.g_ref, f32[4,800,100]{2,1,0:T(8,128)} %copy.44.l_ref, f32[4,400,400]{2,1,0:T(8,128)} %c_ref.1, f32[4,100,400]{2,1,0:T(8,128)} %copy.45.one_ref, ...), custom_call_target="tpu_custom_call" | custom-call | tf_op jit(solution)/shard_map/rotate/pallas_call | solution.py:1254
  437.0 73.4 %conv_backward.1 = (f32[2,576,800]{2,1,0:T(8,128)}, f32[2,112,800]{2,1,0:T(8,128)S(1)}, f32[64,896]{1,0:T(8,128)S(1)}) custom-call(f32[2,576,800]{2,1,0:T(8,128)} %copy-done.5, bf16[2,24,24,800]{3,2,1,0:T(8,128)(2,1)} %bitcast.51, f32[2,576,128]{2,1,0:T(8,128)S(1)} %copy-done.4, f32[50,8,800]{2,1,0:T(8,128)S(1)} %copy-done.6, ...), custom_call_target="tpu_custom_call" | custom-call | tf_op jit(solution)/shard_map/conv_backward/pallas_call | solution.py:931
  511.9 1.4 copy.48
  513.3 1.0 copy.49
  514.3 0.9 divide_subtract_fusion
  515.2 1.4 copy.50
  516.6 1.4 copy.51
  518.0 2.0 copy.57
  (104 shorter events, 13.2 us)
Async XLA Ops:
  0.6 8.5 %copy-start.27 = (s32[4]{0:T(128)S(1)}, s32[4]{0:T(128)}, u32[]{:S(2)}) copy-start(s32[4]{0:T(128)} %param.30) | copy-start | bytes 52
  0.7 11.6 %slice-start = ((f32[57,800]{1,0:T(8,128)}), f32[50,800]{1,0:T(8,128)S(1)}, s32[]{:S(2)}) async-start(f32[57,800]{1,0:T(8,128)} %param.23), calls=%async_computation | async-start | bytes 401408 | tf_op jit(solution)/shard_map/slice | solution.py:1328
  4.3 9.2 %copy-start.2 = (f32[2,576,128]{2,1,0:T(8,128)}, f32[2,576,128]{2,1,0:T(8,128)S(1)}, u32[]{:S(2)}) copy-start(f32[2,576,128]{2,1,0:T(8,128)S(1)} %broadcast_in_dim.65.m_ref) | copy-start | bytes 1769476
  4.3 1.8 copy-start.1
  6.1 7.2 %copy-start.15 = (f32[4,100,400]{2,0,1:T(4,128)S(1)}, f32[4,100,400]{2,0,1:T(4,128)}, u32[]{:S(2)}) copy-start(f32[4,100,400]{2,0,1:T(4,128)} %param.18) | copy-start | bytes 1920004
  7.1 1.0 copy-start.7
  15.1 139.8 %copy-start.18 = (f32[57,800]{1,0:T(8,128)S(1)}, f32[57,800]{1,0:T(8,128)}, u32[]{:S(2)}) copy-start(f32[57,800]{1,0:T(8,128)} %param.23) | copy-start | bytes 547204
  139.5 23.7 %copy-start.28 = (s32[16]{0:T(128)S(1)}, s32[16]{0:T(128)}, u32[]{:S(2)}) copy-start(s32[16]{0:T(128)} %param.29) | copy-start | bytes 196
  160.0 1.3 copy-start.12
  161.3 1.2 copy-start.13
  249.6 12.7 %copy-start.25 = (f32[8,1,400]{2,1,0:T(1,128)S(1)}, f32[8,1,400]{2,1,0:T(1,128)}, u32[]{:S(2)}) copy-start(f32[8,1,400]{2,1,0:T(1,128)} %get-tuple-element.55) | copy-start | bytes 38404
  249.6 12.8 %copy-start.26 = (f32[1,800]{1,0:T(1,128)S(1)}, f32[1,800]{1,0:T(1,128)}, u32[]{:S(2)}) copy-start(f32[1,800]{1,0:T(1,128)} %get-tuple-element.54) | copy-start | bytes 9604
  249.6 21.2 %copy-start.3 = (f32[2,576,128]{2,1,0:T(8,128)S(1)}, f32[2,576,128]{2,1,0:T(8,128)}, u32[]{:S(2)}) copy-start(f32[2,576,128]{2,1,0:T(8,128)} %copy-done.2) | copy-start | bytes 1769476
  270.8 2.2 copy-start
  272.9 2.2 copy-start.8
  277.6 2.0 copy-start.5
  279.6 1.0 copy-start.10
  280.6 139.9 %copy-start.17 = (f32[4,800,100]{1,0,2:T(4,128)S(1)}, f32[4,800,100]{1,0,2:T(4,128)}, u32[]{:S(2)}) copy-start(f32[4,800,100]{1,0,2:T(4,128)} %param.21) | copy-start | bytes 3840004
  419.6 2.7 copy-start.21
  419.6 3.9 copy-start.22
  424.6 12.4 %copy-start.4 = (f32[2,576,128]{2,1,0:T(8,128)S(1)}, f32[2,576,128]{2,1,0:T(8,128)}, u32[]{:S(2)}) copy-start(f32[2,576,128]{2,1,0:T(8,128)} %copy-done.2) | copy-start | bytes 1769476
  424.6 12.4 %copy-start.6 = (f32[50,8,800]{2,1,0:T(8,128)S(1)}, f32[50,8,800]{2,1,0:T(8,128)}, u32[]{:S(2)}) copy-start(f32[50,8,800]{2,1,0:T(8,128)} %broadcast_in_dim.66.t_ref.w_ref) | copy-start | bytes 3840004
  424.6 12.4 %copy-start.9 = (bf16[7,2,5,72,128]{4,3,2,1,0:T(8,128)(2,1)S(1)}, bf16[7,2,5,72,128]{4,3,2,1,0:T(8,128)(2,1)}, u32[]{:S(2)}) copy-start(bf16[7,2,5,72,128]{4,3,2,1,0:T(8,128)(2,1)} %get-tuple-element.56.h_ref) | copy-start | bytes 3870724
  424.6 12.4 %copy-start.11 = (f32[64,896]{1,0:T(8,128)S(1)}, f32[64,896]{1,0:T(8,128)}, u32[]{:S(2)}) copy-start(f32[64,896]{1,0:T(8,128)} %get-tuple-element.59.s_ref) | copy-start | bytes 688132
  510.4 1.1 copy-start.16
  511.5 2.7 copy-start.23
  511.5 2.7 copy-start.24
  511.5 3.7 copy-start.20
  511.9 4.8 copy-start.19
  513.3 4.8 copy-start.14

commit v9 on v8

--- a/solution.py
+++ b/solution.py
@@ -238,71 +238,100 @@
 class WeightGather:
     def __init__(self, grid, pairs, width):
         self.grid, self.pairs, self.width = grid, pairs, width
-        self.count = pairs * (grid.n_tile * grid.n_opt - 1)
+        self.count = pairs * (grid.n_tile * grid.n_opt + 2)
 
     def plan(self, copies, packed, gathered, local):
         grid, width = self.grid, self.width
         own = grid.own()
+        self.middle = (own["a"] == 1) | (own["a"] == 2)
 
         def place(m, rel):
             t, o = grid.at({d: own[d] ^ rel.get(d, 0) for d in own})
             return gathered.at[m, o, pl.ds(pl.multiple_of(t * width, width), width)]
 
-        def onward(m, rel, dims):
+        def send(m, rel, dim, k):
             source = packed.at[m] if not rel else place(m, rel)
-            return [
-                ({**rel, dim: k}, copies.make(source, place(m, rel), grid.beside(own, dim, k)))
-                for dim in dims
-                for k in range(1, grid.size[dim])
-            ]
-
-        orders = [("a", "x", "b", "c") if m % 2 == 0 else ("a", "b", "x", "c") for m in range(self.pairs)]
-        due = {}
-
-        def note(m, fresh, after):
-            for rel, copy in fresh:
-                level = sum(1 for d in rel if d != "c")
-                wave = max(rel.get("a", 0) + level - ("a" in rel), after)
-                due.setdefault(wave, []).append((m, rel, copy))
-            return [copy for _, copy in fresh]
+            return copies.make(source, place(m, rel), grid.beside(own, dim, k))
 
         self.keeps = [pltpu.make_async_copy(packed.at[m], place(m, {}), local.at[m]) for m in range(self.pairs)]
-        self.first, self.later = [], []
+        self.first, self.chain, self.onward, arrivals = [], {}, {}, []
         for m in range(self.pairs):
-            fresh = onward(m, {}, orders[m])
-            note(m, fresh, 0)
-            for rel, copy in fresh:
-                (self.later if rel.get("a", 0) > 1 else self.first).append(copy)
-        self.waves = []
-        for wave in range(4 * sum(grid.size.values())):
-            events = []
-            for m, rel, copy in sorted(due.pop(wave, []), key=lambda e: "c" in e[1]):
-                last = max(orders[m].index(d) for d in rel)
-                events.append((copy, note(m, onward(m, rel, orders[m][last + 1 :]), wave + 1)))
-            self.waves.append(events)
-            if not due:
-                break
+            self.chain["near", m] = send(m, {}, "a", 1)
+            self.chain["over", m] = send(m, {}, "a", 3)
+            self.chain["over2", m] = send(m, {"a": 1}, "a", 3)
+            self.chain["out", m] = send(m, {"a": 3}, "a", 1)
+            self.chain["out2", m] = send(m, {"a": 2}, "a", 1)
+            order = ("x", "b", "c") if m % 2 == 0 else ("b", "x", "c")
+
+            def spread(rel, left):
+                self.onward[m, tuple(rel.items())] = sends = []
+                for i, dim in enumerate(left):
+                    for k in range(1, grid.size[dim]):
+                        copy = send(m, rel, dim, k)
+                        sends.append(copy)
+                        child = {**rel, dim: k}
+                        arrivals.append((m, child, copy))
+                        spread(child, left[i + 1 :])
+
+            for k in range(4):
+                spread({"a": k} if k else {}, order)
+
+        def waves(turn):
+            found = [[] for _ in range(6)]
+            for m, rel, copy in arrivals:
+                found[turn[rel.get("a", 0)] + ("x" in rel) + ("b" in rel)].append((m, rel, copy))
+            return [sorted(wave, key=lambda e: "c" in e[1]) for wave in found]
+
+        self.sides = {True: waves({0: 0, 1: 1, 3: 2, 2: 3}), False: waves({0: 0, 1: 1, 2: 2, 3: 3})}
 
     def start(self):
-        for copy in self.keeps + self.first:
+        for copy in self.keeps:
             copy.start()
-
-    def start_later(self):
-        for copy in self.later:
+        for m in range(self.pairs):
+            self.chain["near", m].start()
+
+            @pl.when(self.middle)
+            def _():
+                self.chain["over", m].start()
+
+            self.pass_on(m, {})
+
+    def pass_on(self, m, rel):
+        for copy in self.onward[m, tuple(rel.items())]:
             copy.start()
 
-    def run(self, waves):
-        for events in waves:
-            for copy, fresh in events:
-                copy.wait_recv()
-                for other in fresh:
-                    other.start()
+    def run(self, wave):
+        along = {True: {1: ("near", 1, "over2"), 2: ("over", 3, "out"), 3: ("over2", 2, "out2")}}
+        along[False] = {1: ("near", 1, None), 2: ("out", 2, None), 3: ("out2", 3, None)}
+        for side in (True, False):
+
+            @pl.when(self.middle == side)
+            def _():
+                if wave in along[side]:
+                    came, k, goes = along[side][wave]
+                    for m in range(self.pairs):
+                        self.chain[came, m].wait_recv()
+                        if goes is not None:
+                            self.chain[goes, m].start()
+                        self.pass_on(m, {"a": k})
+                for m, rel, copy in self.sides[side][wave]:
+                    copy.wait_recv()
+                    self.pass_on(m, rel)
 
     def finish(self):
         for copy in self.keeps:
             copy.wait()
-        for copy in self.first + self.later + [c for events in self.waves for _, fresh in events for c in fresh]:
-            copy.wait_send()
+        for m in range(self.pairs):
+            self.chain["near", m].wait_send()
+
+            @pl.when(self.middle)
+            def _():
+                for name in ("over", "over2", "out", "out2"):
+                    self.chain[name, m].wait_send()
+
+        for sends in self.onward.values():
+            for copy in sends:
+                copy.wait_send()
 
 
 def exchange_forward(grid, rims, packed, neighbours, inputs, mask_lanes, taps, cotangent, flat_mask, weight_row, width):
@@ -333,7 +362,6 @@
         keep = pltpu.make_async_copy(n_ref, nbr_ref.at[t], locals_n.at[0])
         load = pltpu.make_async_copy(nbr_ref, table, locals_n.at[1])
         halo_out = pltpu.make_async_copy(landed, halo_ref, locals_n.at[0])
-        head = 2
 
         @pl.when(step == 0)
         def _():
@@ -356,17 +384,18 @@
                 copy.wait()
             load.start()
             load.wait()
+            gather.run(0)
             halo.pick_and_send(lambda d, k: table[d // slots, d % slots, k])
-            gather.start_later()
-            gather.run(gather.waves[:head])
+            gather.run(1)
+            gather.run(2)
             halo.finish()
             halo_out.start()
 
-        for i, events in enumerate(gather.waves[head:]):
-
-            @pl.when(step == min(last, early + 4 + 3 * i))
+        for i in range(3):
+
+            @pl.when(step == min(last, early + 3 + 4 * i))
             def _():
-                gather.run([events])
+                gather.run(3 + i)
 
         @pl.when(step > early)
         def _():
@@ -438,7 +467,8 @@
     side_a = grid.size["a"]
     piece = part // side_a
     halo = HaloExchange(grid, n_chunk, slots, side)
-    total = halo.count + blocks + side_a * pairs * side_x * side_b * 2
+    hops = [(dim, 1 << i) for dim in ("c", "x", "b", "a") for i in range((grid.size[dim] - 1).bit_length())]
+    total = len(hops) + halo.count + blocks + side_a * pairs * side_x * side_b * 2
     total += pairs * (side_a - 1 + 5 + side_a * (side_b - 1))
     last = n_chunk * slots - 1
     small_rows = small.shape[0]
@@ -446,7 +476,7 @@
 
     def kernel(
         r_ref, g_ref, n_ref, x_ref, m_ref, d_ref, h_ref, s_ref, halo_ref, o_ref, t_ref,
-        arrived, picked, local, here, core, far, across, pad, sums, got, mine, send, recv, load_sems,
+        arrived, picked, local, here, core, far, across, pad, sums, got, mine, heard, send, recv, load_sems,
     ):
         own = grid.own()
         own_x, own_b, own_c = own["x"], own["b"], own["c"]
@@ -516,6 +546,14 @@
                     came = o_ref.at[m, row_of(own_a ^ k, own_b)]
                     back_b[k, j, m] = copies.make(done if k == 0 else came, came, grid.beside(own, "b", j))
         middle = (own_a == 1) | (own_a == 2)
+        hop_copies = [copies.make(mine, heard.at[i], grid.beside(own, dim, k)) for i, (dim, k) in enumerate(hops)]
+
+        def hop(i):
+            if 0 < i <= len(hops):
+                hop_copies[i - 1].wait()
+                mine[...] = mine[...] + heard[i - 1]
+            if i < len(hops):
+                hop_copies[i].start()
 
         def start(found):
             for copy in found:
@@ -554,7 +592,9 @@
         @pl.when(step == last)
         def _():
             halo.pick_and_send(lambda d, k: n_ref[d // slots, d % slots, k])
+            mine[pl.ds(50, small_rows), pl.ds(0, channels)] = s_ref[...]
             for i in range(side_a + 1):
+                hop(i)
                 for m in range(pairs):
                     if i < side_a:
                         k = turns[i]
@@ -572,7 +612,6 @@
                             add_rows(target, sources, piece)
                         if k > 0:
                             to_a[k, m].start()
-            mine[pl.ds(50, small_rows), pl.ds(0, channels)] = s_ref[...]
             for m in range(pairs):
                 wait(to_a[k, m] for k in range(1, side_a))
                 done = here.at[index(0, m), row_of(own_a, own_b)]
@@ -612,6 +651,8 @@
                 arrive("out", 2, None)
                 arrive("out2", 3, None)
 
+            for i in range(side_a + 1, len(hops) + 1):
+                hop(i)
             halo.finish()
             t_ref[...] = mine[...]
             for m in range(pairs):
@@ -656,6 +697,7 @@
             pltpu.VMEM((50, 8, LANES), F32),
             pltpu.VMEM((pairs, side_a - 1, piece, cols), BF),
             pltpu.VMEM(small_shape, F32),
+            pltpu.VMEM((len(hops),) + small_shape, F32),
             pltpu.SemaphoreType.DMA((total,)),
             pltpu.SemaphoreType.DMA((total,)),
             pltpu.SemaphoreType.DMA((blocks,)),
@@ -820,7 +862,7 @@
         o_ref[pl.ds(0, 50), pl.ds(at, LANES)] = jnp.sum(sums[...], axis=1)
 
 
-def conv_backward(grid, d_conv, halos, cotangent, mask_lanes, taps, weight_lanes, change, small):
+def conv_backward(grid, d_conv, halos, cotangent, mask_lanes, taps, weight_lanes, change):
     slots, side, _, channels = cotangent.shape
     n_chunk = halos.shape[0]
     cells = side * side
@@ -828,13 +870,12 @@
     side_a, side_b = grid.size["a"], grid.size["b"]
     part = rows // side_b
     piece = part // side_a
-    hops = [(dim, 1 << i) for dim in ("c", "x", "b", "a") for i in range((grid.size[dim] - 1).bit_length())]
-    total = pairs * (side_a * (side_b - 1) + (side_a - 1)) + len(hops)
+    total = pairs * (side_a * (side_b - 1) + (side_a - 1))
     last = n_chunk * slots - 1
 
     def kernel(
-        d_ref, g_ref, m_ref, w_ref, l_ref, h_ref, c_ref, s_ref, o_ref, change_ref, small_ref,
-        pad, mine, from_b, from_a, heard, send, recv, load_sems,
+        d_ref, g_ref, m_ref, w_ref, l_ref, h_ref, c_ref, o_ref, change_ref,
+        pad, mine, from_b, from_a, send, recv, load_sems,
     ):
         own = grid.own()
         step = pl.program_id(0) * slots + pl.program_id(1)
@@ -860,23 +901,15 @@
                     )
             loads.append(pltpu.make_async_copy(c_ref.at[m, half(own_b)], mine.at[m], load_sems.at[m]))
 
-        hop_copies = [
-            copies.make(small_ref, heard.at[i], grid.beside(own, dim, k)) for i, (dim, k) in enumerate(hops)
-        ]
-
-        def start_turn(i):
-            for m in range(pairs):
-                for copy in firsts[turns[i], m]:
-                    copy.start()
-
         @pl.when(step == 0)
         def _():
-            meet(grid.partners(("a", "b", "x", "c")))
+            meet(grid.partners(("a", "b")))
             for load in loads:
                 load.start()
-            start_turn(0)
-            small_ref[...] = s_ref[...]
-            hop_copies[0].start()
+            for k in turns:
+                for m in range(pairs):
+                    for copy in firsts[k, m]:
+                        copy.start()
 
         for i in range(side):
             pad[pl.ds((i + RIM) * PITCH + 8, side), :] = d_ref[0, pl.ds(i * side, side), :]
@@ -893,30 +926,18 @@
 
         for i, k in enumerate(turns):
 
-            @pl.when(step == min(last, 7 + 6 * i))
+            @pl.when(step == min(last, 5 + 4 * i))
             def _():
                 for m in range(pairs):
                     if i == 0:
                         loads[m].wait()
                     for copy in firsts[k, m]:
                         copy.wait()
-                if i + 1 < side_a:
-                    start_turn(i + 1)
-                for m in range(pairs):
                     rows_here = part_row(own_a ^ k)
                     sources = [from_b.at[j, m, rows_here] for j in range(side_b - 1)]
                     add_rows(mine.at[m, rows_here], sources, piece)
                     if k > 0:
                         seconds[k, m].start()
-
-        for i, copy in enumerate(hop_copies):
-
-            @pl.when(step == min(last, 2 + 3 * i))
-            def _():
-                copy.wait()
-                small_ref[...] = small_ref[...] + heard[i]
-                if i + 1 < len(hops):
-                    hop_copies[i + 1].start()
 
         @pl.when(step == last)
         def _():
@@ -939,19 +960,16 @@
             pl.BlockSpec((8, LANES), lambda c, s: (0, 0)),
             halo_block(halos),
             pl.BlockSpec(memory_space=pl.ANY),
-            pl.BlockSpec(small.shape, lambda c, s: (0, 0)),
         ],
         out_specs=[
             pl.BlockSpec((1, cells, LANES), lambda c, s: (s, 0, c)),
             pl.BlockSpec((pairs, piece, cols), lambda c, s: (0, 0, 0)),
-            pl.BlockSpec(small.shape, lambda c, s: (0, 0)),
         ],
         scratch_shapes=[
             pltpu.VMEM(((side + 2 * RIM) * PITCH, LANES), F32),
             pltpu.VMEM((pairs, part, cols), BF),
             pltpu.VMEM((side_b - 1, pairs, part, cols), BF),
             pltpu.VMEM((side_a - 1, pairs, piece, cols), BF),
-            pltpu.VMEM((len(hops),) + small.shape, F32),
             pltpu.SemaphoreType.DMA((total,)),
             pltpu.SemaphoreType.DMA((total,)),
             pltpu.SemaphoreType.DMA((pairs,)),
@@ -959,11 +977,10 @@
         out_shape=[
             jax.ShapeDtypeStruct((slots, cells, channels), F32),
             jax.ShapeDtypeStruct((pairs, piece, cols), F32),
-            jax.ShapeDtypeStruct(small.shape, F32),
         ],
         compiler_params=remote_params(4, 48),
         name="conv_backward",
-    )(d_conv, cotangent, mask_lanes, taps, weight_lanes, halos, change, small)
+    )(d_conv, cotangent, mask_lanes, taps, weight_lanes, halos, change)
 
 
 def spread_lanes(value, parts, width):
@@ -986,7 +1003,7 @@
 
 
 def row_block(rows):
-    return 3 * LANES if rows % (3 * LANES) == 0 else LANES
+    return LANES
 
 
 def arranged(value, gap_ref, turned_ref, sum_ref, first, parts, width):
@@ -1002,7 +1019,7 @@
 
 
 def arrange(body, args, specs, rows, channels, parts, width, name):
-    step = 3 * LANES if rows % (3 * LANES) == 0 else LANES
+    step = row_block(rows)
 
     def kernel(*refs):
         given, (gap_ref, turned_ref, sum_ref) = refs[: len(args)], refs[len(args) :]
@@ -1166,7 +1183,7 @@
 def close_out(branch, d_shaped, inputs, conv_out, mask_lanes, out_bias, parts, run):
     rows, channels = inputs.shape
     depth = branch.shape[1]
-    step = 3 * LANES if rows % (3 * LANES) == 0 else LANES
+    step = row_block(rows)
 
     def kernel(b_ref, d_ref, x_ref, v_ref, m_ref, o_ref, out_ref, ds_ref, sum_ref):
         branch_here = close_lanes(b_ref[...], parts, run) + o_ref[...]
@@ -1419,8 +1436,8 @@
     first_new, second_new, change = rotate(
         owned, left_basis, column_basis, moment_one, moment_two, correction, grid, width
     )
-    input_grad, change, d_small = conv_backward(
-        grid, d_conv, grad_halos, cotangent, mask_lanes, taps, weight_lanes, change, d_small
+    input_grad, change = conv_backward(
+        grid, d_conv, grad_halos, cotangent, mask_lanes, taps, weight_lanes, change
     )
     change = unpack_pairs(change[:, :run])
     d_small = d_small[: small_params.shape[0], :channels]

time: 524 us -> 494 us (0.943)
  Pallas kernels: 473 us -> 445 us
    pallas_call x1, Pallas kernels: 73.4 us -> 53.1 us  [conv_backward(): pl.pallas_call(kernel, grid=(n_chunk, slots), in_specs=[pl.BlockSpec((1,...]
    pallas_call x1, Pallas kernels: 124 us -> 108 us  [exchange_forward(): pl.pallas_call(kernel, grid=(last + 1,), in_specs=[any_space] * 3 + [pl.B...]
    unnamed x66 -> x70, local copies, waits for them, and re-layouts: 24.8 us -> 26.1 us
where the time goes in v9:
time: 494 us; the launch traced here: 493 us
  Pallas kernels  445 us (90%)
  local copies, waits for them, and re-layouts  37 us (7%)
  other arithmetic  7.37 us (1%)
    pallas_call x1, Pallas kernels, exchange_backward(): pl.pallas_call(kernel, grid=(n_chunk, slots), in_specs=[any_space, any_sp...  143 us
    pallas_call x1, Pallas kernels, exchange_forward(): pl.pallas_call(kernel, grid=(last + 1,), in_specs=[any_space] * 3 + [pl.B...  108 us
    pallas_call x1, Pallas kernels, feed_forward(): pl.pallas_call(kernel, grid_spec=pltpu.PrefetchScalarGridSpec(num_scalar_...  85.1 us
    pallas_call x1, Pallas kernels, conv_backward(): pl.pallas_call(kernel, grid=(n_chunk, slots), in_specs=[pl.BlockSpec((1,...  53.1 us
    unnamed x70, local copies, waits for them, and re-layouts  26.1 us
    pallas_call x2, Pallas kernels, tile_total(): pl.pallas_call(kernel, in_specs=[whole], out_specs=whole, out_shape=jax.S...  19.5 us
    pallas_call x1, Pallas kernels, rotate(): pl.pallas_call(kernel, grid=(pairs,), in_specs=[pl.BlockSpec(memory_space...  12.3 us
    pallas_call x1, Pallas kernels, close_out(): pl.pallas_call(kernel, grid=(rows // step,), in_specs=[line(depth), line(...  11.9 us

profile of v9, /device:TPU:8, one launch (start us, length us, event | category | flops | bytes accessed | tf_op | source)
XLA Modules:
  0.0 493.0 jit_solution(1083693162382429227)
XLA Ops:
  0.7 1.3 dynamic_slice.6
  2.6 1.4 fusion.7
  4.4 1.8 copy-done.1
  7.1 1.0 copy-done.8
  8.1 1.0 broadcast_in_dim.68.f_ref.m_ref
  12.2 1.2 broadcast_in_dim.66.t_ref.w_ref
  15.1 108.4 %exchange_forward.1 = (bf16[7,2,5,72,128]{4,3,2,1,0:T(8,128)(2,1)}, bf16[2,4,896,800]{3,2,1,0:T(8,128)(2,1)}, s32[8,2,8]{2,1,0:T(2,128)}, f32[2,576,800]{2,1,0:T...) custom-call(bf16[7,2,4,72,128]{4,3,2,1,0:T(8,128)(2,1)} %copy-done.8, ...), custom_call_target="tpu_custom_call" | custom-call | tf_op jit(solution)/shard_map/exchange_forward/pallas_call | solution.py:415
  123.5 0.9 reduce_sum.56
  125.1 12.5 %tile_total.2 = f32[3,800]{1,0:T(4,128)S(1)} custom-call(f32[3,800]{1,0:T(4,128)S(1)} %concatenate.9.v_ref), custom_call_target="tpu_custom_call" | custom-call | tf_op jit(solution)/shard_map/tile_total/pallas_call | solution.py:727
  139.4 7.5 %arrange_shaped.1 = (bf16[1152,896]{1,0:T(8,128)(2,1)S(1)}, bf16[800,1152]{1,0:T(8,128)(2,1)S(1)}, f32[1,800]{1,0:T(1,128)}) custom-call(f32[1152,800]{1,0:T(8,128)} %bitcast.43, f32[4,800]{1,0:T(4,128)S(1)} %pad_maximum_fusion.1.refs_1_), custom_call_target="tpu_custom_call" | custom-call | tf_op jit(solution)/shard_map/arrange_shaped/pallas_call | solution.py:1028
  146.9 1.3 copy-done.12
  148.2 1.2 copy-done.13
  150.7 85.1 %feed_forward.1 = (f32[1152,896]{1,0:T(8,128)}, f32[1152,896]{1,0:T(8,128)}, bf16[2,4,896,800]{3,2,1,0:T(8,128)(2,1)}, f32[8,1,400]{2,1,0:T(1,128)}) custom-call(s32[16]{0:T(128)} %select_reduce_fusion.inv_ref, bf16[1152,896]{1,0:T(8,128)(2,1)} %copy-done.12, bf16[800,1152]{1,0:T(8,128)(2,1)} %copy-done.13, bf16[1152,896]{1,0:T(8,128)(2,1)} %get-tuple-element.40.d_ref, ...), custom_call_target="tpu_custom_call" | custom-call | flops 35389440000 | bytes 41943040 | tf_op jit(solution)/shard_map/feed_forward/pallas_call | solution.py:1144
  236.4 11.9 %close_out.1 = (bf16[1152,800]{1,0:T(8,128)(2,1)}, f32[1152,800]{1,0:T(8,128)}, f32[2,1,800]{2,1,0:T(1,128)}) custom-call(f32[1152,896]{1,0:T(8,128)} %get-tuple-element.43.b_ref, f32[1152,896]{1,0:T(8,128)} %get-tuple-element.44.d_ref, bf16[1152,800]{1,0:T(8,128)(2,1)} %bitcast.46, f32[1152,800]{1,0:T(8,128)} %bitcast.44, ...), custom_call_target="tpu_custom_call" | custom-call | tf_op jit(solution)/shard_map/close_out/pallas_call | solution.py:1202
  250.6 7.1 %tile_total.3 = f32[2,800]{1,0:T(2,128)S(1)} custom-call(f32[2,800]{1,0:T(2,128)S(1)} %pad_maximum_fusion.3.v_ref), custom_call_target="tpu_custom_call" | custom-call | tf_op jit(solution)/shard_map/tile_total/pallas_call | solution.py:727
  258.2 2.2 copy-done
  260.4 2.2 copy-done.9
  262.6 2.5 conv_gradient.1
  265.1 2.0 copy-done.5
  267.1 1.0 copy-done.11
  268.1 143.3 %exchange_backward.1 = (bf16[7,2,5,72,128]{4,3,2,1,0:T(8,128)(2,1)}, bf16[2,896,800]{2,1,0:T(8,128)(2,1)}, f32[64,896]{1,0:T(8,128)}) custom-call(bf16[7,2,4,72,128]{4,3,2,1,0:T(8,128)(2,1)} %copy-done.11, bf16[2,4,896,800]{3,2,1,0:T(8,128)(2,1)} %get-tuple-element.50.g_ref, s32[8,2,8]{2,1,0:T(2,128)} %get-tuple-element.51.n_ref, ...), custom_call_target="tpu_custom_call" | custom-call | tf_op jit(solution)/shard_map/exchange_backward/pallas_call | solution.py:671
  412.3 1.8 copy.44.l_ref
  414.1 1.2 copy.45.one_ref
  415.3 1.2 copy.46.two_ref
  416.5 12.3 %rotate.1 = (f32[4,100,400]{2,1,0:T(8,128)}, f32[4,100,400]{2,1,0:T(8,128)}, bf16[2,896,800]{2,1,0:T(8,128)(2,1)}) custom-call(f32[1]{0:T(128)} %bitcast.20.f_ref, bf16[2,896,800]{2,1,0:T(8,128)(2,1)} %get-tuple-element.56.g_ref, f32[4,800,100]{2,1,0:T(8,128)} %copy.44.l_ref, f32[4,400,400]{2,1,0:T(8,128)} %c_ref.1, f32[4,100,400]{2,1,0:T(8,128)} %copy.45.one_ref, ...), custom_call_target="tpu_custom_call" | custom-call | tf_op jit(solution)/shard_map/rotate/pallas_call | solution.py:1271
  428.9 1.3 copy-done.10
  430.2 53.1 %conv_backward.1 = (f32[2,576,800]{2,1,0:T(8,128)}, f32[2,112,800]{2,1,0:T(8,128)S(1)}) custom-call(f32[2,576,800]{2,1,0:T(8,128)} %copy-done.5, bf16[2,24,24,800]{3,2,1,0:T(8,128)(2,1)S(1)} %bitcast.50, f32[2,576,128]{2,1,0:T(8,128)S(1)} %copy-done.4, f32[50,8,800]{2,1,0:T(8,128)S(1)} %copy-done.6, f32[8,128]{1,0:T(8,128)S(1)} %broadcast_in_dim.77.l_ref, ...), custom_call_target="tpu_custom_call" | custom-call | tf_op jit(solution)/shard_map/conv_backward/pallas_call | solution.py:952
  484.8 1.4 copy.48
  486.2 1.0 copy.49
  487.2 1.4 copy.50
  488.6 1.4 copy.51
  491.0 2.0 copy.57
  (108 shorter events, 14.2 us)
Async XLA Ops:
  0.6 8.5 %copy-start.29 = (s32[4]{0:T(128)S(1)}, s32[4]{0:T(128)}, u32[]{:S(2)}) copy-start(s32[4]{0:T(128)} %param.30) | copy-start | bytes 52
  0.7 11.6 %slice-start = ((f32[57,800]{1,0:T(8,128)}), f32[50,800]{1,0:T(8,128)S(1)}, s32[]{:S(2)}) async-start(f32[57,800]{1,0:T(8,128)} %param.23), calls=%async_computation | async-start | bytes 401408 | tf_op jit(solution)/shard_map/slice | solution.py:1345
  4.3 9.2 %copy-start.2 = (f32[2,576,128]{2,1,0:T(8,128)}, f32[2,576,128]{2,1,0:T(8,128)S(1)}, u32[]{:S(2)}) copy-start(f32[2,576,128]{2,1,0:T(8,128)S(1)} %broadcast_in_dim.65.m_ref) | copy-start | bytes 1769476
  4.3 1.8 copy-start.1
  6.1 7.3 %copy-start.15 = (f32[4,100,400]{2,0,1:T(4,128)S(1)}, f32[4,100,400]{2,0,1:T(4,128)}, u32[]{:S(2)}) copy-start(f32[4,100,400]{2,0,1:T(4,128)} %param.18) | copy-start | bytes 1920004
  7.1 1.0 copy-start.8
  15.1 124.2 %copy-start.18 = (f32[57,800]{1,0:T(8,128)S(1)}, f32[57,800]{1,0:T(8,128)}, u32[]{:S(2)}) copy-start(f32[57,800]{1,0:T(8,128)} %param.23) | copy-start | bytes 547204
  123.5 26.6 %copy-start.30 = (s32[16]{0:T(128)S(1)}, s32[16]{0:T(128)}, u32[]{:S(2)}) copy-start(s32[16]{0:T(128)} %param.29) | copy-start | bytes 196
  146.9 1.3 copy-start.12
  148.2 1.2 copy-start.13
  236.4 13.4 %copy-start.27 = (f32[8,1,400]{2,1,0:T(1,128)S(1)}, f32[8,1,400]{2,1,0:T(1,128)}, u32[]{:S(2)}) copy-start(f32[8,1,400]{2,1,0:T(1,128)} %get-tuple-element.54) | copy-start | bytes 38404
  236.4 13.5 %copy-start.28 = (f32[1,800]{1,0:T(1,128)S(1)}, f32[1,800]{1,0:T(1,128)}, u32[]{:S(2)}) copy-start(f32[1,800]{1,0:T(1,128)} %get-tuple-element.53) | copy-start | bytes 9604
  236.4 21.8 %copy-start.3 = (f32[2,576,128]{2,1,0:T(8,128)S(1)}, f32[2,576,128]{2,1,0:T(8,128)}, u32[]{:S(2)}) copy-start(f32[2,576,128]{2,1,0:T(8,128)} %copy-done.2) | copy-start | bytes 1769476
  258.2 2.2 copy-start
  260.4 2.2 copy-start.9
  265.1 2.0 copy-start.5
  267.0 1.0 copy-start.11
  268.1 144.2 %copy-start.17 = (f32[4,800,100]{1,0,2:T(4,128)S(1)}, f32[4,800,100]{1,0,2:T(4,128)}, u32[]{:S(2)}) copy-start(f32[4,800,100]{1,0,2:T(4,128)} %param.21) | copy-start | bytes 3840004
  411.4 2.7 copy-start.22
  411.5 3.8 copy-start.23
  416.5 12.4 %copy-start.4 = (f32[2,576,128]{2,1,0:T(8,128)S(1)}, f32[2,576,128]{2,1,0:T(8,128)}, u32[]{:S(2)}) copy-start(f32[2,576,128]{2,1,0:T(8,128)} %copy-done.2) | copy-start | bytes 1769476
  416.5 12.4 %copy-start.6 = (f32[50,8,800]{2,1,0:T(8,128)S(1)}, f32[50,8,800]{2,1,0:T(8,128)}, u32[]{:S(2)}) copy-start(f32[50,8,800]{2,1,0:T(8,128)} %broadcast_in_dim.66.t_ref.w_ref) | copy-start | bytes 3840004
  416.5 12.4 %copy-start.7 = (bf16[1,2,24,24,800]{4,3,2,1,0:T(8,128)(2,1)S(1)}, bf16[1,2,24,24,800]{4,3,2,1,0:T(8,128)(2,1)}, u32[]{:S(2)}) copy-start(bf16[1,2,24,24,800]{4,3,2,1,0:T(8,128)(2,1)} %param.17) | copy-start | bytes 5529604
  428.9 1.3 copy-start.10
  483.3 1.1 copy-start.16
  483.6 3.6 copy-start.21
  484.4 4.2 copy-start.20
  484.7 5.3 %copy-start.19 = (f32[57,800]{1,0:T(8,128)S(1)}, f32[57,800]{1,0:T(8,128)}, u32[]{:S(2)}) copy-start(f32[57,800]{1,0:T(8,128)} %param.23) | copy-start | bytes 547204
  484.8 5.3 %copy-start.24 = (f32[57,800]{1,0:T(8,128)S(1)}, f32[57,800]{1,0:T(8,128)}, u32[]{:S(2)}) copy-start(f32[57,800]{1,0:T(8,128)} %param.24) | copy-start | bytes 547204
  484.8 5.3 %copy-start.25 = (f32[57,800]{1,0:T(8,128)S(1)}, f32[57,800]{1,0:T(8,128)}, u32[]{:S(2)}) copy-start(f32[57,800]{1,0:T(8,128)} %param.25) | copy-start | bytes 547204
  484.8 5.2 %copy-start.26 = (f32[64,896]{1,0:T(8,128)S(1)}, f32[64,896]{1,0:T(8,128)}, u32[]{:S(2)}) copy-start(f32[64,896]{1,0:T(8,128)} %get-tuple-element.62) | copy-start | bytes 688132
  486.2 4.8 copy-start.14

commit v10 on v9

--- a/solution.py
+++ b/solution.py
@@ -468,11 +468,11 @@
     piece = part // side_a
     halo = HaloExchange(grid, n_chunk, slots, side)
     hops = [(dim, 1 << i) for dim in ("c", "x", "b", "a") for i in range((grid.size[dim] - 1).bit_length())]
-    total = len(hops) + halo.count + blocks + side_a * pairs * side_x * side_b * 2
+    total = len(hops) + 1 + halo.count + blocks + side_a * pairs * side_x * side_b * 2
     total += pairs * (side_a - 1 + 5 + side_a * (side_b - 1))
     last = n_chunk * slots - 1
     small_rows = small.shape[0]
-    small_shape = (up_to(50 + small_rows, 8), n_chunk * LANES)
+    small_shape = (up_to(50 + small_rows, 16), n_chunk * LANES)
 
     def kernel(
         r_ref, g_ref, n_ref, x_ref, m_ref, d_ref, h_ref, s_ref, halo_ref, o_ref, t_ref,
@@ -546,14 +546,25 @@
                     came = o_ref.at[m, row_of(own_a ^ k, own_b)]
                     back_b[k, j, m] = copies.make(done if k == 0 else came, came, grid.beside(own, "b", j))
         middle = (own_a == 1) | (own_a == 2)
-        hop_copies = [copies.make(mine, heard.at[i], grid.beside(own, dim, k)) for i, (dim, k) in enumerate(hops)]
+        lines = small_shape[0] // 2
+        own_half = pl.ds(pl.multiple_of(own_c * lines, 8), lines)
+        other_half = pl.ds(pl.multiple_of((1 - own_c) * lines, 8), lines)
+        hop_copies = [copies.make(mine.at[other_half], heard.at[0], grid.beside(own, "c", 1))]
+        hop_copies += [
+            copies.make(mine.at[own_half], heard.at[i], grid.beside(own, dim, k))
+            for i, (dim, k) in enumerate(hops)
+            if i > 0
+        ]
+        hop_copies.append(copies.make(mine.at[own_half], heard.at[len(hops)], grid.beside(own, "c", 1)))
 
         def hop(i):
             if 0 < i <= len(hops):
                 hop_copies[i - 1].wait()
-                mine[...] = mine[...] + heard[i - 1]
-            if i < len(hops):
+                mine[own_half, :] = mine[own_half, :] + heard[i - 1]
+            if i <= len(hops):
                 hop_copies[i].start()
+            else:
+                hop_copies[i - 1].wait()
 
         def start(found):
             for copy in found:
@@ -651,10 +662,11 @@
                 arrive("out", 2, None)
                 arrive("out2", 3, None)
 
-            for i in range(side_a + 1, len(hops) + 1):
+            for i in range(side_a + 1, len(hops) + 2):
                 hop(i)
             halo.finish()
-            t_ref[...] = mine[...]
+            t_ref[own_half, :] = mine[own_half, :]
+            t_ref[other_half, :] = heard[len(hops)]
             for m in range(pairs):
                 keeps[m].wait()
                 back_a["near", m].wait_send()
@@ -697,7 +709,7 @@
             pltpu.VMEM((50, 8, LANES), F32),
             pltpu.VMEM((pairs, side_a - 1, piece, cols), BF),
             pltpu.VMEM(small_shape, F32),
-            pltpu.VMEM((len(hops),) + small_shape, F32),
+            pltpu.VMEM((len(hops) + 1, small_shape[0] // 2, small_shape[1]), F32),
             pltpu.SemaphoreType.DMA((total,)),
             pltpu.SemaphoreType.DMA((total,)),
             pltpu.SemaphoreType.DMA((blocks,)),
@@ -1003,7 +1015,7 @@
 
 
 def row_block(rows):
-    return LANES
+    return 3 * LANES if rows % (3 * LANES) == 0 else LANES
 
 
 def arranged(value, gap_ref, turned_ref, sum_ref, first, parts, width):

time: 494 us -> 487 us (0.986)
  Pallas kernels: 445 us -> 438 us
where the time goes in v10:
time: 487 us; the launch traced here: 486 us
  Pallas kernels  438 us (90%)
  local copies, waits for them, and re-layouts  37 us (8%)
  other arithmetic  7.37 us (2%)
    pallas_call x1, Pallas kernels, exchange_backward(): pl.pallas_call(kernel, grid=(n_chunk, slots), in_specs=[any_space, any_sp...  141 us
    pallas_call x1, Pallas kernels, exchange_forward(): pl.pallas_call(kernel, grid=(last + 1,), in_specs=[any_space] * 3 + [pl.B...  109 us
    pallas_call x1, Pallas kernels, feed_forward(): pl.pallas_call(kernel, grid_spec=pltpu.PrefetchScalarGridSpec(num_scalar_...  84.9 us
    pallas_call x1, Pallas kernels, conv_backward(): pl.pallas_call(kernel, grid=(n_chunk, slots), in_specs=[pl.BlockSpec((1,...  50.8 us
    unnamed x70, local copies, waits for them, and re-layouts  26.1 us
    pallas_call x2, Pallas kernels, tile_total(): pl.pallas_call(kernel, in_specs=[whole], out_specs=whole, out_shape=jax.S...  19.6 us
    pallas_call x1, Pallas kernels, rotate(): pl.pallas_call(kernel, grid=(pairs,), in_specs=[pl.BlockSpec(memory_space...  12.3 us
    pallas_call x1, Pallas kernels, close_out(): pl.pallas_call(kernel, grid=(rows // step,), in_specs=[line(depth), line(...  11.3 us

profile of v10, /device:TPU:8, one launch (start us, length us, event | category | flops | bytes accessed | tf_op | source)
XLA Modules:
  0.0 486.0 jit_solution(3526248444117276780)
XLA Ops:
  0.7 1.3 dynamic_slice.6
  2.6 1.4 fusion.7
  4.4 1.8 copy-done.1
  7.1 1.0 copy-done.8
  8.1 1.0 broadcast_in_dim.68.f_ref.m_ref
  12.2 1.2 broadcast_in_dim.66.t_ref.w_ref
  15.1 108.8 %exchange_forward.1 = (bf16[7,2,5,72,128]{4,3,2,1,0:T(8,128)(2,1)}, bf16[2,4,896,800]{3,2,1,0:T(8,128)(2,1)}, s32[8,2,8]{2,1,0:T(2,128)}, f32[2,576,800]{2,1,0:T...) custom-call(bf16[7,2,4,72,128]{4,3,2,1,0:T(8,128)(2,1)} %copy-done.8, ...), custom_call_target="tpu_custom_call" | custom-call | tf_op jit(solution)/shard_map/exchange_forward/pallas_call | solution.py:415
  123.9 0.9 reduce_sum.56
  125.5 12.5 %tile_total.2 = f32[3,800]{1,0:T(4,128)S(1)} custom-call(f32[3,800]{1,0:T(4,128)S(1)} %concatenate.9.v_ref), custom_call_target="tpu_custom_call" | custom-call | tf_op jit(solution)/shard_map/tile_total/pallas_call | solution.py:739
  139.8 5.1 %arrange_shaped.1 = (bf16[1152,896]{1,0:T(8,128)(2,1)S(1)}, bf16[800,1152]{1,0:T(8,128)(2,1)S(1)}, f32[1,800]{1,0:T(1,128)}) custom-call(f32[1152,800]{1,0:T(8,128)} %bitcast.43, f32[4,800]{1,0:T(4,128)S(1)} %pad_maximum_fusion.1.refs_1_), custom_call_target="tpu_custom_call" | custom-call | tf_op jit(solution)/shard_map/arrange_shaped/pallas_call | solution.py:1040
  144.9 1.3 copy-done.12
  146.2 1.2 copy-done.13
  148.7 84.9 %feed_forward.1 = (f32[1152,896]{1,0:T(8,128)}, f32[1152,896]{1,0:T(8,128)}, bf16[2,4,896,800]{3,2,1,0:T(8,128)(2,1)}, f32[8,1,400]{2,1,0:T(1,128)}) custom-call(s32[16]{0:T(128)} %select_reduce_fusion.inv_ref, bf16[1152,896]{1,0:T(8,128)(2,1)} %copy-done.12, bf16[800,1152]{1,0:T(8,128)(2,1)} %copy-done.13, bf16[1152,896]{1,0:T(8,128)(2,1)} %get-tuple-element.40.d_ref, ...), custom_call_target="tpu_custom_call" | custom-call | flops 35389440000 | bytes 41943040 | tf_op jit(solution)/shard_map/feed_forward/pallas_call | solution.py:1156
  234.2 11.3 %close_out.1 = (bf16[1152,800]{1,0:T(8,128)(2,1)}, f32[1152,800]{1,0:T(8,128)}, f32[2,1,800]{2,1,0:T(1,128)}) custom-call(f32[1152,896]{1,0:T(8,128)} %get-tuple-element.43.b_ref, f32[1152,896]{1,0:T(8,128)} %get-tuple-element.44.d_ref, bf16[1152,800]{1,0:T(8,128)(2,1)} %bitcast.46, f32[1152,800]{1,0:T(8,128)} %bitcast.44, ...), custom_call_target="tpu_custom_call" | custom-call | tf_op jit(solution)/shard_map/close_out/pallas_call | solution.py:1214
  247.7 7.1 %tile_total.3 = f32[2,800]{1,0:T(2,128)S(1)} custom-call(f32[2,800]{1,0:T(2,128)S(1)} %pad_maximum_fusion.3.v_ref), custom_call_target="tpu_custom_call" | custom-call | tf_op jit(solution)/shard_map/tile_total/pallas_call | solution.py:739
  255.4 2.2 copy-done
  257.6 2.2 copy-done.9
  259.7 2.5 conv_gradient.1
  262.2 2.0 copy-done.5
  264.2 1.0 copy-done.11
  265.2 141.5 %exchange_backward.1 = (bf16[7,2,5,72,128]{4,3,2,1,0:T(8,128)(2,1)}, bf16[2,896,800]{2,1,0:T(8,128)(2,1)}, f32[64,896]{1,0:T(8,128)}) custom-call(bf16[7,2,4,72,128]{4,3,2,1,0:T(8,128)(2,1)} %copy-done.11, bf16[2,4,896,800]{3,2,1,0:T(8,128)(2,1)} %get-tuple-element.50.g_ref, s32[8,2,8]{2,1,0:T(2,128)} %get-tuple-element.51.n_ref, ...), custom_call_target="tpu_custom_call" | custom-call | tf_op jit(solution)/shard_map/exchange_backward/pallas_call | solution.py:683
  407.6 1.8 copy.44.l_ref
  409.4 1.2 copy.45.one_ref
  410.6 1.2 copy.46.two_ref
  411.7 12.3 %rotate.1 = (f32[4,100,400]{2,1,0:T(8,128)}, f32[4,100,400]{2,1,0:T(8,128)}, bf16[2,896,800]{2,1,0:T(8,128)(2,1)}) custom-call(f32[1]{0:T(128)} %bitcast.20.f_ref, bf16[2,896,800]{2,1,0:T(8,128)(2,1)} %get-tuple-element.56.g_ref, f32[4,800,100]{2,1,0:T(8,128)} %copy.44.l_ref, f32[4,400,400]{2,1,0:T(8,128)} %c_ref.1, f32[4,100,400]{2,1,0:T(8,128)} %copy.45.one_ref, ...), custom_call_target="tpu_custom_call" | custom-call | tf_op jit(solution)/shard_map/rotate/pallas_call | solution.py:1283
  424.1 1.3 copy-done.10
  425.4 50.8 %conv_backward.1 = (f32[2,576,800]{2,1,0:T(8,128)}, f32[2,112,800]{2,1,0:T(8,128)S(1)}) custom-call(f32[2,576,800]{2,1,0:T(8,128)} %copy-done.5, bf16[2,24,24,800]{3,2,1,0:T(8,128)(2,1)S(1)} %bitcast.50, f32[2,576,128]{2,1,0:T(8,128)S(1)} %copy-done.4, f32[50,8,800]{2,1,0:T(8,128)S(1)} %copy-done.6, f32[8,128]{1,0:T(8,128)S(1)} %broadcast_in_dim.77.l_ref, ...), custom_call_target="tpu_custom_call" | custom-call | tf_op jit(solution)/shard_map/conv_backward/pallas_call | solution.py:964
  477.8 1.4 copy.48
  479.2 1.0 copy.49
  480.2 1.4 copy.50
  481.6 1.4 copy.51
  484.0 2.0 copy.57
  (108 shorter events, 14.2 us)
Async XLA Ops:
  0.6 8.5 %copy-start.29 = (s32[4]{0:T(128)S(1)}, s32[4]{0:T(128)}, u32[]{:S(2)}) copy-start(s32[4]{0:T(128)} %param.30) | copy-start | bytes 52
  0.7 11.6 %slice-start = ((f32[57,800]{1,0:T(8,128)}), f32[50,800]{1,0:T(8,128)S(1)}, s32[]{:S(2)}) async-start(f32[57,800]{1,0:T(8,128)} %param.23), calls=%async_computation | async-start | bytes 401408 | tf_op jit(solution)/shard_map/slice | solution.py:1357
  4.3 9.2 %copy-start.2 = (f32[2,576,128]{2,1,0:T(8,128)}, f32[2,576,128]{2,1,0:T(8,128)S(1)}, u32[]{:S(2)}) copy-start(f32[2,576,128]{2,1,0:T(8,128)S(1)} %broadcast_in_dim.65.m_ref) | copy-start | bytes 1769476
  4.3 1.8 copy-start.1
  6.1 7.3 %copy-start.15 = (f32[4,100,400]{2,0,1:T(4,128)S(1)}, f32[4,100,400]{2,0,1:T(4,128)}, u32[]{:S(2)}) copy-start(f32[4,100,400]{2,0,1:T(4,128)} %param.18) | copy-start | bytes 1920004
  7.1 1.0 copy-start.8
  15.1 124.7 %copy-start.18 = (f32[57,800]{1,0:T(8,128)S(1)}, f32[57,800]{1,0:T(8,128)}, u32[]{:S(2)}) copy-start(f32[57,800]{1,0:T(8,128)} %param.23) | copy-start | bytes 547204
  123.9 24.2 %copy-start.30 = (s32[16]{0:T(128)S(1)}, s32[16]{0:T(128)}, u32[]{:S(2)}) copy-start(s32[16]{0:T(128)} %param.29) | copy-start | bytes 196
  144.9 1.3 copy-start.12
  146.2 1.2 copy-start.13
  234.2 12.7 %copy-start.27 = (f32[8,1,400]{2,1,0:T(1,128)S(1)}, f32[8,1,400]{2,1,0:T(1,128)}, u32[]{:S(2)}) copy-start(f32[8,1,400]{2,1,0:T(1,128)} %get-tuple-element.54) | copy-start | bytes 38404
  234.2 12.9 %copy-start.28 = (f32[1,800]{1,0:T(1,128)S(1)}, f32[1,800]{1,0:T(1,128)}, u32[]{:S(2)}) copy-start(f32[1,800]{1,0:T(1,128)} %get-tuple-element.53) | copy-start | bytes 9604
  234.2 21.2 %copy-start.3 = (f32[2,576,128]{2,1,0:T(8,128)S(1)}, f32[2,576,128]{2,1,0:T(8,128)}, u32[]{:S(2)}) copy-start(f32[2,576,128]{2,1,0:T(8,128)} %copy-done.2) | copy-start | bytes 1769476
  255.4 2.2 copy-start
  257.6 2.2 copy-start.9
  262.2 2.0 copy-start.5
  264.2 1.0 copy-start.11
  265.2 142.3 %copy-start.17 = (f32[4,800,100]{1,0,2:T(4,128)S(1)}, f32[4,800,100]{1,0,2:T(4,128)}, u32[]{:S(2)}) copy-start(f32[4,800,100]{1,0,2:T(4,128)} %param.21) | copy-start | bytes 3840004
  406.7 2.7 copy-start.22
  406.7 3.8 copy-start.23
  411.7 12.4 %copy-start.4 = (f32[2,576,128]{2,1,0:T(8,128)S(1)}, f32[2,576,128]{2,1,0:T(8,128)}, u32[]{:S(2)}) copy-start(f32[2,576,128]{2,1,0:T(8,128)} %copy-done.2) | copy-start | bytes 1769476
  411.7 12.4 %copy-start.6 = (f32[50,8,800]{2,1,0:T(8,128)S(1)}, f32[50,8,800]{2,1,0:T(8,128)}, u32[]{:S(2)}) copy-start(f32[50,8,800]{2,1,0:T(8,128)} %broadcast_in_dim.66.t_ref.w_ref) | copy-start | bytes 3840004
  411.7 12.4 %copy-start.7 = (bf16[1,2,24,24,800]{4,3,2,1,0:T(8,128)(2,1)S(1)}, bf16[1,2,24,24,800]{4,3,2,1,0:T(8,128)(2,1)}, u32[]{:S(2)}) copy-start(bf16[1,2,24,24,800]{4,3,2,1,0:T(8,128)(2,1)} %param.17) | copy-start | bytes 5529604
  424.1 1.3 copy-start.10
  476.3 1.1 copy-start.16
  476.6 3.6 copy-start.21
  477.4 4.2 copy-start.20
  477.7 5.3 %copy-start.19 = (f32[57,800]{1,0:T(8,128)S(1)}, f32[57,800]{1,0:T(8,128)}, u32[]{:S(2)}) copy-start(f32[57,800]{1,0:T(8,128)} %param.23) | copy-start | bytes 547204
  477.8 5.3 %copy-start.24 = (f32[57,800]{1,0:T(8,128)S(1)}, f32[57,800]{1,0:T(8,128)}, u32[]{:S(2)}) copy-start(f32[57,800]{1,0:T(8,128)} %param.24) | copy-start | bytes 547204
  477.8 5.3 %copy-start.25 = (f32[57,800]{1,0:T(8,128)S(1)}, f32[57,800]{1,0:T(8,128)}, u32[]{:S(2)}) copy-start(f32[57,800]{1,0:T(8,128)} %param.25) | copy-start | bytes 547204
  477.8 5.2 %copy-start.26 = (f32[64,896]{1,0:T(8,128)S(1)}, f32[64,896]{1,0:T(8,128)}, u32[]{:S(2)}) copy-start(f32[64,896]{1,0:T(8,128)} %get-tuple-element.62) | copy-start | bytes 688132
  479.2 4.8 copy-start.14

commit v11 on v10

--- a/solution.py
+++ b/solution.py
@@ -489,7 +489,7 @@
         own_a = own["a"]
         row_of = lambda a, b: pl.ds(pl.multiple_of((b * side_a + a) * piece, 16), piece)
         part_row = lambda a: pl.ds(pl.multiple_of(a * piece, 16), piece)
-        turns = [*range(1, side_a), 0]
+        turns = [*range(side_a - 1, 0, -1), 0]
         cores, loads = [], []
         for i, (k, m) in enumerate(order):
             at = index(k, m)
@@ -896,7 +896,7 @@
         half = lambda b: pl.ds(pl.multiple_of(b * part, 16), part)
         row_of = lambda a, b: pl.ds(pl.multiple_of((b * side_a + a) * piece, 16), piece)
         part_row = lambda a: pl.ds(pl.multiple_of(a * piece, 16), piece)
-        turns = [*range(1, side_a), 0]
+        turns = [*range(side_a - 1, 0, -1), 0]
         firsts, seconds, loads = {}, {}, []
         for m in range(pairs):
             for k in turns:

time: 487 us -> 481 us (0.988)
  Pallas kernels: 438 us -> 429 us
    pallas_call x1, Pallas kernels: 141 us -> 136 us  [exchange_backward(): pl.pallas_call(kernel, grid=(n_chunk, slots), in_specs=[any_space, any_sp...]
where the time goes in v11:
time: 481 us; the launch traced here: 477 us
  Pallas kernels  429 us (89%)
  local copies, waits for them, and re-layouts  37 us (8%)
  other arithmetic  7.37 us (2%)
    pallas_call x1, Pallas kernels, exchange_backward(): pl.pallas_call(kernel, grid=(n_chunk, slots), in_specs=[any_space, any_sp...  136 us
    pallas_call x1, Pallas kernels, exchange_forward(): pl.pallas_call(kernel, grid=(last + 1,), in_specs=[any_space] * 3 + [pl.B...  109 us
    pallas_call x1, Pallas kernels, feed_forward(): pl.pallas_call(kernel, grid_spec=pltpu.PrefetchScalarGridSpec(num_scalar_...  84.9 us
    pallas_call x1, Pallas kernels, conv_backward(): pl.pallas_call(kernel, grid=(n_chunk, slots), in_specs=[pl.BlockSpec((1,...  47.5 us
    unnamed x70, local copies, waits for them, and re-layouts  26.1 us
    pallas_call x2, Pallas kernels, tile_total(): pl.pallas_call(kernel, in_specs=[whole], out_specs=whole, out_shape=jax.S...  19.6 us
    pallas_call x1, Pallas kernels, rotate(): pl.pallas_call(kernel, grid=(pairs,), in_specs=[pl.BlockSpec(memory_space...  12.3 us
    pallas_call x1, Pallas kernels, close_out(): pl.pallas_call(kernel, grid=(rows // step,), in_specs=[line(depth), line(...  11.3 us

profile of v11, /device:TPU:8, one launch (start us, length us, event | category | flops | bytes accessed | tf_op | source)
XLA Modules:
  0.0 477.0 jit_solution(4079121948950376419)
XLA Ops:
  0.7 1.3 dynamic_slice.6
  2.6 1.4 fusion.7
  4.4 1.8 copy-done.1
  7.1 1.0 copy-done.8
  8.1 1.0 broadcast_in_dim.68.f_ref.m_ref
  12.2 1.2 broadcast_in_dim.66.t_ref.w_ref
  15.1 108.8 %exchange_forward.1 = (bf16[7,2,5,72,128]{4,3,2,1,0:T(8,128)(2,1)}, bf16[2,4,896,800]{3,2,1,0:T(8,128)(2,1)}, s32[8,2,8]{2,1,0:T(2,128)}, f32[2,576,800]{2,1,0:T...) custom-call(bf16[7,2,4,72,128]{4,3,2,1,0:T(8,128)(2,1)} %copy-done.8, ...), custom_call_target="tpu_custom_call" | custom-call | tf_op jit(solution)/shard_map/exchange_forward/pallas_call | solution.py:415
  123.9 0.9 reduce_sum.56
  125.5 12.5 %tile_total.2 = f32[3,800]{1,0:T(4,128)S(1)} custom-call(f32[3,800]{1,0:T(4,128)S(1)} %concatenate.9.v_ref), custom_call_target="tpu_custom_call" | custom-call | tf_op jit(solution)/shard_map/tile_total/pallas_call | solution.py:739
  139.8 5.1 %arrange_shaped.1 = (bf16[1152,896]{1,0:T(8,128)(2,1)S(1)}, bf16[800,1152]{1,0:T(8,128)(2,1)S(1)}, f32[1,800]{1,0:T(1,128)}) custom-call(f32[1152,800]{1,0:T(8,128)} %bitcast.43, f32[4,800]{1,0:T(4,128)S(1)} %pad_maximum_fusion.1.refs_1_), custom_call_target="tpu_custom_call" | custom-call | tf_op jit(solution)/shard_map/arrange_shaped/pallas_call | solution.py:1040
  144.9 1.3 copy-done.12
  146.2 1.2 copy-done.13
  148.7 84.9 %feed_forward.1 = (f32[1152,896]{1,0:T(8,128)}, f32[1152,896]{1,0:T(8,128)}, bf16[2,4,896,800]{3,2,1,0:T(8,128)(2,1)}, f32[8,1,400]{2,1,0:T(1,128)}) custom-call(s32[16]{0:T(128)} %select_reduce_fusion.inv_ref, bf16[1152,896]{1,0:T(8,128)(2,1)} %copy-done.12, bf16[800,1152]{1,0:T(8,128)(2,1)} %copy-done.13, bf16[1152,896]{1,0:T(8,128)(2,1)} %get-tuple-element.40.d_ref, ...), custom_call_target="tpu_custom_call" | custom-call | flops 35389440000 | bytes 41943040 | tf_op jit(solution)/shard_map/feed_forward/pallas_call | solution.py:1156
  234.2 11.3 %close_out.1 = (bf16[1152,800]{1,0:T(8,128)(2,1)}, f32[1152,800]{1,0:T(8,128)}, f32[2,1,800]{2,1,0:T(1,128)}) custom-call(f32[1152,896]{1,0:T(8,128)} %get-tuple-element.43.b_ref, f32[1152,896]{1,0:T(8,128)} %get-tuple-element.44.d_ref, bf16[1152,800]{1,0:T(8,128)(2,1)} %bitcast.46, f32[1152,800]{1,0:T(8,128)} %bitcast.44, ...), custom_call_target="tpu_custom_call" | custom-call | tf_op jit(solution)/shard_map/close_out/pallas_call | solution.py:1214
  247.7 7.1 %tile_total.3 = f32[2,800]{1,0:T(2,128)S(1)} custom-call(f32[2,800]{1,0:T(2,128)S(1)} %pad_maximum_fusion.3.v_ref), custom_call_target="tpu_custom_call" | custom-call | tf_op jit(solution)/shard_map/tile_total/pallas_call | solution.py:739
  255.4 2.2 copy-done
  257.6 2.2 copy-done.9
  259.7 2.5 conv_gradient.1
  262.2 2.0 copy-done.5
  264.2 1.0 copy-done.11
  265.2 135.8 %exchange_backward.1 = (bf16[7,2,5,72,128]{4,3,2,1,0:T(8,128)(2,1)}, bf16[2,896,800]{2,1,0:T(8,128)(2,1)}, f32[64,896]{1,0:T(8,128)}) custom-call(bf16[7,2,4,72,128]{4,3,2,1,0:T(8,128)(2,1)} %copy-done.11, bf16[2,4,896,800]{3,2,1,0:T(8,128)(2,1)} %get-tuple-element.50.g_ref, s32[8,2,8]{2,1,0:T(2,128)} %get-tuple-element.51.n_ref, ...), custom_call_target="tpu_custom_call" | custom-call | tf_op jit(solution)/shard_map/exchange_backward/pallas_call | solution.py:683
  401.9 1.8 copy.44.l_ref
  403.7 1.2 copy.45.one_ref
  404.9 1.2 copy.46.two_ref
  406.1 12.3 %rotate.1 = (f32[4,100,400]{2,1,0:T(8,128)}, f32[4,100,400]{2,1,0:T(8,128)}, bf16[2,896,800]{2,1,0:T(8,128)(2,1)}) custom-call(f32[1]{0:T(128)} %bitcast.20.f_ref, bf16[2,896,800]{2,1,0:T(8,128)(2,1)} %get-tuple-element.56.g_ref, f32[4,800,100]{2,1,0:T(8,128)} %copy.44.l_ref, f32[4,400,400]{2,1,0:T(8,128)} %c_ref.1, f32[4,100,400]{2,1,0:T(8,128)} %copy.45.one_ref, ...), custom_call_target="tpu_custom_call" | custom-call | tf_op jit(solution)/shard_map/rotate/pallas_call | solution.py:1283
  418.5 1.3 copy-done.10
  419.8 47.5 %conv_backward.1 = (f32[2,576,800]{2,1,0:T(8,128)}, f32[2,112,800]{2,1,0:T(8,128)S(1)}) custom-call(f32[2,576,800]{2,1,0:T(8,128)} %copy-done.5, bf16[2,24,24,800]{3,2,1,0:T(8,128)(2,1)S(1)} %bitcast.50, f32[2,576,128]{2,1,0:T(8,128)S(1)} %copy-done.4, f32[50,8,800]{2,1,0:T(8,128)S(1)} %copy-done.6, f32[8,128]{1,0:T(8,128)S(1)} %broadcast_in_dim.77.l_ref, ...), custom_call_target="tpu_custom_call" | custom-call | tf_op jit(solution)/shard_map/conv_backward/pallas_call | solution.py:964
  468.8 1.4 copy.48
  470.2 1.0 copy.49
  471.2 1.4 copy.50
  472.6 1.4 copy.51
  475.0 2.0 copy.57
  (108 shorter events, 14.2 us)
Async XLA Ops:
  0.6 8.5 %copy-start.29 = (s32[4]{0:T(128)S(1)}, s32[4]{0:T(128)}, u32[]{:S(2)}) copy-start(s32[4]{0:T(128)} %param.30) | copy-start | bytes 52
  0.7 11.6 %slice-start = ((f32[57,800]{1,0:T(8,128)}), f32[50,800]{1,0:T(8,128)S(1)}, s32[]{:S(2)}) async-start(f32[57,800]{1,0:T(8,128)} %param.23), calls=%async_computation | async-start | bytes 401408 | tf_op jit(solution)/shard_map/slice | solution.py:1357
  4.3 9.2 %copy-start.2 = (f32[2,576,128]{2,1,0:T(8,128)}, f32[2,576,128]{2,1,0:T(8,128)S(1)}, u32[]{:S(2)}) copy-start(f32[2,576,128]{2,1,0:T(8,128)S(1)} %broadcast_in_dim.65.m_ref) | copy-start | bytes 1769476
  4.3 1.8 copy-start.1
  6.1 7.3 %copy-start.15 = (f32[4,100,400]{2,0,1:T(4,128)S(1)}, f32[4,100,400]{2,0,1:T(4,128)}, u32[]{:S(2)}) copy-start(f32[4,100,400]{2,0,1:T(4,128)} %param.18) | copy-start | bytes 1920004
  7.1 1.0 copy-start.8
  15.1 124.7 %copy-start.18 = (f32[57,800]{1,0:T(8,128)S(1)}, f32[57,800]{1,0:T(8,128)}, u32[]{:S(2)}) copy-start(f32[57,800]{1,0:T(8,128)} %param.23) | copy-start | bytes 547204
  123.9 24.2 %copy-start.30 = (s32[16]{0:T(128)S(1)}, s32[16]{0:T(128)}, u32[]{:S(2)}) copy-start(s32[16]{0:T(128)} %param.29) | copy-start | bytes 196
  144.9 1.3 copy-start.12
  146.2 1.2 copy-start.13
  234.2 12.7 %copy-start.27 = (f32[8,1,400]{2,1,0:T(1,128)S(1)}, f32[8,1,400]{2,1,0:T(1,128)}, u32[]{:S(2)}) copy-start(f32[8,1,400]{2,1,0:T(1,128)} %get-tuple-element.54) | copy-start | bytes 38404
  234.2 12.9 %copy-start.28 = (f32[1,800]{1,0:T(1,128)S(1)}, f32[1,800]{1,0:T(1,128)}, u32[]{:S(2)}) copy-start(f32[1,800]{1,0:T(1,128)} %get-tuple-element.53) | copy-start | bytes 9604
  234.2 21.2 %copy-start.3 = (f32[2,576,128]{2,1,0:T(8,128)S(1)}, f32[2,576,128]{2,1,0:T(8,128)}, u32[]{:S(2)}) copy-start(f32[2,576,128]{2,1,0:T(8,128)} %copy-done.2) | copy-start | bytes 1769476
  255.4 2.2 copy-start
  257.6 2.2 copy-start.9
  262.2 2.0 copy-start.5
  264.2 1.0 copy-start.11
  265.2 136.7 %copy-start.17 = (f32[4,800,100]{1,0,2:T(4,128)S(1)}, f32[4,800,100]{1,0,2:T(4,128)}, u32[]{:S(2)}) copy-start(f32[4,800,100]{1,0,2:T(4,128)} %param.21) | copy-start | bytes 3840004
  401.1 2.7 copy-start.22
  401.1 3.8 copy-start.23
  406.1 12.4 %copy-start.4 = (f32[2,576,128]{2,1,0:T(8,128)S(1)}, f32[2,576,128]{2,1,0:T(8,128)}, u32[]{:S(2)}) copy-start(f32[2,576,128]{2,1,0:T(8,128)} %copy-done.2) | copy-start | bytes 1769476
  406.1 12.4 %copy-start.6 = (f32[50,8,800]{2,1,0:T(8,128)S(1)}, f32[50,8,800]{2,1,0:T(8,128)}, u32[]{:S(2)}) copy-start(f32[50,8,800]{2,1,0:T(8,128)} %broadcast_in_dim.66.t_ref.w_ref) | copy-start | bytes 3840004
  406.1 12.4 %copy-start.7 = (bf16[1,2,24,24,800]{4,3,2,1,0:T(8,128)(2,1)S(1)}, bf16[1,2,24,24,800]{4,3,2,1,0:T(8,128)(2,1)}, u32[]{:S(2)}) copy-start(bf16[1,2,24,24,800]{4,3,2,1,0:T(8,128)(2,1)} %param.17) | copy-start | bytes 5529604
  418.5 1.3 copy-start.10
  467.3 1.1 copy-start.16
  467.6 3.6 copy-start.21
  468.5 4.2 copy-start.20
  468.8 5.3 %copy-start.19 = (f32[57,800]{1,0:T(8,128)S(1)}, f32[57,800]{1,0:T(8,128)}, u32[]{:S(2)}) copy-start(f32[57,800]{1,0:T(8,128)} %param.23) | copy-start | bytes 547204
  468.8 5.3 %copy-start.24 = (f32[57,800]{1,0:T(8,128)S(1)}, f32[57,800]{1,0:T(8,128)}, u32[]{:S(2)}) copy-start(f32[57,800]{1,0:T(8,128)} %param.24) | copy-start | bytes 547204
  468.8 5.3 %copy-start.25 = (f32[57,800]{1,0:T(8,128)S(1)}, f32[57,800]{1,0:T(8,128)}, u32[]{:S(2)}) copy-start(f32[57,800]{1,0:T(8,128)} %param.25) | copy-start | bytes 547204
  468.8 5.2 %copy-start.26 = (f32[64,896]{1,0:T(8,128)S(1)}, f32[64,896]{1,0:T(8,128)}, u32[]{:S(2)}) copy-start(f32[64,896]{1,0:T(8,128)} %get-tuple-element.62) | copy-start | bytes 688132
  470.2 4.8 copy-start.14
